TPU v7x, 32 devices: a whole 2x2x4 slice. The times are simulated.
32 devices in a mesh: img: 4 (over z), ch: 8 (over y, x, core).
Axes of the slice: x: 2, y: 2, z: 4, core: 2. Of those that a mesh axis runs over, the one named last changes fastest.
Arguments:
- features: bfloat16 [1024, 4, 576], P('ch', 'img'), may hold values from -6 to 6
- grid: int32 [4], P('img'), may hold values from 16 to 24, as said below
- reduce_w: bfloat16 [2, 1024, 256], P(None, None, 'ch'), may hold values from -0.1875 to 0.1875
- conv_w: bfloat16 [2, 9, 256, 256], P(None, None, None, 'ch'), may hold values from -0.125 to 0.125
- expand_w: bfloat16 [2, 256, 1024], P(None, 'ch'), may hold values from -0.375 to 0.375
- mid_gain: float32 [2, 2, 256], P(None, None, 'ch'), may hold values from 0.5 to 1.5
- mid_bias: float32 [2, 2, 256], P(None, None, 'ch'), may hold values from -2 to 2
- out_gain: float32 [2, 1024], P(None, 'ch'), may hold values from 0.5 to 1.5
- out_bias: float32 [2, 1024], P(None, 'ch'), may hold values from -2 to 2
- read_w1: bfloat16 [1024, 4096], P(None, 'ch'), may hold values from -0.1875 to 0.1875
- read_b1: float32 [4096], P('ch'), may hold values from -2 to 2
- read_w2: bfloat16 [4096, 4096], P('ch'), may hold values from -0.09375 to 0.09375
- read_b2: float32 [4096], P('ch'), may hold values from -2 to 2
- cotangent: bfloat16 [4096, 4, 144], P('ch', 'img'), may hold values from -6 to 6
Outputs:
- tokens: bfloat16 [4096, 4, 144], P('ch', 'img')
- features_grad: float32 [1024, 4, 576], P('ch', 'img')
- reduce_w_grad: float32 [2, 1024, 256], P(None, None, 'ch')
- conv_w_grad: float32 [2, 9, 256, 256], P(None, None, None, 'ch')
- expand_w_grad: float32 [2, 256, 1024], P(None, 'ch')
- mid_gain_grad: float32 [2, 2, 256], P(None, None, 'ch')
- mid_bias_grad: float32 [2, 2, 256], P(None, None, 'ch')
- out_gain_grad: float32 [2, 1024], P(None, 'ch')
- out_bias_grad: float32 [2, 1024], P(None, 'ch')
- read_w1_grad: float32 [1024, 4096], P(None, 'ch')
- read_b1_grad: float32 [4096], P('ch')
- read_w2_grad: float32 [4096, 4096], P('ch')
- read_b2_grad: float32 [4096], P('ch')
Inputs may be any that keep to these rules, and one draw needn't show every extreme that they name: `grid`: each image is 16 or 24 patches a side; both sides occur in every draw.
All inputs are finite; a program needn't handle non-finite values.
Results may differ from a plain program's by a relative error of at most 0.028.
Values may be sent and summed in bfloat16 or wider, within the bound.
No kernel may reach another device: no remote copies, remote signals or barrier semaphores. Data moves between devices by JAX's collectives and lax.ppermute only.
A program may use at most 128 MiB of HBM per device.

v0:
```python
import jax
import jax.numpy as jnp
from jax import lax
from jax.sharding import PartitionSpec as P

GRID = 24
POOLED = 12


PRECISE = lax.Precision.HIGHEST
EPSILON = 1e-06
OFFSETS = [(-1, -1), (-1, 0), (-1, 1), (0, -1), (0, 0), (0, 1), (1, -1), (1, 0), (1, 1)]


def valid_mask(grid, side):
    place = jnp.arange(side, dtype=jnp.int32)
    inside = (place[None, :] < grid[:, None]).astype(jnp.float32)
    return (inside[:, :, None] * inside[:, None, :]).reshape(grid.shape[0], side * side)


def pool_table(grid):
    target = jnp.arange(POOLED, dtype=jnp.int32)
    place = jnp.arange(GRID, dtype=jnp.int32)
    extent = grid[:, None]
    begin = target[None, :] * extent // POOLED
    finish = ((target[None, :] + 1) * extent + POOLED - 1) // POOLED
    inside = (place[None, None, :] >= begin[:, :, None]) & (
        place[None, None, :] < finish[:, :, None]
    )
    return inside.astype(jnp.float32) / (finish - begin)[:, :, None].astype(jnp.float32)


def shifted(field, side, rise, step):
    leading = field.shape[:-1]
    square = field.reshape(leading + (side, side))
    padded = jnp.pad(square, [(0, 0)] * len(leading) + [(1, 1), (1, 1)])
    window = padded[..., 1 + rise : 1 + rise + side, 1 + step : 1 + step + side]
    return window.reshape(leading + (side * side,))


def pooled_of(field, table):
    square = field.reshape(field.shape[0], field.shape[1], GRID, GRID)
    across = jnp.einsum("cbrk,bir->cbik", square, table, precision=PRECISE)
    result = jnp.einsum("cbik,bjk->cbij", across, table, precision=PRECISE)
    return result.reshape(field.shape[0], field.shape[1], POOLED * POOLED)


def spread_back(upstream, table):
    square = upstream.reshape(upstream.shape[0], upstream.shape[1], POOLED, POOLED)
    across = jnp.einsum("cbij,bjk->cbik", square, table, precision=PRECISE)
    result = jnp.einsum("cbik,bir->cbrk", across, table, precision=PRECISE)
    return result.reshape(upstream.shape[0], upstream.shape[1], GRID * GRID)


def silu_grad(values, upstream):
    return jax.vjp(jax.nn.silu, values)[1](upstream)[0]


def gelu_grad(values, upstream):
    return jax.vjp(jax.nn.gelu, values)[1](upstream)[0]


def gather_channels(local):
    return lax.all_gather(local, "ch", axis=0, tiled=True)


def gather_grads(local):
    return lax.all_gather(local, "ch", axis=0, tiled=True)


def spread_sum(weight, data):
    return lax.psum_scatter(
        jnp.einsum("mc,mbs->cbs", weight, data, preferred_element_type=jnp.float32),
        "ch",
        scatter_dimension=0,
        tiled=True,
    )


def gather_sum(weight, data):
    return lax.psum_scatter(
        jnp.einsum("cm,mbs->cbs", weight, data, preferred_element_type=jnp.float32).astype(
            jnp.bfloat16
        ),
        "ch",
        scatter_dimension=0,
        tiled=True,
    ).astype(jnp.float32)


def norm_forward(values, gain, bias):
    total = values.shape[0] * lax.axis_size("ch")
    first_sum, second_sum = lax.psum(
        (jnp.sum(values, axis=0), jnp.sum(values * values, axis=0)), "ch"
    )
    center = first_sum / total
    spread = second_sum / total - center * center
    factor = lax.rsqrt(spread + EPSILON)
    unit = (values - center) * factor
    return (unit * gain[:, None, None] + bias[:, None, None], unit, factor)


def norm_backward(upstream, unit, factor, gain):
    total = unit.shape[0] * lax.axis_size("ch")
    scaled = upstream * gain[:, None, None]
    first_sum, second_sum = lax.psum(
        (jnp.sum(scaled, axis=0), jnp.sum(scaled * unit, axis=0)), "ch"
    )
    values_grad = factor * (scaled - first_sum / total - unit * (second_sum / total))
    return (values_grad, jnp.sum(upstream * unit, axis=(1, 2)), jnp.sum(upstream, axis=(1, 2)))


def block_forward(inputs, weights, layer, mask, side):
    reduce_w, conv_w, expand_w, mid_gain, mid_bias, out_gain, out_bias = weights
    source = gather_channels(inputs)
    reduced = jnp.einsum("cm,cbs->mbs", reduce_w[layer], source, preferred_element_type=jnp.float32)
    first_norm, first_unit, first_factor = norm_forward(
        reduced, mid_gain[layer, 0], mid_bias[layer, 0]
    )
    first_act = (jax.nn.silu(first_norm) * mask).astype(jnp.bfloat16)
    conv_source = lax.all_gather(first_act, "ch", axis=0, tiled=True)
    conv_out = jnp.zeros((conv_w.shape[3],) + conv_source.shape[1:], jnp.float32)
    for index, (rise, step) in enumerate(OFFSETS):
        conv_out = conv_out + jnp.einsum(
            "mbs,mn->nbs",
            shifted(conv_source, side, rise, step),
            conv_w[layer, index],
            preferred_element_type=jnp.float32,
        )
    second_norm, second_unit, second_factor = norm_forward(
        conv_out, mid_gain[layer, 1], mid_bias[layer, 1]
    )
    second_act = jax.nn.silu(second_norm).astype(jnp.bfloat16)
    expanded = spread_sum(expand_w[layer], second_act)
    third_norm, third_unit, third_factor = norm_forward(expanded, out_gain[layer], out_bias[layer])
    summed = third_norm + inputs.astype(jnp.float32)
    result = jax.nn.silu(summed) * mask
    saved = (
        source,
        first_norm,
        first_unit,
        first_factor,
        conv_source,
        second_norm,
        second_unit,
        second_factor,
        second_act,
        third_unit,
        third_factor,
        summed,
    )
    return (result, saved)


def block_backward(upstream, inputs, weights, layer, mask, side):
    reduce_w, conv_w, expand_w, mid_gain, mid_bias, out_gain, out_bias = weights
    result, saved = block_forward(inputs, weights, layer, mask, side)
    (
        source,
        first_norm,
        first_unit,
        first_factor,
        conv_source,
        second_norm,
        second_unit,
        second_factor,
        second_act,
        third_unit,
        third_factor,
        summed,
    ) = saved
    summed_grad = silu_grad(summed, upstream * mask)
    expanded_grad, out_gain_grad, out_bias_grad = norm_backward(
        summed_grad, third_unit, third_factor, out_gain[layer]
    )
    expanded_full = gather_grads(expanded_grad.astype(jnp.bfloat16))
    act_grad = jnp.einsum(
        "mc,cbs->mbs", expand_w[layer], expanded_full, preferred_element_type=jnp.float32
    )
    expand_grad = jnp.einsum(
        "mbs,cbs->mc", second_act, expanded_full, preferred_element_type=jnp.float32
    )
    conv_grad, second_gain, second_bias = norm_backward(
        silu_grad(second_norm, act_grad), second_unit, second_factor, mid_gain[layer, 1]
    )
    conv_low = conv_grad.astype(jnp.bfloat16)
    source_grad = jnp.zeros(conv_source.shape, jnp.float32)
    kernel_grads = []
    for index, (rise, step) in enumerate(OFFSETS):
        kernel_grads.append(
            jnp.einsum(
                "mbs,nbs->mn",
                shifted(conv_source, side, rise, step),
                conv_low,
                preferred_element_type=jnp.float32,
            )
        )
        back_term = jnp.einsum(
            "mn,nbs->mbs", conv_w[layer, index], conv_low, preferred_element_type=jnp.float32
        )
        source_grad = source_grad + shifted(back_term, side, -rise, -step)
    first_act_grad = lax.psum_scatter(
        source_grad.astype(jnp.bfloat16), "ch", scatter_dimension=0, tiled=True
    ).astype(jnp.float32)
    reduced_grad, first_gain, first_bias = norm_backward(
        silu_grad(first_norm, first_act_grad * mask), first_unit, first_factor, mid_gain[layer, 0]
    )
    reduced_low = reduced_grad.astype(jnp.bfloat16)
    reduce_grad = jnp.einsum("cbs,mbs->cm", source, reduced_low, preferred_element_type=jnp.float32)
    inputs_grad = gather_sum(reduce_w[layer], reduced_low)
    inputs_grad = inputs_grad + summed_grad
    grads = (
        reduce_grad,
        jnp.stack(kernel_grads),
        expand_grad,
        jnp.stack([first_gain, second_gain]),
        jnp.stack([first_bias, second_bias]),
        out_gain_grad,
        out_bias_grad,
    )
    return (inputs_grad, grads)


def per_device(
    features,
    grid,
    reduce_w,
    conv_w,
    expand_w,
    mid_gain,
    mid_bias,
    out_gain,
    out_bias,
    read_w1,
    read_b1,
    read_w2,
    read_b2,
    cotangent,
):
    weights = (reduce_w, conv_w, expand_w, mid_gain, mid_bias, out_gain, out_bias)
    mask = valid_mask(grid, GRID)[None]
    table = pool_table(grid)
    first, unused_first = block_forward(features, weights, 0, mask, GRID)
    pooled = pooled_of(first, table).astype(jnp.bfloat16)
    second, unused_second = block_forward(pooled, weights, 1, 1.0, POOLED)
    readin = second.astype(jnp.bfloat16)
    readin_full = gather_channels(readin)
    hidden = (
        jnp.einsum("cbt,ch->hbt", readin_full, read_w1, preferred_element_type=jnp.float32)
        + read_b1[:, None, None]
    )
    hidden_act = jax.nn.gelu(hidden).astype(jnp.bfloat16)
    tokens = (spread_sum(read_w2, hidden_act) + read_b2[:, None, None]).astype(jnp.bfloat16)
    second_b_grad = jnp.sum(cotangent.astype(jnp.float32), axis=(1, 2))
    grad_full = gather_grads(cotangent)
    act_grad = jnp.einsum("ho,obt->hbt", read_w2, grad_full, preferred_element_type=jnp.float32)
    second_w_grad = jnp.einsum(
        "hbt,obt->ho", hidden_act, grad_full, preferred_element_type=jnp.float32
    )
    hidden_low = gelu_grad(hidden, act_grad).astype(jnp.bfloat16)
    first_b_grad = jnp.sum(hidden_low.astype(jnp.float32), axis=(1, 2))
    first_w_grad = jnp.einsum(
        "cbt,hbt->ch", readin_full, hidden_low, preferred_element_type=jnp.float32
    )
    second_grad = gather_sum(read_w1, hidden_low)
    pooled_grad, post_grads = block_backward(second_grad, pooled, weights, 1, 1.0, POOLED)
    first_grad = spread_back(pooled_grad, table)
    features_grad, pre_grads = block_backward(first_grad, features, weights, 0, mask, GRID)
    stacked = [jnp.stack([early, later]) for early, later in zip(pre_grads, post_grads)]
    reduce_grad, kernel_grad, expand_grad, gain_grad, bias_grad, outgain_grad, outbias_grad = (
        stacked
    )
    totals = (
        lax.psum(reduce_grad.astype(jnp.bfloat16), "img").astype(jnp.float32),
        lax.psum(kernel_grad.astype(jnp.bfloat16), "img").astype(jnp.float32),
        lax.psum(expand_grad.astype(jnp.bfloat16), "img").astype(jnp.float32),
        lax.psum(gain_grad.astype(jnp.bfloat16), "img").astype(jnp.float32),
        lax.psum(bias_grad.astype(jnp.bfloat16), "img").astype(jnp.float32),
        lax.psum(outgain_grad.astype(jnp.bfloat16), "img").astype(jnp.float32),
        lax.psum(outbias_grad.astype(jnp.bfloat16), "img").astype(jnp.float32),
        lax.psum(first_w_grad.astype(jnp.bfloat16), "img").astype(jnp.float32),
        lax.psum(first_b_grad.astype(jnp.bfloat16), "img").astype(jnp.float32),
        lax.psum(second_w_grad.astype(jnp.bfloat16), "img").astype(jnp.float32),
        lax.psum(second_b_grad.astype(jnp.bfloat16), "img").astype(jnp.float32),
    )
    return (tokens, features_grad) + tuple(totals)


def solution(mesh):
    return jax.shard_map(
        per_device,
        mesh=mesh,
        in_specs=(
            P("ch", "img", None),
            P("img"),
            P(None, None, "ch"),
            P(None, None, None, "ch"),
            P(None, "ch", None),
            P(None, None, "ch"),
            P(None, None, "ch"),
            P(None, "ch"),
            P(None, "ch"),
            P(None, "ch"),
            P("ch"),
            P("ch", None),
            P("ch"),
            P("ch", "img", None),
        ),
        out_specs=(
            P("ch", "img", None),
            P("ch", "img", None),
            P(None, None, "ch"),
            P(None, None, None, "ch"),
            P(None, "ch", None),
            P(None, None, "ch"),
            P(None, None, "ch"),
            P(None, "ch"),
            P(None, "ch"),
            P(None, "ch"),
            P("ch"),
            P("ch", None),
            P("ch"),
        ),
        check_vma=False,
    )
```

profile of v0, /device:TPU:0, one launch (start us, length us, event | category | flops | bytes accessed | tf_op | source)
XLA Modules:
  0.0 909.5 jit_solution(13346404330440405244)
XLA Ops:
  10.3 26.5 %all-gather.6.cloned.1.call-done = bf16[1024,1,576]{0,2,1:T(8,128)(2,1)} async-done(((bf16[128,1,576]{0,2,1:T(8,128)(2,1)}), bf16[1024,1,576]{0,2,1:T(8,128)(2,1)}) %all-gather.6.cloned.1.call-update) | async-done | bytes 1179664 | tf_op jit(solution)/shard_map/all_gather | solution.py:64
  36.8 1.8 fusion.266
  38.6 13.3 %all-reduce.31 = (f32[1,576]{1,0:T(1,128)S(1)}, f32[1,576]{1,0:T(1,128)S(1)}) all-reduce(f32[1,576]{1,0:T(1,128)S(1)} %reduce_sum.445, f32[1,576]{1,0:T(1,128)S(1)} %reduce_sum.447), channel_id=1, replica_groups=mesh['img'=4,'ch'=8] {'ch'}, use_global_device_ids=true, to_apply=%region_1.2 | all-reduce | flops 1152 | bytes 9216 | tf_op jit(solution)/shard_map/psum | solution.py:93
  52.7 9.4 %all-gather = bf16[256,576]{1,0:T(8,128)(2,1)S(1)} all-gather(bf16[32,576]{1,0:T(8,128)(2,1)S(1)} %multiply_convert_fusion.3), channel_id=2, replica_groups=mesh['img'=4,'ch'=8] {'ch'}, dimensions={0}, use_global_device_ids=true | all-gather | bytes 331776 | tf_op jit(solution)/shard_map/all_gather | solution.py:121
  65.2 13.4 %all-reduce.30 = (f32[1,576]{1,0:T(1,128)S(1)}, f32[1,576]{1,0:T(1,128)S(1)}) all-reduce(f32[1,576]{1,0:T(1,128)S(1)} %reduce_sum.449, f32[1,576]{1,0:T(1,128)S(1)} %reduce_sum.451), channel_id=1, replica_groups=mesh['img'=4,'ch'=8] {'ch'}, use_global_device_ids=true, to_apply=%region_5.6 | all-reduce | flops 1152 | bytes 9216 | tf_op jit(solution)/shard_map/psum | solution.py:93
  79.2 2.0 convolution_bitcast_fusion.1
  82.5 40.5 %reduce-scatter.13.cloned.1.call-done = f32[128,1,576]{0,2,1:T(8,128)} async-done(((f32[1024,1,576]{0,2,1:T(8,128)}), f32[128,1,576]{0,2,1:T(8,128)}) %reduce-scatter.13.cloned.1.call-update) | async-done | bytes 294928 | tf_op jit(solution)/shard_map/reduce_scatter | solution.py:72
  124.2 13.0 %all-reduce.29 = (f32[1,576]{1,0:T(1,128)S(1)}, f32[1,576]{1,0:T(1,128)S(1)}) all-reduce(f32[1,576]{1,0:T(1,128)S(1)} %reduce_sum.453, f32[1,576]{1,0:T(1,128)S(1)} %reduce_sum.455), channel_id=1, replica_groups=mesh['img'=4,'ch'=8] {'ch'}, use_global_device_ids=true, to_apply=%region_10.11 | all-reduce | flops 1152 | bytes 9216 | tf_op jit(solution)/shard_map/psum | solution.py:93
  139.3 9.4 %all_gather.30 = bf16[1024,1,144]{0,2,1:T(8,128)(2,1)S(1)} all-gather(bf16[128,1,144]{0,2,1:T(8,128)(2,1)S(1)} %convert_element_type.349), channel_id=1, replica_groups=mesh['img'=4,'ch'=8] {'ch'}, dimensions={0}, use_global_device_ids=true | all-gather | bytes 331776 | tf_op jit(solution)/shard_map/all_gather | solution.py:64
  149.8 13.2 %all-reduce.28 = (f32[1,144]{1,0:T(1,128)S(1)}, f32[1,144]{1,0:T(1,128)S(1)}) all-reduce(f32[1,144]{1,0:T(1,128)S(1)} %bitcast.904, f32[1,144]{1,0:T(1,128)S(1)} %bitcast.903), channel_id=1, replica_groups=mesh['img'=4,'ch'=8] {'ch'}, use_global_device_ids=true, to_apply=%region_16.17 | all-reduce | flops 288 | bytes 2304 | tf_op jit(solution)/shard_map/psum | solution.py:93
  163.7 8.3 all-gather.1
  180.6 1.7 fusion.195
  183.8 1.7 fusion.197
  187.0 1.7 fusion.199
  193.5 13.2 %all-reduce.27 = (f32[1,144]{1,0:T(1,128)S(1)}, f32[1,144]{1,0:T(1,128)S(1)}) all-reduce(f32[1,144]{1,0:T(1,128)S(1)} %bitcast.894, f32[1,144]{1,0:T(1,128)S(1)} %bitcast.893), channel_id=1, replica_groups=mesh['img'=4,'ch'=8] {'ch'}, use_global_device_ids=true, to_apply=%region_20.21 | all-reduce | flops 288 | bytes 2304 | tf_op jit(solution)/shard_map/psum | solution.py:93
  206.7 2.0 convolution_bitcast_fusion.3
  209.4 33.3 %reduce-scatter.15.cloned.1.call-done = f32[128,1,144]{0,2,1:T(8,128)} async-done(((f32[1024,1,144]{0,2,1:T(8,128)}), f32[128,1,144]{0,2,1:T(8,128)}) %reduce-scatter.15.cloned.1.call-update) | async-done | bytes 73744 | tf_op jit(solution)/shard_map/reduce_scatter | solution.py:72
  243.7 12.3 %all-reduce.26 = (f32[1,144]{1,0:T(1,128)S(1)}, f32[1,144]{1,0:T(1,128)S(1)}) all-reduce(f32[1,144]{1,0:T(1,128)S(1)} %bitcast.906, f32[1,144]{1,0:T(1,128)S(1)} %bitcast.905), channel_id=1, replica_groups=mesh['img'=4,'ch'=8] {'ch'}, use_global_device_ids=true, to_apply=%region_25.26 | all-reduce | flops 288 | bytes 2304 | tf_op jit(solution)/shard_map/psum | solution.py:93
  257.1 9.8 %all_gather.32 = bf16[1024,1,144]{0,2,1:T(8,128)(2,1)S(1)} all-gather(bf16[128,1,144]{0,2,1:T(8,128)(2,1)S(1)} %multiply_convert_fusion.5), channel_id=1, replica_groups=mesh['img'=4,'ch'=8] {'ch'}, dimensions={0}, use_global_device_ids=true | all-gather | bytes 331776 | tf_op jit(solution)/shard_map/all_gather | solution.py:64
  269.1 4.8 fusion.275
  275.8 2.1 copy.177
  278.0 34.2 %reduce-scatter.19.cloned.1.call-done = bf16[128,144]{1,0:T(8,128)(2,1)} async-done(((bf16[1024,144]{1,0:T(8,128)(2,1)}), bf16[128,144]{1,0:T(8,128)(2,1)}) %reduce-scatter.19.cloned.1.call-update) | async-done | bytes 36880
  313.9 12.2 %all-reduce.25 = (f32[1,144]{1,0:T(1,128)S(1)}, f32[1,144]{1,0:T(1,128)S(1)}) all-reduce(f32[1,144]{1,0:T(1,128)S(1)} %bitcast.895, f32[1,144]{1,0:T(1,128)S(1)} %bitcast.896), channel_id=1, replica_groups=mesh['img'=4,'ch'=8] {'ch'}, use_global_device_ids=true, to_apply=%region_31.32 | all-reduce | flops 288 | bytes 2304 | tf_op jit(solution)/shard_map/psum | solution.py:106
  326.3 9.4 %all_gather.34 = bf16[1024,1,144]{0,2,1:T(8,128)(2,1)S(1)} all-gather(bf16[128,1,144]{0,2,1:T(8,128)(2,1)S(1)} %multiply_convert_fusion.4), channel_id=1, replica_groups=mesh['img'=4,'ch'=8] {'ch'}, dimensions={0}, use_global_device_ids=true | all-gather | bytes 331776 | tf_op jit(solution)/shard_map/all_gather | solution.py:68
  336.5 13.2 %all-reduce.24 = (f32[1,144]{1,0:T(1,128)S(1)}, f32[1,144]{1,0:T(1,128)S(1)}) all-reduce(f32[1,144]{1,0:T(1,128)S(1)} %bitcast.907, f32[1,144]{1,0:T(1,128)S(1)} %bitcast.908), channel_id=1, replica_groups=mesh['img'=4,'ch'=8] {'ch'}, use_global_device_ids=true, to_apply=%region_35.36 | all-reduce | flops 288 | bytes 2304 | tf_op jit(solution)/shard_map/psum | solution.py:106
  353.4 1.6 add.678
  355.0 1.6 pad_slice_fusion.19
  358.2 1.6 pad_slice_fusion.18
  367.4 51.7 %all-reduce.38.cloned.1.call-done = bf16[256,1,144]{2,1,0:T(2,128)(2,1)} async-done(((bf16[256,1,144]{2,1,0:T(2,128)(2,1)}), bf16[256,1,144]{2,1,0:T(2,128)(2,1)}) %all-reduce.38.cloned.1.call-update) | async-done | bytes 73744
  420.6 12.0 %all-reduce.23 = (f32[1,144]{1,0:T(1,128)S(1)}, f32[1,144]{1,0:T(1,128)S(1)}) all-reduce(f32[1,144]{1,0:T(1,128)S(1)} %bitcast.897, f32[1,144]{1,0:T(1,128)S(1)} %bitcast.898), channel_id=1, replica_groups=mesh['img'=4,'ch'=8] {'ch'}, use_global_device_ids=true, to_apply=%region_40.41 | all-reduce | flops 288 | bytes 2304 | tf_op jit(solution)/shard_map/psum | solution.py:106
  434.4 33.6 %reduce-scatter.21.cloned.1.call-done = bf16[128,144]{1,0:T(8,128)(2,1)} async-done(((bf16[1024,144]{1,0:T(8,128)(2,1)}), bf16[128,144]{1,0:T(8,128)(2,1)}) %reduce-scatter.21.cloned.1.call-update) | async-done | bytes 36880
  472.0 12.5 %all-reduce.22 = (f32[1,576]{1,0:T(1,128)S(1)}, f32[1,576]{1,0:T(1,128)S(1)}) all-reduce(f32[1,576]{1,0:T(1,128)S(1)} %reduce_sum.483, f32[1,576]{1,0:T(1,128)S(1)} %reduce_sum.481), channel_id=1, replica_groups=mesh['img'=4,'ch'=8] {'ch'}, use_global_device_ids=true, to_apply=%region_45.46 | all-reduce | flops 1152 | bytes 9216 | tf_op jit(solution)/shard_map/psum | solution.py:106
  485.7 4.4 convolution_bitcast_fusion
  490.1 19.9 %all-gather.10.cloned.1.call-done = bf16[1024,1,576]{0,2,1:T(8,128)(2,1)} async-done(((bf16[128,1,576]{0,2,1:T(8,128)(2,1)}), bf16[1024,1,576]{0,2,1:T(8,128)(2,1)}) %all-gather.10.cloned.1.call-update) | async-done | bytes 1179664 | tf_op jit(solution)/shard_map/all_gather | solution.py:68
  510.0 2.4 fusion.135
  512.5 13.3 %all-reduce.21 = (f32[1,576]{1,0:T(1,128)S(1)}, f32[1,576]{1,0:T(1,128)S(1)}) all-reduce(f32[1,576]{1,0:T(1,128)S(1)} %reduce_sum.487, f32[1,576]{1,0:T(1,128)S(1)} %reduce_sum.485), channel_id=1, replica_groups=mesh['img'=4,'ch'=8] {'ch'}, use_global_device_ids=true, to_apply=%region_49.50 | all-reduce | flops 1152 | bytes 9216 | tf_op jit(solution)/shard_map/psum | solution.py:106
  534.1 1.8 fusion.18
  535.9 2.1 copy.169
  539.7 4.8 convolution_convert_fusion
  551.0 42.3 %all-reduce.40.cloned.1.call-done = bf16[256,1,576]{2,1,0:T(2,128)(2,1)} async-done(((bf16[256,1,576]{2,1,0:T(2,128)(2,1)}), bf16[256,1,576]{2,1,0:T(2,128)(2,1)}) %all-reduce.40.cloned.1.call-update) | async-done | bytes 294928
  594.6 12.1 %all-reduce.20 = (f32[1,576]{1,0:T(1,128)S(1)}, f32[1,576]{1,0:T(1,128)S(1)}) all-reduce(f32[1,576]{1,0:T(1,128)S(1)} %reduce_sum.491, f32[1,576]{1,0:T(1,128)S(1)} %reduce_sum.489), channel_id=1, replica_groups=mesh['img'=4,'ch'=8] {'ch'}, use_global_device_ids=true, to_apply=%region_54.55 | all-reduce | flops 1152 | bytes 9216 | tf_op jit(solution)/shard_map/psum | solution.py:106
  613.8 11.7 %all-reduce.32 = (bf16[2,2,32]{2,1,0:T(2,128)(2,1)S(1)}, bf16[2,2,32]{2,1,0:T(2,128)(2,1)S(1)}, bf16[2,128]{1,0:T(2,128)(2,1)S(1)}, bf16[2,128]{1,0:T(2,128)(2,1...) all-reduce(bf16[2,2,32]{2,1,0:T(2,128)(2,1)S(1)} %pad_maximum_fusio, ...), channel_id=1, replica_groups=mesh['img'=4,'ch'=8] {'img'}, use_global_device_ids=true, to_apply=%region_63.64 | all-reduce | flops 1792 | bytes 7168 | tf_op jit(solution)/shard_map/psum | solution.py:277
  628.9 9.8 %reduce-scatter.17.cloned.1.call-done = f32[512,1,144]{0,2,1:T(8,128)} async-done(((f32[4096,1,144]{0,2,1:T(8,128)}), f32[512,1,144]{0,2,1:T(8,128)}) %reduce-scatter.17.cloned.1.call-update) | async-done | bytes 294928 | tf_op jit(solution)/shard_map/reduce_scatter | solution.py:72
  638.7 1.6 add_convert_fusion
  640.4 39.5 %reduce-scatter.23.cloned.1.call-done = bf16[128,576]{1,0:T(8,128)(2,1)} async-done(((bf16[1024,576]{1,0:T(8,128)(2,1)}), bf16[128,576]{1,0:T(8,128)(2,1)}) %reduce-scatter.23.cloned.1.call-update) | async-done | bytes 147472
  681.7 210.2 %all-reduce.42.cloned.1.call-done = (bf16[2,1024,32]{1,2,0:T(8,128)(2,1)}, bf16[2,9,256,32]{2,3,1,0:T(8,128)(2,1)}, bf16[2,32,1024]{2,1,0:T(8,128)(2,1)}, bf16[1024,512]{1,0:T(8,128)(2,1)}, bf16[512,4096]{1,0:T(8,128)(2,1)}) async-done(((bf16[2,1024,32]{1,2,0:T(8,128)(2,1)}, bf16[2,9,256,32]{2,3,1,0:T(8,128)(2,1)}, bf16[2,32,1024]{2,1,0:T(8,128)(2,1)}, bf16[1024,512]{1,0:T(8,128)(2,1)}, ...) | async-done | bytes 5799952 | tf_op jit(solution)/shard_map/psum | solution.py:274
  891.9 6.8 convert_element_type.395
  898.7 1.6 convert_element_type.392
  (478 shorter events, 90.9 us)
Async XLA Ops:
  7.2 259.8 %copy-start = (bf16[1024,512]{1,0:T(8,128)(2,1)S(1)}, bf16[1024,512]{1,0:T(8,128)(2,1)}, u32[]{:S(2)}) copy-start(bf16[1024,512]{1,0:T(8,128)(2,1)} %param.23) | copy-start | bytes 3145732
  7.2 29.6 %all-gather.6.cloned.1.call-start = ((), (), s32[]{:S(2)}) async-start(), calls=%async_computation.6 | async-start | bytes 1327104 | tf_op jit(solution)/shard_map/all_gather | solution.py:64
  7.9 115.1 %reduce-scatter.13.cloned.1.call-start = ((), (), s32[]{:S(2)}) async-start(), calls=%async_computation.7 | async-start | bytes 2654208 | tf_op jit(solution)/shard_map/reduce_scatter | solution.py:72
  8.9 128.3 %copy-start.65 = (f32[576]{0:T(1024)}, f32[576]{0:T(1024)S(1)}, u32[]{:S(2)}) copy-start(f32[576]{0:T(1024)S(1)} %mul.807) | copy-start | bytes 6916
  10.3 41.7 %copy-start.86 = (f32[32]{0:T(128)}, f32[32]{0:T(128)S(1)}, u32[]{:S(2)}) copy-start(f32[32]{0:T(128)S(1)} %get-tuple-element.140) | copy-start | bytes 388
  10.3 52.0 %copy-start.113 = (f32[32]{0:T(128)}, f32[32]{0:T(128)S(1)}, u32[]{:S(2)}) copy-start(f32[32]{0:T(128)S(1)} %get-tuple-element.117) | copy-start | bytes 388
  10.3 68.4 %copy-start.88 = (f32[32]{0:T(128)}, f32[32]{0:T(128)S(1)}, u32[]{:S(2)}) copy-start(f32[32]{0:T(128)S(1)} %get-tuple-element.141) | copy-start | bytes 388
  10.3 68.4 %copy-start.104 = (f32[32]{0:T(128)}, f32[32]{0:T(128)S(1)}, u32[]{:S(2)}) copy-start(f32[32]{0:T(128)S(1)} %get-tuple-element.116) | copy-start | bytes 388
  10.3 152.7 %copy-start.91 = (f32[32]{0:T(128)}, f32[32]{0:T(128)S(1)}, u32[]{:S(2)}) copy-start(f32[32]{0:T(128)S(1)} %get-tuple-element.142) | copy-start | bytes 388
  10.3 152.7 %copy-start.115 = (f32[32]{0:T(128)}, f32[32]{0:T(128)S(1)}, u32[]{:S(2)}) copy-start(f32[32]{0:T(128)S(1)} %get-tuple-element.115) | copy-start | bytes 388
  81.2 56.0 %copy-start.14 = (bf16[128,1,576]{0,2,1:T(8,128)(2,1)S(1)}, bf16[128,1,576]{0,2,1:T(8,128)(2,1)}, u32[]{:S(2)}) copy-start(bf16[128,1,576]{0,2,1:T(8,128)(2,1)} %param.14) | copy-start | bytes 442372
  81.3 161.4 %reduce-scatter.15.cloned.1.call-start = ((), (), s32[]{:S(2)}) async-start(), calls=%async_computation.8 | async-start | bytes 663552 | tf_op jit(solution)/shard_map/reduce_scatter | solution.py:72
  81.3 57.9 %copy-start.98 = (f32[12]{0:T(128)}, f32[12]{0:T(128)S(1)}, u32[]{:S(2)}) copy-start(f32[12]{0:T(128)S(1)} %subtract_convert_fusion) | copy-start | bytes 148
  81.9 57.3 %copy-start.100 = (s32[12]{0:T(128)}, s32[12]{0:T(128)S(1)}, u32[]{:S(2)}) copy-start(s32[12]{0:T(128)S(1)} %get-tuple-element.137) | copy-start | bytes 148
  81.9 57.3 %copy-start.102 = (s32[12]{0:T(128)}, s32[12]{0:T(128)S(1)}, u32[]{:S(2)}) copy-start(s32[12]{0:T(128)S(1)} %get-tuple-element.138) | copy-start | bytes 148
  82.5 56.8 %copy-start.93 = (f32[128]{0:T(128)}, f32[128]{0:T(128)S(1)}, u32[]{:S(2)}) copy-start(f32[128]{0:T(128)S(1)} %get-tuple-element.143) | copy-start | bytes 1540
  82.5 56.8 %copy-start.111 = (f32[128]{0:T(128)}, f32[128]{0:T(128)S(1)}, u32[]{:S(2)}) copy-start(f32[128]{0:T(128)S(1)} %get-tuple-element.128) | copy-start | bytes 1540
  206.7 50.4 %copy-start.72 = (f32[1,144]{1,0:T(1,128)}, f32[1,144]{1,0:T(1,128)S(1)}, u32[]{:S(2)}) copy-start(f32[1,144]{1,0:T(1,128)S(1)} %get-tuple-element.122) | copy-start | bytes 1732
  206.7 50.4 %copy-start.75 = (f32[1,144]{1,0:T(1,128)}, f32[1,144]{1,0:T(1,128)S(1)}, u32[]{:S(2)}) copy-start(f32[1,144]{1,0:T(1,128)S(1)} %get-tuple-element.121) | copy-start | bytes 1732
  208.8 60.4 %all-gather.8.cloned.1.call-start = ((), (), s32[]{:S(2)}) async-start(), calls=%async_computation.10 | async-start | bytes 1327104 | tf_op jit(solution)/shard_map/all_gather | solution.py:68
  209.4 102.9 %reduce-scatter.19.cloned.1.call-start = ((), (), s32[]{:S(2)}) async-start(), calls=%async_computation.12 | async-start | bytes 589824
  275.8 37.4 %copy-start.107 = (f32[128]{0:T(128)S(1)}, f32[128]{0:T(128)}, u32[]{:S(2)}) copy-start(f32[128]{0:T(128)} %get-tuple-element.144) | copy-start | bytes 1540
  275.8 59.8 %copy-start.57 = (bf16[2,32,1024]{2,1,0:T(8,128)(2,1)S(1)}, bf16[2,32,1024]{2,1,0:T(8,128)(2,1)}, u32[]{:S(2)}) copy-start(bf16[2,32,1024]{2,1,0:T(8,128)(2,1)} %param.18) | copy-start | bytes 393220
  275.8 59.8 %copy-start.73 = (f32[1,144]{1,0:T(1,128)S(1)}, f32[1,144]{1,0:T(1,128)}, u32[]{:S(2)}) copy-start(f32[1,144]{1,0:T(1,128)} %copy-done.72) | copy-start | bytes 1732
  275.8 59.8 %copy-start.76 = (f32[1,144]{1,0:T(1,128)S(1)}, f32[1,144]{1,0:T(1,128)}, u32[]{:S(2)}) copy-start(f32[1,144]{1,0:T(1,128)} %copy-done.75) | copy-start | bytes 1732
  275.8 59.8 %copy-start.96 = (f32[32]{0:T(128)S(1)}, f32[32]{0:T(128)}, u32[]{:S(2)}) copy-start(f32[32]{0:T(128)} %get-tuple-element.139) | copy-start | bytes 388
  275.8 59.8 %copy-start.109 = (f32[32]{0:T(128)S(1)}, f32[32]{0:T(128)}, u32[]{:S(2)}) copy-start(f32[32]{0:T(128)} %get-tuple-element.118) | copy-start | bytes 388
  277.9 72.1 %copy-start.23 = (bf16[2,9,256,32]{2,3,1,0:T(8,128)(2,1)S(1)}, bf16[2,9,256,32]{2,3,1,0:T(8,128)(2,1)}, u32[]{:S(2)}) copy-start(bf16[2,9,256,32]{2,3,1,0:T(8,128)(2,1)} %param.17) | copy-start | bytes 884740
  277.9 141.1 %all-reduce.38.cloned.1.call-start = ((), (), s32[]{:S(2)}) async-start(), calls=%async_computation.15 | async-start | bytes 524288
  363.7 56.1 %copy-start.42 = (f32[144,32]{0,1:T(8,128)S(1)}, f32[144,32]{0,1:T(8,128)}, u32[]{:S(2)}) copy-start(f32[144,32]{0,1:T(8,128)} %copy-done.41) | copy-start | bytes 55300
  363.7 56.1 %copy-start.79 = (f32[1,144]{1,0:T(1,128)S(1)}, f32[1,144]{1,0:T(1,128)}, u32[]{:S(2)}) copy-start(f32[1,144]{1,0:T(1,128)} %copy-done.78) | copy-start | bytes 1732
  363.7 56.1 %copy-start.85 = (f32[1,144]{1,0:T(1,128)S(1)}, f32[1,144]{1,0:T(1,128)}, u32[]{:S(2)}) copy-start(f32[1,144]{1,0:T(1,128)} %copy-done.84) | copy-start | bytes 1732
  363.7 56.1 %copy-start.92 = (f32[32]{0:T(128)S(1)}, f32[32]{0:T(128)}, u32[]{:S(2)}) copy-start(f32[32]{0:T(128)} %copy-done.91) | copy-start | bytes 388
  363.7 56.1 %copy-start.116 = (f32[32]{0:T(128)S(1)}, f32[32]{0:T(128)}, u32[]{:S(2)}) copy-start(f32[32]{0:T(128)} %copy-done.115) | copy-start | bytes 388
  363.8 68.9 %copy-start.43 = (bf16[2,1024,32]{1,2,0:T(8,128)(2,1)S(1)}, bf16[2,1024,32]{1,2,0:T(8,128)(2,1)}, u32[]{:S(2)}) copy-start(bf16[2,1024,32]{1,2,0:T(8,128)(2,1)} %param.16) | copy-start | bytes 393220
  366.1 101.9 %reduce-scatter.21.cloned.1.call-start = ((), (), s32[]{:S(2)}) async-start(), calls=%async_computation.13 | async-start | bytes 589824
  434.3 75.7 %all-gather.10.cloned.1.call-start = ((), (), s32[]{:S(2)}) async-start(), calls=%async_computation.11 | async-start | bytes 1327104 | tf_op jit(solution)/shard_map/all_gather | solution.py:68
  485.6 107.7 %all-reduce.40.cloned.1.call-start = ((), (), s32[]{:S(2)}) async-start(), calls=%async_computation.16 | async-start | bytes 1310720
  538.0 100.7 %reduce-scatter.17.cloned.1.call-start = ((), (), s32[]{:S(2)}) async-start(), calls=%async_computation.9 | async-start | bytes 2654208 | tf_op jit(solution)/shard_map/reduce_scatter | solution.py:72
  539.7 140.2 %reduce-scatter.23.cloned.1.call-start = ((), (), s32[]{:S(2)}) async-start(), calls=%async_computation.14 | async-start | bytes 1474560
  547.6 46.7 %copy-start.17 = (f32[32,576]{1,0:T(8,128)S(1)}, f32[32,576]{1,0:T(8,128)}, u32[]{:S(2)}) copy-start(f32[32,576]{1,0:T(8,128)} %copy-done.16) | copy-start | bytes 221188
  547.6 46.7 %copy-start.67 = (f32[576]{0:T(1024)S(1)}, f32[576]{0:T(1024)}, u32[]{:S(2)}) copy-start(f32[576]{0:T(1024)} %copy-done.65) | copy-start | bytes 6916
  547.6 46.7 %copy-start.69 = (f32[576]{0:T(1024)S(1)}, f32[576]{0:T(1024)}, u32[]{:S(2)}) copy-start(f32[576]{0:T(1024)} %copy-done.68) | copy-start | bytes 6916
  547.6 46.7 %copy-start.71 = (f32[576]{0:T(1024)S(1)}, f32[576]{0:T(1024)}, u32[]{:S(2)}) copy-start(f32[576]{0:T(1024)} %copy-done.70) | copy-start | bytes 6916
  547.7 46.7 %copy-start.87 = (f32[32]{0:T(128)S(1)}, f32[32]{0:T(128)}, u32[]{:S(2)}) copy-start(f32[32]{0:T(128)} %copy-done.86) | copy-start | bytes 388
  547.7 46.7 %copy-start.114 = (f32[32]{0:T(128)S(1)}, f32[32]{0:T(128)}, u32[]{:S(2)}) copy-start(f32[32]{0:T(128)} %copy-done.113) | copy-start | bytes 388
  548.0 58.8 %copy-start.44 = (bf16[2,1024,32]{1,2,0:T(8,128)(2,1)S(1)}, bf16[2,1024,32]{1,2,0:T(8,128)(2,1)}, u32[]{:S(2)}) copy-start(bf16[2,1024,32]{1,2,0:T(8,128)(2,1)} %param.16) | copy-start | bytes 393220
  608.8 283.1 %all-reduce.42.cloned.1.call-start = ((), (), s32[]{:S(2)}) async-start(), calls=%async_computation.17 | async-start | bytes 11599872 | tf_op jit(solution)/shard_map/psum | solution.py:274
  (97 other events, 1079.8 us)
Sparse Core Ops, SparseCore 0:
  9.9 26.8 all-gather.5
  81.4 41.5 reduce-scatter.12
  208.9 33.7 reduce-scatter.14
  244.6 24.5 all-gather.7
  278.0 34.1 reduce-scatter.18
  366.2 52.7 all-reduce.37
  434.5 33.4 reduce-scatter.20
  485.7 24.2 all-gather.9
  538.1 55.1 all-reduce.39
  596.9 41.7 reduce-scatter.16
  642.5 37.2 reduce-scatter.22
  683.6 208.2 all-reduce.41
where the time goes:
time: 912 us; the launch traced here: 909 us
  waiting for transfers between devices  544 us (60%)
  blocking collectives  212 us (23%)
  matrix products  60.4 us (7%)
  local copies, waits for them, and re-layouts  46 us (5%)
  other arithmetic  29.3 us (3%)
  between operations  17.7 us (2%)
    psum x1, waiting for transfers between devices, per_device(): lax.psum(reduce_grad.astype(jnp.bfloat16), 'img').astype(jnp.float32)  210 us
    unnamed x17, waiting for transfers between devices  203 us
    reduce_scatter x3, waiting for transfers between devices, spread_sum(): lax.psum_scatter(jnp.einsum('mc,mbs->cbs', weight, data, preferred_elemen...  83.6 us
    psum x6, blocking collectives, norm_forward(): lax.psum((jnp.sum(values, axis=0), jnp.sum(values * values, axis=0)), 'ch')  78.4 us
    psum x6, blocking collectives, norm_backward(): lax.psum((jnp.sum(scaled, axis=0), jnp.sum(scaled * unit, axis=0)), 'ch')  75.2 us
    all_gather x1, waiting for transfers between devices, gather_channels(): return lax.all_gather(local, 'ch', axis=0, tiled=True)  26.5 us
    all_gather x2, waiting for transfers between devices, gather_grads(): return lax.all_gather(local, 'ch', axis=0, tiled=True)  21 us
    all_gather x2, blocking collectives, gather_channels(): return lax.all_gather(local, 'ch', axis=0, tiled=True)  19.2 us
  transfers between devices with their start and end apart: 12, of which 12 were waited for; matrix products, arithmetic and copies ran while one was open for 4% of the time, Pallas kernels for 0%

commit v1 on v0

v1 whole, which is shorter than its diff:
```python
import functools

import jax
import jax.numpy as jnp
from jax import lax
from jax.experimental import pallas as pl
from jax.experimental.pallas import tpu as pltpu
from jax.sharding import PartitionSpec as P

GRID = 24
POOLED = 12
EPSILON = 1e-06
OFFSETS = [(-1, -1), (-1, 0), (-1, 1), (0, -1), (0, 0), (0, 1), (1, -1), (1, 0), (1, 1)]
TAPS = len(OFFSETS)
LANES = 128
BF16 = jnp.bfloat16
F32 = jnp.float32
VMEM = pl.BlockSpec(memory_space=pltpu.VMEM)
SMEM = pl.BlockSpec(memory_space=pltpu.SMEM)
HBM = pl.BlockSpec(memory_space=pl.ANY)


def dot_nn(left, right):
    return lax.dot_general(left, right, (((1,), (0,)), ((), ())), preferred_element_type=F32)


def dot_nt(left, right):
    return lax.dot_general(left, right, (((1,), (1,)), ((), ())), preferred_element_type=F32)


def dot_tn(left, right):
    return lax.dot_general(left, right, (((0,), (0,)), ((), ())), preferred_element_type=F32)


def sds(shape, dtype):
    return jax.ShapeDtypeStruct(tuple(shape), dtype)


def call(kernel, out_shape, in_specs, scratch=(), out_specs=None, vmem=32, flops=0, moved=0, grid=()):
    return pl.pallas_call(
        kernel,
        out_shape=out_shape,
        grid=grid,
        in_specs=in_specs,
        out_specs=out_specs if out_specs is not None else jax.tree.map(lambda _: VMEM, out_shape),
        scratch_shapes=list(scratch),
        compiler_params=pltpu.CompilerParams(vmem_limit_bytes=vmem << 20),
        cost_estimate=pl.CostEstimate(flops=flops, bytes_accessed=moved, transcendentals=0),
    )


def ppermute_xor(x, axis, mask):
    return lax.ppermute(x, axis, [(i, i ^ mask) for i in range(lax.axis_size(axis))])


def gather_pieces(x):
    n = lax.axis_size("ch")
    if n > 8:
        whole = lax.all_gather(x, "ch", axis=0)
        me = lax.axis_index("ch")
        return [lax.dynamic_index_in_dim(whole, me ^ r, 0, keepdims=False) for r in range(n)]
    pieces = [None] * n
    pieces[0] = x
    for r in range(2, n, 2):
        pieces[r] = ppermute_xor(x, "ch", r)
    for r in range(0, n, 2):
        pieces[r + 1] = ppermute_xor(pieces[r], "ch", 1)
    return pieces


def along_images(x):
    return [ppermute_xor(x, "img", m) for m in range(1, lax.axis_size("img"))]


def columns(chan, mid):
    reduce_end = chan
    conv_end = reduce_end + TAPS * mid
    expand_end = conv_end + chan
    return reduce_end, conv_end, expand_end, expand_end + LANES, expand_end + 2 * LANES


def split_low(value):
    high = value.astype(BF16).astype(F32)
    return high, value - high


def pack_kernel(slots, *refs):
    if slots:
        feat, *refs = refs
    red, conv, exp, mid_gain, mid_bias, out_gain, out_bias, packet, scr = refs
    held = red.shape[0]
    chan, mid = red.shape[1], conv.shape[2]
    base = 0
    if slots:
        for b in range(slots // held):
            packet[:, b * LANES : (b + 1) * LANES] = feat[b * held : (b + 1) * held, :]
        base = slots // held * LANES
    reduce_end, conv_end, expand_end, mid_end, end = columns(chan, mid)
    packet[:, base : base + reduce_end] = red[...]
    for j in range(TAPS):
        at = base + reduce_end + j * mid
        packet[:, at : at + mid] = conv[j]
    packet[:, base + conv_end : base + expand_end] = exp[...]
    scr[...] = jnp.zeros_like(scr)
    for which in range(2):
        for kind, ref in enumerate((mid_gain, mid_bias)):
            high, low = split_low(ref[which : which + 1, :])
            at = 4 * which + 2 * kind
            scr[at : at + 1, 0:held] = high
            scr[at + 1 : at + 2, 0:held] = low
    packet[:, base + expand_end : base + mid_end] = scr[...].T[0:held, :].astype(BF16)
    scr[...] = jnp.zeros_like(scr)
    for kind, ref in enumerate((out_gain, out_bias)):
        high, low = split_low(ref[...])
        scr[2 * kind : 2 * kind + 1, :] = high
        scr[2 * kind + 1 : 2 * kind + 2, :] = low
    packet[:, base + mid_end : base + end] = scr[0:held, :].astype(BF16)


def pack(layer, feat, red, conv, exp, mid_gain, mid_bias, out_gain, out_bias):
    held, chan = red.shape[1:]
    mid = conv.shape[3]
    width = columns(chan, mid)[-1]
    slots = 0 if feat is None else feat.shape[0]
    width += slots // held * LANES

    def layered(x):
        return pl.BlockSpec((None,) + x.shape[1:], lambda i: (layer,) + (0,) * (x.ndim - 1))

    args = [red, conv, exp, mid_gain, mid_bias, out_gain[:, None, :], out_bias[:, None, :]]
    specs = [layered(x) for x in args]
    if slots:
        args, specs = [feat] + args, [VMEM] + specs
    return call(
        functools.partial(pack_kernel, slots),
        sds((held, width), BF16),
        specs,
        [pltpu.VMEM((LANES, LANES), F32)],
        vmem=8,
        moved=2 * held * width * 2,
        grid=(1,),
    )(*args)


def assemble(me, slots, pieces, x_ref, w_ref, mid_ref, out_ref, scr):
    held = pieces[0].shape[0]
    chan, mid = out_ref.shape[1], w_ref.shape[0]
    reduce_end, conv_end, expand_end, mid_end, end = columns(chan, mid)
    base = slots // held * LANES
    for r, piece in enumerate(pieces):
        owner = me ^ r
        rows = pl.ds(pl.multiple_of(owner * held, held), held)
        lanes = pl.ds(pl.multiple_of(owner * LANES, LANES), LANES)
        for b in range(slots // held):
            x_ref[b * held : (b + 1) * held, lanes] = piece[:, b * LANES : (b + 1) * LANES]
        w_ref[rows, :] = piece[:, base : base + expand_end]
        scr[rows, :] = piece[:, base + expand_end : base + mid_end].astype(F32)
        block = piece[:, base + mid_end : base + end].astype(F32)
        out_ref[0:1, lanes] = block[0:1, :] + block[1:2, :]
        out_ref[1:2, lanes] = block[2:3, :] + block[3:4, :]
    flat = scr[...].T
    for q in range(4):
        mid_ref[q : q + 1, :] = flat[2 * q : 2 * q + 1, :] + flat[2 * q + 1 : 2 * q + 2, :]


def sigmoid(value):
    return 0.5 * jnp.tanh(0.5 * value) + 0.5


def silu(value):
    return value * sigmoid(value)


def silu_slope(value):
    gate = sigmoid(value)
    return gate * (1.0 + value * (1.0 - gate))


def unit_of(values):
    inverse = 1.0 / values.shape[-1]
    center = jnp.sum(values, axis=-1, keepdims=True) * inverse
    spread = jnp.sum(values * values, axis=-1, keepdims=True) * inverse - center * center
    factor = lax.rsqrt(spread + EPSILON)
    return (values - center) * factor, factor


def chunked(slots, step, body, carry=None):
    def wrapped(i, c):
        return body(pl.ds(pl.multiple_of(i * step, step), step), pl.multiple_of(i * step, step), c)

    return lax.fori_loop(0, slots // step, wrapped, carry)


def pad_of(side):
    return -(-(side + 1) // 16) * 16


def shift_columns(field, side, slots, aux_ref):
    pad = pad_of(side)
    field[0, pad : pad + slots, :] = field[1, pad - 1 : pad - 1 + slots, :] * aux_ref[:, 1:2]
    field[2, pad : pad + slots, :] = field[1, pad + 1 : pad + 1 + slots, :] * aux_ref[:, 2:3]


def clear_edges(field, side, slots):
    pad = pad_of(side)
    for k in range(3):
        field[k, 0:pad, :] = jnp.zeros((pad, field.shape[2]), F32)
        field[k, pad + slots : pad + slots + pad, :] = jnp.zeros((pad, field.shape[2]), F32)


def tap(field, side, slots, rise, step):
    at = pad_of(side) + rise * side
    return field[step + 1, at : at + slots, :].astype(BF16)


def forward_body(side, aux, x_ref, w_ref, mid_ref, out_ref, u1, u2, u3, fac, pat, field, act, finish):
    slots = x_ref.shape[0]
    chan, mid = out_ref.shape[1], w_ref.shape[0]
    reduce_end, conv_end, expand_end, _, _ = columns(chan, mid)
    pad = pad_of(side)
    clear_edges(field, side, slots)
    u1[...] = dot_nt(x_ref[...], w_ref[:, 0:reduce_end])

    def first(rows, start, carry):
        unit, factor = unit_of(u1[rows, :])
        u1[rows, :] = unit
        fac[0, rows, :] = jnp.broadcast_to(factor, (unit.shape[0], LANES))
        value = silu(unit * mid_ref[0:1, :] + mid_ref[1:2, :]) * aux[rows, 0:1]
        field[1, pl.ds(pad + start, unit.shape[0]), :] = value
        return carry

    chunked(slots, 48, first)
    shift_columns(field, side, slots, aux)
    for j, (rise, step) in enumerate(OFFSETS):
        pat[:, j * mid : (j + 1) * mid] = tap(field, side, slots, rise, step)
    u2[...] = dot_nt(pat[...], w_ref[:, reduce_end:conv_end])

    def second(rows, start, carry):
        unit, factor = unit_of(u2[rows, :])
        u2[rows, :] = unit
        fac[1, rows, :] = jnp.broadcast_to(factor, (unit.shape[0], LANES))
        act[rows, :] = silu(unit * mid_ref[2:3, :] + mid_ref[3:4, :]).astype(BF16)
        return carry

    chunked(slots, 48, second)
    u3[...] = dot_nn(act[...], w_ref[:, conv_end:expand_end])

    def third(rows, start, carry):
        unit, factor = unit_of(u3[rows, :])
        u3[rows, :] = unit
        fac[2, rows, :] = jnp.broadcast_to(factor, (unit.shape[0], LANES))
        summed = unit * out_ref[0:1, :] + out_ref[1:2, :] + x_ref[rows, :].astype(F32)
        finish[rows, :] = (silu(summed) * aux[rows, 0:1]).astype(BF16)
        return carry

    chunked(slots, 16, third)


def forward_kernel(side, pooling, assembled, count, *refs):
    refs = list(refs)
    me_ref, aux = refs.pop(0), refs.pop(0)
    spread = refs.pop(0) if pooling else None
    if assembled:
        x_ref, w_ref, mid_ref, out_ref = refs[:4]
        result, u1, u2, u3, fac, pat = refs[4:10]
        scratch = refs[10:]
    else:
        if not pooling:
            x_ref = refs.pop(0)
        pieces, refs = refs[:count], refs[count:]
        if pooling:
            x_ref = refs.pop(0)
        w_ref, mid_ref, out_ref, result, u1, u2, u3, fac, pat = refs[:9]
        scratch = refs[9:]
    field, act, scr, *rest = scratch
    slots = x_ref.shape[0]
    if not assembled:
        assemble(me_ref[0], slots if pooling else 0, pieces, x_ref, w_ref, mid_ref, out_ref, scr)
    finish = rest[0] if pooling else result
    forward_body(side, aux, x_ref, w_ref, mid_ref, out_ref, u1, u2, u3, fac, pat, field, act, finish)
    if pooling:
        result[...] = dot_nn(spread[...], finish[...]).astype(BF16)


def block_forward(side, chan, mid, me, aux, spread, x, pieces, assembled):
    slots = side * side
    pooling = spread is not None
    width = columns(chan, mid)[2]
    given = [me, aux] + ([spread] if pooling else [])
    kept = [
        sds((spread.shape[0] if pooling else slots, chan), BF16),
        sds((slots, mid), F32),
        sds((slots, mid), F32),
        sds((slots, chan), F32),
        sds((3, slots, LANES), F32),
        sds((slots, TAPS * mid), BF16),
    ]
    whole = [sds((mid, width), BF16), sds((8, mid), F32), sds((8, chan), F32)]
    if assembled is not None:
        args = given + list(assembled)
        outs = kept
    elif pooling:
        args = given + list(pieces)
        outs = [sds((slots, chan), BF16)] + whole + kept
    else:
        args = given + [x] + list(pieces)
        outs = whole + kept
    scratch = [
        pltpu.VMEM((3, slots + 2 * pad_of(side), mid), F32),
        pltpu.VMEM((slots, mid), BF16),
        pltpu.VMEM((mid, LANES), F32),
    ]
    if pooling:
        scratch.append(pltpu.VMEM((slots, chan), BF16))
    got = call(
        functools.partial(
            forward_kernel, side, pooling, assembled is not None, 0 if pieces is None else len(pieces)
        ),
        outs,
        [SMEM] + [VMEM] * (len(args) - 1),
        scratch,
        flops=2 * slots * mid * (2 * chan + TAPS * mid),
        moved=30 * slots * chan,
        vmem=40,
    )(*args)
    if assembled is not None:
        source = list(assembled)
    elif pooling:
        source, got = list(got[:4]), got[4:]
    else:
        source, got = [x] + list(got[:3]), got[3:]
    return got[0], source + list(got[1:])


def fold(value):
    return jnp.sum(value.reshape(value.shape[0] // 8, 8, value.shape[1]), axis=0)


def norm_back(upstream, unit, factor, gain):
    inverse = 1.0 / unit.shape[-1]
    scaled = upstream * gain
    first = jnp.sum(scaled, axis=-1, keepdims=True) * inverse
    second = jnp.sum(scaled * unit, axis=-1, keepdims=True) * inverse
    return factor * (scaled - first - unit * second)


def backward_kernel(side, halves, own_lanes, *refs):
    refs = list(refs)
    me_ref, aux = refs.pop(0), refs.pop(0)
    up_a, up_b = refs.pop(0), refs.pop(0)
    x_ref, w_ref, mid_ref, out_ref, u1, u2, u3, fac, pat = refs[:9]
    x_grad, grads, grads_low, out_grads = refs[9:13]
    up, sg, eg, turned, field, dense, accum = refs[13:]
    slots = x_ref.shape[0]
    chan, mid = out_ref.shape[1], w_ref.shape[0]
    held = grads.shape[0]
    reduce_end, conv_end, expand_end, mid_end, end = columns(chan, mid)
    pad = pad_of(side)
    me = me_ref[0]
    own_rows = pl.ds(pl.multiple_of(me * held, held), held)

    if halves:
        core = me & 1
        half = up_a.shape[1]
        up[:, pl.ds(pl.multiple_of(core * half, half), half)] = up_a[...].astype(F32)
        up[:, pl.ds(pl.multiple_of((1 - core) * half, half), half)] = up_b[...].astype(F32)
    else:
        up[...] = dot_nn(up_a[...], up_b[...])
    clear_edges(field, side, slots)

    def third(rows, start, carry):
        gain_acc, bias_acc = carry
        unit = u3[rows, :]
        summed = unit * out_ref[0:1, :] + out_ref[1:2, :] + x_ref[rows, :].astype(F32)
        grad = silu_slope(summed) * (up[rows, :] * aux[rows, 0:1])
        sg[rows, :] = grad
        eg[rows, :] = norm_back(grad, unit, fac[2, rows, 0:1], out_ref[0:1, :]).astype(BF16)
        return gain_acc + fold(grad * unit), bias_acc + fold(grad)

    zero = jnp.zeros((8, chan), F32)
    gain_acc, bias_acc = chunked(slots, 16, third, (zero, zero))
    out_grads[...] = jnp.zeros_like(out_grads)
    out_grads[0:1, :] = jnp.sum(gain_acc, axis=0, keepdims=True)
    out_grads[1:2, :] = jnp.sum(bias_acc, axis=0, keepdims=True)

    dense[...] = silu(u2[...] * mid_ref[2:3, :] + mid_ref[3:4, :])
    turned[...] = dense[...].T
    grads[:, conv_end:expand_end] = dot_nn(turned[own_rows, :].astype(BF16), eg[...])
    dense[...] = dot_nt(eg[...], w_ref[:, conv_end:expand_end])
    small = jnp.zeros((8, mid), F32)

    def second(rows, start, carry):
        gain_sum, bias_sum = carry
        unit = u2[rows, :]
        grad = silu_slope(unit * mid_ref[2:3, :] + mid_ref[3:4, :]) * dense[rows, :]
        back = norm_back(grad, unit, fac[1, rows, 0:1], mid_ref[2:3, :])
        field[1, pl.ds(pad + start, unit.shape[0]), :] = back
        return gain_sum + fold(grad * unit), bias_sum + fold(grad)

    gain_two, bias_two = chunked(slots, 48, second, (small, small))
    shift_columns(field, side, slots, aux)
    turned[...] = field[1, pad : pad + slots, :].T
    grads[:, reduce_end:conv_end] = dot_nn(turned[own_rows, :].astype(BF16), pat[...])
    for j, (rise, step) in enumerate(OFFSETS):
        at = reduce_end + j * mid
        term = dot_nn(tap(field, side, slots, -rise, -step), w_ref[:, at : at + mid])
        dense[...] = term if j == 0 else dense[...] + term

    def first(rows, start, carry):
        gain_sum, bias_sum = carry
        unit = u1[rows, :]
        grad = silu_slope(unit * mid_ref[0:1, :] + mid_ref[1:2, :]) * (dense[rows, :] * aux[rows, 0:1])
        dense[rows, :] = norm_back(grad, unit, fac[0, rows, 0:1], mid_ref[0:1, :])
        return gain_sum + fold(grad * unit), bias_sum + fold(grad)

    gain_one, bias_one = chunked(slots, 48, first, (small, small))
    turned[...] = dense[...].T
    grads[:, 0:reduce_end] = dot_nn(turned[own_rows, :].astype(BF16), x_ref[...])
    low = dense[...].astype(BF16)
    if own_lanes:
        lanes = pl.ds(pl.multiple_of(me * own_lanes, own_lanes), own_lanes)
        x_grad[...] = (dot_nn(low, w_ref[:, lanes]) + sg[:, lanes]).astype(x_grad.dtype)
    else:
        x_grad[...] = (dot_nn(low, w_ref[:, 0:reduce_end]) + sg[...]).astype(x_grad.dtype)

    accum[...] = jnp.zeros_like(accum)
    for q, value in enumerate((gain_one, bias_one, gain_two, bias_two)):
        accum[q : q + 1, :] = jnp.sum(value, axis=0, keepdims=True)
    turned[:, 0:LANES] = accum[...].T
    grads[:, expand_end:mid_end] = turned[own_rows, 0:LANES]
    grads[:, mid_end:end] = jnp.zeros((held, LANES), F32)
    if chan // (mid // held) == LANES:
        lanes = pl.ds(pl.multiple_of(me * LANES, LANES), LANES)
        grads[0:8, mid_end:end] = out_grads[:, lanes]
    grads_low[...] = grads[...].astype(BF16)


def block_backward(side, held, me, aux, upstream, saved, own_lanes, x_dtype):
    slots, chan = saved[0].shape
    mid = saved[1].shape[0]
    halves = upstream[0].shape[0] == slots and upstream[0].shape[1] * 2 == chan
    end = columns(chan, mid)[-1]
    outs = [
        sds((slots, own_lanes or chan), x_dtype),
        sds((held, end), F32),
        sds((held, end), BF16),
        sds((8, chan), F32),
    ]
    scratch = [
        pltpu.VMEM((slots, chan), F32),
        pltpu.VMEM((slots, chan), F32),
        pltpu.VMEM((slots, chan), BF16),
        pltpu.VMEM((mid, slots), F32),
        pltpu.VMEM((3, slots + 2 * pad_of(side), mid), F32),
        pltpu.VMEM((slots, mid), F32),
        pltpu.VMEM((LANES, mid), F32),
    ]
    return call(
        functools.partial(backward_kernel, side, halves, own_lanes),
        outs,
        [SMEM] + [VMEM] * (3 + len(saved)),
        scratch,
        flops=3 * slots * mid * (2 * chan + TAPS * mid),
        moved=40 * slots * chan,
        vmem=40,
    )(me, aux, *upstream, *saved)


GELU_A = 0.7978845608028654
GELU_B = 0.044715


def gelu_both(value):
    square = value * value
    curve = jnp.tanh(GELU_A * (value + GELU_B * value * square))
    slope = 0.5 * (1.0 + curve) + 0.5 * value * (1.0 - curve * curve) * (
        GELU_A * (1.0 + 3.0 * GELU_B * square)
    )
    return 0.5 * value * (1.0 + curve), slope


def act_grad_kernel(count, me_ref, w2, *refs):
    pieces, out = refs[:count], refs[count]
    width = pieces[0].shape[1]
    for r, piece in enumerate(pieces):
        lanes = pl.ds(pl.multiple_of((me_ref[0] ^ r) * width, width), width)
        term = dot_nt(piece[...], w2[:, lanes])
        out[...] = term if r == 0 else out[...] + term


def act_grad(me, w2, pieces):
    rows, width = pieces[0].shape
    hidden = w2.shape[0]
    return call(
        functools.partial(act_grad_kernel, len(pieces)),
        sds((rows, hidden), F32),
        [SMEM] + [VMEM] * (1 + len(pieces)),
        vmem=24,
        flops=2 * rows * hidden * w2.shape[1],
        moved=2 * hidden * w2.shape[1],
    )(me, w2, *pieces)


def readout_kernel(me_ref, readin, w1, b1, grad, act, mine, theirs, full):
    hidden = dot_nn(readin[...], w1[...]) + b1[...]
    value, slope = gelu_both(hidden)
    act[...] = value.astype(BF16)
    full[...] = dot_nt((slope * grad[...]).astype(BF16), w1[...])
    half = mine.shape[1]
    core = me_ref[0] & 1
    mine[...] = full[:, pl.ds(pl.multiple_of(core * half, half), half)]
    theirs[...] = full[:, pl.ds(pl.multiple_of((1 - core) * half, half), half)].astype(BF16)


def readout(me, readin, w1, b1, grad):
    rows, chan = readin.shape
    hidden = w1.shape[1]
    return call(
        readout_kernel,
        [
            sds((rows, hidden), BF16),
            sds((rows, chan // 2), F32),
            sds((rows, chan // 2), BF16),
        ],
        [SMEM] + [VMEM] * 4,
        [pltpu.VMEM((rows, chan), F32)],
        vmem=16,
        flops=4 * rows * hidden * chan,
        moved=2 * hidden * chan,
    )(me, readin, w1, b1, grad)


def tokens_kernel(me_ref, act, w2, keep, send):
    width = keep.shape[2]
    for q in range(keep.shape[0]):
        for odd, out in ((0, keep), (1, send)):
            lanes = pl.ds(pl.multiple_of((me_ref[0] ^ (2 * q + odd)) * width, width), width)
            out[q] = dot_nn(act[...], w2[:, lanes]).astype(out.dtype)


def tokens_share(me, act, w2, n):
    rows, hidden = act.shape
    width = w2.shape[1] // n
    return call(
        tokens_kernel,
        [sds((n // 2, rows, width), F32), sds((n // 2, rows, width), BF16)],
        [SMEM] + [VMEM] * 2,
        vmem=24,
        flops=2 * rows * hidden * w2.shape[1],
        moved=2 * hidden * w2.shape[1],
    )(me, act, w2)


def hidden_kernel(count, b1, w1, grad, grad_rest, *refs):
    readins = refs[:count]
    act, w1_grad, b1_grad, stacked, low = refs[count:]
    rows = readins[0].shape[0]
    for m, readin in enumerate(readins):
        stacked[m * rows : (m + 1) * rows, :] = readin[...]
    hidden = dot_nn(stacked[...], w1[...]) + b1[...]
    value, slope = gelu_both(hidden)
    act[...] = value.astype(BF16)
    low[0:rows, :] = (slope[0:rows] * grad[...]).astype(BF16)
    low[rows:, :] = (slope[rows:] * grad_rest[...]).astype(BF16)
    b1_grad[...] = jnp.sum(low[...].astype(F32), axis=0, keepdims=True)
    w1_grad[...] = dot_tn(stacked[...], low[...])


def hidden_all(b1, w1, grad, grad_rest, readins):
    rows, chan = readins[0].shape
    total = rows * len(readins)
    hidden = w1.shape[1]
    return call(
        functools.partial(hidden_kernel, len(readins)),
        [sds((total, hidden), BF16), sds((chan, hidden), F32), sds((1, hidden), F32)],
        [VMEM] * (4 + len(readins)),
        [pltpu.VMEM((total, chan), BF16), pltpu.VMEM((total, hidden), BF16)],
        vmem=24,
        flops=4 * total * hidden * chan,
        moved=8 * hidden * chan,
    )(b1, w1, grad, grad_rest, *readins)


def w2_kernel(count, me_ref, act, *refs):
    own, rest = refs[:count], refs[count : 2 * count]
    out, b2_grad, buffer, both, sems = refs[2 * count :]
    rows, width = own[0].shape
    turned = act[...].astype(F32).T.astype(BF16)
    copies = []
    for r in range(count):
        slot = r % 2
        if r >= 2:
            copies[r - 2].wait()
        both[0:rows, :] = own[r][...]
        both[rows:, :] = rest[r][...]
        if r == 0:
            b2_grad[...] = jnp.sum(both[...].astype(F32), axis=0, keepdims=True)
        buffer[slot] = dot_nn(turned, both[...])
        lanes = pl.ds(pl.multiple_of((me_ref[0] ^ r) * width, width), width)
        copy = pltpu.make_async_copy(buffer.at[slot], out.at[:, lanes], sems.at[slot])
        copy.start()
        copies.append(copy)
    for copy in copies[-2:]:
        copy.wait()


def w2_gradient(me, act, own, rest):
    total, hidden = act.shape
    rows, width = own[0].shape
    n = len(own)
    return call(
        functools.partial(w2_kernel, n),
        [sds((hidden, width * n), F32), sds((1, width), F32)],
        [SMEM] + [VMEM] * (1 + 2 * n),
        [
            pltpu.VMEM((2, hidden, width), F32),
            pltpu.VMEM((total, width), BF16),
            pltpu.SemaphoreType.DMA((2,)),
        ],
        [HBM, VMEM],
        vmem=24,
        flops=2 * total * hidden * width * n,
        moved=4 * hidden * width * n,
    )(me, act, *own, *rest)


def finish_kernel(count, *refs):
    early, late = refs[:count], refs[count : 2 * count]
    red, conv, exp, mid_gain, mid_bias, out_gain, out_bias, scr = refs[2 * count :]
    chan, mid = red.shape[2], conv.shape[3]
    held = red.shape[1]
    reduce_end, conv_end, expand_end, mid_end, end = columns(chan, mid)
    for k, parts in enumerate((early, late)):

        def summed(start, stop):
            value = parts[0][:, start:stop]
            for part in parts[1:]:
                value = value + part[:, start:stop].astype(F32)
            return value

        red[k] = summed(0, reduce_end)
        for j in range(TAPS):
            conv[k, j] = summed(reduce_end + j * mid, reduce_end + (j + 1) * mid)
        exp[k] = summed(conv_end, expand_end)
        scr[...] = jnp.zeros_like(scr)
        scr[0:held, :] = summed(expand_end, mid_end)
        flat = scr[...].T
        for which in range(2):
            mid_gain[k, which : which + 1, :] = flat[2 * which : 2 * which + 1, 0:held]
            mid_bias[k, which : which + 1, :] = flat[2 * which + 1 : 2 * which + 2, 0:held]
        block = summed(mid_end, end)
        out_gain[k : k + 1, :] = block[0:1, 0 : out_gain.shape[1]]
        out_bias[k : k + 1, :] = block[1:2, 0 : out_bias.shape[1]]


def finish(early, late, chan, mid, share):
    held = early[0].shape[0]
    outs = [
        sds((2, held, chan), F32),
        sds((2, TAPS, held, mid), F32),
        sds((2, held, chan), F32),
        sds((2, 2, held), F32),
        sds((2, 2, held), F32),
        sds((2, share), F32),
        sds((2, share), F32),
    ]
    return call(
        functools.partial(finish_kernel, len(early)),
        outs,
        [VMEM] * (2 * len(early)),
        [pltpu.VMEM((LANES, LANES), F32)],
        vmem=16,
        flops=8 * held * chan,
        moved=40 * held * chan,
    )(*early, *late)


def pool_table(grid):
    target = jnp.arange(POOLED, dtype=jnp.int32)
    place = jnp.arange(GRID, dtype=jnp.int32)
    begin = target * grid // POOLED
    ending = ((target + 1) * grid + POOLED - 1) // POOLED
    inside = (place[None, :] >= begin[:, None]) & (place[None, :] < ending[:, None])
    return inside.astype(F32) / (ending - begin)[:, None].astype(F32)


def slot_facts(valid, side):
    place = jnp.arange(side * side, dtype=jnp.int32)
    left = (place % side > 0).astype(F32)
    right = (place % side < side - 1).astype(F32)
    zero = jnp.zeros_like(left)
    return jnp.stack([valid, left, right] + [zero] * 5, axis=1)


def per_device(
    features,
    grid,
    reduce_w,
    conv_w,
    expand_w,
    mid_gain,
    mid_bias,
    out_gain,
    out_bias,
    read_w1,
    read_b1,
    read_w2,
    read_b2,
    cotangent,
):
    n = lax.axis_size("ch")
    chan, mid = reduce_w.shape[1], conv_w.shape[2]
    held, share = reduce_w.shape[2], features.shape[0]
    aligned = share == LANES and held % 16 == 0
    index = lax.axis_index("ch").astype(jnp.int32)
    me = index[None]

    feat = jnp.transpose(features[:, 0, :])
    cot = jnp.transpose(cotangent[:, 0, :])
    red = jnp.transpose(reduce_w, (0, 2, 1))
    conv = jnp.transpose(conv_w, (0, 1, 3, 2))

    if aligned:
        packed = [
            pack(k, feat if k == 0 else None, red, conv, expand_w, mid_gain, mid_bias, out_gain, out_bias)
            for k in range(2)
        ]
        pieces = [gather_pieces(p) for p in packed]
        whole = [None, None]
        x_whole = None
    else:
        rows = jnp.concatenate(
            [red, jnp.transpose(conv, (0, 2, 1, 3)).reshape(2, held, TAPS * mid), expand_w], axis=2
        )
        rows = lax.all_gather(rows, "ch", axis=1, tiled=True)
        mids = jnp.stack([mid_gain, mid_bias], axis=2).reshape(2, 4, held)
        mids = jnp.pad(lax.all_gather(mids, "ch", axis=2, tiled=True), ((0, 0), (0, 4), (0, 0)))
        outs = jnp.stack([out_gain, out_bias], axis=1)
        outs = jnp.pad(lax.all_gather(outs, "ch", axis=2, tiled=True), ((0, 0), (0, 6), (0, 0)))
        whole = [(rows[k], mids[k], outs[k]) for k in range(2)]
        x_whole = lax.all_gather(feat, "ch", axis=1, tiled=True)
        pieces = [None, None]

    side = jnp.arange(GRID, dtype=jnp.int32)
    inside = (side < grid[0]).astype(F32)
    facts = slot_facts((inside[:, None] * inside[None, :]).reshape(-1), GRID)
    facts_low = slot_facts(jnp.ones((POOLED * POOLED,), F32), POOLED)
    table = pool_table(grid[0])
    spread = jnp.einsum("ir,jq->ijrq", table, table).reshape(POOLED * POOLED, GRID * GRID)
    spread_back = jnp.transpose(spread).astype(BF16)
    spread = spread.astype(BF16)

    pooled, saved_first = block_forward(
        GRID, chan, mid, me, facts, spread, None, pieces[0], None if aligned else (x_whole,) + whole[0]
    )
    readin, saved_second = block_forward(
        POOLED, chan, mid, me, facts_low, None, pooled, pieces[1], None if aligned else (pooled,) + whole[1]
    )

    cot_own = gather_pieces(cot)
    own_grad = act_grad(me, read_w2, cot_own)
    bias_one = read_b1[None, :]
    act, mine, theirs = readout(me, readin, read_w1, bias_one, own_grad)

    half = (mine + ppermute_xor(theirs, "ch", 1).astype(F32)).astype(BF16)
    total = half.astype(F32)
    for r in range(2, n, 2):
        total = total + ppermute_xor(half, "ch", r).astype(F32)
    total = total.astype(BF16)
    second_grad = (total, ppermute_xor(total, "ch", 1))

    pooled_grad, late_grads, late_low, late_out = block_backward(
        POOLED, held, me, facts_low, second_grad, saved_second, 0, BF16
    )
    feat_grad, early_grads, early_low, early_out = block_backward(
        GRID, held, me, facts, (spread_back, pooled_grad), saved_first, share if aligned else 0, F32
    )

    early = [early_grads] + along_images(early_low)
    late = [late_grads] + along_images(late_low)
    red_grad, conv_grad, exp_grad, mid_gain_grad, mid_bias_grad, out_gain_grad, out_bias_grad = finish(
        early, late, chan, mid, share
    )
    if not aligned:
        feat_grad = lax.dynamic_slice_in_dim(feat_grad, index * share, share, 1)
        both = jnp.stack([early_out, late_out])
        both = lax.dynamic_slice_in_dim(both, index * share, share, 2)
        both = lax.psum(both.astype(BF16), "img").astype(F32)
        out_gain_grad, out_bias_grad = both[:, 0], both[:, 1]

    keep, send = tokens_share(me, act, read_w2, n)
    got = ppermute_xor(send, "ch", 1)
    parts = [keep[q] + got[q].astype(F32) for q in range(n // 2)]
    tokens = parts[0]
    for q in range(1, n // 2):
        tokens = tokens + ppermute_xor(parts[q].astype(BF16), "ch", 2 * q).astype(F32)
    tokens = (tokens + read_b2[None, :]).astype(BF16)

    cot_rest = gather_pieces(jnp.concatenate(along_images(cot), axis=0))
    rest_grad = act_grad(me, read_w2, cot_rest)
    readins = [readin] + along_images(readin)
    act_all, w1_grad, b1_grad = hidden_all(bias_one, read_w1, own_grad, rest_grad, readins)
    w2_grad, b2_grad = w2_gradient(me, act_all, cot_own, cot_rest)

    return (
        jnp.transpose(tokens)[:, None, :],
        jnp.transpose(feat_grad)[:, None, :],
        jnp.transpose(red_grad, (0, 2, 1)),
        jnp.transpose(conv_grad, (0, 1, 3, 2)),
        exp_grad,
        mid_gain_grad,
        mid_bias_grad,
        out_gain_grad,
        out_bias_grad,
        w1_grad,
        b1_grad[0],
        w2_grad,
        b2_grad[0],
    )


def solution(mesh):
    return jax.shard_map(
        per_device,
        mesh=mesh,
        in_specs=(
            P("ch", "img", None),
            P("img"),
            P(None, None, "ch"),
            P(None, None, None, "ch"),
            P(None, "ch", None),
            P(None, None, "ch"),
            P(None, None, "ch"),
            P(None, "ch"),
            P(None, "ch"),
            P(None, "ch"),
            P("ch"),
            P("ch", None),
            P("ch"),
            P("ch", "img", None),
        ),
        out_specs=(
            P("ch", "img", None),
            P("ch", "img", None),
            P(None, None, "ch"),
            P(None, None, None, "ch"),
            P(None, "ch", None),
            P(None, None, "ch"),
            P(None, None, "ch"),
            P(None, "ch"),
            P(None, "ch"),
            P(None, "ch"),
            P("ch"),
            P("ch", None),
            P("ch"),
        ),
        check_vma=False,
    )
```

time: 912 us -> 239 us (0.26)
  waiting for transfers between devices: 544 us -> 72.2 us
  blocking collectives: 212 us -> 0 us
  Pallas kernels: 0 us -> 63.3 us
  matrix products: 60.4 us -> 0 us
  starting transfers between devices: 0.49 us -> 46.3 us
  other arithmetic: 29.3 us -> 4.3 us
  between operations: 17.7 us -> 2.13 us
    psum x1 -> x0, waiting for transfers between devices: 210 us -> none  [per_device(): lax.psum(reduce_grad.astype(jnp.bfloat16), 'img').astype(jnp.float32)]
    unnamed x17 -> x0, waiting for transfers between devices: 203 us -> none
    psum x13 -> x0, blocking collectives: 165 us -> none  [the longest x6 78.4 us: norm_forward(): lax.psum((jnp.sum(values, axis=0), jnp.sum(values * values, axis=0)), 'ch')]
    reduce_scatter x3 -> x0, waiting for transfers between devices: 83.6 us -> none  [spread_sum(): lax.psum_scatter(jnp.einsum('mc,mbs->cbs', weight, data, preferred_elemen...]
    ppermute x0 -> x49, waiting for transfers between devices: none -> 72.2 us  [ppermute_xor(): lax.ppermute(x, axis, [(i, i ^ mask) for i in range(lax.axis_size(axis))])]
    pallas_call x0 -> x13, Pallas kernels: none -> 63.3 us  [the longest x2 20.8 us: block_backward(): call(functools.partial(backward_kernel, side, halves, own_lanes), outs, [...]
    dot_general x76 -> x0, matrix products: 60.4 us -> none  [the longest x18 13.1 us: block_backward(): jnp.einsum('mn,nbs->mbs', conv_w[layer, index], conv_low, preferred_eleme...]
    all_gather x3 -> x0, waiting for transfers between devices: 47.5 us -> none  [the longest x1 26.5 us: gather_channels(): return lax.all_gather(local, 'ch', axis=0, tiled=True)]
  transfers between devices with their start and end apart: 12 -> 49, of which waited for: 12 -> 7; matrix products, arithmetic and copies ran while one was open for 4% -> 5% of each run, Pallas kernels for 0% -> 27%
where the time goes in v1:
time: 239 us; the launch traced here: 235 us
  waiting for transfers between devices  72.2 us (30%)
  Pallas kernels  63.3 us (26%)
  local copies, waits for them, and re-layouts  47 us (20%)
  starting transfers between devices  46.3 us (19%)
  other arithmetic  4.3 us (2%)
    ppermute x49, waiting for transfers between devices, ppermute_xor(): lax.ppermute(x, axis, [(i, i ^ mask) for i in range(lax.axis_size(axis))])  72.2 us
    ppermute x49, starting transfers between devices, ppermute_xor(): lax.ppermute(x, axis, [(i, i ^ mask) for i in range(lax.axis_size(axis))])  46.3 us
    unnamed x182, local copies, waits for them, and re-layouts  40.3 us
    pallas_call x2, Pallas kernels, block_backward(): call(functools.partial(backward_kernel, side, halves, own_lanes), outs, [...  20.8 us
    pallas_call x2, Pallas kernels, block_forward(): call(functools.partial(forward_kernel, side, pooling, assembled is not No...  19.3 us
    pallas_call x1, Pallas kernels, w2_gradient(): call(functools.partial(w2_kernel, n), [sds((hidden, width * n), F32), sds...  9.34 us
    pallas_call x2, Pallas kernels, act_grad(): call(functools.partial(act_grad_kernel, len(pieces)), sds((rows, hidden),...  5.6 us
  transfers between devices with their start and end apart: 49, of which 7 were waited for; matrix products, arithmetic and copies ran while one was open for 5% of the time, Pallas kernels for 27%

profile of v1, /device:TPU:0, one launch (start us, length us, event | category | flops | bytes accessed | tf_op | source)
XLA Modules:
  0.0 235.3 jit_solution(9156817338889327749)
XLA Ops:
  1.2 2.6 %collective-permute-start.15 = (bf16[144,512]{1,0:T(8,128)(2,1)}, bf16[144,512]{1,0:T(8,128)(2,1)S(1)}, u32[]{:S(2)}, u32[]{:S(2)}) collective-permute-start(bf16[144,512]{1,0:T(8,128)(2,1)} %bitcast.57), channel_id=1, source_target_pairs={{0,2},{1,3},{2,0},{3,1},{4,6},{5,7},{6,4},{7,5},{8,10},{9,11},{10,... | collective-permute-start | bytes 442376 | tf_op jit(solution)/shard_map/ppermute | solution.py:53
  3.7 1.5 collective-permute-start.17
  5.3 2.0 collective-permute-start.36
  8.0 2.7 %collective-permute-start.37 = (bf16[144,512]{1,0:T(8,128)(2,1)}, bf16[144,512]{1,0:T(8,128)(2,1)S(1)}, u32[]{:S(2)}, u32[]{:S(2)}) collective-permute-start(bf16[144,512]{1,0:T(8,128)(2,1)} %bitcast.61), channel_id=1, source_target_pairs={{0,16},{8,24},{16,0},{24,8},{1,17},{9,25},{17,1},{25,9},{2,18},{10... | collective-permute-start | bytes 442376 | tf_op jit(solution)/shard_map/ppermute | solution.py:53
  23.5 1.6 collective-permute-start.8
  25.7 1.5 collective-permute-start.3
  27.8 7.2 %collective-permute-done.38 = bf16[144,512]{1,0:T(8,128)(2,1)S(1)} collective-permute-done((bf16[144,512]{1,0:T(8,128)(2,1)}, bf16[144,512]{1,0:T(8,128)(2,1)S(1)}, u32[]{:S(2)}, u32[]{:S(2)}) %collective-permute-start.38) | collective-permute-done | bytes 147488 | tf_op jit(solution)/shard_map/ppermute | solution.py:53
  35.0 2.4 %collective-permute-start.12 = (bf16[32,4608]{1,0:T(8,128)(2,1)}, bf16[32,4608]{1,0:T(8,128)(2,1)}, u32[]{:S(2)}, u32[]{:S(2)}) collective-permute-start(bf16[32,4608]{1,0:T(8,128)(2,1)} %shard_map.239.refs_3_), channel_id=1, source_target_pairs={{0,6},{1,7},{2,4},{3,5},{4,2},{5,3},{6,0},{7,1},{8,14},{9,15},{10,... | collective-permute-start | bytes 884744 | tf_op jit(solution)/shard_map/ppermute | solution.py:53
  37.5 1.1 fusion
  38.6 15.2 %collective-permute-done.10.refs_7_ = bf16[32,4608]{1,0:T(8,128)(2,1)} collective-permute-done((bf16[32,4608]{1,0:T(8,128)(2,1)}, bf16[32,4608]{1,0:T(8,128)(2,1)}, u32[]{:S(2)}, u32[]{:S(2)}) %collective-permute-start.10) | collective-permute-done | bytes 294944 | tf_op jit(solution)/shard_map/ppermute | solution.py:53
  53.8 2.4 %collective-permute-start.5 = (bf16[32,6912]{1,0:T(8,128)(2,1)S(1)}, bf16[32,6912]{1,0:T(8,128)(2,1)S(1)}, u32[]{:S(2)}, u32[]{:S(2)}) collective-permute-start(bf16[32,6912]{1,0:T(8,128)(2,1)S(1)} %shard_map.237.refs_3_), channel_id=1, source_target_pairs={{0,6},{1,7},{2,4},{3,5},{4,2},{5,3},{6,0},{7,1},{8,14},{9,15},{10,... | collective-permute-start | bytes 1327112 | tf_op jit(solution)/shard_map/ppermute | solution.py:53
  57.3 1.1 collective-permute-done.18.refs_5_
  58.6 4.4 %collective-permute-done.5.refs_9_ = bf16[32,6912]{1,0:T(8,128)(2,1)S(1)} collective-permute-done((bf16[32,6912]{1,0:T(8,128)(2,1)S(1)}, bf16[32,6912]{1,0:T(8,128)(2,1)S(1)}, u32[]{:S(2)}, u32[]{:S(2)}) %collective-permute-start.5) | collective-permute-done | bytes 442400 | tf_op jit(solution)/shard_map/ppermute | solution.py:53
  64.8 2.5 %convert_element_type.148.refs_2_ = bf16[144,576]{1,0:T(8,128)(2,1)} reshape(bf16[12,12,24,24]{3,2,1,0:T(8,128)(2,1)} %fusion) | data formatting | bytes 331776 | tf_op jit(solution)/shard_map/convert_element_type | solution.py:751
  70.4 2.2 copy-done
  72.6 1.5 shard_map.241.grad
  74.3 1.6 collective-permute-start.40
  75.8 1.0 copy-done.41
  77.9 1.0 copy-done.86
  78.9 1.0 copy-done.88
  79.9 14.4 %shard_map.238 = (bf16[576,1024]{1,0:T(8,128)(2,1)S(1)}, bf16[256,4352]{1,0:T(8,128)(2,1)S(1)}, f32[8,256]{1,0:T(8,128)S(1)}, f32[8,1024]{1,0:T(8,128)S(1)}, bf1...) custom-call(s32[1]{0:T(128)} %bitcast.refs_0_.me_ref, ...), custom_call_target="tpu_custom_call" | custom-call | flops 1283457024 | bytes 17694720 | tf_op jit(solution)/shard_map/pallas_call | solution.py:315
  94.3 1.3 copy-done.4
  98.9 4.9 %shard_map.240 = (bf16[256,4352]{1,0:T(8,128)(2,1)S(1)}, f32[8,256]{1,0:T(8,128)S(1)}, f32[8,1024]{1,0:T(8,128)S(1)}, bf16[144,1024]{1,0:T(8,128)(2,1)S(1)}, f32...) custom-call(s32[1]{0:T(128)} %bitcast.refs_0_.me_ref, ...), custom_call_target="tpu_custom_call" | custom-call | flops 320864256 | bytes 4423680 | tf_op jit(solution)/shard_map/pallas_call | solution.py:315
  105.1 1.5 collective-permute-start.42
  107.1 2.5 %collective-permute-start.28 = (bf16[144,512]{1,0:T(8,128)(2,1)S(1)}, bf16[144,512]{1,0:T(8,128)(2,1)S(1)}, u32[]{:S(2)}, u32[]{:S(2)}) collective-permute-start(bf16[144,512]{1,0:T(8,128)(2,1)S(1)} %add_convert_fusion.1), channel_id=1, source_target_pairs={{0,6},{1,7},{2,4},{3,5},{4,2},{5,3},{6,0},{7,1},{8,14},{9,15},{10,... | collective-permute-start | bytes 442376 | tf_op jit(solution)/shard_map/ppermute | solution.py:53
  110.7 20.3 %collective-permute-done.42.refs_4_.refs_12_ = bf16[432,512]{1,0:T(8,128)(2,1)} collective-permute-done((bf16[432,512]{1,0:T(8,128)(2,1)}, bf16[432,512]{1,0:T(8,128)(2,1)}, u32[]{:S(2)}, u32[]{:S(2)}) %collective-permute-start.42) | collective-permute-done | bytes 442400 | tf_op jit(solution)/shard_map/ppermute | solution.py:53
  131.6 2.0 collective-permute-done.27
  134.3 1.6 shard_map.243
  138.1 1.8 copy.32
  139.9 1.6 copy-done.7
  142.5 1.1 copy-done.25
  144.4 1.1 copy-done.33
  150.9 4.7 %shard_map.244 = (bf16[144,1024]{1,0:T(8,128)(2,1)S(1)}, f32[32,4608]{1,0:T(8,128)S(1)}, bf16[32,4608]{1,0:T(8,128)(2,1)S(1)}, f32[8,1024]{1,0:T(8,128)}) custom-call(s32[1]{0:T(128)} %bitcast.refs_0_.me_ref, f32[144,8]{1,0:T(8,128)S(1)} %copy-done.27, bf16[144,512]{1,0:T(8,128)(2,1)S(1)} %copy-done.35, bf16[144,512]{1,0:T(8,128)(2,1)S(1)} %copy-done.68, ...), custom_call_target="tpu_custom_call" | custom-call | flops 481296384 | bytes 5898240 | tf_op jit(solution)/shard_map/pallas_call | solution.py:458
  156.4 3.6 %collective-permute-start.48 = (bf16[144,1024]{1,0:T(8,128)(2,1)}, bf16[144,1024]{1,0:T(8,128)(2,1)S(1)}, u32[]{:S(2)}, u32[]{:S(2)}) collective-permute-start(bf16[144,1024]{1,0:T(8,128)(2,1)} %copy-done.42), channel_id=1, source_target_pairs={{0,24},{8,16},{16,8},{24,0},{1,25},{9,17},{17,9},{25,1},{2,26},{10... | collective-permute-start | bytes 884744 | tf_op jit(solution)/shard_map/ppermute | solution.py:53
  160.1 1.6 copy-done.5
  161.7 1.1 copy-done.31
  163.5 16.1 %shard_map.245 = (f32[576,128]{1,0:T(8,128)}, f32[32,4608]{1,0:T(8,128)S(1)}, bf16[32,4608]{1,0:T(8,128)(2,1)S(1)}, f32[8,1024]{1,0:T(8,128)}) custom-call(s32[1]{0:T(128)} %bitcast.refs_0_.me_ref, f32[576,8]{1,0:T(8,128)S(1)} %copy-done.11, bf16[576,144]{1,0:T(8,128)(2,1)S(1)} %bitcast.50, bf16[144,1024]{1,0:T(8,128)(2,1)S(1)} %get-tuple-element.70.refs_3_, ...), custom_call_target="tpu_custom_call" | custom-call | flops 1925185536 | bytes 23592960 | tf_op jit(solution)/shard_map/pallas_call | solution.py:458
  179.7 4.1 %shard_map.247.grad_rest = f32[432,512]{1,0:T(8,128)S(1)} custom-call(s32[1]{0:T(128)} %bitcast.refs_0_.me_ref, bf16[512,4096]{1,0:T(8,128)(2,1)S(1)} %copy-done.2, bf16[432,512]{1,0:T(8,128)(2,1)} %constant_dynamic-update-slice_fusion.refs_0_.refs_8_, bf16[432,512]{1,0:T(8,128)(2,1)} %collective-permute-done.39.refs_1_.refs_9_, ...), custom_call_target="tpu_custom_call" | custom-call | flops 1811939328 | bytes 4194304 | tf_op jit(solution)/shard_map/pallas_call | solution.py:494
  184.5 3.6 %collective-permute-start.32 = (bf16[32,4608]{1,0:T(8,128)(2,1)S(1)}, bf16[32,4608]{1,0:T(8,128)(2,1)S(1)}, u32[]{:S(2)}, u32[]{:S(2)}) collective-permute-start(bf16[32,4608]{1,0:T(8,128)(2,1)S(1)} %get-tuple-element.82), channel_id=1, source_target_pairs={{0,24},{8,16},{16,8},{24,0},{1,25},{9,17},{17,9},{25,1},{2,26},{10... | collective-permute-start | bytes 884744 | tf_op jit(solution)/shard_map/ppermute | solution.py:53
  188.3 3.7 %shard_map.248 = (bf16[576,512]{1,0:T(8,128)(2,1)S(1)}, f32[1024,512]{1,0:T(8,128)}, f32[1,512]{1,0:T(1,128)}) custom-call(f32[1,512]{1,0:T(1,128)S(1)} %bitcast.70, bf16[1024,512]{1,0:T(8,128)(2,1)S(1)} %copy-done.20, f32[144,512]{1,0:T(8,128)S(1)} %copy-done.14, f32[432,512]{1,0:T(8,128)S(1)} %shard_map.247.grad_rest, bf16[144,1024]{1,0:T(8,128)(2,1)S(1)} %copy-done.43, ...), custom_call_target="tpu_custom_call" | custom-call | flops 1207959552 | bytes 4194304 | tf_op jit(solution)/shard_map/pallas_call | solution.py:573
  192.8 3.6 %collective-permute-start.35 = (bf16[32,4608]{1,0:T(8,128)(2,1)S(1)}, bf16[32,4608]{1,0:T(8,128)(2,1)S(1)}, u32[]{:S(2)}, u32[]{:S(2)}) collective-permute-start(bf16[32,4608]{1,0:T(8,128)(2,1)S(1)} %get-tuple-element.84), channel_id=1, source_target_pairs={{0,24},{8,16},{16,8},{24,0},{1,25},{9,17},{17,9},{25,1},{2,26},{10... | collective-permute-start | bytes 884744 | tf_op jit(solution)/shard_map/ppermute | solution.py:53
  196.4 1.2 fusion.5
  197.6 21.9 %collective-permute-done.31.refs_2_ = bf16[32,4608]{1,0:T(8,128)(2,1)S(1)} collective-permute-done((bf16[32,4608]{1,0:T(8,128)(2,1)S(1)}, bf16[32,4608]{1,0:T(8,128)(2,1)S(1)}, u32[]{:S(2)}, u32[]{:S(2)}) %collective-permute-start.31) | collective-permute-done | bytes 294944 | tf_op jit(solution)/shard_map/ppermute | solution.py:53
  219.5 1.5 collective-permute-start.24
  221.5 1.5 collective-permute-start.22
  223.0 9.3 %shard_map.249 = (f32[512,4096]{1,0:T(8,128)}, f32[1,512]{1,0:T(1,128)}) custom-call(s32[1]{0:T(128)} %bitcast.refs_0_.me_ref, bf16[576,512]{1,0:T(8,128)(2,1)S(1)} %get-tuple-element.94.act, bf16[144,512]{1,0:T(8,128)(2,1)S(1)} %bitcast.64, bf16[144,512]{1,0:T(8,128)(2,1)S(1)} %copy-done.50, bf16[144,512]{1,0:T(8,128)(2,1)S(1)} %copy-done.52, ...), custom_call_target="tpu_custom_call" | custom-call | flops 2415919104 | bytes 8388608 | tf_op jit(solution)/shard_map/pallas_call | solution.py:611
  232.4 1.1 shard_map.246
  233.6 1.7 fusion.8
  (270 shorter events, 42.2 us)
Async XLA Ops:
  0.6 7.3 %collective-permute-start.14 = (bf16[144,512]{1,0:T(8,128)(2,1)}, bf16[144,512]{1,0:T(8,128)(2,1)S(1)}, u32[]{:S(2)}, u32[]{:S(2)}) collective-permute-start(bf16[144,512]{1,0:T(8,128)(2,1)} %bitcast.56), channel_id=1, source_target_pairs={{0,1},{1,0},{2,3},{3,2},{4,5},{5,4},{6,7},{7,6},{8,9},{9,8},{10,11... | collective-permute-start | bytes 442376 | tf_op jit(solution)/shard_map/ppermute | solution.py:53
  1.2 22.3 %collective-permute-start.15 = (bf16[144,512]{1,0:T(8,128)(2,1)}, bf16[144,512]{1,0:T(8,128)(2,1)S(1)}, u32[]{:S(2)}, u32[]{:S(2)}) collective-permute-start(bf16[144,512]{1,0:T(8,128)(2,1)} %bitcast.57), channel_id=1, source_target_pairs={{0,2},{1,3},{2,0},{3,1},{4,6},{5,7},{6,4},{7,5},{8,10},{9,11},{10,... | collective-permute-start | bytes 442376 | tf_op jit(solution)/shard_map/ppermute | solution.py:53
  3.7 21.4 %collective-permute-start.17 = (bf16[144,512]{1,0:T(8,128)(2,1)}, bf16[144,512]{1,0:T(8,128)(2,1)S(1)}, u32[]{:S(2)}, u32[]{:S(2)}) collective-permute-start(bf16[144,512]{1,0:T(8,128)(2,1)} %bitcast.58), channel_id=1, source_target_pairs={{0,4},{1,5},{2,6},{3,7},{4,0},{5,1},{6,2},{7,3},{8,12},{9,13},{10,... | collective-permute-start | bytes 442376 | tf_op jit(solution)/shard_map/ppermute | solution.py:53
  5.2 20.5 %collective-permute-start.19 = (bf16[144,512]{1,0:T(8,128)(2,1)}, bf16[144,512]{1,0:T(8,128)(2,1)S(1)}, u32[]{:S(2)}, u32[]{:S(2)}) collective-permute-start(bf16[144,512]{1,0:T(8,128)(2,1)} %bitcast.59), channel_id=1, source_target_pairs={{0,6},{1,7},{2,4},{3,5},{4,2},{5,3},{6,0},{7,1},{8,14},{9,15},{10,... | collective-permute-start | bytes 442376 | tf_op jit(solution)/shard_map/ppermute | solution.py:53
  5.3 22.0 %collective-permute-start.36 = (bf16[144,512]{1,0:T(8,128)(2,1)}, bf16[144,512]{1,0:T(8,128)(2,1)S(1)}, u32[]{:S(2)}, u32[]{:S(2)}) collective-permute-start(bf16[144,512]{1,0:T(8,128)(2,1)} %bitcast.60), channel_id=1, source_target_pairs={{0,8},{8,0},{16,24},{24,16},{1,9},{9,1},{17,25},{25,17},{2,10},{10... | collective-permute-start | bytes 442376 | tf_op jit(solution)/shard_map/ppermute | solution.py:53
  8.0 19.8 %collective-permute-start.37 = (bf16[144,512]{1,0:T(8,128)(2,1)}, bf16[144,512]{1,0:T(8,128)(2,1)S(1)}, u32[]{:S(2)}, u32[]{:S(2)}) collective-permute-start(bf16[144,512]{1,0:T(8,128)(2,1)} %bitcast.61), channel_id=1, source_target_pairs={{0,16},{8,24},{16,0},{24,8},{1,17},{9,25},{17,1},{25,9},{2,18},{10... | collective-permute-start | bytes 442376 | tf_op jit(solution)/shard_map/ppermute | solution.py:53
  23.5 13.9 %collective-permute-start.8 = (bf16[32,4608]{1,0:T(8,128)(2,1)}, bf16[32,4608]{1,0:T(8,128)(2,1)}, u32[]{:S(2)}, u32[]{:S(2)}) collective-permute-start(bf16[32,4608]{1,0:T(8,128)(2,1)} %shard_map.239.refs_3_), channel_id=1, source_target_pairs={{0,2},{1,3},{2,0},{3,1},{4,6},{5,7},{6,4},{7,5},{8,10},{9,11},{10,... | collective-permute-start | bytes 884744 | tf_op jit(solution)/shard_map/ppermute | solution.py:53
  25.1 31.6 %collective-permute-start.1 = (bf16[32,6912]{1,0:T(8,128)(2,1)S(1)}, bf16[32,6912]{1,0:T(8,128)(2,1)S(1)}, u32[]{:S(2)}, u32[]{:S(2)}) collective-permute-start(bf16[32,6912]{1,0:T(8,128)(2,1)S(1)} %shard_map.237.refs_3_), channel_id=1, source_target_pairs={{0,2},{1,3},{2,0},{3,1},{4,6},{5,7},{6,4},{7,5},{8,10},{9,11},{10,... | collective-permute-start | bytes 1327112 | tf_op jit(solution)/shard_map/ppermute | solution.py:53
  25.7 31.1 %collective-permute-start.3 = (bf16[32,6912]{1,0:T(8,128)(2,1)S(1)}, bf16[32,6912]{1,0:T(8,128)(2,1)S(1)}, u32[]{:S(2)}, u32[]{:S(2)}) collective-permute-start(bf16[32,6912]{1,0:T(8,128)(2,1)S(1)} %shard_map.237.refs_3_), channel_id=1, source_target_pairs={{0,4},{1,5},{2,6},{3,7},{4,0},{5,1},{6,2},{7,3},{8,12},{9,13},{10,... | collective-permute-start | bytes 1327112 | tf_op jit(solution)/shard_map/ppermute | solution.py:53
  27.3 26.5 %collective-permute-start.10 = (bf16[32,4608]{1,0:T(8,128)(2,1)}, bf16[32,4608]{1,0:T(8,128)(2,1)}, u32[]{:S(2)}, u32[]{:S(2)}) collective-permute-start(bf16[32,4608]{1,0:T(8,128)(2,1)} %shard_map.239.refs_3_), channel_id=1, source_target_pairs={{0,4},{1,5},{2,6},{3,7},{4,0},{5,1},{6,2},{7,3},{8,12},{9,13},{10,... | collective-permute-start | bytes 884744 | tf_op jit(solution)/shard_map/ppermute | solution.py:53
  27.8 7.3 %collective-permute-start.38 = (bf16[144,512]{1,0:T(8,128)(2,1)}, bf16[144,512]{1,0:T(8,128)(2,1)S(1)}, u32[]{:S(2)}, u32[]{:S(2)}) collective-permute-start(bf16[144,512]{1,0:T(8,128)(2,1)} %bitcast.62), channel_id=1, source_target_pairs={{0,24},{8,16},{16,8},{24,0},{1,25},{9,17},{17,9},{25,1},{2,26},{10... | collective-permute-start | bytes 442376 | tf_op jit(solution)/shard_map/ppermute | solution.py:53
  35.0 21.2 %collective-permute-start.12 = (bf16[32,4608]{1,0:T(8,128)(2,1)}, bf16[32,4608]{1,0:T(8,128)(2,1)}, u32[]{:S(2)}, u32[]{:S(2)}) collective-permute-start(bf16[32,4608]{1,0:T(8,128)(2,1)} %shard_map.239.refs_3_), channel_id=1, source_target_pairs={{0,6},{1,7},{2,4},{3,5},{4,2},{5,3},{6,0},{7,1},{8,14},{9,15},{10,... | collective-permute-start | bytes 884744 | tf_op jit(solution)/shard_map/ppermute | solution.py:53
  37.5 18.8 %collective-permute-start.16 = (bf16[144,512]{1,0:T(8,128)(2,1)S(1)}, bf16[144,512]{1,0:T(8,128)(2,1)S(1)}, u32[]{:S(2)}, u32[]{:S(2)}) collective-permute-start(bf16[144,512]{1,0:T(8,128)(2,1)S(1)} %collective-permute-done.15.refs_2_), channel_id=1, source_target_pairs={{0,1},{1,0},{2,3},{3,2},{4,5},{5,4},{6,7},{7,6},{8,9},{9,8},{10,11... | collective-permute-start | bytes 442376 | tf_op jit(solution)/shard_map/ppermute | solution.py:53
  53.8 9.2 %collective-permute-start.5 = (bf16[32,6912]{1,0:T(8,128)(2,1)S(1)}, bf16[32,6912]{1,0:T(8,128)(2,1)S(1)}, u32[]{:S(2)}, u32[]{:S(2)}) collective-permute-start(bf16[32,6912]{1,0:T(8,128)(2,1)S(1)} %shard_map.237.refs_3_), channel_id=1, source_target_pairs={{0,6},{1,7},{2,4},{3,5},{4,2},{5,3},{6,0},{7,1},{8,14},{9,15},{10,... | collective-permute-start | bytes 1327112 | tf_op jit(solution)/shard_map/ppermute | solution.py:53
  56.2 12.3 %collective-permute-start = (bf16[32,6912]{1,0:T(8,128)(2,1)S(1)}, bf16[32,6912]{1,0:T(8,128)(2,1)}, u32[]{:S(2)}, u32[]{:S(2)}) collective-permute-start(bf16[32,6912]{1,0:T(8,128)(2,1)S(1)} %shard_map.237.refs_3_), channel_id=1, source_target_pairs={{0,1},{1,0},{2,3},{3,2},{4,5},{5,4},{6,7},{7,6},{8,9},{9,8},{10,11... | collective-permute-start | bytes 1327112 | tf_op jit(solution)/shard_map/ppermute | solution.py:53
  56.7 11.8 %collective-permute-start.2 = (bf16[32,6912]{1,0:T(8,128)(2,1)S(1)}, bf16[32,6912]{1,0:T(8,128)(2,1)}, u32[]{:S(2)}, u32[]{:S(2)}) collective-permute-start(bf16[32,6912]{1,0:T(8,128)(2,1)S(1)} %collective-permute-done.1.refs_5_), channel_id=1, source_target_pairs={{0,1},{1,0},{2,3},{3,2},{4,5},{5,4},{6,7},{7,6},{8,9},{9,8},{10,11... | collective-permute-start | bytes 1327112 | tf_op jit(solution)/shard_map/ppermute | solution.py:53
  56.8 12.2 %collective-permute-start.4 = (bf16[32,6912]{1,0:T(8,128)(2,1)S(1)}, bf16[32,6912]{1,0:T(8,128)(2,1)}, u32[]{:S(2)}, u32[]{:S(2)}) collective-permute-start(bf16[32,6912]{1,0:T(8,128)(2,1)S(1)} %collective-permute-done.3.refs_7_), channel_id=1, source_target_pairs={{0,1},{1,0},{2,3},{3,2},{4,5},{5,4},{6,7},{7,6},{8,9},{9,8},{10,11... | collective-permute-start | bytes 1327112 | tf_op jit(solution)/shard_map/ppermute | solution.py:53
  58.4 9.5 %collective-permute-start.20 = (bf16[144,512]{1,0:T(8,128)(2,1)S(1)}, bf16[144,512]{1,0:T(8,128)(2,1)S(1)}, u32[]{:S(2)}, u32[]{:S(2)}) collective-permute-start(bf16[144,512]{1,0:T(8,128)(2,1)S(1)} %collective-permute-done.19.refs_6_), channel_id=1, source_target_pairs={{0,1},{1,0},{2,3},{3,2},{4,5},{5,4},{6,7},{7,6},{8,9},{9,8},{10,11... | collective-permute-start | bytes 442376 | tf_op jit(solution)/shard_map/ppermute | solution.py:53
  63.0 11.3 %collective-permute-start.6 = (bf16[32,6912]{1,0:T(8,128)(2,1)S(1)}, bf16[32,6912]{1,0:T(8,128)(2,1)}, u32[]{:S(2)}, u32[]{:S(2)}) collective-permute-start(bf16[32,6912]{1,0:T(8,128)(2,1)S(1)} %collective-permute-done.5.refs_9_), channel_id=1, source_target_pairs={{0,1},{1,0},{2,3},{3,2},{4,5},{5,4},{6,7},{7,6},{8,9},{9,8},{10,11... | collective-permute-start | bytes 1327112 | tf_op jit(solution)/shard_map/ppermute | solution.py:53
  68.0 30.9 %collective-permute-start.7 = (bf16[32,4608]{1,0:T(8,128)(2,1)}, bf16[32,4608]{1,0:T(8,128)(2,1)S(1)}, u32[]{:S(2)}, u32[]{:S(2)}) collective-permute-start(bf16[32,4608]{1,0:T(8,128)(2,1)} %shard_map.239.refs_3_), channel_id=1, source_target_pairs={{0,1},{1,0},{2,3},{3,2},{4,5},{5,4},{6,7},{7,6},{8,9},{9,8},{10,11... | collective-permute-start | bytes 884744 | tf_op jit(solution)/shard_map/ppermute | solution.py:53
  68.5 30.4 %collective-permute-start.9 = (bf16[32,4608]{1,0:T(8,128)(2,1)}, bf16[32,4608]{1,0:T(8,128)(2,1)S(1)}, u32[]{:S(2)}, u32[]{:S(2)}) collective-permute-start(bf16[32,4608]{1,0:T(8,128)(2,1)} %collective-permute-done.8.refs_5_), channel_id=1, source_target_pairs={{0,1},{1,0},{2,3},{3,2},{4,5},{5,4},{6,7},{7,6},{8,9},{9,8},{10,11... | collective-permute-start | bytes 884744 | tf_op jit(solution)/shard_map/ppermute | solution.py:53
  68.5 30.3 %collective-permute-start.11 = (bf16[32,4608]{1,0:T(8,128)(2,1)}, bf16[32,4608]{1,0:T(8,128)(2,1)S(1)}, u32[]{:S(2)}, u32[]{:S(2)}) collective-permute-start(bf16[32,4608]{1,0:T(8,128)(2,1)} %collective-permute-done.10.refs_7_), channel_id=1, source_target_pairs={{0,1},{1,0},{2,3},{3,2},{4,5},{5,4},{6,7},{7,6},{8,9},{9,8},{10,11... | collective-permute-start | bytes 884744 | tf_op jit(solution)/shard_map/ppermute | solution.py:53
  69.0 29.9 %collective-permute-start.13 = (bf16[32,4608]{1,0:T(8,128)(2,1)}, bf16[32,4608]{1,0:T(8,128)(2,1)S(1)}, u32[]{:S(2)}, u32[]{:S(2)}) collective-permute-start(bf16[32,4608]{1,0:T(8,128)(2,1)} %collective-permute-done.12.refs_9_), channel_id=1, source_target_pairs={{0,1},{1,0},{2,3},{3,2},{4,5},{5,4},{6,7},{7,6},{8,9},{9,8},{10,11... | collective-permute-start | bytes 884744 | tf_op jit(solution)/shard_map/ppermute | solution.py:53
  74.3 35.9 %collective-permute-start.40 = (bf16[432,512]{1,0:T(8,128)(2,1)}, bf16[432,512]{1,0:T(8,128)(2,1)}, u32[]{:S(2)}, u32[]{:S(2)}) collective-permute-start(bf16[432,512]{1,0:T(8,128)(2,1)} %constant_dynamic-update-slice_fusion.refs_0_.refs_8_), channel_id=1, source_target_pairs={{0,2},{1,3},{2,0},{3,1},{4,6},{5,7},{6,4},{7,5},{8,10},{9,11},{10,... | collective-permute-start | bytes 1327112 | tf_op jit(solution)/shard_map/ppermute | solution.py:53
  104.9 2.2 collective-permute-start.25
  105.1 25.9 %collective-permute-start.42 = (bf16[432,512]{1,0:T(8,128)(2,1)}, bf16[432,512]{1,0:T(8,128)(2,1)}, u32[]{:S(2)}, u32[]{:S(2)}) collective-permute-start(bf16[432,512]{1,0:T(8,128)(2,1)} %constant_dynamic-update-slice_fusion.refs_0_.refs_8_), channel_id=1, source_target_pairs={{0,4},{1,5},{2,6},{3,7},{4,0},{5,1},{6,2},{7,3},{8,12},{9,13},{10,... | collective-permute-start | bytes 1327112 | tf_op jit(solution)/shard_map/ppermute | solution.py:53
  106.6 27.6 %collective-permute-start.44 = (bf16[432,512]{1,0:T(8,128)(2,1)}, bf16[432,512]{1,0:T(8,128)(2,1)}, u32[]{:S(2)}, u32[]{:S(2)}) collective-permute-start(bf16[432,512]{1,0:T(8,128)(2,1)} %constant_dynamic-update-slice_fusion.refs_0_.refs_8_), channel_id=1, source_target_pairs={{0,6},{1,7},{2,4},{3,5},{4,2},{5,3},{6,0},{7,1},{8,14},{9,15},{10,... | collective-permute-start | bytes 1327112 | tf_op jit(solution)/shard_map/ppermute | solution.py:53
  107.1 23.9 %collective-permute-start.28 = (bf16[144,512]{1,0:T(8,128)(2,1)S(1)}, bf16[144,512]{1,0:T(8,128)(2,1)S(1)}, u32[]{:S(2)}, u32[]{:S(2)}) collective-permute-start(bf16[144,512]{1,0:T(8,128)(2,1)S(1)} %add_convert_fusion.1), channel_id=1, source_target_pairs={{0,6},{1,7},{2,4},{3,5},{4,2},{5,3},{6,0},{7,1},{8,14},{9,15},{10,... | collective-permute-start | bytes 442376 | tf_op jit(solution)/shard_map/ppermute | solution.py:53
  109.7 23.9 %collective-permute-start.27 = (bf16[144,512]{1,0:T(8,128)(2,1)S(1)}, bf16[144,512]{1,0:T(8,128)(2,1)S(1)}, u32[]{:S(2)}, u32[]{:S(2)}) collective-permute-start(bf16[144,512]{1,0:T(8,128)(2,1)S(1)} %add_convert_fusion.1), channel_id=1, source_target_pairs={{0,4},{1,5},{2,6},{3,7},{4,0},{5,1},{6,2},{7,3},{8,12},{9,13},{10,... | collective-permute-start | bytes 442376 | tf_op jit(solution)/shard_map/ppermute | solution.py:53
  110.2 23.4 %collective-permute-start.26 = (bf16[144,512]{1,0:T(8,128)(2,1)S(1)}, bf16[144,512]{1,0:T(8,128)(2,1)S(1)}, u32[]{:S(2)}, u32[]{:S(2)}) collective-permute-start(bf16[144,512]{1,0:T(8,128)(2,1)S(1)} %add_convert_fusion.1), channel_id=1, source_target_pairs={{0,2},{1,3},{2,0},{3,1},{4,6},{5,7},{6,4},{7,5},{8,10},{9,11},{10,... | collective-permute-start | bytes 442376 | tf_op jit(solution)/shard_map/ppermute | solution.py:53
  131.1 24.5 %collective-permute-start.39 = (bf16[432,512]{1,0:T(8,128)(2,1)}, bf16[432,512]{1,0:T(8,128)(2,1)}, u32[]{:S(2)}, u32[]{:S(2)}) collective-permute-start(bf16[432,512]{1,0:T(8,128)(2,1)} %constant_dynamic-update-slice_fusion.refs_0_.refs_8_), channel_id=1, source_target_pairs={{0,1},{1,0},{2,3},{3,2},{4,5},{5,4},{6,7},{7,6},{8,9},{9,8},{10,11... | collective-permute-start | bytes 1327112 | tf_op jit(solution)/shard_map/ppermute | solution.py:53
  131.1 25.0 %collective-permute-start.41 = (bf16[432,512]{1,0:T(8,128)(2,1)}, bf16[432,512]{1,0:T(8,128)(2,1)}, u32[]{:S(2)}, u32[]{:S(2)}) collective-permute-start(bf16[432,512]{1,0:T(8,128)(2,1)} %collective-permute-done.40.refs_2_.refs_10_), channel_id=1, source_target_pairs={{0,1},{1,0},{2,3},{3,2},{4,5},{5,4},{6,7},{7,6},{8,9},{9,8},{10,11... | collective-permute-start | bytes 1327112 | tf_op jit(solution)/shard_map/ppermute | solution.py:53
  133.5 22.9 %collective-permute-start.43 = (bf16[432,512]{1,0:T(8,128)(2,1)}, bf16[432,512]{1,0:T(8,128)(2,1)}, u32[]{:S(2)}, u32[]{:S(2)}) collective-permute-start(bf16[432,512]{1,0:T(8,128)(2,1)} %collective-permute-done.42.refs_4_.refs_12_), channel_id=1, source_target_pairs={{0,1},{1,0},{2,3},{3,2},{4,5},{5,4},{6,7},{7,6},{8,9},{9,8},{10,11... | collective-permute-start | bytes 1327112 | tf_op jit(solution)/shard_map/ppermute | solution.py:53
  133.6 3.3 %collective-permute-start.29 = (bf16[144,512]{1,0:T(8,128)(2,1)S(1)}, bf16[144,512]{1,0:T(8,128)(2,1)S(1)}, u32[]{:S(2)}, u32[]{:S(2)}) collective-permute-start(bf16[144,512]{1,0:T(8,128)(2,1)S(1)} %add_convert_fusion.refs_2_), channel_id=1, source_target_pairs={{0,1},{1,0},{2,3},{3,2},{4,5},{5,4},{6,7},{7,6},{8,9},{9,8},{10,11... | collective-permute-start | bytes 442376 | tf_op jit(solution)/shard_map/ppermute | solution.py:53
  134.2 45.4 %collective-permute-start.45 = (bf16[432,512]{1,0:T(8,128)(2,1)}, bf16[432,512]{1,0:T(8,128)(2,1)}, u32[]{:S(2)}, u32[]{:S(2)}) collective-permute-start(bf16[432,512]{1,0:T(8,128)(2,1)} %collective-permute-done.44.refs_6_.refs_14_), channel_id=1, source_target_pairs={{0,1},{1,0},{2,3},{3,2},{4,5},{5,4},{6,7},{7,6},{8,9},{9,8},{10,11... | collective-permute-start | bytes 1327112 | tf_op jit(solution)/shard_map/ppermute | solution.py:53
  137.6 54.4 %collective-permute-start.21 = (bf16[4,144,512]{2,1,0:T(8,128)(2,1)}, bf16[4,144,512]{2,1,0:T(8,128)(2,1)}, u32[]{:S(2)}, u32[]{:S(2)}) collective-permute-start(bf16[4,144,512]{2,1,0:T(8,128)(2,1)} %get-tuple-element.59), channel_id=1, source_target_pairs={{0,1},{1,0},{2,3},{3,2},{4,5},{5,4},{6,7},{7,6},{8,9},{9,8},{10,11... | collective-permute-start | bytes 1769480 | tf_op jit(solution)/shard_map/ppermute | solution.py:53
  155.6 28.2 %collective-permute-start.46 = (bf16[144,1024]{1,0:T(8,128)(2,1)}, bf16[144,1024]{1,0:T(8,128)(2,1)S(1)}, u32[]{:S(2)}, u32[]{:S(2)}) collective-permute-start(bf16[144,1024]{1,0:T(8,128)(2,1)} %copy-done.42), channel_id=1, source_target_pairs={{0,8},{8,0},{16,24},{24,16},{1,9},{9,1},{17,25},{25,17},{2,10},{10... | collective-permute-start | bytes 884744 | tf_op jit(solution)/shard_map/ppermute | solution.py:53
  156.1 28.5 %collective-permute-start.47 = (bf16[144,1024]{1,0:T(8,128)(2,1)}, bf16[144,1024]{1,0:T(8,128)(2,1)S(1)}, u32[]{:S(2)}, u32[]{:S(2)}) collective-permute-start(bf16[144,1024]{1,0:T(8,128)(2,1)} %copy-done.42), channel_id=1, source_target_pairs={{0,16},{8,24},{16,0},{24,8},{1,17},{9,25},{17,1},{25,9},{2,18},{10... | collective-permute-start | bytes 884744 | tf_op jit(solution)/shard_map/ppermute | solution.py:53
  156.4 31.7 %collective-permute-start.48 = (bf16[144,1024]{1,0:T(8,128)(2,1)}, bf16[144,1024]{1,0:T(8,128)(2,1)S(1)}, u32[]{:S(2)}, u32[]{:S(2)}) collective-permute-start(bf16[144,1024]{1,0:T(8,128)(2,1)} %copy-done.42), channel_id=1, source_target_pairs={{0,24},{8,16},{16,8},{24,0},{1,25},{9,17},{17,9},{25,1},{2,26},{10... | collective-permute-start | bytes 884744 | tf_op jit(solution)/shard_map/ppermute | solution.py:53
  179.7 13.1 %collective-permute-start.30 = (bf16[32,4608]{1,0:T(8,128)(2,1)S(1)}, bf16[32,4608]{1,0:T(8,128)(2,1)S(1)}, u32[]{:S(2)}, u32[]{:S(2)}) collective-permute-start(bf16[32,4608]{1,0:T(8,128)(2,1)S(1)} %get-tuple-element.82), channel_id=1, source_target_pairs={{0,8},{8,0},{16,24},{24,16},{1,9},{9,1},{17,25},{25,17},{2,10},{10... | collective-permute-start | bytes 884744 | tf_op jit(solution)/shard_map/ppermute | solution.py:53
  183.8 35.7 %collective-permute-start.31 = (bf16[32,4608]{1,0:T(8,128)(2,1)S(1)}, bf16[32,4608]{1,0:T(8,128)(2,1)S(1)}, u32[]{:S(2)}, u32[]{:S(2)}) collective-permute-start(bf16[32,4608]{1,0:T(8,128)(2,1)S(1)} %get-tuple-element.82), channel_id=1, source_target_pairs={{0,16},{8,24},{16,0},{24,8},{1,17},{9,25},{17,1},{25,9},{2,18},{10... | collective-permute-start | bytes 884744 | tf_op jit(solution)/shard_map/ppermute | solution.py:53
  184.5 36.4 %collective-permute-start.32 = (bf16[32,4608]{1,0:T(8,128)(2,1)S(1)}, bf16[32,4608]{1,0:T(8,128)(2,1)S(1)}, u32[]{:S(2)}, u32[]{:S(2)}) collective-permute-start(bf16[32,4608]{1,0:T(8,128)(2,1)S(1)} %get-tuple-element.82), channel_id=1, source_target_pairs={{0,24},{8,16},{16,8},{24,0},{1,25},{9,17},{17,9},{25,1},{2,26},{10... | collective-permute-start | bytes 884744 | tf_op jit(solution)/shard_map/ppermute | solution.py:53
  188.2 33.3 %collective-permute-start.33 = (bf16[32,4608]{1,0:T(8,128)(2,1)S(1)}, bf16[32,4608]{1,0:T(8,128)(2,1)S(1)}, u32[]{:S(2)}, u32[]{:S(2)}) collective-permute-start(bf16[32,4608]{1,0:T(8,128)(2,1)S(1)} %get-tuple-element.84), channel_id=1, source_target_pairs={{0,8},{8,0},{16,24},{24,16},{1,9},{9,1},{17,25},{25,17},{2,10},{10... | collective-permute-start | bytes 884744 | tf_op jit(solution)/shard_map/ppermute | solution.py:53
  192.0 40.4 %collective-permute-start.34 = (bf16[32,4608]{1,0:T(8,128)(2,1)S(1)}, bf16[32,4608]{1,0:T(8,128)(2,1)S(1)}, u32[]{:S(2)}, u32[]{:S(2)}) collective-permute-start(bf16[32,4608]{1,0:T(8,128)(2,1)S(1)} %get-tuple-element.84), channel_id=1, source_target_pairs={{0,16},{8,24},{16,0},{24,8},{1,17},{9,25},{17,1},{25,9},{2,18},{10... | collective-permute-start | bytes 884744 | tf_op jit(solution)/shard_map/ppermute | solution.py:53
  192.8 39.6 %collective-permute-start.35 = (bf16[32,4608]{1,0:T(8,128)(2,1)S(1)}, bf16[32,4608]{1,0:T(8,128)(2,1)S(1)}, u32[]{:S(2)}, u32[]{:S(2)}) collective-permute-start(bf16[32,4608]{1,0:T(8,128)(2,1)S(1)} %get-tuple-element.84), channel_id=1, source_target_pairs={{0,24},{8,16},{16,8},{24,0},{1,25},{9,17},{17,9},{25,1},{2,26},{10... | collective-permute-start | bytes 884744 | tf_op jit(solution)/shard_map/ppermute | solution.py:53
  219.5 14.1 %collective-permute-start.24 = (bf16[144,512]{1,0:T(8,128)(2,1)S(1)}, bf16[144,512]{1,0:T(8,128)(2,1)S(1)}, u32[]{:S(2)}, u32[]{:S(2)}) collective-permute-start(bf16[144,512]{1,0:T(8,128)(2,1)S(1)} %get-tuple-element.98), channel_id=1, source_target_pairs={{0,6},{1,7},{2,4},{3,5},{4,2},{5,3},{6,0},{7,1},{8,14},{9,15},{10,... | collective-permute-start | bytes 442376 | tf_op jit(solution)/shard_map/ppermute | solution.py:53
  221.0 12.6 %collective-permute-start.23 = (bf16[144,512]{1,0:T(8,128)(2,1)S(1)}, bf16[144,512]{1,0:T(8,128)(2,1)S(1)}, u32[]{:S(2)}, u32[]{:S(2)}) collective-permute-start(bf16[144,512]{1,0:T(8,128)(2,1)S(1)} %get-tuple-element.99), channel_id=1, source_target_pairs={{0,4},{1,5},{2,6},{3,7},{4,0},{5,1},{6,2},{7,3},{8,12},{9,13},{10,... | collective-permute-start | bytes 442376 | tf_op jit(solution)/shard_map/ppermute | solution.py:53
  221.5 12.1 %collective-permute-start.22 = (bf16[144,512]{1,0:T(8,128)(2,1)S(1)}, bf16[144,512]{1,0:T(8,128)(2,1)S(1)}, u32[]{:S(2)}, u32[]{:S(2)}) collective-permute-start(bf16[144,512]{1,0:T(8,128)(2,1)S(1)} %get-tuple-element.97), channel_id=1, source_target_pairs={{0,2},{1,3},{2,0},{3,1},{4,6},{5,7},{6,4},{7,5},{8,10},{9,11},{10,... | collective-permute-start | bytes 442376 | tf_op jit(solution)/shard_map/ppermute | solution.py:53
  (91 other events, 1192.4 us)

commit v2 on v1

v2 whole, which is shorter than its diff:
```python
import functools

import jax
import jax.numpy as jnp
from jax import lax
from jax.experimental import pallas as pl
from jax.experimental.pallas import tpu as pltpu
from jax.sharding import PartitionSpec as P

GRID = 24
POOLED = 12
EPSILON = 1e-06
OFFSETS = [(-1, -1), (-1, 0), (-1, 1), (0, -1), (0, 0), (0, 1), (1, -1), (1, 0), (1, 1)]
TAPS = len(OFFSETS)
LANES = 128
BF16 = jnp.bfloat16
F32 = jnp.float32
SMEM = pl.BlockSpec(memory_space=pltpu.SMEM)
ANY = pl.BlockSpec(memory_space=pl.ANY)


def dot_nn(left, right):
    return lax.dot_general(left, right, (((1,), (0,)), ((), ())), preferred_element_type=F32)


def dot_nt(left, right):
    return lax.dot_general(left, right, (((1,), (1,)), ((), ())), preferred_element_type=F32)


def dot_tn(left, right):
    return lax.dot_general(left, right, (((0,), (0,)), ((), ())), preferred_element_type=F32)


def sds(shape, dtype):
    return jax.ShapeDtypeStruct(tuple(shape), dtype)


class Inward:
    def __init__(self, source, buffer, sem):
        self.copy = pltpu.make_async_copy(source, buffer, sem)
        self.buffer, self.waited = buffer, False
        self.copy.start()

    def __call__(self):
        if not self.waited:
            self.copy.wait()
            self.waited = True
        return self.buffer


class Outward:
    def __init__(self, target, buffer, sem):
        self.copy = pltpu.make_async_copy(buffer, target, sem)
        self.buffer, self.sent = buffer, False

    def __call__(self):
        return self.buffer

    def send(self):
        if not self.sent:
            self.copy.start()
            self.sent = True


def call(body, outs, scalars, args, scratch=(), vmem=60, flops=0, moved=0, plain=(), after=()):
    count = (len(scalars), len(args), len(plain), len(after), len(outs))

    def kernel(*refs):
        refs = list(refs)

        def take(k):
            got = refs[:k]
            del refs[:k]
            return got

        scalar_refs, sources, plain_refs, _, targets = [take(k) for k in count]
        in_buffers, out_buffers = take(len(args)), take(len(outs))
        in_sems = refs.pop(0) if args else None
        out_sems = refs.pop(0)
        inward = [Inward(s, b, in_sems.at[i]) for i, (s, b) in enumerate(zip(sources, in_buffers))]
        outward = [Outward(t, b, out_sems.at[i]) for i, (t, b) in enumerate(zip(targets, out_buffers))]
        body(scalar_refs, inward, outward, plain_refs, *refs)
        for item in inward:
            item()
        for item in outward:
            item.send()
        for item in outward:
            item.copy.wait()

    shapes = [pltpu.VMEM(x.shape, x.dtype) for x in list(args) + list(outs)]
    sems = ([pltpu.SemaphoreType.DMA((len(args),))] if args else []) + [
        pltpu.SemaphoreType.DMA((len(outs),))
    ]
    return pl.pallas_call(
        kernel,
        out_shape=list(outs),
        in_specs=[SMEM] * len(scalars) + [ANY] * (len(args) + len(plain) + len(after)),
        out_specs=[ANY] * len(outs),
        scratch_shapes=shapes + sems + list(scratch),
        compiler_params=pltpu.CompilerParams(vmem_limit_bytes=vmem << 20),
        cost_estimate=pl.CostEstimate(flops=flops, bytes_accessed=moved, transcendentals=0),
    )(*scalars, *args, *plain, *after)


def gate(values, *after):
    def nothing(*refs):
        pass

    return pl.pallas_call(
        nothing,
        out_shape=[sds(v.shape, v.dtype) for v in values],
        in_specs=[ANY] * (len(values) + len(after)),
        out_specs=[ANY] * len(values),
        input_output_aliases={i: i for i in range(len(values))},
    )(*values, *after)


def join_body(scalars, ins, outs, plain):
    at = 0
    for item in ins:
        rows = item.buffer.shape[0]
        outs[0]()[at : at + rows, :] = item()[...]
        at += rows


def join(*parts, after=()):
    rows = sum(x.shape[0] for x in parts)
    shape = sds((rows, parts[0].shape[1]), parts[0].dtype)
    return call(join_body, [shape], [], list(parts), after=after)[0]


def add_body(scalars, ins, outs, plain):
    outs[0]()[...] = (ins[0]()[...].astype(F32) + ins[1]()[...].astype(F32)).astype(BF16)


def add(left, right, after=()):
    return call(add_body, [sds(left.shape, BF16)], [], [left, right], after=after)[0]


def ppermute_xor(x, axis, mask):
    return lax.ppermute(x, axis, [(i, i ^ mask) for i in range(lax.axis_size(axis))])


def neighbours(x):
    n = lax.axis_size("ch")
    return {r: ppermute_xor(x, "ch", r) for r in range(n - 2, 0, -2)}


def with_cores(x, far):
    n = lax.axis_size("ch")
    pieces = [None] * n
    for r in range(0, n, 2):
        pieces[r] = far[r] if r else x
        pieces[r + 1] = ppermute_xor(pieces[r], "ch", 1)
    return pieces


def along_images(x):
    return [ppermute_xor(x, "img", m) for m in range(1, lax.axis_size("img"))]


def rows_of(value, index, count):
    return value[pl.ds(pl.multiple_of(index * count, count), count), :]


def half_of(value, second, count):
    return jnp.where(second == 1, value[count : 2 * count, :], value[0:count, :])


def columns(chan, mid):
    reduce_end = chan
    conv_end = reduce_end + TAPS * mid
    expand_end = conv_end + chan
    return reduce_end, conv_end, expand_end, expand_end + LANES, expand_end + 2 * LANES


def split_low(value):
    high = value.astype(BF16).astype(F32)
    return high, value - high


def pack_body(layer, scalars, ins, outs, plain, scr, *bufs):
    feat, mid_gain, mid_bias, out_gain, out_bias = ins
    red, conv, exp = plain
    red_buf, conv_buf, exp_buf, sems = bufs
    copies = [
        pltpu.make_async_copy(source.at[layer], buffer, sems.at[i])
        for i, (source, buffer) in enumerate(((red, red_buf), (conv, conv_buf), (exp, exp_buf)))
    ]
    for copy in copies:
        copy.start()
    packet = outs[0]()
    held, chan, mid = red_buf.shape[0], red_buf.shape[1], conv_buf.shape[2]
    reduce_end, conv_end, expand_end, mid_end, end = columns(chan, mid)
    scr[...] = jnp.zeros_like(scr)
    for which in range(2):
        for kind, ref in enumerate((mid_gain(), mid_bias())):
            high, low = split_low(ref[layer, which : which + 1, :])
            at = 4 * which + 2 * kind
            scr[at : at + 1, 0:held] = high
            scr[at + 1 : at + 2, 0:held] = low
    packet[:, expand_end:mid_end] = scr[...].T[0:held, :].astype(BF16)
    scr[...] = jnp.zeros_like(scr)
    for kind, ref in enumerate((out_gain(), out_bias())):
        high, low = split_low(ref[layer : layer + 1, :])
        scr[2 * kind : 2 * kind + 1, :] = high
        scr[2 * kind + 1 : 2 * kind + 2, :] = low
    packet[:, mid_end:end] = scr[0:held, :].astype(BF16)
    feat = feat()
    if layer == 0:
        for b in range(feat.shape[0] // held):
            packet[:, end + b * LANES : end + (b + 1) * LANES] = feat[b * held : (b + 1) * held, :]
    else:
        outs[1]()[...] = feat[...]
    for copy in copies:
        copy.wait()
    packet[:, 0:reduce_end] = red_buf[...]
    for j in range(TAPS):
        packet[:, reduce_end + j * mid : reduce_end + (j + 1) * mid] = conv_buf[j]
    packet[:, conv_end:expand_end] = exp_buf[...]


def pack(layer, extra, red, conv, exp, mid_gain, mid_bias, out_gain, out_bias, after=()):
    held, chan = red.shape[1:]
    mid = conv.shape[3]
    width = columns(chan, mid)[-1]
    if layer:
        outs = [sds((held, width), BF16), sds(extra.shape, BF16)]
    else:
        width += extra.shape[0] * extra.shape[1] // held
        outs = [sds((held, width), BF16)]
    return call(
        functools.partial(pack_body, layer),
        outs,
        [],
        [extra, mid_gain, mid_bias, out_gain, out_bias],
        [
            pltpu.VMEM((LANES, LANES), F32),
            pltpu.VMEM(red.shape[1:], BF16),
            pltpu.VMEM(conv.shape[1:], BF16),
            pltpu.VMEM(exp.shape[1:], BF16),
            pltpu.SemaphoreType.DMA((3,)),
        ],
        moved=2 * held * width * 2,
        plain=[red, conv, exp],
        after=after,
    )


def assemble(me, pieces, x_ref, w_ref, mid_ref, out_ref, stage, scr, sems):
    held = pieces[0].shape[0]
    chan, mid = out_ref.shape[1], w_ref.shape[0]
    reduce_end, conv_end, expand_end, mid_end, end = columns(chan, mid)
    width = stage.shape[2]
    copies, weights = [], []
    for r, piece in enumerate(pieces):
        copies.append(
            pltpu.make_async_copy(piece.at[:, expand_end : expand_end + width], stage.at[r], sems.at[0, r])
        )
        copies[-1].start()
    for r, piece in enumerate(pieces):
        rows = pl.ds(pl.multiple_of((me ^ r) * held, held), held)
        weights.append(pltpu.make_async_copy(piece.at[:, 0:expand_end], w_ref.at[rows, :], sems.at[1, r]))
        weights[-1].start()
    for r in range(len(pieces)):
        copies[r].wait()
        rows = pl.ds(pl.multiple_of((me ^ r) * held, held), held)
        lanes = pl.ds(pl.multiple_of((me ^ r) * LANES, LANES), LANES)
        scr[rows, :] = stage[r, :, 0:LANES].astype(F32)
        block = stage[r, :, LANES : 2 * LANES].astype(F32)
        out_ref[0:1, lanes] = block[0:1, :] + block[1:2, :]
        out_ref[1:2, lanes] = block[2:3, :] + block[3:4, :]
        for b in range(width // LANES - 2):
            at = (b + 2) * LANES
            x_ref[b * held : (b + 1) * held, lanes] = stage[r, :, at : at + LANES]
    flat = scr[...].T
    for q in range(4):
        mid_ref[q : q + 1, :] = flat[2 * q : 2 * q + 1, :] + flat[2 * q + 1 : 2 * q + 2, :]
    for copy in weights:
        copy.wait()


def sigmoid(value):
    return 0.5 * jnp.tanh(0.5 * value) + 0.5


def silu(value):
    return value * sigmoid(value)


def silu_slope(value):
    gate = sigmoid(value)
    return gate * (1.0 + value * (1.0 - gate))


def unit_of(values):
    inverse = 1.0 / values.shape[-1]
    center = jnp.sum(values, axis=-1, keepdims=True) * inverse
    spread = jnp.sum(values * values, axis=-1, keepdims=True) * inverse - center * center
    factor = lax.rsqrt(spread + EPSILON)
    return (values - center) * factor, factor


def chunked(slots, body, carry=None):
    return body(slice(0, slots), 0, carry)


def pad_of(side):
    return -(-(side + 1) // 16) * 16


def shift_columns(field, side, slots, aux_ref):
    pad = pad_of(side)
    field[0, pad : pad + slots, :] = field[1, pad - 1 : pad - 1 + slots, :] * aux_ref[:, 1:2]
    field[2, pad : pad + slots, :] = field[1, pad + 1 : pad + 1 + slots, :] * aux_ref[:, 2:3]


def clear_edges(field, side, slots):
    pad = pad_of(side)
    for k in range(3):
        field[k, 0:pad, :] = jnp.zeros((pad, field.shape[2]), F32)
        field[k, pad + slots : pad + slots + pad, :] = jnp.zeros((pad, field.shape[2]), F32)


def tap(field, side, slots, rise, step):
    at = pad_of(side) + rise * side
    return field[step + 1, at : at + slots, :].astype(BF16)


def forward_body(side, aux, x_ref, w_ref, mid_ref, out_ref, keep, field, act, finish):
    u1, u2, u3, fac, pat = [item() for item in keep]
    slots = x_ref.shape[0]
    chan, mid = out_ref.shape[1], w_ref.shape[0]
    reduce_end, conv_end, expand_end, _, _ = columns(chan, mid)
    pad = pad_of(side)
    clear_edges(field, side, slots)
    u1[...] = dot_nt(x_ref[...], w_ref[:, 0:reduce_end])

    def first(rows, start, carry):
        unit, factor = unit_of(u1[rows, :])
        u1[rows, :] = unit
        fac[rows, 0:1] = factor
        value = silu(unit * mid_ref[0:1, :] + mid_ref[1:2, :]) * aux[rows, 0:1]
        field[1, pl.ds(pad + start, unit.shape[0]), :] = value
        return carry

    chunked(slots, first)
    keep[0].send()
    shift_columns(field, side, slots, aux)
    for j, (rise, step) in enumerate(OFFSETS):
        pat[:, j * mid : (j + 1) * mid] = tap(field, side, slots, rise, step)
    keep[4].send()
    u2[...] = dot_nt(pat[...], w_ref[:, reduce_end:conv_end])

    def second(rows, start, carry):
        unit, factor = unit_of(u2[rows, :])
        u2[rows, :] = unit
        fac[rows, 1:2] = factor
        act[rows, :] = silu(unit * mid_ref[2:3, :] + mid_ref[3:4, :]).astype(BF16)
        return carry

    chunked(slots, second)
    keep[1].send()
    u3[...] = dot_nn(act[...], w_ref[:, conv_end:expand_end])

    def third(rows, start, carry):
        unit, factor = unit_of(u3[rows, :])
        u3[rows, :] = unit
        fac[rows, 2:3] = factor
        summed = unit * out_ref[0:1, :] + out_ref[1:2, :] + x_ref[rows, :].astype(F32)
        finish[rows, :] = (silu(summed) * aux[rows, 0:1]).astype(BF16)
        return carry

    chunked(slots, third)
    keep[2].send()
    keep[3].send()


def forward_kernel(side, pooling, assembled, scalars, ins, outs, plain, *scratch):
    field, act, *rest = scratch
    ins, outs = list(ins), list(outs)
    aux = ins.pop(0)()
    if pooling:
        spread, finish = ins.pop(0), rest.pop(0)
    if assembled:
        sources = [item() for item in ins]
    else:
        if pooling:
            sources = [outs.pop(0)]
        else:
            sources = [ins.pop(0)]
        sources += outs[:3]
        outs = outs[3:]
        refs = [item() for item in sources]
        assemble(scalars[0][0], plain, *refs, *rest)
        for item in sources:
            if isinstance(item, Outward):
                item.send()
        sources = refs
    result = outs[0]
    if not pooling:
        finish = result()
    forward_body(side, aux, *sources, outs[1:], field, act, finish)
    if pooling:
        result()[...] = dot_nn(spread()[...], finish[...]).astype(BF16)


def block_forward(side, chan, mid, me, aux, spread, x, pieces, assembled):
    slots = side * side
    pooling = spread is not None
    width = columns(chan, mid)[2]
    given = [aux] + ([spread] if pooling else [])
    kept = [
        sds((spread.shape[0] if pooling else slots, chan), BF16),
        sds((slots, mid), F32),
        sds((slots, mid), F32),
        sds((slots, chan), F32),
        sds((slots, LANES), F32),
        sds((slots, TAPS * mid), BF16),
    ]
    whole = [sds((mid, width), BF16), sds((8, mid), F32), sds((8, chan), F32)]
    scratch = [
        pltpu.VMEM((3, slots + 2 * pad_of(side), mid), F32),
        pltpu.VMEM((slots, mid), BF16),
    ]
    if pooling:
        scratch.append(pltpu.VMEM((slots, chan), BF16))
    plain = []
    if assembled is not None:
        args, outs = given + list(assembled), kept
    else:
        args, outs = (given, [sds((slots, chan), BF16)]) if pooling else (given + [x], [])
        outs = outs + whole + kept
        plain = list(pieces)
        held = mid // len(pieces)
        extra = 2 * LANES + (slots * LANES // held if pooling else 0)
        scratch += [
            pltpu.VMEM((len(pieces), held, extra), BF16),
            pltpu.VMEM((mid, LANES), F32),
            pltpu.SemaphoreType.DMA((2, len(pieces))),
        ]
    got = call(
        functools.partial(forward_kernel, side, pooling, assembled is not None),
        outs,
        [me],
        args,
        scratch,
        flops=2 * slots * mid * (2 * chan + TAPS * mid),
        moved=30 * slots * chan,
        plain=plain,
    )
    got = list(got)
    if assembled is not None:
        source = list(assembled)
    elif pooling:
        source, got = got[:4], got[4:]
    else:
        source, got = [x] + got[:3], got[3:]
    return got[0], source + got[1:]


def fold(value):
    return jnp.sum(value.reshape(value.shape[0] // 8, 8, value.shape[1]), axis=0)


def norm_back(upstream, unit, factor, gain):
    inverse = 1.0 / unit.shape[-1]
    scaled = upstream * gain
    first = jnp.sum(scaled, axis=-1, keepdims=True) * inverse
    second = jnp.sum(scaled * unit, axis=-1, keepdims=True) * inverse
    return factor * (scaled - first - unit * second)


def back_upper(side, me, aux, up, x_ref, w_in, mid_in, out_ref, u2_in, u3, fac, pat_in, sg, eg, turned, field, dense, accum, out_rows, grads):
    slots, chan = eg.shape
    mid = dense.shape[1]
    held = grads.shape[0]
    reduce_end, conv_end, expand_end, _, _ = columns(chan, mid)
    pad = pad_of(side)
    clear_edges(field, side, slots)

    def third(rows, start, carry):
        gain_acc, bias_acc = carry
        unit = u3[rows, :]
        summed = unit * out_ref[0:1, :] + out_ref[1:2, :] + x_ref[rows, :].astype(F32)
        grad = silu_slope(summed) * (up[rows, :] * aux[rows, 0:1])
        sg[rows, :] = grad
        eg[rows, :] = norm_back(grad, unit, fac[rows, 2:3], out_ref[0:1, :]).astype(BF16)
        return gain_acc + fold(grad * unit), bias_acc + fold(grad)

    zero = jnp.zeros((8, chan), F32)
    gain_acc, bias_acc = chunked(slots, third, (zero, zero))
    out_rows[...] = jnp.zeros_like(out_rows)
    out_rows[0:1, :] = jnp.sum(gain_acc, axis=0, keepdims=True)
    out_rows[1:2, :] = jnp.sum(bias_acc, axis=0, keepdims=True)

    u2, mid_ref, w_ref = u2_in(), mid_in(), w_in()
    dense[...] = silu(u2[...] * mid_ref[2:3, :] + mid_ref[3:4, :])
    turned[...] = dense[...].T
    grads[:, conv_end:expand_end] = dot_nn(rows_of(turned, me, held).astype(BF16), eg[...])
    dense[...] = dot_nt(eg[...], w_ref[:, conv_end:expand_end])
    small = jnp.zeros((8, mid), F32)

    def second(rows, start, carry):
        gain_sum, bias_sum = carry
        unit = u2[rows, :]
        grad = silu_slope(unit * mid_ref[2:3, :] + mid_ref[3:4, :]) * dense[rows, :]
        back = norm_back(grad, unit, fac[rows, 1:2], mid_ref[2:3, :])
        field[1, pl.ds(pad + start, unit.shape[0]), :] = back
        return gain_sum + fold(grad * unit), bias_sum + fold(grad)

    gain_two, bias_two = chunked(slots, second, (small, small))
    accum[2:3, :] = jnp.sum(gain_two, axis=0, keepdims=True)
    accum[3:4, :] = jnp.sum(bias_two, axis=0, keepdims=True)
    turned[...] = field[1, pad : pad + slots, :].T
    pat = pat_in()
    grads[:, reduce_end:conv_end] = dot_nn(rows_of(turned, me, held).astype(BF16), pat[...])


def back_lower(side, me, aux, x_ref, w_ref, mid_ref, u1_in, fac, turned, field, dense, accum, out_rows, grads, tail):
    slots, mid = dense.shape
    chan = x_ref.shape[1]
    held = grads.shape[0]
    reduce_end = columns(chan, mid)[0]
    shift_columns(field, side, slots, aux)
    for j, (rise, step) in enumerate(OFFSETS):
        at = reduce_end + j * mid
        term = dot_nn(tap(field, side, slots, -rise, -step), w_ref[:, at : at + mid])
        dense[...] = term if j == 0 else dense[...] + term
    u1 = u1_in()
    small = jnp.zeros((8, mid), F32)

    def first(rows, start, carry):
        gain_sum, bias_sum = carry
        unit = u1[rows, :]
        grad = silu_slope(unit * mid_ref[0:1, :] + mid_ref[1:2, :]) * (dense[rows, :] * aux[rows, 0:1])
        dense[rows, :] = norm_back(grad, unit, fac[rows, 0:1], mid_ref[0:1, :])
        return gain_sum + fold(grad * unit), bias_sum + fold(grad)

    gain_one, bias_one = chunked(slots, first, (small, small))
    accum[0:1, :] = jnp.sum(gain_one, axis=0, keepdims=True)
    accum[1:2, :] = jnp.sum(bias_one, axis=0, keepdims=True)
    turned[...] = dense[...].T
    grads[:, 0:reduce_end] = dot_nn(rows_of(turned, me, held).astype(BF16), x_ref[...])
    turned[:, 0:LANES] = accum[...].T
    grads[:, tail : tail + LANES] = rows_of(turned, me, held)[:, 0:LANES]
    grads[:, tail + LANES : tail + 2 * LANES] = jnp.zeros((held, LANES), F32)
    if chan // (mid // held) == LANES:
        lanes = pl.ds(pl.multiple_of(me * LANES, LANES), LANES)
        grads[0:8, tail + LANES : tail + 2 * LANES] = out_rows[:, lanes]


def split_rows(grads, plane, mine, theirs):
    count = mine.buffer.shape[0]
    theirs()[...] = half_of(grads, 1 - plane, count).astype(BF16)
    theirs.send()
    mine()[...] = half_of(grads, plane, count)
    mine.send()


def back_scratch(side, slots, chan, mid):
    return [
        pltpu.VMEM((slots, chan), F32),
        pltpu.VMEM((slots, chan), BF16),
        pltpu.VMEM((mid, slots), F32),
        pltpu.VMEM((3, slots + 2 * pad_of(side), mid), F32),
        pltpu.VMEM((slots, mid), F32),
        pltpu.VMEM((LANES, mid), F32),
    ]


def late_kernel(side, scalars, ins, outs, plain, up, grads, sg, eg, turned, field, dense, accum):
    aux, x_in, w_in, mid_in, out_in, u1_in, u2_in, u3_in, fac_in, pat_in, *pieces = ins
    x_grad, mine, theirs, out_rows = outs
    me, plane = scalars[0][0], scalars[0][1] & 1
    half = pieces[0].buffer.shape[1]
    for odd in range(2):
        core = (me & 1) ^ odd
        total = pieces[odd]()[...].astype(F32)
        for piece in pieces[odd + 2 :: 2]:
            total = total + piece()[...].astype(F32)
        up[:, pl.ds(pl.multiple_of(core * half, half), half)] = total
    aux, x_ref, out_ref, u3, fac = aux(), x_in(), out_in(), u3_in(), fac_in()
    chan, mid = eg.shape[1], dense.shape[1]
    reduce_end, _, expand_end, _, _ = columns(chan, mid)
    accum[...] = jnp.zeros_like(accum)
    back_upper(
        side, me, aux, up, x_ref, w_in, mid_in, out_ref, u2_in, u3, fac, pat_in,
        sg, eg, turned, field, dense, accum, out_rows(), grads,
    )
    back_lower(
        side, me, aux, x_ref, w_in(), mid_in(), u1_in, fac, turned, field, dense, accum, out_rows(), grads, expand_end,
    )
    split_rows(grads, plane, mine, theirs)
    x_grad()[...] = (dot_nn(dense[...].astype(BF16), w_in()[:, 0:reduce_end]) + sg[...]).astype(BF16)


def late_backward(side, held, me, aux, pieces, saved):
    slots, chan = saved[0].shape
    mid = saved[1].shape[0]
    end = columns(chan, mid)[-1]
    return call(
        functools.partial(late_kernel, side),
        [
            sds((slots, chan), BF16),
            sds((held // 2, end), F32),
            sds((held // 2, end), BF16),
            sds((8, chan), F32),
        ],
        [me],
        [aux, *saved, *pieces],
        [pltpu.VMEM((slots, chan), F32), pltpu.VMEM((held, end), F32)] + back_scratch(side, slots, chan, mid),
        flops=3 * slots * mid * (2 * chan + TAPS * mid),
        moved=40 * slots * chan,
    )


def upper_kernel(side, own_lanes, scalars, ins, outs, plain, up, grads, sg, eg, turned, field, dense, accum):
    aux, spread, pooled_grad, x_in, out_in, u3_in, fac_in, mid_in, u2_in, w_in, pat_in = ins
    mine, theirs, conv_grad, sg_own, accum_out, out_rows = outs
    me, plane = scalars[0][0], scalars[0][1] & 1
    slots = eg.shape[0]
    up[...] = dot_tn(spread()[...], pooled_grad()[...])
    aux, x_ref, out_ref, u3, fac = aux(), x_in(), out_in(), u3_in(), fac_in()
    accum[...] = jnp.zeros_like(accum)
    back_upper(
        side, me, aux, up, x_ref, w_in, mid_in, out_ref, u2_in, u3, fac, pat_in,
        sg, eg, turned, field, dense, accum, out_rows(), grads,
    )
    start = columns(eg.shape[1], dense.shape[1])[0]
    count = mine.buffer.shape[0]
    width = mine.buffer.shape[1]
    theirs()[...] = half_of(grads, 1 - plane, count)[:, start : start + width].astype(BF16)
    theirs.send()
    mine()[...] = half_of(grads, plane, count)[:, start : start + width]
    mine.send()
    pad = pad_of(side)
    conv_grad()[...] = field[1, pad : pad + slots, :]
    accum_out()[...] = accum[0:8, :]
    if own_lanes:
        sg_own()[...] = sg[:, pl.ds(pl.multiple_of(me * own_lanes, own_lanes), own_lanes)]
    else:
        sg_own()[...] = sg[...]


def upper_backward(side, held, me, aux, spread, pooled_grad, saved, own_lanes):
    x, w, mids, outs, u1, u2, u3, fac, pat = saved
    slots, chan = x.shape
    mid = w.shape[0]
    reduce_end, _, expand_end, _, end = columns(chan, mid)
    return call(
        functools.partial(upper_kernel, side, own_lanes),
        [
            sds((held // 2, expand_end - reduce_end), F32),
            sds((held // 2, expand_end - reduce_end), BF16),
            sds((slots, mid), F32),
            sds((slots, own_lanes or chan), F32),
            sds((8, mid), F32),
            sds((8, chan), F32),
        ],
        [me],
        [aux, spread, pooled_grad, x, outs, u3, fac, mids, u2, w, pat],
        [pltpu.VMEM((slots, chan), F32), pltpu.VMEM((held, end), F32)] + back_scratch(side, slots, chan, mid),
        flops=2 * slots * mid * (2 * chan + TAPS * mid),
        moved=40 * slots * chan,
    )


def lower_kernel(side, own_lanes, scalars, ins, outs, plain, turned, field, dense, accum):
    aux, conv_grad, w_in, u1_in, fac, mid_in, x_in, sg_own, accum_in, out_rows = ins
    x_grad, grads, grads_low = outs
    me = scalars[0][0]
    slots, mid = dense.shape
    pad = pad_of(side)
    clear_edges(field, side, slots)
    field[1, pad : pad + slots, :] = conv_grad()[...]
    accum[...] = jnp.zeros_like(accum)
    accum[0:8, :] = accum_in()[...]
    w_ref, x_ref = w_in(), x_in()
    reduce_end = x_ref.shape[1]
    back_lower(
        side, me, aux(), x_ref, w_ref, mid_in(), u1_in, fac(), turned, field, dense, accum, out_rows(), grads(), reduce_end,
    )
    grads_low()[...] = grads()[...].astype(BF16)
    grads_low.send()
    grads.send()
    low = dense[...].astype(BF16)
    if own_lanes:
        lanes = pl.ds(pl.multiple_of(me * own_lanes, own_lanes), own_lanes)
        x_grad()[...] = dot_nn(low, w_ref[:, lanes]) + sg_own()[...]
    else:
        x_grad()[...] = dot_nn(low, w_ref[:, 0:reduce_end]) + sg_own()[...]


def lower_backward(side, held, me, aux, upper, saved, own_lanes):
    x, w, mids, outs, u1, u2, u3, fac, pat = saved
    slots, chan = x.shape
    mid = w.shape[0]
    conv_grad, sg_own, accum, out_rows = upper
    return call(
        functools.partial(lower_kernel, side, own_lanes),
        [
            sds((slots, own_lanes or chan), F32),
            sds((held, chan + 2 * LANES), F32),
            sds((held, chan + 2 * LANES), BF16),
        ],
        [me],
        [aux, conv_grad, w, u1, fac, mids, x, sg_own, accum, out_rows],
        back_scratch(side, slots, chan, mid)[2:],
        flops=slots * mid * (2 * chan + TAPS * mid),
        moved=20 * slots * chan,
    )


GELU_A = 0.7978845608028654
GELU_B = 0.044715


def gelu_both(value):
    square = value * value
    curve = jnp.tanh(GELU_A * (value + GELU_B * value * square))
    slope = 0.5 * (1.0 + curve) + 0.5 * value * (1.0 - curve * curve) * (
        GELU_A * (1.0 + 3.0 * GELU_B * square)
    )
    return 0.5 * value * (1.0 + curve), slope


def place_pieces(me, plain, natural, sems):
    copies = []
    for r, piece in enumerate(plain):
        share = piece.shape[1]
        lanes = pl.ds(pl.multiple_of((me ^ r) * share, share), share)
        copies.append(pltpu.make_async_copy(piece, natural.at[:, lanes], sems.at[r]))
        copies[-1].start()
    return copies


def readout_kernel(placed, scalars, ins, outs, plain, full, *sems):
    readin, w1, b1, w2, *rest = ins
    act, mine, theirs, grad, half_in, *more = outs
    me = scalars[0][0]
    if placed:
        cot = more[0]()
        copies = place_pieces(me, plain, cot, sems[0])
    else:
        cot, copies = rest[0](), []
    half = full.shape[1] // 2
    core = me & 1
    lanes = pl.ds(pl.multiple_of(core * half, half), half)
    half_in()[...] = readin()[:, lanes]
    half_in.send()
    hidden = dot_nn(readin()[...], w1()[...]) + b1()[...]
    value, slope = gelu_both(hidden)
    act()[...] = value.astype(BF16)
    act.send()
    for copy in copies:
        copy.wait()
    for item in more:
        item.send()
    grad()[...] = dot_nt(cot[...], w2()[...])
    grad.send()
    full[...] = dot_nt((slope * grad()[...]).astype(BF16), w1()[...])
    theirs()[...] = full[:, pl.ds(pl.multiple_of((1 - core) * half, half), half)].astype(BF16)
    theirs.send()
    mine()[...] = full[:, lanes]


def readout(me, readin, w1, b1, w2, pieces, whole):
    rows, chan = readin.shape
    hidden, width = w2.shape
    outs = [
        sds((rows, hidden), BF16),
        sds((rows, chan // 2), F32),
        sds((rows, chan // 2), BF16),
        sds((rows, hidden), F32),
        sds((rows, chan // 2), BF16),
    ]
    args, scratch = [readin, w1, b1, w2], [pltpu.VMEM((rows, chan), F32)]
    if pieces is None:
        args.append(whole)
    else:
        outs.append(sds((rows, width), BF16))
        scratch.append(pltpu.SemaphoreType.DMA((len(pieces),)))
    got = call(
        functools.partial(readout_kernel, pieces is not None),
        outs,
        [me],
        args,
        scratch,
        flops=2 * rows * hidden * (2 * chan + width),
        moved=2 * hidden * (chan + width),
        plain=pieces or [],
    )
    return list(got) + ([whole] if pieces is None else [])


def tokens_kernel(scalars, ins, outs, plain):
    act, w2 = [item() for item in ins]
    keep, send = [item() for item in outs]
    width = keep.shape[2]
    for odd, out in ((1, send), (0, keep)):
        for q in range(keep.shape[0]):
            lanes = pl.ds(pl.multiple_of((scalars[0][0] ^ (2 * q + odd)) * width, width), width)
            out[q] = dot_nn(act[...], w2[:, lanes]).astype(out.dtype)
        outs[odd].send()


def tokens_share(me, act, w2, n):
    rows, hidden = act.shape
    width = w2.shape[1] // n
    return call(
        tokens_kernel,
        [sds((n // 2, rows, width), F32), sds((n // 2, rows, width), BF16)],
        [me],
        [act, w2],
        flops=2 * rows * hidden * w2.shape[1],
        moved=2 * hidden * w2.shape[1],
    )


def hidden_kernel(placed, scalars, ins, outs, plain, stacked, low, *sems):
    w1, b1, w2, grad, readin, *parts = ins
    act, w1_grad, b1_grad, *more = outs
    me = scalars[0][0]
    if placed:
        cot = more[0]()
        copies = place_pieces(me, plain, cot, sems[0])
    else:
        cot, copies = parts.pop()(), []
    other = parts.pop()
    half = other.buffer.shape[1]
    rows = readin.buffer.shape[0]
    lanes = [pl.ds(pl.multiple_of(((me & 1) ^ odd) * half, half), half) for odd in range(2)]
    stacked[0:rows, :] = readin()[...]
    at = rows
    for part in parts:
        count = part.buffer.shape[0]
        stacked[at : at + count, lanes[0]] = part()[...]
        at += count
    stacked[rows:, lanes[1]] = other()[...]
    hidden = dot_nn(stacked[...], w1()[...]) + b1()[...]
    value, slope = gelu_both(hidden)
    act()[...] = value.astype(BF16)
    act.send()
    low[0:rows, :] = (slope[0:rows] * grad()[...]).astype(BF16)
    for copy in copies:
        copy.wait()
    for item in more:
        item.send()
    low[rows:, :] = (slope[rows:] * dot_nt(cot[...], w2()[...])).astype(BF16)
    b1_grad()[...] = jnp.sum(low[...].astype(F32), axis=0, keepdims=True)
    w1_grad()[...] = dot_tn(stacked[...], low[...])


def hidden_all(me, b1, w1, w2, grad, readin, parts, other, pieces, whole):
    rows, chan = readin.shape
    total = rows + other.shape[0]
    hidden, width = w2.shape
    outs = [sds((total, hidden), BF16), sds((chan, hidden), F32), sds((1, hidden), F32)]
    args = [w1, b1, w2, grad, readin, *parts, other]
    scratch = [pltpu.VMEM((total, chan), BF16), pltpu.VMEM((total, hidden), BF16)]
    if pieces is None:
        args.append(whole)
    else:
        outs.append(sds((total - rows, width), BF16))
        scratch.append(pltpu.SemaphoreType.DMA((len(pieces),)))
    got = call(
        functools.partial(hidden_kernel, pieces is not None),
        outs,
        [me],
        args,
        scratch,
        flops=2 * total * hidden * (2 * chan + width),
        moved=2 * hidden * (3 * chan + width),
        plain=pieces or [],
    )
    return list(got) + ([whole] if pieces is None else [])


def w2_kernel(n, scalars, ins, outs, plain, both, buffer, sems):
    act, own, rest = [item() for item in ins]
    b2_grad = outs[0]()
    (out,) = plain[1:] if len(plain) > 1 else plain
    rows = own.shape[0]
    width = own.shape[1] // n
    turned = act[...].astype(F32).T.astype(BF16)
    lanes = pl.ds(pl.multiple_of(scalars[0][0] * width, width), width)
    b2_grad[...] = jnp.sum(own[:, lanes].astype(F32), axis=0, keepdims=True) + jnp.sum(
        rest[:, lanes].astype(F32), axis=0, keepdims=True
    )
    copies = []
    for r in range(n):
        slot = r % 2
        if r >= 2:
            copies[r - 2].wait()
        both[0:rows, :] = own[:, r * width : (r + 1) * width]
        both[rows:, :] = rest[:, r * width : (r + 1) * width]
        buffer[slot] = dot_nn(turned, both[...])
        copy = pltpu.make_async_copy(
            buffer.at[slot], out.at[:, r * width : (r + 1) * width], sems.at[slot]
        )
        copy.start()
        copies.append(copy)
    for copy in copies[-2:]:
        copy.wait()


def w2_gradient(me, act, own, rest, n):
    total, hidden = act.shape
    chan = own.shape[1]
    width = chan // n

    def kernel(me_ref, act_ref, own_ref, rest_ref, out, b2_out, *scratch):
        act_buf, own_buf, rest_buf, b2_buf, sems, out_sem, *more = scratch
        ins = [
            Inward(a, b, sems.at[i])
            for i, (a, b) in enumerate(((act_ref, act_buf), (own_ref, own_buf), (rest_ref, rest_buf)))
        ]
        b2_grad = Outward(b2_out, b2_buf, out_sem)
        w2_kernel(n, [me_ref], ins, [b2_grad], [out], *more)
        b2_grad.send()
        b2_grad.copy.wait()

    return pl.pallas_call(
        kernel,
        out_shape=[sds((hidden, chan), F32), sds((1, width), F32)],
        in_specs=[SMEM] + [ANY] * 3,
        out_specs=[ANY] * 2,
        scratch_shapes=[
            pltpu.VMEM(act.shape, BF16),
            pltpu.VMEM(own.shape, BF16),
            pltpu.VMEM(rest.shape, BF16),
            pltpu.VMEM((1, width), F32),
            pltpu.SemaphoreType.DMA((3,)),
            pltpu.SemaphoreType.DMA,
            pltpu.VMEM((total, width), BF16),
            pltpu.VMEM((2, hidden, width), F32),
            pltpu.SemaphoreType.DMA((2,)),
        ],
        compiler_params=pltpu.CompilerParams(vmem_limit_bytes=60 << 20),
        cost_estimate=pl.CostEstimate(
            flops=2 * total * hidden * chan, bytes_accessed=4 * hidden * chan, transcendentals=0
        ),
    )(me, act, own, rest)


def finish_kernel(count, scalars, ins, outs, plain, scr):
    red, conv, exp, mid_gain, mid_bias, out_gain, out_bias = [item() for item in outs]
    late, middle, parts = ins[0:2], ins[2:4], ins[4:]
    chan, mid = red.shape[2], conv.shape[3]
    held = red.shape[1]
    reduce_end, conv_end, expand_end, mid_end, end = columns(chan, mid)
    plane = scalars[0][1] & 1
    few = held // 2

    def from_pair(pair, base, k):
        mine, other = [item()[...] for item in pair]
        for odd in range(2):
            value = jnp.where(plane == odd, mine, other)
            rows = slice(odd * few, odd * few + few)
            for j in range(TAPS):
                at = reduce_end + j * mid - base
                conv[k, j, rows, :] = value[:, at : at + mid].astype(F32)
            exp[k, rows, :] = value[:, conv_end - base : expand_end - base].astype(F32)
            if base == 0:
                red[k, rows, :] = value[:, 0:reduce_end].astype(F32)
                scr[k, rows, :] = value[:, expand_end:end].astype(F32)

    scr[...] = jnp.zeros_like(scr)
    from_pair(late, 0, 1)
    from_pair(middle, reduce_end, 0)
    total = parts[0]()[...]
    for part in parts[1:]:
        total = total + part()[...].astype(F32)
    red[0] = total[:, 0:reduce_end]
    scr[0, 0:held, :] = total[:, reduce_end:]
    for k in range(2):
        flat = scr[k, :, 0:LANES].T
        for which in range(2):
            mid_gain[k, which : which + 1, :] = flat[2 * which : 2 * which + 1, 0:held]
            mid_bias[k, which : which + 1, :] = flat[2 * which + 1 : 2 * which + 2, 0:held]
        out_gain[k : k + 1, :] = scr[k, 0:1, LANES : LANES + out_gain.shape[1]]
        out_bias[k : k + 1, :] = scr[k, 1:2, LANES : LANES + out_bias.shape[1]]


def finish(me, late, middle, parts, chan, mid, share):
    held = parts[0].shape[0]
    outs = [
        sds((2, held, chan), F32),
        sds((2, TAPS, held, mid), F32),
        sds((2, held, chan), F32),
        sds((2, 2, held), F32),
        sds((2, 2, held), F32),
        sds((2, share), F32),
        sds((2, share), F32),
    ]
    return call(
        functools.partial(finish_kernel, len(parts)),
        outs,
        [me],
        [*late, *middle, *parts],
        [pltpu.VMEM((2, LANES, 2 * LANES), F32)],
        flops=8 * held * chan,
        moved=40 * held * chan,
    )


def iota(shape, dim):
    return lax.broadcasted_iota(jnp.int32, shape, dim).astype(F32)


def whole_part(value, divisor):
    return jnp.floor((value + 0.5) * (1.0 / divisor))


def table_at(target, place, extent):
    begin = whole_part(target * extent, POOLED)
    ending = whole_part((target + 1.0) * extent + (POOLED - 1), POOLED)
    inside = jnp.where((place >= begin) & (place < ending), 1.0, 0.0)
    return inside / (ending - begin)


def facts_kernel(scalars, ins, outs, plain):
    extent = scalars[0][0].astype(F32)
    for side, out in ((GRID, outs[0]), (POOLED, outs[1])):
        slots = side * side
        place = iota((slots, 1), 0)
        row = whole_part(place, side)
        column = place - row * side
        out()[:, 1:2] = jnp.where(column > 0.5, 1.0, 0.0)
        out()[:, 2:3] = jnp.where(column < side - 1.5, 1.0, 0.0)
        if side == GRID:
            out()[:, 0:1] = jnp.where((row < extent) & (column < extent), 1.0, 0.0)
        else:
            out()[:, 0:1] = jnp.ones((slots, 1), F32)
    shape = outs[2]().shape
    target, place = iota((shape[0], 1), 0), iota((1, shape[1]), 1)
    up, across = whole_part(target, POOLED), whole_part(place, GRID)
    rows = table_at(up, across, extent)
    lanes = table_at(target - up * POOLED, place - across * GRID, extent)
    outs[2]()[...] = (rows * lanes).astype(BF16)


def facts(grid):
    slots, few = GRID * GRID, POOLED * POOLED
    return call(
        facts_kernel,
        [sds((slots, LANES), F32), sds((few, LANES), F32), sds((few, slots), BF16)],
        [grid],
        [],
    )


def per_device(
    features,
    grid,
    reduce_w,
    conv_w,
    expand_w,
    mid_gain,
    mid_bias,
    out_gain,
    out_bias,
    read_w1,
    read_b1,
    read_w2,
    read_b2,
    cotangent,
):
    n = lax.axis_size("ch")
    chan, mid = reduce_w.shape[1], conv_w.shape[2]
    held, share = reduce_w.shape[2], features.shape[0]
    aligned = share == LANES and held % 16 == 0
    index = lax.axis_index("ch").astype(jnp.int32)
    planes = lax.axis_size("img")
    me = jnp.stack([index, lax.axis_index("img").astype(jnp.int32)])

    feat = jnp.transpose(features[:, 0, :])
    cot = jnp.transpose(cotangent[:, 0, :])
    red = jnp.transpose(reduce_w, (0, 2, 1))
    conv = jnp.transpose(conv_w, (0, 1, 3, 2))
    norms = (mid_gain, mid_bias, out_gain, out_bias)
    few = cot.shape[0]
    slot_facts, few_facts, spread = facts(grid)

    if aligned:
        (first_packet,) = pack(0, feat, red, conv, expand_w, *norms)
        far = neighbours(first_packet)
        second_packet, cot = pack(1, cot, red, conv, expand_w, *norms, after=[first_packet])
        first_pieces = with_cores(first_packet, far)
        (second_packet,) = gate([second_packet], *far.values())
        far = neighbours(second_packet)
        first_whole = second_whole = None
    else:
        rows = jnp.concatenate(
            [red, jnp.transpose(conv, (0, 2, 1, 3)).reshape(2, held, TAPS * mid), expand_w], axis=2
        )
        rows = lax.all_gather(rows, "ch", axis=1, tiled=True)
        mids = jnp.stack([mid_gain, mid_bias], axis=2).reshape(2, 4, held)
        mids = jnp.pad(lax.all_gather(mids, "ch", axis=2, tiled=True), ((0, 0), (0, 4), (0, 0)))
        outs = jnp.stack([out_gain, out_bias], axis=1)
        outs = jnp.pad(lax.all_gather(outs, "ch", axis=2, tiled=True), ((0, 0), (0, 6), (0, 0)))
        x_whole = lax.all_gather(feat, "ch", axis=1, tiled=True)
        first_whole = (x_whole, rows[0], mids[0], outs[0])
        second_whole = (rows[1], mids[1], outs[1])
        first_pieces = second_pieces = None

    cot_rest, held_cot = [], cot
    for mask in (1 << k for k in range(planes.bit_length() - 1)):
        cot_rest.append(ppermute_xor(held_cot, "img", mask))
        if 2 * mask < planes:
            held_cot = join(held_cot, cot_rest[-1])
    cot_rest = join(*cot_rest)

    pooled, saved_first = block_forward(
        GRID, chan, mid, me, slot_facts, spread, None, first_pieces, first_whole
    )
    if aligned:
        far = dict(zip(far, gate(list(far.values()), pooled)))
        second_pieces = with_cores(second_packet, far)
        (cot,) = gate([cot], *far.values())
        far = neighbours(cot)
    else:
        second_whole = (pooled,) + second_whole
    readin, saved_second = block_forward(
        POOLED, chan, mid, me, few_facts, None, pooled, second_pieces, second_whole
    )

    bias_one = read_b1[None, :]
    if aligned:
        far = dict(zip(far, gate(list(far.values()), readin)))
        cot_pieces, cot_own = with_cores(cot, far), None
    else:
        cot_pieces, cot_own = None, lax.all_gather(cot, "ch", axis=1, tiled=True)
    act, mine, theirs, own_grad, half_in, cot_own = readout(
        me, readin, read_w1, bias_one, read_w2, cot_pieces, cot_own
    )

    half = add(mine, ppermute_xor(theirs, "ch", 1))
    far = neighbours(half)
    keep, send = tokens_share(me, act, read_w2, n)
    far = dict(zip(far, gate(list(far.values()), send)))
    grad_pieces = with_cores(half, far)

    parts, held_in = [], half_in
    for mask in (1 << k for k in range(planes.bit_length() - 1)):
        parts.append(ppermute_xor(held_in, "img", mask))
        if 2 * mask < planes:
            held_in = join(held_in, parts[-1])

    (cot_rest,) = gate([cot_rest], *far.values())
    if aligned:
        far = neighbours(cot_rest)

    pooled_grad, late_mine, late_theirs, late_out = late_backward(
        POOLED, held, me, few_facts, grad_pieces, saved_second
    )
    late_got = ppermute_xor(late_theirs, "img", 1)
    own_lanes = share if aligned else 0
    middle_mine, middle_theirs, *upper = upper_backward(
        GRID, held, me, slot_facts, spread, pooled_grad, saved_first, own_lanes
    )
    middle_got = ppermute_xor(middle_theirs, "img", 1)
    late_half = add(late_mine, late_got, after=[upper[0]])
    late_more = [ppermute_xor(late_half, "img", 2)]
    feat_grad, last_grads, last_low = lower_backward(
        GRID, held, me, slot_facts, upper, saved_first, own_lanes
    )
    last = [last_grads] + along_images(last_low)
    middle_half = add(middle_mine, middle_got, after=[last_grads])
    middle_more = [ppermute_xor(middle_half, "img", 2)]
    late_half = add(late_half, late_more[-1], after=[last_grads])
    for mask in (1 << k for k in range(2, planes.bit_length() - 1)):
        late_half = add(late_half, ppermute_xor(late_half, "img", mask))
    late = (late_half, ppermute_xor(late_half, "img", 1))

    other = ppermute_xor(join(*parts, after=[upper[0]]), "ch", 1)
    if aligned:
        far = dict(zip(far, gate(list(far.values()), last_grads)))
        rest_pieces, cot_rest = with_cores(cot_rest, far), None
    else:
        rest_pieces, cot_rest = None, lax.all_gather(cot_rest, "ch", axis=1, tiled=True)
    act_all, w1_grad, b1_grad, cot_rest = hidden_all(
        me, bias_one, read_w1, read_w2, own_grad, readin, parts, other, rest_pieces, cot_rest
    )
    middle_half = add(middle_half, middle_more[-1], after=[act_all])
    for mask in (1 << k for k in range(2, planes.bit_length() - 1)):
        middle_half = add(middle_half, ppermute_xor(middle_half, "img", mask))
    middle = (middle_half, ppermute_xor(middle_half, "img", 1))

    got = ppermute_xor(send, "ch", 1)
    parts = [keep[q] + got[q].astype(F32) for q in range(n // 2)]
    tokens = parts[0]
    for q in range(1, n // 2):
        tokens = tokens + ppermute_xor(parts[q].astype(BF16), "ch", 2 * q).astype(F32)
    tokens = (tokens + read_b2[None, :]).astype(BF16)

    w2_grad, b2_grad = w2_gradient(me, act_all, cot_own, cot_rest, n)
    red_grad, conv_grad, exp_grad, mid_gain_grad, mid_bias_grad, out_gain_grad, out_bias_grad = finish(
        me, late, middle, last, chan, mid, share
    )
    if not aligned:
        feat_grad = lax.dynamic_slice_in_dim(feat_grad, index * share, share, 1)
        both = jnp.stack([upper[3], late_out])
        both = lax.dynamic_slice_in_dim(both, index * share, share, 2)
        both = lax.psum(both.astype(BF16), "img").astype(F32)
        out_gain_grad, out_bias_grad = both[:, 0], both[:, 1]

    return (
        jnp.transpose(tokens)[:, None, :],
        jnp.transpose(feat_grad)[:, None, :],
        jnp.transpose(red_grad, (0, 2, 1)),
        jnp.transpose(conv_grad, (0, 1, 3, 2)),
        exp_grad,
        mid_gain_grad,
        mid_bias_grad,
        out_gain_grad,
        out_bias_grad,
        w1_grad,
        b1_grad[0],
        w2_grad,
        b2_grad[0],
    )


def solution(mesh):
    return jax.shard_map(
        per_device,
        mesh=mesh,
        in_specs=(
            P("ch", "img", None),
            P("img"),
            P(None, None, "ch"),
            P(None, None, None, "ch"),
            P(None, "ch", None),
            P(None, None, "ch"),
            P(None, None, "ch"),
            P(None, "ch"),
            P(None, "ch"),
            P(None, "ch"),
            P("ch"),
            P("ch", None),
            P("ch"),
            P("ch", "img", None),
        ),
        out_specs=(
            P("ch", "img", None),
            P("ch", "img", None),
            P(None, None, "ch"),
            P(None, None, None, "ch"),
            P(None, "ch", None),
            P(None, None, "ch"),
            P(None, None, "ch"),
            P(None, "ch"),
            P(None, "ch"),
            P(None, "ch"),
            P("ch"),
            P("ch", None),
            P("ch"),
        ),
        check_vma=False,
    )
```

time: 239 us -> 187 us (0.78); the launches traced: 235 us -> 187 us
  waiting for transfers between devices: 72.2 us -> 30.9 us
  local copies, waits for them, and re-layouts: 47 us -> 7.16 us
  Pallas kernels: 63.3 us -> 96.3 us
    ppermute x49 -> x54, waiting for transfers between devices: 72.2 us -> 30.9 us  [ppermute_xor(): lax.ppermute(x, axis, [(i, i ^ mask) for i in range(lax.axis_size(axis))])]
    unnamed x182 -> x104, local copies, waits for them, and re-layouts: 40.3 us -> 7.16 us
    pallas_call x13 -> x29, Pallas kernels: 63.3 us -> 96.3 us  [the longest x21 85.5 us: call(): pl.pallas_call(kernel, out_shape=list(outs), in_specs=[SMEM] * len(scalar...]
    convert_element_type x2 -> x0, local copies, waits for them, and re-layouts: 4.29 us -> none  [per_device(): spread = spread.astype(BF16)]
    ppermute x49 -> x54, starting transfers between devices: 46.3 us -> 46.7 us  [ppermute_xor(): lax.ppermute(x, axis, [(i, i ^ mask) for i in range(lax.axis_size(axis))])]
  transfers between devices with their start and end apart: 49 -> 54, of which waited for: 7 -> 11; matrix products, arithmetic and copies ran while one was open for 5% -> 2% of each run, Pallas kernels for 27% -> 45%
where the time goes in v2:
time: 187 us
  Pallas kernels  96.3 us (51%)
  starting transfers between devices  46.7 us (25%)
  waiting for transfers between devices  30.9 us (17%)
  local copies, waits for them, and re-layouts  7.16 us (4%)
  other arithmetic  3.21 us (2%)
  between operations  2.38 us (1%)
    pallas_call x21, Pallas kernels, call(): pl.pallas_call(kernel, out_shape=list(outs), in_specs=[SMEM] * len(scalar...  85.5 us
    ppermute x54, starting transfers between devices, ppermute_xor(): lax.ppermute(x, axis, [(i, i ^ mask) for i in range(lax.axis_size(axis))])  46.7 us
    ppermute x54, waiting for transfers between devices, ppermute_xor(): lax.ppermute(x, axis, [(i, i ^ mask) for i in range(lax.axis_size(axis))])  30.9 us
    pallas_call x1, Pallas kernels, w2_gradient(): pl.pallas_call(kernel, out_shape=[sds((hidden, chan), F32), sds((1, width...  10.7 us
    unnamed x104, local copies, waits for them, and re-layouts  7.16 us
  transfers between devices with their start and end apart: 54, of which 11 were waited for; matrix products, arithmetic and copies ran while one was open for 2% of the time, Pallas kernels for 45%

profile of v2, /device:TPU:0, one launch (start us, length us, event | category | flops | bytes accessed | tf_op | source)
XLA Modules:
  0.0 186.6 jit_solution(3112874606794898859)
XLA Ops:
  0.6 1.9 %shard_map.238.refs_3_.refs_8_ = bf16[32,6912]{1,0:T(8,128)(2,1)} custom-call(bf16[576,128]{1,0:T(8,128)(2,1)} %bitcast.44, f32[2,2,32]{2,1,0:T(2,128)} %refs_1_.4, f32[2,2,32]{2,1,0:T(2,128)} %refs_2_.5, f32[2,128]{1,0:T(2,128)} %refs_3_.4, f32[2,128]{1,0:T(2,128)} %refs_4_.4, bf16[2,32,1024]{2,1,0:T(8,128)(2,1)} %bitcast.42, ...), custom_call_target="tpu_custom_call" | custom-call | bytes 884736 | tf_op jit(solution)/shard_map/pallas_call | solution.py:94
  2.6 3.0 %collective-permute-start.1 = (bf16[32,6912]{1,0:T(8,128)(2,1)}, bf16[32,6912]{1,0:T(8,128)(2,1)S(1)}, u32[]{:S(2)}, u32[]{:S(2)}) collective-permute-start(bf16[32,6912]{1,0:T(8,128)(2,1)} %shard_map.238.refs_3_.refs_8_), channel_id=1, source_target_pairs={{0,2},{1,3},{2,0},{3,1},{4,6},{5,7},{6,4},{7,5},{8,10},{9,11},{10,... | collective-permute-start | bytes 1327112 | tf_op jit(solution)/shard_map/ppermute | solution.py:141
  5.6 1.5 collective-permute-start.3
  7.1 9.7 %collective-permute-done.1.refs_5_.refs_3_ = bf16[32,6912]{1,0:T(8,128)(2,1)S(1)} collective-permute-done((bf16[32,6912]{1,0:T(8,128)(2,1)}, bf16[32,6912]{1,0:T(8,128)(2,1)S(1)}, u32[]{:S(2)}, u32[]{:S(2)}) %collective-permute-start.1) | collective-permute-done | bytes 442400 | tf_op jit(solution)/shard_map/ppermute | solution.py:141
  16.8 10.1 %collective-permute-done.3.refs_7_.refs_2_ = bf16[32,6912]{1,0:T(8,128)(2,1)S(1)} collective-permute-done((bf16[32,6912]{1,0:T(8,128)(2,1)}, bf16[32,6912]{1,0:T(8,128)(2,1)S(1)}, u32[]{:S(2)}, u32[]{:S(2)}) %collective-permute-start.3) | collective-permute-done | bytes 442400 | tf_op jit(solution)/shard_map/ppermute | solution.py:141
  27.4 1.9 %shard_map.240 = (bf16[32,4608]{1,0:T(8,128)(2,1)}, bf16[144,512]{1,0:T(8,128)(2,1)}) custom-call(bf16[144,512]{1,0:T(8,128)(2,1)} %bitcast.45, f32[2,2,32]{2,1,0:T(2,128)} %refs_1_.4, f32[2,2,32]{2,1,0:T(2,128)} %refs_2_.5, f32[2,128]{1,0:T(2,128)} %refs_3_.4, f32[2,128]{1,0:T(2,128)} %refs_4_.4, bf16[2,32,1024]{2,1,0:T(8,128)(2,1)} %bitcast.43, ...), custom_call_target="tpu_custom_call" | custom-call | bytes 589824 | tf_op jit(solution)/shard_map/pallas_call | solution.py:94
  29.4 1.6 collective-permute-start.8
  31.8 1.1 collective-permute-start.10
  33.6 1.1 shard_map.237
  35.4 10.0 %shard_map.239 = (bf16[576,1024]{1,0:T(8,128)(2,1)}, bf16[256,4352]{1,0:T(8,128)(2,1)}, f32[8,256]{1,0:T(8,128)}, f32[8,1024]{1,0:T(8,128)}, bf16[144,1024]{1,0:...) custom-call(s32[2]{0:T(128)} %pad_add_fusion.refs_0_.me_ref, ...), custom_call_target="tpu_custom_call" | custom-call | flops 1283457024 | bytes 17694720 | tf_op jit(solution)/shard_map/pallas_call | solution.py:94
  47.3 1.6 collective-permute-start.41
  48.9 4.7 %collective-permute-done.41.refs_1_.refs_0_ = bf16[144,512]{1,0:T(8,128)(2,1)S(1)} collective-permute-done((bf16[144,512]{1,0:T(8,128)(2,1)S(1)}, bf16[144,512]{1,0:T(8,128)(2,1)S(1)}, u32[]{:S(2)}, u32[]{:S(2)}) %collective-permute-start.41) | collective-permute-done | bytes 147488 | tf_op jit(solution)/shard_map/ppermute | solution.py:141
  54.2 1.7 shard_map.258
  56.0 1.6 collective-permute-start.15
  60.5 6.3 %shard_map.243 = (bf16[256,4352]{1,0:T(8,128)(2,1)}, f32[8,256]{1,0:T(8,128)}, f32[8,1024]{1,0:T(8,128)}, bf16[144,1024]{1,0:T(8,128)(2,1)}, f32[144,256]{1,0:T(...) custom-call(s32[2]{0:T(128)} %pad_add_fusion.refs_0_.me_ref, ...), custom_call_target="tpu_custom_call" | custom-call | flops 320864256 | bytes 4423680 | tf_op jit(solution)/shard_map/pallas_call | solution.py:94
  70.4 6.8 %shard_map.246 = (bf16[144,512]{1,0:T(8,128)(2,1)}, f32[144,512]{1,0:T(8,128)}, bf16[144,512]{1,0:T(8,128)(2,1)}, f32[144,512]{1,0:T(8,128)}, bf16[144,512]{1,0:T(8,128)(2,1)}, /*index=5*/bf16[144,4096]{1,0:T(8,128)(2,1)}) custom-call(s32[2]{0:T(128)} %pad_add_fusion.refs_0_.me_ref, bf16[144,1024]{1,0:T(8,128)(2,1)} %get-tuple-element.90.refs_3_.refs_1_.refs_5_, ...), custom_call_target="tpu_custom_call" | custom-call | flops 905969664 | bytes 5242880 | tf_op jit(solution)/shard_map/pallas_call | solution.py:94
  77.6 2.6 %collective-permute-start.42 = (bf16[288,512]{1,0:T(8,128)(2,1)S(1)}, bf16[288,512]{1,0:T(8,128)(2,1)S(1)}, u32[]{:S(2)}, u32[]{:S(2)}) collective-permute-start(bf16[288,512]{1,0:T(8,128)(2,1)S(1)} %copy-done.26), channel_id=1, source_target_pairs={{0,16},{8,24},{16,0},{24,8},{1,17},{9,25},{17,1},{25,9},{2,18},{10... | collective-permute-start | bytes 884744 | tf_op jit(solution)/shard_map/ppermute | solution.py:141
  80.8 1.7 shard_map.248.refs_11_
  82.6 1.6 collective-permute-start.27
  84.1 4.8 %shard_map.247 = (f32[4,144,512]{2,1,0:T(8,128)}, bf16[4,144,512]{2,1,0:T(8,128)(2,1)}) custom-call(s32[2]{0:T(128)} %pad_add_fusion.refs_0_.me_ref, bf16[144,512]{1,0:T(8,128)(2,1)} %get-tuple-element.95.refs_1_, bf16[512,4096]{1,0:T(8,128)(2,1)} %refs_3_.5), custom_call_target="tpu_custom_call" | custom-call | flops 603979776 | bytes 4194304 | tf_op jit(solution)/shard_map/pallas_call | solution.py:94
  89.0 1.1 collective-permute-start.28
  91.1 1.6 collective-permute-start.38
  92.7 2.5 %collective-permute-done.28.refs_1_ = bf16[144,512]{1,0:T(8,128)(2,1)S(1)} collective-permute-done((bf16[144,512]{1,0:T(8,128)(2,1)S(1)}, bf16[144,512]{1,0:T(8,128)(2,1)S(1)}, u32[]{:S(2)}, u32[]{:S(2)}) %collective-permute-start.28) | collective-permute-done | bytes 147488 | tf_op jit(solution)/shard_map/ppermute | solution.py:141
  97.4 1.8 shard_map.259.refs_0_
  99.3 1.8 collective-permute-start.44
  102.0 1.7 shard_map.256
  104.0 1.3 collective-permute-start.39
  106.2 7.2 %shard_map.250 = (bf16[144,1024]{1,0:T(8,128)(2,1)}, f32[16,4608]{1,0:T(8,128)}, bf16[16,4608]{1,0:T(8,128)(2,1)}, f32[8,1024]{1,0:T(8,128)}) custom-call(s32[2]{0:T(128)} %pad_add_fusion.refs_0_.me_ref, f32[144,128]{1,0:T(8,128)} %get-tuple-element.82.refs_1_, bf16[144,1024]{1,0:T(8,128)(2,1)} %get-tuple-element.85.refs_3_.refs_2_, ...), custom_call_target="tpu_custom_call" | custom-call | flops 481296384 | bytes 5898240 | tf_op jit(solution)/shard_map/pallas_call | solution.py:94
  113.4 9.2 %shard_map.251 = (f32[16,3328]{1,0:T(8,128)}, bf16[16,3328]{1,0:T(8,128)(2,1)}, f32[576,256]{1,0:T(8,128)}, f32[576,128]{1,0:T(8,128)}, f32[8,256]{1,0:T(8,128)}, /*index=5*/f32[8,1024]{1,0:T(8,128)}) custom-call(s32[2]{0:T(128)} %pad_add_fusion.refs_0_.me_ref, f32[576,128]{1,0:T(8,128)} %get-tuple-element.83.refs_1_, ...), custom_call_target="tpu_custom_call" | custom-call | flops 1283457024 | bytes 23592960 | tf_op jit(solution)/shard_map/pallas_call | solution.py:94
  122.7 2.6 %collective-permute-start.33 = (bf16[16,4608]{1,0:T(8,128)(2,1)S(1)}, bf16[16,4608]{1,0:T(8,128)(2,1)S(1)}, u32[]{:S(2)}, u32[]{:S(2)}) collective-permute-start(bf16[16,4608]{1,0:T(8,128)(2,1)S(1)} %copy-done.51), channel_id=1, source_target_pairs={{0,8},{8,0},{16,24},{24,16},{1,9},{9,1},{17,25},{25,17},{2,10},{10... | collective-permute-start | bytes 442376 | tf_op jit(solution)/shard_map/ppermute | solution.py:141
  126.0 1.5 collective-permute-start.24
  128.5 1.4 collective-permute-start.23
  130.8 1.7 shard_map.253.refs_0_
  132.6 1.0 collective-permute-start.34
  133.6 1.6 collective-permute-start.36
  135.2 1.8 shard_map.257
  137.1 6.8 %shard_map.252 = (f32[576,128]{1,0:T(8,128)}, f32[32,1280]{1,0:T(8,128)}, bf16[32,1280]{1,0:T(8,128)(2,1)}) custom-call(s32[2]{0:T(128)} %pad_add_fusion.refs_0_.me_ref, f32[576,128]{1,0:T(8,128)} %get-tuple-element.83.refs_1_, f32[576,256]{1,0:T(8,128)} %get-tuple-element.120.refs_2_, bf16[256,4352]{1,0:T(8,128)(2,1)} %get-tuple-element.118.refs_10_.refs_3_, ...), custom_call_target="tpu_custom_call" | custom-call | flops 641728512 | bytes 11796480 | tf_op jit(solution)/shard_map/pallas_call | solution.py:94
  145.1 1.7 shard_map.255.refs_0_
  146.8 1.7 shard_map.254.refs_1_
  148.5 1.8 fusion.7
  150.8 2.0 %collective-permute-start.52 = (bf16[32,1280]{1,0:T(8,128)(2,1)}, bf16[32,1280]{1,0:T(8,128)(2,1)S(1)}, u32[]{:S(2)}, u32[]{:S(2)}) collective-permute-start(bf16[32,1280]{1,0:T(8,128)(2,1)} %get-tuple-element.137), channel_id=1, source_target_pairs={{0,16},{8,24},{16,0},{24,8},{1,17},{9,25},{17,1},{25,9},{2,18},{10... | collective-permute-start | bytes 245768 | tf_op jit(solution)/shard_map/ppermute | solution.py:141
  152.8 2.0 %collective-permute-start.53 = (bf16[32,1280]{1,0:T(8,128)(2,1)}, bf16[32,1280]{1,0:T(8,128)(2,1)S(1)}, u32[]{:S(2)}, u32[]{:S(2)}) collective-permute-start(bf16[32,1280]{1,0:T(8,128)(2,1)} %get-tuple-element.137), channel_id=1, source_target_pairs={{0,24},{8,16},{16,8},{24,0},{1,25},{9,17},{17,9},{25,1},{2,26},{10... | collective-permute-start | bytes 245768 | tf_op jit(solution)/shard_map/ppermute | solution.py:141
  154.7 1.2 collective-permute-start.37
  156.0 1.2 collective-permute-start.35
  157.2 10.9 %shard_map.262 = (bf16[576,512]{1,0:T(8,128)(2,1)}, f32[1024,512]{1,0:T(8,128)}, f32[1,512]{1,0:T(1,128)}, bf16[432,4096]{1,0:T(8,128)(2,1)}) custom-call(s32[2]{0:T(128)} %pad_add_fusion.refs_0_.me_ref, bf16[1024,512]{1,0:T(8,128)(2,1)} %refs_1_.5, f32[1,512]{1,0:T(1,128)} %bitcast.47, bf16[512,4096]{1,0:T(8,128)(2,1)} %refs_3_.5, ...), custom_call_target="tpu_custom_call" | custom-call | flops 3623878656 | bytes 7340032 | tf_op jit(solution)/shard_map/pallas_call | solution.py:94
  168.7 1.6 shard_map.263.refs_3_
  171.3 10.7 %shard_map.265 = (f32[512,4096]{1,0:T(8,128)}, f32[1,512]{1,0:T(1,128)}) custom-call(s32[2]{0:T(128)} %pad_add_fusion.refs_0_.me_ref, bf16[576,512]{1,0:T(8,128)(2,1)} %get-tuple-element.136.refs_2_.act_ref, bf16[144,4096]{1,0:T(8,128)(2,1)} %get-tuple-element.147.own_ref, bf16[432,4096]{1,0:T(8,128)(2,1)} %get-tuple-element.148.rest_ref), custom_call_target="tpu_custom_call" | custom-call | flops 2415919104 | bytes 8388608 | tf_op jit(solution)/shard_map/pallas_call | solution.py:924
  183.4 3.1 %shard_map.264 = (f32[2,32,1024]{2,1,0:T(8,128)}, f32[2,9,32,256]{3,2,1,0:T(8,128)}, f32[2,32,1024]{2,1,0:T(8,128)}, f32[2,2,32]{2,1,0:T(2,128)}, f32[2,2,32]{2,...) custom-call(s32[2]{0:T(128)} %pad_add_fusion.refs_0_.me_ref, bf16[16,4608]{1,0:T(8,128)(2,1)} %shard_map.254.refs_1_, ...), custom_call_target="tpu_custom_call" | custom-call | flops 262144 | bytes 1310720 | tf_op jit(solution)/shard_map/pallas_call | solution.py:94
  (196 shorter events, 24.5 us)
Async XLA Ops:
  2.6 14.2 %collective-permute-start.1 = (bf16[32,6912]{1,0:T(8,128)(2,1)}, bf16[32,6912]{1,0:T(8,128)(2,1)S(1)}, u32[]{:S(2)}, u32[]{:S(2)}) collective-permute-start(bf16[32,6912]{1,0:T(8,128)(2,1)} %shard_map.238.refs_3_.refs_8_), channel_id=1, source_target_pairs={{0,2},{1,3},{2,0},{3,1},{4,6},{5,7},{6,4},{7,5},{8,10},{9,11},{10,... | collective-permute-start | bytes 1327112 | tf_op jit(solution)/shard_map/ppermute | solution.py:141
  5.6 21.3 %collective-permute-start.3 = (bf16[32,6912]{1,0:T(8,128)(2,1)}, bf16[32,6912]{1,0:T(8,128)(2,1)S(1)}, u32[]{:S(2)}, u32[]{:S(2)}) collective-permute-start(bf16[32,6912]{1,0:T(8,128)(2,1)} %shard_map.238.refs_3_.refs_8_), channel_id=1, source_target_pairs={{0,4},{1,5},{2,6},{3,7},{4,0},{5,1},{6,2},{7,3},{8,12},{9,13},{10,... | collective-permute-start | bytes 1327112 | tf_op jit(solution)/shard_map/ppermute | solution.py:141
  7.1 19.8 %collective-permute-start.5 = (bf16[32,6912]{1,0:T(8,128)(2,1)}, bf16[32,6912]{1,0:T(8,128)(2,1)S(1)}, u32[]{:S(2)}, u32[]{:S(2)}) collective-permute-start(bf16[32,6912]{1,0:T(8,128)(2,1)} %shard_map.238.refs_3_.refs_8_), channel_id=1, source_target_pairs={{0,6},{1,7},{2,4},{3,5},{4,2},{5,3},{6,0},{7,1},{8,14},{9,15},{10,... | collective-permute-start | bytes 1327112 | tf_op jit(solution)/shard_map/ppermute | solution.py:141
  7.1 23.8 %collective-permute-start = (bf16[32,6912]{1,0:T(8,128)(2,1)}, bf16[32,6912]{1,0:T(8,128)(2,1)S(1)}, u32[]{:S(2)}, u32[]{:S(2)}) collective-permute-start(bf16[32,6912]{1,0:T(8,128)(2,1)} %shard_map.238.refs_3_.refs_8_), channel_id=1, source_target_pairs={{0,1},{1,0},{2,3},{3,2},{4,5},{5,4},{6,7},{7,6},{8,9},{9,8},{10,11... | collective-permute-start | bytes 1327112 | tf_op jit(solution)/shard_map/ppermute | solution.py:141
  16.8 15.0 %collective-permute-start.2 = (bf16[32,6912]{1,0:T(8,128)(2,1)S(1)}, bf16[32,6912]{1,0:T(8,128)(2,1)S(1)}, u32[]{:S(2)}, u32[]{:S(2)}) collective-permute-start(bf16[32,6912]{1,0:T(8,128)(2,1)S(1)} %collective-permute-done.1.refs_5_.refs_3_), channel_id=1, source_target_pairs={{0,1},{1,0},{2,3},{3,2},{4,5},{5,4},{6,7},{7,6},{8,9},{9,8},{10,11... | collective-permute-start | bytes 1327112 | tf_op jit(solution)/shard_map/ppermute | solution.py:141
  26.9 8.4 %collective-permute-start.4 = (bf16[32,6912]{1,0:T(8,128)(2,1)S(1)}, bf16[32,6912]{1,0:T(8,128)(2,1)}, u32[]{:S(2)}, u32[]{:S(2)}) collective-permute-start(bf16[32,6912]{1,0:T(8,128)(2,1)S(1)} %collective-permute-done.3.refs_7_.refs_2_), channel_id=1, source_target_pairs={{0,1},{1,0},{2,3},{3,2},{4,5},{5,4},{6,7},{7,6},{8,9},{9,8},{10,11... | collective-permute-start | bytes 1327112 | tf_op jit(solution)/shard_map/ppermute | solution.py:141
  26.9 8.4 %collective-permute-start.6 = (bf16[32,6912]{1,0:T(8,128)(2,1)S(1)}, bf16[32,6912]{1,0:T(8,128)(2,1)}, u32[]{:S(2)}, u32[]{:S(2)}) collective-permute-start(bf16[32,6912]{1,0:T(8,128)(2,1)S(1)} %collective-permute-done.5.refs_9_.refs_1_), channel_id=1, source_target_pairs={{0,1},{1,0},{2,3},{3,2},{4,5},{5,4},{6,7},{7,6},{8,9},{9,8},{10,11... | collective-permute-start | bytes 1327112 | tf_op jit(solution)/shard_map/ppermute | solution.py:141
  29.4 15.9 %collective-permute-start.8 = (bf16[32,4608]{1,0:T(8,128)(2,1)}, bf16[32,4608]{1,0:T(8,128)(2,1)S(1)}, u32[]{:S(2)}, u32[]{:S(2)}) collective-permute-start(bf16[32,4608]{1,0:T(8,128)(2,1)} %shard_map.241.refs_3_), channel_id=1, source_target_pairs={{0,6},{1,7},{2,4},{3,5},{4,2},{5,3},{6,0},{7,1},{8,14},{9,15},{10,... | collective-permute-start | bytes 884744 | tf_op jit(solution)/shard_map/ppermute | solution.py:141
  31.0 15.0 %collective-permute-start.9 = (bf16[32,4608]{1,0:T(8,128)(2,1)}, bf16[32,4608]{1,0:T(8,128)(2,1)S(1)}, u32[]{:S(2)}, u32[]{:S(2)}) collective-permute-start(bf16[32,4608]{1,0:T(8,128)(2,1)} %shard_map.241.refs_3_), channel_id=1, source_target_pairs={{0,4},{1,5},{2,6},{3,7},{4,0},{5,1},{6,2},{7,3},{8,12},{9,13},{10,... | collective-permute-start | bytes 884744 | tf_op jit(solution)/shard_map/ppermute | solution.py:141
  31.8 14.3 %collective-permute-start.10 = (bf16[32,4608]{1,0:T(8,128)(2,1)}, bf16[32,4608]{1,0:T(8,128)(2,1)S(1)}, u32[]{:S(2)}, u32[]{:S(2)}) collective-permute-start(bf16[32,4608]{1,0:T(8,128)(2,1)} %shard_map.241.refs_3_), channel_id=1, source_target_pairs={{0,2},{1,3},{2,0},{3,1},{4,6},{5,7},{6,4},{7,5},{8,10},{9,11},{10,... | collective-permute-start | bytes 884744 | tf_op jit(solution)/shard_map/ppermute | solution.py:141
  35.3 22.3 %collective-permute-start.7 = (bf16[32,4608]{1,0:T(8,128)(2,1)}, bf16[32,4608]{1,0:T(8,128)(2,1)S(1)}, u32[]{:S(2)}, u32[]{:S(2)}) collective-permute-start(bf16[32,4608]{1,0:T(8,128)(2,1)} %shard_map.241.refs_3_), channel_id=1, source_target_pairs={{0,1},{1,0},{2,3},{3,2},{4,5},{5,4},{6,7},{7,6},{8,9},{9,8},{10,11... | collective-permute-start | bytes 884744 | tf_op jit(solution)/shard_map/ppermute | solution.py:141
  46.8 11.8 %collective-permute-start.11 = (bf16[32,4608]{1,0:T(8,128)(2,1)}, bf16[32,4608]{1,0:T(8,128)(2,1)S(1)}, u32[]{:S(2)}, u32[]{:S(2)}) collective-permute-start(bf16[32,4608]{1,0:T(8,128)(2,1)} %get-tuple-element.87.refs_5_.refs_3_), channel_id=1, source_target_pairs={{0,1},{1,0},{2,3},{3,2},{4,5},{5,4},{6,7},{7,6},{8,9},{9,8},{10,11... | collective-permute-start | bytes 884744 | tf_op jit(solution)/shard_map/ppermute | solution.py:141
  46.8 12.8 %collective-permute-start.12 = (bf16[32,4608]{1,0:T(8,128)(2,1)}, bf16[32,4608]{1,0:T(8,128)(2,1)S(1)}, u32[]{:S(2)}, u32[]{:S(2)}) collective-permute-start(bf16[32,4608]{1,0:T(8,128)(2,1)} %get-tuple-element.88.refs_7_.refs_2_), channel_id=1, source_target_pairs={{0,1},{1,0},{2,3},{3,2},{4,5},{5,4},{6,7},{7,6},{8,9},{9,8},{10,11... | collective-permute-start | bytes 884744 | tf_op jit(solution)/shard_map/ppermute | solution.py:141
  47.3 12.3 %collective-permute-start.13 = (bf16[32,4608]{1,0:T(8,128)(2,1)}, bf16[32,4608]{1,0:T(8,128)(2,1)S(1)}, u32[]{:S(2)}, u32[]{:S(2)}) collective-permute-start(bf16[32,4608]{1,0:T(8,128)(2,1)} %get-tuple-element.89.refs_9_.refs_1_), channel_id=1, source_target_pairs={{0,1},{1,0},{2,3},{3,2},{4,5},{5,4},{6,7},{7,6},{8,9},{9,8},{10,11... | collective-permute-start | bytes 884744 | tf_op jit(solution)/shard_map/ppermute | solution.py:141
  47.3 6.2 %collective-permute-start.41 = (bf16[144,512]{1,0:T(8,128)(2,1)S(1)}, bf16[144,512]{1,0:T(8,128)(2,1)S(1)}, u32[]{:S(2)}, u32[]{:S(2)}) collective-permute-start(bf16[144,512]{1,0:T(8,128)(2,1)S(1)} %copy-done.4), channel_id=1, source_target_pairs={{0,8},{8,0},{16,24},{24,16},{1,9},{9,1},{17,25},{25,17},{2,10},{10... | collective-permute-start | bytes 442376 | tf_op jit(solution)/shard_map/ppermute | solution.py:141
  56.0 10.8 %collective-permute-start.15 = (bf16[144,512]{1,0:T(8,128)(2,1)}, bf16[144,512]{1,0:T(8,128)(2,1)S(1)}, u32[]{:S(2)}, u32[]{:S(2)}) collective-permute-start(bf16[144,512]{1,0:T(8,128)(2,1)} %shard_map.244.refs_5_), channel_id=1, source_target_pairs={{0,6},{1,7},{2,4},{3,5},{4,2},{5,3},{6,0},{7,1},{8,14},{9,15},{10,... | collective-permute-start | bytes 442376 | tf_op jit(solution)/shard_map/ppermute | solution.py:141
  57.6 9.3 %collective-permute-start.16 = (bf16[144,512]{1,0:T(8,128)(2,1)}, bf16[144,512]{1,0:T(8,128)(2,1)S(1)}, u32[]{:S(2)}, u32[]{:S(2)}) collective-permute-start(bf16[144,512]{1,0:T(8,128)(2,1)} %shard_map.244.refs_5_), channel_id=1, source_target_pairs={{0,4},{1,5},{2,6},{3,7},{4,0},{5,1},{6,2},{7,3},{8,12},{9,13},{10,... | collective-permute-start | bytes 442376 | tf_op jit(solution)/shard_map/ppermute | solution.py:141
  58.6 8.3 %collective-permute-start.17 = (bf16[144,512]{1,0:T(8,128)(2,1)}, bf16[144,512]{1,0:T(8,128)(2,1)S(1)}, u32[]{:S(2)}, u32[]{:S(2)}) collective-permute-start(bf16[144,512]{1,0:T(8,128)(2,1)} %shard_map.244.refs_5_), channel_id=1, source_target_pairs={{0,2},{1,3},{2,0},{3,1},{4,6},{5,7},{6,4},{7,5},{8,10},{9,11},{10,... | collective-permute-start | bytes 442376 | tf_op jit(solution)/shard_map/ppermute | solution.py:141
  59.6 8.9 %collective-permute-start.14 = (bf16[144,512]{1,0:T(8,128)(2,1)}, bf16[144,512]{1,0:T(8,128)(2,1)S(1)}, u32[]{:S(2)}, u32[]{:S(2)}) collective-permute-start(bf16[144,512]{1,0:T(8,128)(2,1)} %shard_map.244.refs_5_), channel_id=1, source_target_pairs={{0,1},{1,0},{2,3},{3,2},{4,5},{5,4},{6,7},{7,6},{8,9},{9,8},{10,11... | collective-permute-start | bytes 442376 | tf_op jit(solution)/shard_map/ppermute | solution.py:141
  77.6 19.1 %collective-permute-start.42 = (bf16[288,512]{1,0:T(8,128)(2,1)S(1)}, bf16[288,512]{1,0:T(8,128)(2,1)S(1)}, u32[]{:S(2)}, u32[]{:S(2)}) collective-permute-start(bf16[288,512]{1,0:T(8,128)(2,1)S(1)} %copy-done.26), channel_id=1, source_target_pairs={{0,16},{8,24},{16,0},{24,8},{1,17},{9,25},{17,1},{25,9},{2,18},{10... | collective-permute-start | bytes 884744 | tf_op jit(solution)/shard_map/ppermute | solution.py:141
  82.6 8.5 %collective-permute-start.27 = (bf16[144,512]{1,0:T(8,128)(2,1)}, bf16[144,512]{1,0:T(8,128)(2,1)S(1)}, u32[]{:S(2)}, u32[]{:S(2)}) collective-permute-start(bf16[144,512]{1,0:T(8,128)(2,1)} %shard_map.248.refs_11_), channel_id=1, source_target_pairs={{0,6},{1,7},{2,4},{3,5},{4,2},{5,3},{6,0},{7,1},{8,14},{9,15},{10,... | collective-permute-start | bytes 442376 | tf_op jit(solution)/shard_map/ppermute | solution.py:141
  88.9 33.7 %collective-permute-start.21 = (bf16[4,144,512]{2,1,0:T(8,128)(2,1)}, bf16[4,144,512]{2,1,0:T(8,128)(2,1)S(1)}, u32[]{:S(2)}, u32[]{:S(2)}) collective-permute-start(bf16[4,144,512]{2,1,0:T(8,128)(2,1)} %get-tuple-element.97.refs_3_), channel_id=1, source_target_pairs={{0,1},{1,0},{2,3},{3,2},{4,5},{5,4},{6,7},{7,6},{8,9},{9,8},{10,11... | collective-permute-start | bytes 1769480 | tf_op jit(solution)/shard_map/ppermute | solution.py:141
  89.0 6.3 %collective-permute-start.28 = (bf16[144,512]{1,0:T(8,128)(2,1)S(1)}, bf16[144,512]{1,0:T(8,128)(2,1)S(1)}, u32[]{:S(2)}, u32[]{:S(2)}) collective-permute-start(bf16[144,512]{1,0:T(8,128)(2,1)S(1)} %copy-done.10), channel_id=1, source_target_pairs={{0,4},{1,5},{2,6},{3,7},{4,0},{5,1},{6,2},{7,3},{8,12},{9,13},{10,... | collective-permute-start | bytes 442376 | tf_op jit(solution)/shard_map/ppermute | solution.py:141
  90.1 5.9 %collective-permute-start.29 = (bf16[144,512]{1,0:T(8,128)(2,1)S(1)}, bf16[144,512]{1,0:T(8,128)(2,1)S(1)}, u32[]{:S(2)}, u32[]{:S(2)}) collective-permute-start(bf16[144,512]{1,0:T(8,128)(2,1)S(1)} %copy-done.10), channel_id=1, source_target_pairs={{0,2},{1,3},{2,0},{3,1},{4,6},{5,7},{6,4},{7,5},{8,10},{9,11},{10,... | collective-permute-start | bytes 442376 | tf_op jit(solution)/shard_map/ppermute | solution.py:141
  91.1 6.1 %collective-permute-start.38 = (bf16[144,512]{1,0:T(8,128)(2,1)S(1)}, bf16[144,512]{1,0:T(8,128)(2,1)S(1)}, u32[]{:S(2)}, u32[]{:S(2)}) collective-permute-start(bf16[144,512]{1,0:T(8,128)(2,1)S(1)} %copy-done.38), channel_id=1, source_target_pairs={{0,8},{8,0},{16,24},{24,16},{1,9},{9,1},{17,25},{25,17},{2,10},{10... | collective-permute-start | bytes 442376 | tf_op jit(solution)/shard_map/ppermute | solution.py:141
  96.7 7.3 %collective-permute-start.31 = (bf16[144,512]{1,0:T(8,128)(2,1)}, bf16[144,512]{1,0:T(8,128)(2,1)S(1)}, u32[]{:S(2)}, u32[]{:S(2)}) collective-permute-start(bf16[144,512]{1,0:T(8,128)(2,1)} %get-tuple-element.109.refs_15_.refs_2_), channel_id=1, source_target_pairs={{0,1},{1,0},{2,3},{3,2},{4,5},{5,4},{6,7},{7,6},{8,9},{9,8},{10,11... | collective-permute-start | bytes 442376 | tf_op jit(solution)/shard_map/ppermute | solution.py:141
  97.2 8.2 %collective-permute-start.32 = (bf16[144,512]{1,0:T(8,128)(2,1)}, bf16[144,512]{1,0:T(8,128)(2,1)S(1)}, u32[]{:S(2)}, u32[]{:S(2)}) collective-permute-start(bf16[144,512]{1,0:T(8,128)(2,1)} %get-tuple-element.110.refs_17_.refs_1_), channel_id=1, source_target_pairs={{0,1},{1,0},{2,3},{3,2},{4,5},{5,4},{6,7},{7,6},{8,9},{9,8},{10,11... | collective-permute-start | bytes 442376 | tf_op jit(solution)/shard_map/ppermute | solution.py:141
  99.3 30.6 %collective-permute-start.44 = (bf16[432,512]{1,0:T(8,128)(2,1)}, bf16[432,512]{1,0:T(8,128)(2,1)S(1)}, u32[]{:S(2)}, u32[]{:S(2)}) collective-permute-start(bf16[432,512]{1,0:T(8,128)(2,1)} %shard_map.260.refs_9_), channel_id=1, source_target_pairs={{0,6},{1,7},{2,4},{3,5},{4,2},{5,3},{6,0},{7,1},{8,14},{9,15},{10,... | collective-permute-start | bytes 1327112 | tf_op jit(solution)/shard_map/ppermute | solution.py:141
  101.1 31.4 %collective-permute-start.45 = (bf16[432,512]{1,0:T(8,128)(2,1)}, bf16[432,512]{1,0:T(8,128)(2,1)S(1)}, u32[]{:S(2)}, u32[]{:S(2)}) collective-permute-start(bf16[432,512]{1,0:T(8,128)(2,1)} %shard_map.260.refs_9_), channel_id=1, source_target_pairs={{0,4},{1,5},{2,6},{3,7},{4,0},{5,1},{6,2},{7,3},{8,12},{9,13},{10,... | collective-permute-start | bytes 1327112 | tf_op jit(solution)/shard_map/ppermute | solution.py:141
  104.0 22.0 %collective-permute-start.39 = (bf16[288,512]{1,0:T(8,128)(2,1)}, bf16[288,512]{1,0:T(8,128)(2,1)S(1)}, u32[]{:S(2)}, u32[]{:S(2)}) collective-permute-start(bf16[288,512]{1,0:T(8,128)(2,1)} %shard_map.256), channel_id=1, source_target_pairs={{0,16},{8,24},{16,0},{24,8},{1,17},{9,25},{17,1},{25,9},{2,18},{10... | collective-permute-start | bytes 884744 | tf_op jit(solution)/shard_map/ppermute | solution.py:141
  105.3 28.3 %collective-permute-start.46 = (bf16[432,512]{1,0:T(8,128)(2,1)}, bf16[432,512]{1,0:T(8,128)(2,1)S(1)}, u32[]{:S(2)}, u32[]{:S(2)}) collective-permute-start(bf16[432,512]{1,0:T(8,128)(2,1)} %shard_map.260.refs_9_), channel_id=1, source_target_pairs={{0,2},{1,3},{2,0},{3,1},{4,6},{5,7},{6,4},{7,5},{8,10},{9,11},{10,... | collective-permute-start | bytes 1327112 | tf_op jit(solution)/shard_map/ppermute | solution.py:141
  122.7 5.9 %collective-permute-start.33 = (bf16[16,4608]{1,0:T(8,128)(2,1)S(1)}, bf16[16,4608]{1,0:T(8,128)(2,1)S(1)}, u32[]{:S(2)}, u32[]{:S(2)}) collective-permute-start(bf16[16,4608]{1,0:T(8,128)(2,1)S(1)} %copy-done.51), channel_id=1, source_target_pairs={{0,8},{8,0},{16,24},{24,16},{1,9},{9,1},{17,25},{25,17},{2,10},{10... | collective-permute-start | bytes 442376 | tf_op jit(solution)/shard_map/ppermute | solution.py:141
  126.0 18.0 %collective-permute-start.24 = (bf16[144,512]{1,0:T(8,128)(2,1)}, bf16[144,512]{1,0:T(8,128)(2,1)}, u32[]{:S(2)}, u32[]{:S(2)}) collective-permute-start(bf16[144,512]{1,0:T(8,128)(2,1)} %get-tuple-element.152), channel_id=1, source_target_pairs={{0,6},{1,7},{2,4},{3,5},{4,2},{5,3},{6,0},{7,1},{8,14},{9,15},{10,... | collective-permute-start | bytes 442376 | tf_op jit(solution)/shard_map/ppermute | solution.py:141
  128.5 16.0 %collective-permute-start.23 = (bf16[144,512]{1,0:T(8,128)(2,1)}, bf16[144,512]{1,0:T(8,128)(2,1)}, u32[]{:S(2)}, u32[]{:S(2)}) collective-permute-start(bf16[144,512]{1,0:T(8,128)(2,1)} %get-tuple-element.153), channel_id=1, source_target_pairs={{0,4},{1,5},{2,6},{3,7},{4,0},{5,1},{6,2},{7,3},{8,12},{9,13},{10,... | collective-permute-start | bytes 442376 | tf_op jit(solution)/shard_map/ppermute | solution.py:141
  129.9 14.7 %collective-permute-start.22 = (bf16[144,512]{1,0:T(8,128)(2,1)}, bf16[144,512]{1,0:T(8,128)(2,1)}, u32[]{:S(2)}, u32[]{:S(2)}) collective-permute-start(bf16[144,512]{1,0:T(8,128)(2,1)} %get-tuple-element.151), channel_id=1, source_target_pairs={{0,2},{1,3},{2,0},{3,1},{4,6},{5,7},{6,4},{7,5},{8,10},{9,11},{10,... | collective-permute-start | bytes 442376 | tf_op jit(solution)/shard_map/ppermute | solution.py:141
  132.6 12.4 %collective-permute-start.34 = (bf16[16,4608]{1,0:T(8,128)(2,1)}, bf16[16,4608]{1,0:T(8,128)(2,1)}, u32[]{:S(2)}, u32[]{:S(2)}) collective-permute-start(bf16[16,4608]{1,0:T(8,128)(2,1)} %shard_map.253.refs_0_), channel_id=1, source_target_pairs={{0,16},{8,24},{16,0},{24,8},{1,17},{9,25},{17,1},{25,9},{2,18},{10... | collective-permute-start | bytes 442376 | tf_op jit(solution)/shard_map/ppermute | solution.py:141
  133.6 10.3 %collective-permute-start.36 = (bf16[16,3328]{1,0:T(8,128)(2,1)}, bf16[16,3328]{1,0:T(8,128)(2,1)}, u32[]{:S(2)}, u32[]{:S(2)}) collective-permute-start(bf16[16,3328]{1,0:T(8,128)(2,1)} %get-tuple-element.130), channel_id=1, source_target_pairs={{0,8},{8,0},{16,24},{24,16},{1,9},{9,1},{17,25},{25,17},{2,10},{10... | collective-permute-start | bytes 319496 | tf_op jit(solution)/shard_map/ppermute | solution.py:141
  143.9 6.4 %collective-permute-start.43 = (bf16[432,512]{1,0:T(8,128)(2,1)S(1)}, bf16[432,512]{1,0:T(8,128)(2,1)S(1)}, u32[]{:S(2)}, u32[]{:S(2)}) collective-permute-start(bf16[432,512]{1,0:T(8,128)(2,1)S(1)} %copy-done.3), channel_id=1, source_target_pairs={{0,1},{1,0},{2,3},{3,2},{4,5},{5,4},{6,7},{7,6},{8,9},{9,8},{10,11... | collective-permute-start | bytes 1327112 | tf_op jit(solution)/shard_map/ppermute | solution.py:141
  144.0 6.8 %collective-permute-start.40 = (bf16[432,512]{1,0:T(8,128)(2,1)}, bf16[432,512]{1,0:T(8,128)(2,1)S(1)}, u32[]{:S(2)}, u32[]{:S(2)}) collective-permute-start(bf16[432,512]{1,0:T(8,128)(2,1)} %shard_map.257), channel_id=1, source_target_pairs={{0,1},{1,0},{2,3},{3,2},{4,5},{5,4},{6,7},{7,6},{8,9},{9,8},{10,11... | collective-permute-start | bytes 1327112 | tf_op jit(solution)/shard_map/ppermute | solution.py:141
  144.5 8.3 %collective-permute-start.47 = (bf16[432,512]{1,0:T(8,128)(2,1)}, bf16[432,512]{1,0:T(8,128)(2,1)S(1)}, u32[]{:S(2)}, u32[]{:S(2)}) collective-permute-start(bf16[432,512]{1,0:T(8,128)(2,1)} %get-tuple-element.133.refs_11_), channel_id=1, source_target_pairs={{0,1},{1,0},{2,3},{3,2},{4,5},{5,4},{6,7},{7,6},{8,9},{9,8},{10,11... | collective-permute-start | bytes 1327112 | tf_op jit(solution)/shard_map/ppermute | solution.py:141
  144.6 10.2 %collective-permute-start.48 = (bf16[432,512]{1,0:T(8,128)(2,1)}, bf16[432,512]{1,0:T(8,128)(2,1)}, u32[]{:S(2)}, u32[]{:S(2)}) collective-permute-start(bf16[432,512]{1,0:T(8,128)(2,1)} %get-tuple-element.134.refs_13_), channel_id=1, source_target_pairs={{0,1},{1,0},{2,3},{3,2},{4,5},{5,4},{6,7},{7,6},{8,9},{9,8},{10,11... | collective-permute-start | bytes 1327112 | tf_op jit(solution)/shard_map/ppermute | solution.py:141
  145.0 10.9 %collective-permute-start.49 = (bf16[432,512]{1,0:T(8,128)(2,1)}, bf16[432,512]{1,0:T(8,128)(2,1)}, u32[]{:S(2)}, u32[]{:S(2)}) collective-permute-start(bf16[432,512]{1,0:T(8,128)(2,1)} %get-tuple-element.135.refs_15_), channel_id=1, source_target_pairs={{0,1},{1,0},{2,3},{3,2},{4,5},{5,4},{6,7},{7,6},{8,9},{9,8},{10,11... | collective-permute-start | bytes 1327112 | tf_op jit(solution)/shard_map/ppermute | solution.py:141
  150.3 31.6 %collective-permute-start.51 = (bf16[32,1280]{1,0:T(8,128)(2,1)}, bf16[32,1280]{1,0:T(8,128)(2,1)S(1)}, u32[]{:S(2)}, u32[]{:S(2)}) collective-permute-start(bf16[32,1280]{1,0:T(8,128)(2,1)} %get-tuple-element.137), channel_id=1, source_target_pairs={{0,8},{8,0},{16,24},{24,16},{1,9},{9,1},{17,25},{25,17},{2,10},{10... | collective-permute-start | bytes 245768 | tf_op jit(solution)/shard_map/ppermute | solution.py:141
  150.8 31.2 %collective-permute-start.52 = (bf16[32,1280]{1,0:T(8,128)(2,1)}, bf16[32,1280]{1,0:T(8,128)(2,1)S(1)}, u32[]{:S(2)}, u32[]{:S(2)}) collective-permute-start(bf16[32,1280]{1,0:T(8,128)(2,1)} %get-tuple-element.137), channel_id=1, source_target_pairs={{0,16},{8,24},{16,0},{24,8},{1,17},{9,25},{17,1},{25,9},{2,18},{10... | collective-permute-start | bytes 245768 | tf_op jit(solution)/shard_map/ppermute | solution.py:141
  152.8 29.3 %collective-permute-start.53 = (bf16[32,1280]{1,0:T(8,128)(2,1)}, bf16[32,1280]{1,0:T(8,128)(2,1)S(1)}, u32[]{:S(2)}, u32[]{:S(2)}) collective-permute-start(bf16[32,1280]{1,0:T(8,128)(2,1)} %get-tuple-element.137), channel_id=1, source_target_pairs={{0,24},{8,16},{16,8},{24,0},{1,25},{9,17},{17,9},{25,1},{2,26},{10... | collective-permute-start | bytes 245768 | tf_op jit(solution)/shard_map/ppermute | solution.py:141
  154.7 13.3 %collective-permute-start.37 = (bf16[16,3328]{1,0:T(8,128)(2,1)}, bf16[16,3328]{1,0:T(8,128)(2,1)S(1)}, u32[]{:S(2)}, u32[]{:S(2)}) collective-permute-start(bf16[16,3328]{1,0:T(8,128)(2,1)} %shard_map.255.refs_0_), channel_id=1, source_target_pairs={{0,16},{8,24},{16,0},{24,8},{1,17},{9,25},{17,1},{25,9},{2,18},{10... | collective-permute-start | bytes 319496 | tf_op jit(solution)/shard_map/ppermute | solution.py:141
  156.0 26.1 %collective-permute-start.35 = (bf16[16,4608]{1,0:T(8,128)(2,1)}, bf16[16,4608]{1,0:T(8,128)(2,1)S(1)}, u32[]{:S(2)}, u32[]{:S(2)}) collective-permute-start(bf16[16,4608]{1,0:T(8,128)(2,1)} %shard_map.254.refs_1_), channel_id=1, source_target_pairs={{0,8},{8,0},{16,24},{24,16},{1,9},{9,1},{17,25},{25,17},{2,10},{10... | collective-permute-start | bytes 442376 | tf_op jit(solution)/shard_map/ppermute | solution.py:141
  170.4 11.7 %collective-permute-start.50 = (bf16[16,3328]{1,0:T(8,128)(2,1)}, bf16[16,3328]{1,0:T(8,128)(2,1)S(1)}, u32[]{:S(2)}, u32[]{:S(2)}) collective-permute-start(bf16[16,3328]{1,0:T(8,128)(2,1)} %shard_map.263.refs_3_), channel_id=1, source_target_pairs={{0,8},{8,0},{16,24},{24,16},{1,9},{9,1},{17,25},{25,17},{2,10},{10... | collective-permute-start | bytes 319496 | tf_op jit(solution)/shard_map/ppermute | solution.py:141
  (58 other events, 217.2 us)

commit v3 on v2

--- a/solution.py
+++ b/solution.py
@@ -50,8 +50,8 @@
 
 class Outward:
     def __init__(self, target, buffer, sem):
-        self.copy = pltpu.make_async_copy(buffer, target, sem)
-        self.buffer, self.sent = buffer, False
+        self.copy = None if buffer is None else pltpu.make_async_copy(buffer, target, sem)
+        self.target, self.buffer, self.sent = target, buffer, False
 
     def __call__(self):
         return self.buffer
@@ -62,7 +62,7 @@
             self.sent = True
 
 
-def call(body, outs, scalars, args, scratch=(), vmem=60, flops=0, moved=0, plain=(), after=()):
+def call(body, outs, scalars, args, scratch=(), vmem=60, flops=0, moved=0, plain=(), after=(), direct=()):
     count = (len(scalars), len(args), len(plain), len(after), len(outs))
 
     def kernel(*refs):
@@ -74,20 +74,23 @@
             return got
 
         scalar_refs, sources, plain_refs, _, targets = [take(k) for k in count]
-        in_buffers, out_buffers = take(len(args)), take(len(outs))
+        in_buffers = take(len(args))
+        out_buffers = [None if i in direct else refs.pop(0) for i in range(len(outs))]
         in_sems = refs.pop(0) if args else None
         out_sems = refs.pop(0)
         inward = [Inward(s, b, in_sems.at[i]) for i, (s, b) in enumerate(zip(sources, in_buffers))]
         outward = [Outward(t, b, out_sems.at[i]) for i, (t, b) in enumerate(zip(targets, out_buffers))]
+        made = [item for item in outward if item.buffer is not None]
         body(scalar_refs, inward, outward, plain_refs, *refs)
         for item in inward:
             item()
-        for item in outward:
+        for item in made:
             item.send()
-        for item in outward:
+        for item in made:
             item.copy.wait()
 
-    shapes = [pltpu.VMEM(x.shape, x.dtype) for x in list(args) + list(outs)]
+    results = [x for i, x in enumerate(outs) if i not in direct]
+    shapes = [pltpu.VMEM(x.shape, x.dtype) for x in list(args) + results]
     sems = ([pltpu.SemaphoreType.DMA((len(args),))] if args else []) + [
         pltpu.SemaphoreType.DMA((len(outs),))
     ]
@@ -129,14 +132,6 @@
     return call(join_body, [shape], [], list(parts), after=after)[0]
 
 
-def add_body(scalars, ins, outs, plain):
-    outs[0]()[...] = (ins[0]()[...].astype(F32) + ins[1]()[...].astype(F32)).astype(BF16)
-
-
-def add(left, right, after=()):
-    return call(add_body, [sds(left.shape, BF16)], [], [left, right], after=after)[0]
-
-
 def ppermute_xor(x, axis, mask):
     return lax.ppermute(x, axis, [(i, i ^ mask) for i in range(lax.axis_size(axis))])
 
@@ -159,6 +154,20 @@
     return [ppermute_xor(x, "img", m) for m in range(1, lax.axis_size("img"))]
 
 
+def pair_sum(mine, low, after):
+    masks = [1 << k for k in range(lax.axis_size("img").bit_length() - 1)]
+    total, got = mine, ppermute_xor(low, "img", masks[0])
+    for mask in masks[1:]:
+        (got,) = gate([got], after)
+        total = (total.astype(F32) + got.astype(F32)).astype(BF16)
+        got = ppermute_xor(total, "img", mask)
+    return total, got
+
+
+def summed(left, right):
+    return (left.astype(F32) + right.astype(F32)).astype(BF16)
+
+
 def rows_of(value, index, count):
     return value[pl.ds(pl.multiple_of(index * count, count), count), :]
 
@@ -177,6 +186,11 @@
 def split_low(value):
     high = value.astype(BF16).astype(F32)
     return high, value - high
+
+
+def cot_block(index, width):
+    per = width // LANES
+    return (index // per * 16, index % per * LANES), (index % 2 * 16, index // 2 * LANES)
 
 
 def pack_body(layer, scalars, ins, outs, plain, scr, *bufs):
@@ -211,6 +225,11 @@
         for b in range(feat.shape[0] // held):
             packet[:, end + b * LANES : end + (b + 1) * LANES] = feat[b * held : (b + 1) * held, :]
     else:
+        for index in range(feat.shape[0] // 16 * (feat.shape[1] // LANES)):
+            (row, lane), (low_row, low_lane) = cot_block(index, feat.shape[1])
+            packet[low_row : low_row + 16, end + low_lane : end + low_lane + LANES] = feat[
+                row : row + 16, lane : lane + LANES
+            ]
         outs[1]()[...] = feat[...]
     for copy in copies:
         copy.wait()
@@ -223,12 +242,10 @@
 def pack(layer, extra, red, conv, exp, mid_gain, mid_bias, out_gain, out_bias, after=()):
     held, chan = red.shape[1:]
     mid = conv.shape[3]
-    width = columns(chan, mid)[-1]
+    width = columns(chan, mid)[-1] + extra.shape[0] * extra.shape[1] // held
+    outs = [sds((held, width), BF16)]
     if layer:
-        outs = [sds((held, width), BF16), sds(extra.shape, BF16)]
-    else:
-        width += extra.shape[0] * extra.shape[1] // held
-        outs = [sds((held, width), BF16)]
+        outs.append(sds(extra.shape, BF16))
     return call(
         functools.partial(pack_body, layer),
         outs,
@@ -247,7 +264,7 @@
     )
 
 
-def assemble(me, pieces, x_ref, w_ref, mid_ref, out_ref, stage, scr, sems):
+def assemble(me, pieces, x_ref, w_ref, mid_ref, out_ref, stage, scr, sems, then=()):
     held = pieces[0].shape[0]
     chan, mid = out_ref.shape[1], w_ref.shape[0]
     reduce_end, conv_end, expand_end, mid_end, end = columns(chan, mid)
@@ -262,6 +279,8 @@
         rows = pl.ds(pl.multiple_of((me ^ r) * held, held), held)
         weights.append(pltpu.make_async_copy(piece.at[:, 0:expand_end], w_ref.at[rows, :], sems.at[1, r]))
         weights[-1].start()
+    for copy in then:
+        copy.start()
     for r in range(len(pieces)):
         copies[r].wait()
         rows = pl.ds(pl.multiple_of((me ^ r) * held, held), held)
@@ -270,7 +289,7 @@
         block = stage[r, :, LANES : 2 * LANES].astype(F32)
         out_ref[0:1, lanes] = block[0:1, :] + block[1:2, :]
         out_ref[1:2, lanes] = block[2:3, :] + block[3:4, :]
-        for b in range(width // LANES - 2):
+        for b in range(width // LANES - 2 if x_ref is not None else 0):
             at = (b + 2) * LANES
             x_ref[b * held : (b + 1) * held, lanes] = stage[r, :, at : at + LANES]
     flat = scr[...].T
@@ -385,18 +404,8 @@
     if assembled:
         sources = [item() for item in ins]
     else:
-        if pooling:
-            sources = [outs.pop(0)]
-        else:
-            sources = [ins.pop(0)]
-        sources += outs[:3]
-        outs = outs[3:]
-        refs = [item() for item in sources]
-        assemble(scalars[0][0], plain, *refs, *rest)
-        for item in sources:
-            if isinstance(item, Outward):
-                item.send()
-        sources = refs
+        sources, outs = [item() for item in outs[:4]], outs[4:]
+        assemble(scalars[0][0], plain, *sources, *rest)
     result = outs[0]
     if not pooling:
         finish = result()
@@ -405,40 +414,50 @@
         result()[...] = dot_nn(spread()[...], finish[...]).astype(BF16)
 
 
-def block_forward(side, chan, mid, me, aux, spread, x, pieces, assembled):
-    slots = side * side
-    pooling = spread is not None
-    width = columns(chan, mid)[2]
-    given = [aux] + ([spread] if pooling else [])
-    kept = [
-        sds((spread.shape[0] if pooling else slots, chan), BF16),
+def kept_shapes(slots, chan, mid):
+    return [
         sds((slots, mid), F32),
         sds((slots, mid), F32),
         sds((slots, chan), F32),
         sds((slots, LANES), F32),
         sds((slots, TAPS * mid), BF16),
     ]
-    whole = [sds((mid, width), BF16), sds((8, mid), F32), sds((8, chan), F32)]
-    scratch = [
+
+
+def whole_shapes(chan, mid):
+    return [sds((mid, columns(chan, mid)[2]), BF16), sds((8, mid), F32), sds((8, chan), F32)]
+
+
+def forward_scratch(side, mid):
+    slots = side * side
+    return [
         pltpu.VMEM((3, slots + 2 * pad_of(side), mid), F32),
         pltpu.VMEM((slots, mid), BF16),
     ]
+
+
+def assemble_scratch(pieces, mid, extra):
+    held = mid // len(pieces)
+    return [
+        pltpu.VMEM((len(pieces), held, 2 * LANES + extra), BF16),
+        pltpu.VMEM((mid, LANES), F32),
+        pltpu.SemaphoreType.DMA((2, len(pieces))),
+    ]
+
+
+def block_forward(side, chan, mid, me, aux, spread, pieces, assembled):
+    slots = side * side
+    pooling = spread is not None
+    args = [aux] + ([spread] if pooling else [])
+    outs = [sds((spread.shape[0] if pooling else slots, chan), BF16)] + kept_shapes(slots, chan, mid)
+    scratch = forward_scratch(side, mid)
     if pooling:
         scratch.append(pltpu.VMEM((slots, chan), BF16))
-    plain = []
     if assembled is not None:
-        args, outs = given + list(assembled), kept
+        args += list(assembled)
     else:
-        args, outs = (given, [sds((slots, chan), BF16)]) if pooling else (given + [x], [])
-        outs = outs + whole + kept
-        plain = list(pieces)
-        held = mid // len(pieces)
-        extra = 2 * LANES + (slots * LANES // held if pooling else 0)
-        scratch += [
-            pltpu.VMEM((len(pieces), held, extra), BF16),
-            pltpu.VMEM((mid, LANES), F32),
-            pltpu.SemaphoreType.DMA((2, len(pieces))),
-        ]
+        outs = [sds((slots, chan), BF16)] + whole_shapes(chan, mid) + outs
+        scratch += assemble_scratch(pieces, mid, slots * LANES * len(pieces) // mid)
     got = call(
         functools.partial(forward_kernel, side, pooling, assembled is not None),
         outs,
@@ -447,15 +466,10 @@
         scratch,
         flops=2 * slots * mid * (2 * chan + TAPS * mid),
         moved=30 * slots * chan,
-        plain=plain,
+        plain=list(pieces or []),
     )
     got = list(got)
-    if assembled is not None:
-        source = list(assembled)
-    elif pooling:
-        source, got = got[:4], got[4:]
-    else:
-        source, got = [x] + got[:3], got[3:]
+    source, got = (list(assembled), got) if assembled is not None else (got[:4], got[4:])
     return got[0], source + got[1:]
 
 
@@ -550,11 +564,11 @@
         grads[0:8, tail + LANES : tail + 2 * LANES] = out_rows[:, lanes]
 
 
-def split_rows(grads, plane, mine, theirs):
-    count = mine.buffer.shape[0]
-    theirs()[...] = half_of(grads, 1 - plane, count).astype(BF16)
+def split_rows(grads, plane, mine, theirs, start):
+    count, width = mine.buffer.shape
+    theirs()[...] = half_of(grads, 1 - plane, count)[:, start : start + width].astype(BF16)
     theirs.send()
-    mine()[...] = half_of(grads, plane, count)
+    mine()[...] = half_of(grads, plane, count)[:, start : start + width]
     mine.send()
 
 
@@ -591,7 +605,7 @@
     back_lower(
         side, me, aux, x_ref, w_in(), mid_in(), u1_in, fac, turned, field, dense, accum, out_rows(), grads, expand_end,
     )
-    split_rows(grads, plane, mine, theirs)
+    split_rows(grads, plane, mine, theirs, 0)
     x_grad()[...] = (dot_nn(dense[...].astype(BF16), w_in()[:, 0:reduce_end]) + sg[...]).astype(BF16)
 
 
@@ -627,13 +641,7 @@
         side, me, aux, up, x_ref, w_in, mid_in, out_ref, u2_in, u3, fac, pat_in,
         sg, eg, turned, field, dense, accum, out_rows(), grads,
     )
-    start = columns(eg.shape[1], dense.shape[1])[0]
-    count = mine.buffer.shape[0]
-    width = mine.buffer.shape[1]
-    theirs()[...] = half_of(grads, 1 - plane, count)[:, start : start + width].astype(BF16)
-    theirs.send()
-    mine()[...] = half_of(grads, plane, count)[:, start : start + width]
-    mine.send()
+    split_rows(grads, plane, mine, theirs, columns(eg.shape[1], dense.shape[1])[0])
     pad = pad_of(side)
     conv_grad()[...] = field[1, pad : pad + slots, :]
     accum_out()[...] = accum[0:8, :]
@@ -725,223 +733,201 @@
     return 0.5 * value * (1.0 + curve), slope
 
 
-def place_pieces(me, plain, natural, sems):
-    copies = []
-    for r, piece in enumerate(plain):
-        share = piece.shape[1]
-        lanes = pl.ds(pl.multiple_of((me ^ r) * share, share), share)
-        copies.append(pltpu.make_async_copy(piece, natural.at[:, lanes], sems.at[r]))
-        copies[-1].start()
-    return copies
-
-
-def readout_kernel(placed, scalars, ins, outs, plain, full, *sems):
-    readin, w1, b1, w2, *rest = ins
-    act, mine, theirs, grad, half_in, *more = outs
-    me = scalars[0][0]
-    if placed:
-        cot = more[0]()
-        copies = place_pieces(me, plain, cot, sems[0])
-    else:
-        cot, copies = rest[0](), []
+def readout_body(me, readin, w1, b1, w2, cot, outs, full):
+    act, mine, theirs, grad, half_in, keep, send = outs
     half = full.shape[1] // 2
     core = me & 1
     lanes = pl.ds(pl.multiple_of(core * half, half), half)
-    half_in()[...] = readin()[:, lanes]
+    half_in()[...] = readin[:, lanes]
     half_in.send()
-    hidden = dot_nn(readin()[...], w1()[...]) + b1()[...]
+    hidden = dot_nn(readin[...], w1()[...]) + b1[...]
     value, slope = gelu_both(hidden)
-    act()[...] = value.astype(BF16)
-    act.send()
-    for copy in copies:
-        copy.wait()
-    for item in more:
-        item.send()
-    grad()[...] = dot_nt(cot[...], w2()[...])
+    act[...] = value.astype(BF16)
+    grad()[...] = dot_nt(cot()[...], w2()[...])
     grad.send()
     full[...] = dot_nt((slope * grad()[...]).astype(BF16), w1()[...])
     theirs()[...] = full[:, pl.ds(pl.multiple_of((1 - core) * half, half), half)].astype(BF16)
     theirs.send()
     mine()[...] = full[:, lanes]
-
-
-def readout(me, readin, w1, b1, w2, pieces, whole):
-    rows, chan = readin.shape
-    hidden, width = w2.shape
-    outs = [
-        sds((rows, hidden), BF16),
+    mine.send()
+    width = keep.buffer.shape[2]
+    for odd, out in ((1, send), (0, keep)):
+        for q in range(out.buffer.shape[0]):
+            lanes = pl.ds(pl.multiple_of((me ^ (2 * q + odd)) * width, width), width)
+            out()[q] = dot_nn(act[...], w2()[:, lanes]).astype(BF16)
+        out.send()
+
+
+def readout_shapes(rows, chan, hidden, width, n):
+    return [
         sds((rows, chan // 2), F32),
         sds((rows, chan // 2), BF16),
         sds((rows, hidden), F32),
         sds((rows, chan // 2), BF16),
+        sds((n // 2, rows, width // n), BF16),
+        sds((n // 2, rows, width // n), BF16),
     ]
-    args, scratch = [readin, w1, b1, w2], [pltpu.VMEM((rows, chan), F32)]
-    if pieces is None:
-        args.append(whole)
-    else:
-        outs.append(sds((rows, width), BF16))
-        scratch.append(pltpu.SemaphoreType.DMA((len(pieces),)))
+
+
+def readout_kernel(scalars, ins, outs, plain, full, act):
+    readin, w1, b1, w2, cot = ins
+    readout_body(scalars[0][0], readin(), w1, b1(), w2, cot, [act, *outs], full)
+
+
+def readout(me, readin, w1, b1, w2, cot, n):
+    rows, chan = readin.shape
+    return call(
+        readout_kernel,
+        readout_shapes(rows, chan, *w2.shape, n),
+        [me],
+        [readin, w1, b1, w2, cot],
+        [pltpu.VMEM((rows, chan), F32), pltpu.VMEM((rows, w2.shape[0]), BF16)],
+    )
+
+
+class Later:
+    def __init__(self, source, buffer, sem):
+        self.copy, self.buffer, self.waited = pltpu.make_async_copy(source, buffer, sem), buffer, False
+
+    def start(self):
+        self.copy.start()
+
+    def __call__(self):
+        if not self.waited:
+            self.copy.wait()
+            self.waited = True
+        return self.buffer
+
+
+def second_kernel(side, count, scalars, ins, outs, plain, field, act, stage, scr, sems, full, hid, w1_buf, w2_buf, wsems):
+    aux, x, b1 = [item() for item in ins]
+    pieces, (w1, w2) = plain[:count], plain[count:]
+    w1, w2 = Later(w1, w1_buf, wsems.at[0]), Later(w2, w2_buf, wsems.at[1])
+    me = scalars[0][0]
+    sources = [item() for item in outs[:3]]
+    assemble(me, pieces, None, *sources, stage, scr, sems, (w1, w2))
+    for item in outs[:3]:
+        item.send()
+    readin, keep, rest, cot_out = outs[3], outs[4:9], outs[9:15], outs[15]
+    cot = cot_out()
+    share = cot.shape[1] // count
+    for r in range(count):
+        start = (me ^ r) * share
+        for index in range((stage.shape[2] - 2 * LANES) // LANES * 2):
+            (row, lane), (low_row, low_lane) = cot_block(index, share)
+            lanes = pl.ds(pl.multiple_of(start + lane, LANES), LANES)
+            low_lane = 2 * LANES + low_lane
+            cot[row : row + 16, lanes] = stage[r, low_row : low_row + 16, low_lane : low_lane + LANES]
+    cot_out.send()
+    forward_body(side, aux, x, *sources, keep, field, act, readin())
+    readin.send()
+    readout_body(me, readin(), w1, b1, w2, cot_out, [hid, *rest], full)
+
+
+def second_forward(side, chan, mid, me, aux, x, pieces, w1, b1, w2):
+    slots = side * side
+    hidden, width = w2.shape
     got = call(
-        functools.partial(readout_kernel, pieces is not None),
-        outs,
+        functools.partial(second_kernel, side, len(pieces)),
+        whole_shapes(chan, mid)
+        + [sds((slots, chan), BF16)]
+        + kept_shapes(slots, chan, mid)
+        + readout_shapes(slots, chan, hidden, width, len(pieces))
+        + [sds((slots, width), BF16)],
         [me],
-        args,
-        scratch,
-        flops=2 * rows * hidden * (2 * chan + width),
-        moved=2 * hidden * (chan + width),
-        plain=pieces or [],
-    )
-    return list(got) + ([whole] if pieces is None else [])
-
-
-def tokens_kernel(scalars, ins, outs, plain):
-    act, w2 = [item() for item in ins]
-    keep, send = [item() for item in outs]
-    width = keep.shape[2]
-    for odd, out in ((1, send), (0, keep)):
-        for q in range(keep.shape[0]):
-            lanes = pl.ds(pl.multiple_of((scalars[0][0] ^ (2 * q + odd)) * width, width), width)
-            out[q] = dot_nn(act[...], w2[:, lanes]).astype(out.dtype)
-        outs[odd].send()
-
-
-def tokens_share(me, act, w2, n):
-    rows, hidden = act.shape
-    width = w2.shape[1] // n
-    return call(
-        tokens_kernel,
-        [sds((n // 2, rows, width), F32), sds((n // 2, rows, width), BF16)],
-        [me],
-        [act, w2],
-        flops=2 * rows * hidden * w2.shape[1],
-        moved=2 * hidden * w2.shape[1],
-    )
-
-
-def hidden_kernel(placed, scalars, ins, outs, plain, stacked, low, *sems):
-    w1, b1, w2, grad, readin, *parts = ins
-    act, w1_grad, b1_grad, *more = outs
+        [aux, x, b1],
+        forward_scratch(side, mid)
+        + assemble_scratch(pieces, mid, slots * width // mid)
+        + [
+            pltpu.VMEM((slots, chan), F32),
+            pltpu.VMEM((slots, hidden), BF16),
+            pltpu.VMEM(w1.shape, BF16),
+            pltpu.VMEM(w2.shape, BF16),
+            pltpu.SemaphoreType.DMA((2,)),
+        ],
+        flops=2 * slots * (mid * (2 * chan + TAPS * mid) + hidden * (2 * chan + width)),
+        moved=30 * slots * chan + 2 * hidden * (chan + width),
+        plain=[*pieces, w1, w2],
+    )
+    got = list(got)
+    return got[3], [x] + got[:3] + got[4:9], got[9:]
+
+
+def tail_kernel(placed, scalars, ins, outs, plain, stacked, low, cot, w2_buf, buffer, sems, out_sems):
+    readin, w1, b1, *parts, grad = ins
+    w1_grad, b1_grad, b2_grad, w2_out = outs
     me = scalars[0][0]
-    if placed:
-        cot = more[0]()
-        copies = place_pieces(me, plain, cot, sems[0])
-    else:
-        cot, copies = parts.pop()(), []
-    other = parts.pop()
-    half = other.buffer.shape[1]
     rows = readin.buffer.shape[0]
+    own, w2, *rest = plain
+    w2 = Later(w2, w2_buf, sems.at[1 + len(rest)])
+    copies = [pltpu.make_async_copy(own, cot.at[0:rows, :], sems.at[0])]
+    for r, piece in enumerate(rest):
+        share = piece.shape[1]
+        lanes = pl.ds(pl.multiple_of((me ^ r) * share, share), share) if placed else slice(0, share)
+        copies.append(pltpu.make_async_copy(piece, cot.at[rows:, lanes], sems.at[1 + r]))
+    for copy in copies:
+        copy.start()
+    w2.start()
+    split = len(parts) // 2
+    half = parts[0].buffer.shape[1]
     lanes = [pl.ds(pl.multiple_of(((me & 1) ^ odd) * half, half), half) for odd in range(2)]
     stacked[0:rows, :] = readin()[...]
-    at = rows
-    for part in parts:
-        count = part.buffer.shape[0]
-        stacked[at : at + count, lanes[0]] = part()[...]
-        at += count
-    stacked[rows:, lanes[1]] = other()[...]
+    for odd, group in enumerate((parts[:split], parts[split:])):
+        at = rows
+        for part in group:
+            count = part.buffer.shape[0]
+            stacked[at : at + count, lanes[odd]] = part()[...]
+            at += count
     hidden = dot_nn(stacked[...], w1()[...]) + b1()[...]
     value, slope = gelu_both(hidden)
-    act()[...] = value.astype(BF16)
-    act.send()
-    low[0:rows, :] = (slope[0:rows] * grad()[...]).astype(BF16)
+    turned = value.T.astype(BF16)
     for copy in copies:
         copy.wait()
-    for item in more:
-        item.send()
-    low[rows:, :] = (slope[rows:] * dot_nt(cot[...], w2()[...])).astype(BF16)
+    width = buffer.shape[2]
+    flights = []
+    for r in range(cot.shape[1] // width):
+        if r >= 2:
+            flights[r - 2].wait()
+        lanes = slice(r * width, (r + 1) * width)
+        buffer[r % 2] = dot_nn(turned, cot[:, lanes])
+        flights.append(pltpu.make_async_copy(buffer.at[r % 2], w2_out.target.at[:, lanes], out_sems.at[r % 2]))
+        flights[-1].start()
+    low[0:rows, :] = (slope[0:rows] * grad()[...]).astype(BF16)
+    low[rows:, :] = (slope[rows:] * dot_nt(cot[rows:, :], w2()[...])).astype(BF16)
+    w1_grad()[...] = dot_tn(stacked[...], low[...])
+    w1_grad.send()
     b1_grad()[...] = jnp.sum(low[...].astype(F32), axis=0, keepdims=True)
-    w1_grad()[...] = dot_tn(stacked[...], low[...])
-
-
-def hidden_all(me, b1, w1, w2, grad, readin, parts, other, pieces, whole):
+    share = b2_grad.buffer.shape[1]
+    lanes = pl.ds(pl.multiple_of(me * share, share), share)
+    b2_grad()[...] = jnp.sum(cot[:, lanes].astype(F32), axis=0, keepdims=True)
+    for flight in flights[-2:]:
+        flight.wait()
+
+
+def tail(me, b1, w1, w2, grad, readin, parts, own, rest, placed, n):
     rows, chan = readin.shape
-    total = rows + other.shape[0]
+    total = rows + sum(x.shape[0] for x in parts) // 2
     hidden, width = w2.shape
-    outs = [sds((total, hidden), BF16), sds((chan, hidden), F32), sds((1, hidden), F32)]
-    args = [w1, b1, w2, grad, readin, *parts, other]
-    scratch = [pltpu.VMEM((total, chan), BF16), pltpu.VMEM((total, hidden), BF16)]
-    if pieces is None:
-        args.append(whole)
-    else:
-        outs.append(sds((total - rows, width), BF16))
-        scratch.append(pltpu.SemaphoreType.DMA((len(pieces),)))
-    got = call(
-        functools.partial(hidden_kernel, pieces is not None),
-        outs,
+    chunk = min(width, 1024)
+    return call(
+        functools.partial(tail_kernel, placed),
+        [sds((chan, hidden), F32), sds((1, hidden), F32), sds((1, width // n), F32), sds((hidden, width), F32)],
         [me],
-        args,
-        scratch,
-        flops=2 * total * hidden * (2 * chan + width),
-        moved=2 * hidden * (3 * chan + width),
-        plain=pieces or [],
-    )
-    return list(got) + ([whole] if pieces is None else [])
-
-
-def w2_kernel(n, scalars, ins, outs, plain, both, buffer, sems):
-    act, own, rest = [item() for item in ins]
-    b2_grad = outs[0]()
-    (out,) = plain[1:] if len(plain) > 1 else plain
-    rows = own.shape[0]
-    width = own.shape[1] // n
-    turned = act[...].astype(F32).T.astype(BF16)
-    lanes = pl.ds(pl.multiple_of(scalars[0][0] * width, width), width)
-    b2_grad[...] = jnp.sum(own[:, lanes].astype(F32), axis=0, keepdims=True) + jnp.sum(
-        rest[:, lanes].astype(F32), axis=0, keepdims=True
-    )
-    copies = []
-    for r in range(n):
-        slot = r % 2
-        if r >= 2:
-            copies[r - 2].wait()
-        both[0:rows, :] = own[:, r * width : (r + 1) * width]
-        both[rows:, :] = rest[:, r * width : (r + 1) * width]
-        buffer[slot] = dot_nn(turned, both[...])
-        copy = pltpu.make_async_copy(
-            buffer.at[slot], out.at[:, r * width : (r + 1) * width], sems.at[slot]
-        )
-        copy.start()
-        copies.append(copy)
-    for copy in copies[-2:]:
-        copy.wait()
-
-
-def w2_gradient(me, act, own, rest, n):
-    total, hidden = act.shape
-    chan = own.shape[1]
-    width = chan // n
-
-    def kernel(me_ref, act_ref, own_ref, rest_ref, out, b2_out, *scratch):
-        act_buf, own_buf, rest_buf, b2_buf, sems, out_sem, *more = scratch
-        ins = [
-            Inward(a, b, sems.at[i])
-            for i, (a, b) in enumerate(((act_ref, act_buf), (own_ref, own_buf), (rest_ref, rest_buf)))
-        ]
-        b2_grad = Outward(b2_out, b2_buf, out_sem)
-        w2_kernel(n, [me_ref], ins, [b2_grad], [out], *more)
-        b2_grad.send()
-        b2_grad.copy.wait()
-
-    return pl.pallas_call(
-        kernel,
-        out_shape=[sds((hidden, chan), F32), sds((1, width), F32)],
-        in_specs=[SMEM] + [ANY] * 3,
-        out_specs=[ANY] * 2,
-        scratch_shapes=[
-            pltpu.VMEM(act.shape, BF16),
-            pltpu.VMEM(own.shape, BF16),
-            pltpu.VMEM(rest.shape, BF16),
-            pltpu.VMEM((1, width), F32),
-            pltpu.SemaphoreType.DMA((3,)),
-            pltpu.SemaphoreType.DMA,
+        [readin, w1, b1, *parts, grad],
+        [
+            pltpu.VMEM((total, chan), BF16),
+            pltpu.VMEM((total, hidden), BF16),
             pltpu.VMEM((total, width), BF16),
-            pltpu.VMEM((2, hidden, width), F32),
+            pltpu.VMEM(w2.shape, BF16),
+            pltpu.VMEM((2, hidden, chunk), F32),
+            pltpu.SemaphoreType.DMA((2 + len(rest),)),
             pltpu.SemaphoreType.DMA((2,)),
         ],
-        compiler_params=pltpu.CompilerParams(vmem_limit_bytes=60 << 20),
-        cost_estimate=pl.CostEstimate(
-            flops=2 * total * hidden * chan, bytes_accessed=4 * hidden * chan, transcendentals=0
-        ),
-    )(me, act, own, rest)
+        flops=4 * total * hidden * (chan + width),
+        moved=2 * hidden * (3 * chan + 3 * width),
+        plain=[own, w2, *rest],
+        direct=(3,),
+    )
 
 
 def finish_kernel(count, scalars, ins, outs, plain, scr):
@@ -1083,14 +1069,27 @@
     few = cot.shape[0]
     slot_facts, few_facts, spread = facts(grid)
 
+    bias_one = read_b1[None, :]
+
     if aligned:
         (first_packet,) = pack(0, feat, red, conv, expand_w, *norms)
         far = neighbours(first_packet)
         second_packet, cot = pack(1, cot, red, conv, expand_w, *norms, after=[first_packet])
+
+    cot_rest = join(*along_images(cot))
+
+    if aligned:
+        far = dict(zip(far, gate(list(far.values()), second_packet, cot_rest, spread)))
         first_pieces = with_cores(first_packet, far)
         (second_packet,) = gate([second_packet], *far.values())
         far = neighbours(second_packet)
-        first_whole = second_whole = None
+        pooled, saved_first = block_forward(GRID, chan, mid, me, slot_facts, spread, first_pieces, None)
+        far = dict(zip(far, gate(list(far.values()), pooled)))
+        second_pieces = with_cores(second_packet, far)
+        readin, saved_second, got = second_forward(
+            POOLED, chan, mid, me, few_facts, pooled, second_pieces, read_w1, bias_one, read_w2
+        )
+        mine, theirs, own_grad, half_in, keep, send, cot_own = got
     else:
         rows = jnp.concatenate(
             [red, jnp.transpose(conv, (0, 2, 1, 3)).reshape(2, held, TAPS * mid), expand_w], axis=2
@@ -1101,101 +1100,73 @@
         outs = jnp.stack([out_gain, out_bias], axis=1)
         outs = jnp.pad(lax.all_gather(outs, "ch", axis=2, tiled=True), ((0, 0), (0, 6), (0, 0)))
         x_whole = lax.all_gather(feat, "ch", axis=1, tiled=True)
-        first_whole = (x_whole, rows[0], mids[0], outs[0])
-        second_whole = (rows[1], mids[1], outs[1])
-        first_pieces = second_pieces = None
-
-    cot_rest, held_cot = [], cot
-    for mask in (1 << k for k in range(planes.bit_length() - 1)):
-        cot_rest.append(ppermute_xor(held_cot, "img", mask))
-        if 2 * mask < planes:
-            held_cot = join(held_cot, cot_rest[-1])
-    cot_rest = join(*cot_rest)
-
-    pooled, saved_first = block_forward(
-        GRID, chan, mid, me, slot_facts, spread, None, first_pieces, first_whole
-    )
+        pooled, saved_first = block_forward(
+            GRID, chan, mid, me, slot_facts, spread, None, (x_whole, rows[0], mids[0], outs[0])
+        )
+        readin, saved_second = block_forward(
+            POOLED, chan, mid, me, few_facts, None, None, (pooled, rows[1], mids[1], outs[1])
+        )
+        cot_own = lax.all_gather(cot, "ch", axis=1, tiled=True)
+        mine, theirs, own_grad, half_in, keep, send = readout(me, readin, read_w1, bias_one, read_w2, cot_own, n)
+
+    half = summed(mine, ppermute_xor(theirs, "ch", 1))
+    far = neighbours(half)
     if aligned:
-        far = dict(zip(far, gate(list(far.values()), pooled)))
-        second_pieces = with_cores(second_packet, far)
-        (cot,) = gate([cot], *far.values())
-        far = neighbours(cot)
-    else:
-        second_whole = (pooled,) + second_whole
-    readin, saved_second = block_forward(
-        POOLED, chan, mid, me, few_facts, None, pooled, second_pieces, second_whole
-    )
-
-    bias_one = read_b1[None, :]
-    if aligned:
-        far = dict(zip(far, gate(list(far.values()), readin)))
-        cot_pieces, cot_own = with_cores(cot, far), None
-    else:
-        cot_pieces, cot_own = None, lax.all_gather(cot, "ch", axis=1, tiled=True)
-    act, mine, theirs, own_grad, half_in, cot_own = readout(
-        me, readin, read_w1, bias_one, read_w2, cot_pieces, cot_own
-    )
-
-    half = add(mine, ppermute_xor(theirs, "ch", 1))
-    far = neighbours(half)
-    keep, send = tokens_share(me, act, read_w2, n)
-    far = dict(zip(far, gate(list(far.values()), send)))
+        (cot_rest,) = gate([cot_rest], half)
+        cot_far = neighbours(cot_rest)
     grad_pieces = with_cores(half, far)
-
-    parts, held_in = [], half_in
-    for mask in (1 << k for k in range(planes.bit_length() - 1)):
-        parts.append(ppermute_xor(held_in, "img", mask))
-        if 2 * mask < planes:
-            held_in = join(held_in, parts[-1])
-
-    (cot_rest,) = gate([cot_rest], *far.values())
-    if aligned:
-        far = neighbours(cot_rest)
+    (half_in,) = gate([half_in], *far.values())
+    parts = [ppermute_xor(half_in, "img", m) for m in (1, 2) if m < planes]
 
     pooled_grad, late_mine, late_theirs, late_out = late_backward(
         POOLED, held, me, few_facts, grad_pieces, saved_second
     )
     late_got = ppermute_xor(late_theirs, "img", 1)
+    (half_in,) = gate([half_in], pooled_grad)
+    parts += [ppermute_xor(half_in, "img", m) for m in range(3, planes)]
     own_lanes = share if aligned else 0
     middle_mine, middle_theirs, *upper = upper_backward(
         GRID, held, me, slot_facts, spread, pooled_grad, saved_first, own_lanes
     )
     middle_got = ppermute_xor(middle_theirs, "img", 1)
-    late_half = add(late_mine, late_got, after=[upper[0]])
-    late_more = [ppermute_xor(late_half, "img", 2)]
+    (late_got,) = gate([late_got], upper[0])
+    late_half = summed(late_mine, late_got)
+    late_got = ppermute_xor(late_half, "img", 2)
+    parts = gate(parts, upper[0])
+    parts = [*parts, *[ppermute_xor(x, "ch", 1) for x in parts]]
+    if aligned:
+        cot_far = dict(zip(cot_far, gate(list(cot_far.values()), upper[0])))
+        rest_pieces = with_cores(cot_rest, cot_far)
+    else:
+        rest_pieces = [lax.all_gather(cot_rest, "ch", axis=1, tiled=True)]
     feat_grad, last_grads, last_low = lower_backward(
         GRID, held, me, slot_facts, upper, saved_first, own_lanes
     )
     last = [last_grads] + along_images(last_low)
-    middle_half = add(middle_mine, middle_got, after=[last_grads])
-    middle_more = [ppermute_xor(middle_half, "img", 2)]
-    late_half = add(late_half, late_more[-1], after=[last_grads])
+    late_got, middle_got = gate([late_got, middle_got], last_grads)
+    middle_half = summed(middle_mine, middle_got)
+    middle_got = ppermute_xor(middle_half, "img", 2)
+    late_half = summed(late_half, late_got)
     for mask in (1 << k for k in range(2, planes.bit_length() - 1)):
-        late_half = add(late_half, ppermute_xor(late_half, "img", mask))
+        late_half = summed(late_half, ppermute_xor(late_half, "img", mask))
     late = (late_half, ppermute_xor(late_half, "img", 1))
-
-    other = ppermute_xor(join(*parts, after=[upper[0]]), "ch", 1)
-    if aligned:
-        far = dict(zip(far, gate(list(far.values()), last_grads)))
-        rest_pieces, cot_rest = with_cores(cot_rest, far), None
-    else:
-        rest_pieces, cot_rest = None, lax.all_gather(cot_rest, "ch", axis=1, tiled=True)
-    act_all, w1_grad, b1_grad, cot_rest = hidden_all(
-        me, bias_one, read_w1, read_w2, own_grad, readin, parts, other, rest_pieces, cot_rest
-    )
-    middle_half = add(middle_half, middle_more[-1], after=[act_all])
+    w1_grad, b1_grad, b2_grad, w2_grad = tail(
+        me, bias_one, read_w1, read_w2, own_grad, readin, parts, cot_own, rest_pieces, aligned, n
+    )
+    (middle_got,) = gate([middle_got], b1_grad)
+    middle_half = summed(middle_half, middle_got)
     for mask in (1 << k for k in range(2, planes.bit_length() - 1)):
-        middle_half = add(middle_half, ppermute_xor(middle_half, "img", mask))
+        middle_half = summed(middle_half, ppermute_xor(middle_half, "img", mask))
     middle = (middle_half, ppermute_xor(middle_half, "img", 1))
 
     got = ppermute_xor(send, "ch", 1)
-    parts = [keep[q] + got[q].astype(F32) for q in range(n // 2)]
-    tokens = parts[0]
+    (got,) = gate([got], b1_grad)
+    shares = [summed(keep[q], got[q]) for q in range(n // 2)]
+    tokens = shares[0].astype(F32)
     for q in range(1, n // 2):
-        tokens = tokens + ppermute_xor(parts[q].astype(BF16), "ch", 2 * q).astype(F32)
+        tokens = tokens + ppermute_xor(shares[q], "ch", 2 * q).astype(F32)
     tokens = (tokens + read_b2[None, :]).astype(BF16)
 
-    w2_grad, b2_grad = w2_gradient(me, act_all, cot_own, cot_rest, n)
     red_grad, conv_grad, exp_grad, mid_gain_grad, mid_bias_grad, out_gain_grad, out_bias_grad = finish(
         me, late, middle, last, chan, mid, share
     )

time: 187 us -> 167 us (0.89)
  Pallas kernels: 96.3 us -> 69.3 us
  other arithmetic: 3.21 us -> 8.18 us
  local copies, waits for them, and re-layouts: 7.16 us -> 9.19 us
    pallas_call x21 -> x11, Pallas kernels: 85.5 us -> 69.3 us  [call(): pl.pallas_call(kernel, out_shape=list(outs), in_specs=[SMEM] * len(scalar...]
    pallas_call x1 -> x0, Pallas kernels: 10.7 us -> none  [w2_gradient(): pl.pallas_call(kernel, out_shape=[sds((hidden, chan), F32), sds((1, width...]
    convert_element_type x1 -> x6, other arithmetic: 0.81 us -> 5.89 us  [summed(): return (left.astype(F32) + right.astype(F32)).astype(BF16)]
    unnamed x104 -> x110, local copies, waits for them, and re-layouts: 7.16 us -> 9.19 us
    ppermute x54 -> x51, waiting for transfers between devices: 30.9 us -> 30.1 us  [ppermute_xor(): lax.ppermute(x, axis, [(i, i ^ mask) for i in range(lax.axis_size(axis))])]
    ppermute x54 -> x51, starting transfers between devices: 46.7 us -> 47.5 us  [ppermute_xor(): lax.ppermute(x, axis, [(i, i ^ mask) for i in range(lax.axis_size(axis))])]
  transfers between devices with their start and end apart: 54 -> 51, of which waited for: 11 -> 12; matrix products, arithmetic and copies ran while one was open for 2% -> 3% of each run, Pallas kernels for 45% -> 34%
where the time goes in v3:
time: 167 us; the launch traced here: 166 us
  Pallas kernels  69.3 us (41%)
  starting transfers between devices  47.5 us (28%)
  waiting for transfers between devices  30.1 us (18%)
  local copies, waits for them, and re-layouts  9.19 us (6%)
  other arithmetic  8.18 us (5%)
  between operations  1.95 us (1%)
    pallas_call x11, Pallas kernels, call(): pl.pallas_call(kernel, out_shape=list(outs), in_specs=[SMEM] * len(scalar...  69.3 us
    ppermute x51, starting transfers between devices, ppermute_xor(): lax.ppermute(x, axis, [(i, i ^ mask) for i in range(lax.axis_size(axis))])  47.5 us
    ppermute x51, waiting for transfers between devices, ppermute_xor(): lax.ppermute(x, axis, [(i, i ^ mask) for i in range(lax.axis_size(axis))])  30.1 us
    unnamed x110, local copies, waits for them, and re-layouts  9.19 us
    convert_element_type x6, other arithmetic, summed(): return (left.astype(F32) + right.astype(F32)).astype(BF16)  5.89 us
  transfers between devices with their start and end apart: 51, of which 12 were waited for; matrix products, arithmetic and copies ran while one was open for 3% of the time, Pallas kernels for 34%

profile of v3, /device:TPU:0, one launch (start us, length us, event | category | flops | bytes accessed | tf_op | source)
XLA Modules:
  0.0 166.2 jit_solution(18228666819316434473)
XLA Ops:
  0.6 1.9 %shard_map.238.refs_8_.refs_3_ = bf16[32,6912]{1,0:T(8,128)(2,1)} custom-call(bf16[576,128]{1,0:T(8,128)(2,1)} %bitcast.39, f32[2,2,32]{2,1,0:T(2,128)} %refs_1_.3, f32[2,2,32]{2,1,0:T(2,128)} %refs_2_.4, f32[2,128]{1,0:T(2,128)} %refs_3_.3, f32[2,128]{1,0:T(2,128)} %refs_4_.3, bf16[2,32,1024]{2,1,0:T(8,128)(2,1)} %bitcast.37, ...), custom_call_target="tpu_custom_call" | custom-call | bytes 884736 | tf_op jit(solution)/shard_map/pallas_call | solution.py:97
  2.6 3.0 %collective-permute-start.3 = (bf16[32,6912]{1,0:T(8,128)(2,1)}, bf16[32,6912]{1,0:T(8,128)(2,1)S(1)}, u32[]{:S(2)}, u32[]{:S(2)}) collective-permute-start(bf16[32,6912]{1,0:T(8,128)(2,1)} %shard_map.238.refs_8_.refs_3_), channel_id=1, source_target_pairs={{0,2},{1,3},{2,0},{3,1},{4,6},{5,7},{6,4},{7,5},{8,10},{9,11},{10,... | collective-permute-start | bytes 1327112 | tf_op jit(solution)/shard_map/ppermute | solution.py:136
  5.6 1.5 collective-permute-start.2
  7.1 2.0 %shard_map.239 = (bf16[32,6912]{1,0:T(8,128)(2,1)}, bf16[144,512]{1,0:T(8,128)(2,1)}) custom-call(bf16[144,512]{1,0:T(8,128)(2,1)} %bitcast.40, f32[2,2,32]{2,1,0:T(2,128)} %refs_1_.3, f32[2,2,32]{2,1,0:T(2,128)} %refs_2_.4, f32[2,128]{1,0:T(2,128)} %refs_3_.3, f32[2,128]{1,0:T(2,128)} %refs_4_.3, bf16[2,32,1024]{2,1,0:T(8,128)(2,1)} %bitcast.38, ...), custom_call_target="tpu_custom_call" | custom-call | bytes 884736 | tf_op jit(solution)/shard_map/pallas_call | solution.py:97
  9.1 4.1 %collective-permute-start.6 = (bf16[144,512]{1,0:T(8,128)(2,1)}, bf16[144,512]{1,0:T(8,128)(2,1)S(1)}, u32[]{:S(2)}, u32[]{:S(2)}) collective-permute-start(bf16[144,512]{1,0:T(8,128)(2,1)} %get-tuple-element.85), channel_id=1, source_target_pairs={{0,24},{8,16},{16,8},{24,0},{1,25},{9,17},{17,9},{25,1},{2,26},{10... | collective-permute-start | bytes 442376 | tf_op jit(solution)/shard_map/ppermute | solution.py:136
  13.3 4.9 %collective-permute-done.6.refs_2_ = bf16[144,512]{1,0:T(8,128)(2,1)S(1)} collective-permute-done((bf16[144,512]{1,0:T(8,128)(2,1)}, bf16[144,512]{1,0:T(8,128)(2,1)S(1)}, u32[]{:S(2)}, u32[]{:S(2)}) %collective-permute-start.6) | collective-permute-done | bytes 147488 | tf_op jit(solution)/shard_map/ppermute | solution.py:136
  18.2 5.4 %collective-permute-start.4 = (bf16[144,512]{1,0:T(8,128)(2,1)}, bf16[144,512]{1,0:T(8,128)(2,1)S(1)}, u32[]{:S(2)}, u32[]{:S(2)}) collective-permute-start(bf16[144,512]{1,0:T(8,128)(2,1)} %get-tuple-element.85), channel_id=1, source_target_pairs={{0,8},{8,0},{16,24},{24,16},{1,9},{9,1},{17,25},{25,17},{2,10},{10... | collective-permute-start | bytes 442376 | tf_op jit(solution)/shard_map/ppermute | solution.py:136
  24.2 1.1 shard_map.237
  25.4 2.8 %collective-permute-done.4.refs_0_ = bf16[144,512]{1,0:T(8,128)(2,1)S(1)} collective-permute-done((bf16[144,512]{1,0:T(8,128)(2,1)}, bf16[144,512]{1,0:T(8,128)(2,1)S(1)}, u32[]{:S(2)}, u32[]{:S(2)}) %collective-permute-start.4) | collective-permute-done | bytes 147488 | tf_op jit(solution)/shard_map/ppermute | solution.py:136
  28.8 1.9 %shard_map.240.refs_4_.refs_0_ = bf16[432,512]{1,0:T(8,128)(2,1)} custom-call(bf16[144,512]{1,0:T(8,128)(2,1)} %copy-done.35, bf16[144,512]{1,0:T(8,128)(2,1)} %copy-done.34, bf16[144,512]{1,0:T(8,128)(2,1)} %copy-done.33), custom_call_target="tpu_custom_call" | custom-call | tf_op jit(solution)/shard_map/pallas_call | solution.py:97
  32.3 1.5 collective-permute-start.13
  33.8 1.5 collective-permute-start.12
  35.4 0.9 collective-permute-start.11
  37.8 10.9 %shard_map.242 = (bf16[576,1024]{1,0:T(8,128)(2,1)}, bf16[256,4352]{1,0:T(8,128)(2,1)}, f32[8,256]{1,0:T(8,128)}, f32[8,1024]{1,0:T(8,128)}, bf16[144,1024]{1,0:...) custom-call(s32[2]{0:T(128)} %pad_add_fusion.refs_0_, ...), custom_call_target="tpu_custom_call" | custom-call | flops 1283457024 | bytes 17694720 | tf_op jit(solution)/shard_map/pallas_call | solution.py:97
  48.8 7.0 %collective-permute-done.12.refs_1_ = bf16[32,6912]{1,0:T(8,128)(2,1)S(1)} collective-permute-done((bf16[32,6912]{1,0:T(8,128)(2,1)}, bf16[32,6912]{1,0:T(8,128)(2,1)S(1)}, u32[]{:S(2)}, u32[]{:S(2)}) %collective-permute-start.12) | collective-permute-done | bytes 442400 | tf_op jit(solution)/shard_map/ppermute | solution.py:136
  57.3 1.5 collective-permute-done.14.refs_7_
  60.8 10.6 %shard_map.245 = (bf16[256,4352]{1,0:T(8,128)(2,1)}, f32[8,256]{1,0:T(8,128)}, f32[8,1024]{1,0:T(8,128)}, bf16[144,1024]{1,0:T(8,128)(2,1)}, f32[144,256]{1,0:T(...) custom-call(s32[2]{0:T(128)} %pad_add_fusion.refs_0_, ...), custom_call_target="tpu_custom_call" | custom-call | flops 1226833920 | bytes 9666560 | tf_op jit(solution)/shard_map/pallas_call | solution.py:97
  71.6 1.4 collective-permute-done.18
  73.1 1.0 add_convert_fusion.6.refs_11_.refs_1_
  74.1 1.1 collective-permute-start.21
  75.2 1.0 collective-permute-start.20
  76.2 1.4 collective-permute-start.19
  77.6 3.2 %collective-permute-done.21.refs_3_.refs_13_ = bf16[144,512]{1,0:T(8,128)(2,1)S(1)} collective-permute-done((bf16[144,512]{1,0:T(8,128)(2,1)S(1)}, bf16[144,512]{1,0:T(8,128)(2,1)S(1)}, u32[]{:S(2)}, u32[]{:S(2)}) %collective-permute-start.21) | collective-permute-done | bytes 147488 | tf_op jit(solution)/shard_map/ppermute | solution.py:136
  80.8 1.7 %collective-permute-done.20.refs_2_.refs_15_ = bf16[144,512]{1,0:T(8,128)(2,1)S(1)} collective-permute-done((bf16[144,512]{1,0:T(8,128)(2,1)S(1)}, bf16[144,512]{1,0:T(8,128)(2,1)S(1)}, u32[]{:S(2)}, u32[]{:S(2)}) %collective-permute-start.20) | collective-permute-done | bytes 147488 | tf_op jit(solution)/shard_map/ppermute | solution.py:136
  82.5 1.6 collective-permute-done.19.refs_1_.refs_17_
  84.8 2.3 %collective-permute-start.23 = (bf16[144,512]{1,0:T(8,128)(2,1)}, bf16[144,512]{1,0:T(8,128)(2,1)S(1)}, u32[]{:S(2)}, u32[]{:S(2)}) collective-permute-start(bf16[144,512]{1,0:T(8,128)(2,1)} %shard_map.246.refs_0_), channel_id=1, source_target_pairs={{0,16},{8,24},{16,0},{24,8},{1,17},{9,25},{17,1},{25,9},{2,18},{10... | collective-permute-start | bytes 442376 | tf_op jit(solution)/shard_map/ppermute | solution.py:136
  88.0 7.4 %shard_map.247 = (bf16[144,1024]{1,0:T(8,128)(2,1)}, f32[16,4608]{1,0:T(8,128)}, bf16[16,4608]{1,0:T(8,128)(2,1)}, f32[8,1024]{1,0:T(8,128)}) custom-call(s32[2]{0:T(128)} %pad_add_fusion.refs_0_, f32[144,128]{1,0:T(8,128)} %get-tuple-element.81.refs_1_, bf16[144,1024]{1,0:T(8,128)(2,1)} %get-tuple-element.89.refs_3_.refs_2_, ...), custom_call_target="tpu_custom_call" | custom-call | flops 481296384 | bytes 5898240 | tf_op jit(solution)/shard_map/pallas_call | solution.py:97
  95.4 2.1 %collective-permute-start.42 = (bf16[16,4608]{1,0:T(8,128)(2,1)}, bf16[16,4608]{1,0:T(8,128)(2,1)S(1)}, u32[]{:S(2)}, u32[]{:S(2)}) collective-permute-start(bf16[16,4608]{1,0:T(8,128)(2,1)} %get-tuple-element.132), channel_id=1, source_target_pairs={{0,8},{8,0},{16,24},{24,16},{1,9},{9,1},{17,25},{25,17},{2,10},{10... | collective-permute-start | bytes 442376 | tf_op jit(solution)/shard_map/ppermute | solution.py:136
  98.3 1.5 collective-permute-start.34
  99.8 1.1 collective-permute-start.33
  101.7 9.2 %shard_map.249 = (f32[16,3328]{1,0:T(8,128)}, bf16[16,3328]{1,0:T(8,128)(2,1)}, f32[576,256]{1,0:T(8,128)}, f32[576,128]{1,0:T(8,128)}, f32[8,256]{1,0:T(8,128)}, /*index=5*/f32[8,1024]{1,0:T(8,128)}) custom-call(s32[2]{0:T(128)} %pad_add_fusion.refs_0_, f32[576,128]{1,0:T(8,128)} %get-tuple-element.82.refs_1_, ...), custom_call_target="tpu_custom_call" | custom-call | flops 1283457024 | bytes 23592960 | tf_op jit(solution)/shard_map/pallas_call | solution.py:97
  111.6 0.9 add_convert_fusion.1
  113.4 2.8 %collective-permute-start.44 = (bf16[16,3328]{1,0:T(8,128)(2,1)}, bf16[16,3328]{1,0:T(8,128)(2,1)S(1)}, u32[]{:S(2)}, u32[]{:S(2)}) collective-permute-start(bf16[16,3328]{1,0:T(8,128)(2,1)} %get-tuple-element.133), channel_id=1, source_target_pairs={{0,8},{8,0},{16,24},{24,16},{1,9},{9,1},{17,25},{25,17},{2,10},{10... | collective-permute-start | bytes 319496 | tf_op jit(solution)/shard_map/ppermute | solution.py:136
  116.2 6.8 %shard_map.255 = (f32[576,128]{1,0:T(8,128)}, f32[32,1280]{1,0:T(8,128)}, bf16[32,1280]{1,0:T(8,128)(2,1)}) custom-call(s32[2]{0:T(128)} %pad_add_fusion.refs_0_, f32[576,128]{1,0:T(8,128)} %get-tuple-element.82.refs_1_, f32[576,256]{1,0:T(8,128)} %get-tuple-element.116.refs_3_.refs_2_.refs_1_, bf16[256,4352]{1,0:T(8,128)(2,1)} %get-tuple-element.114.refs_10_.refs_3_, ...), custom_call_target="tpu_custom_call" | custom-call | flops 641728512 | bytes 11796480 | tf_op jit(solution)/shard_map/pallas_call | solution.py:97
  125.7 0.9 add_convert_fusion.refs_1_
  127.5 0.9 add_convert_fusion.8
  128.4 1.2 collective-permute-done.31.refs_9_
  131.1 2.9 %collective-permute-start.48 = (bf16[32,1280]{1,0:T(8,128)(2,1)S(1)}, bf16[32,1280]{1,0:T(8,128)(2,1)S(1)}, u32[]{:S(2)}, u32[]{:S(2)}) collective-permute-start(bf16[32,1280]{1,0:T(8,128)(2,1)S(1)} %copy-done.54), channel_id=1, source_target_pairs={{0,8},{8,0},{16,24},{24,16},{1,9},{9,1},{17,25},{25,17},{2,10},{10... | collective-permute-start | bytes 245768 | tf_op jit(solution)/shard_map/ppermute | solution.py:136
  134.8 14.5 %shard_map.253 = (f32[1024,512]{1,0:T(8,128)}, f32[1,512]{1,0:T(1,128)}, f32[1,512]{1,0:T(1,128)}, f32[512,4096]{1,0:T(8,128)}) custom-call(s32[2]{0:T(128)} %pad_add_fusion.refs_0_, bf16[144,1024]{1,0:T(8,128)(2,1)} %get-tuple-element.95.refs_1_, bf16[1024,512]{1,0:T(8,128)(2,1)} %refs_2_.5, f32[1,512]{1,0:T(1,128)} %bitcast.43, ...), custom_call_target="tpu_custom_call" | custom-call | flops 6039797760 | bytes 15728640 | tf_op jit(solution)/shard_map/pallas_call | solution.py:97
  150.2 1.2 fusion.5
  151.4 0.9 collective-permute-start.39
  152.3 1.6 collective-permute-start.41
  153.9 1.1 collective-permute-start.40
  155.0 0.9 add_convert_fusion.7.refs_3_
  156.0 1.4 collective-permute-start.47
  157.4 3.4 %collective-permute-done.47.refs_4_ = bf16[16,3328]{1,0:T(8,128)(2,1)S(1)} collective-permute-done((bf16[16,3328]{1,0:T(8,128)(2,1)S(1)}, bf16[16,3328]{1,0:T(8,128)(2,1)S(1)}, u32[]{:S(2)}, u32[]{:S(2)}) %collective-permute-start.47) | collective-permute-done | bytes 106528 | tf_op jit(solution)/shard_map/ppermute | solution.py:136
  161.4 3.1 %shard_map.259 = (f32[2,32,1024]{2,1,0:T(8,128)}, f32[2,9,32,256]{3,2,1,0:T(8,128)}, f32[2,32,1024]{2,1,0:T(8,128)}, f32[2,2,32]{2,1,0:T(2,128)}, f32[2,2,32]{2,...) custom-call(s32[2]{0:T(128)} %pad_add_fusion.refs_0_, bf16[16,4608]{1,0:T(8,128)(2,1)} %copy-done.9, ...), custom_call_target="tpu_custom_call" | custom-call | flops 262144 | bytes 1310720 | tf_op jit(solution)/shard_map/pallas_call | solution.py:97
  164.5 1.7 %fusion.8 = bf16[512,1,144]{0,2,1:T(8,128)(2,1)} fusion(bf16[144,512]{1,0:T(8,128)(2,1)S(1)} %collective-permute-done.41, bf16[144,512]{1,0:T(8,128)(2,1)S(1)} %collective-permute-done.40, bf16[144,512]{1,0:T(8,128)(2,1)S(1)} %collective-permute-done.39, bf16[4,144,512]{2,1,0:T(8,128)(2,1)} %shard_map.254, f32[512]{0:T(512)S(1)} %copy-done.43, ...), kind=kLoop, calls=%fused_computation.18 | loop fusion | flops 958464 | bytes 886784 | tf_op jit(solution)/shard_map/broadcast_in_dim | solution.py:1181
  (195 shorter events, 19.4 us)
Async XLA Ops:
  2.6 28.1 %collective-permute-start.3 = (bf16[32,6912]{1,0:T(8,128)(2,1)}, bf16[32,6912]{1,0:T(8,128)(2,1)S(1)}, u32[]{:S(2)}, u32[]{:S(2)}) collective-permute-start(bf16[32,6912]{1,0:T(8,128)(2,1)} %shard_map.238.refs_8_.refs_3_), channel_id=1, source_target_pairs={{0,2},{1,3},{2,0},{3,1},{4,6},{5,7},{6,4},{7,5},{8,10},{9,11},{10,... | collective-permute-start | bytes 1327112 | tf_op jit(solution)/shard_map/ppermute | solution.py:136
  5.6 25.1 %collective-permute-start.2 = (bf16[32,6912]{1,0:T(8,128)(2,1)}, bf16[32,6912]{1,0:T(8,128)(2,1)S(1)}, u32[]{:S(2)}, u32[]{:S(2)}) collective-permute-start(bf16[32,6912]{1,0:T(8,128)(2,1)} %shard_map.238.refs_8_.refs_3_), channel_id=1, source_target_pairs={{0,4},{1,5},{2,6},{3,7},{4,0},{5,1},{6,2},{7,3},{8,12},{9,13},{10,... | collective-permute-start | bytes 1327112 | tf_op jit(solution)/shard_map/ppermute | solution.py:136
  7.1 23.6 %collective-permute-start.1 = (bf16[32,6912]{1,0:T(8,128)(2,1)}, bf16[32,6912]{1,0:T(8,128)(2,1)S(1)}, u32[]{:S(2)}, u32[]{:S(2)}) collective-permute-start(bf16[32,6912]{1,0:T(8,128)(2,1)} %shard_map.238.refs_8_.refs_3_), channel_id=1, source_target_pairs={{0,6},{1,7},{2,4},{3,5},{4,2},{5,3},{6,0},{7,1},{8,14},{9,15},{10,... | collective-permute-start | bytes 1327112 | tf_op jit(solution)/shard_map/ppermute | solution.py:136
  9.1 9.0 %collective-permute-start.6 = (bf16[144,512]{1,0:T(8,128)(2,1)}, bf16[144,512]{1,0:T(8,128)(2,1)S(1)}, u32[]{:S(2)}, u32[]{:S(2)}) collective-permute-start(bf16[144,512]{1,0:T(8,128)(2,1)} %get-tuple-element.85), channel_id=1, source_target_pairs={{0,24},{8,16},{16,8},{24,0},{1,25},{9,17},{17,9},{25,1},{2,26},{10... | collective-permute-start | bytes 442376 | tf_op jit(solution)/shard_map/ppermute | solution.py:136
  13.3 12.0 %collective-permute-start.5 = (bf16[144,512]{1,0:T(8,128)(2,1)}, bf16[144,512]{1,0:T(8,128)(2,1)S(1)}, u32[]{:S(2)}, u32[]{:S(2)}) collective-permute-start(bf16[144,512]{1,0:T(8,128)(2,1)} %get-tuple-element.85), channel_id=1, source_target_pairs={{0,16},{8,24},{16,0},{24,8},{1,17},{9,25},{17,1},{25,9},{2,18},{10... | collective-permute-start | bytes 442376 | tf_op jit(solution)/shard_map/ppermute | solution.py:136
  18.2 10.0 %collective-permute-start.4 = (bf16[144,512]{1,0:T(8,128)(2,1)}, bf16[144,512]{1,0:T(8,128)(2,1)S(1)}, u32[]{:S(2)}, u32[]{:S(2)}) collective-permute-start(bf16[144,512]{1,0:T(8,128)(2,1)} %get-tuple-element.85), channel_id=1, source_target_pairs={{0,8},{8,0},{16,24},{24,16},{1,9},{9,1},{17,25},{25,17},{2,10},{10... | collective-permute-start | bytes 442376 | tf_op jit(solution)/shard_map/ppermute | solution.py:136
  25.3 8.5 %collective-permute-start = (bf16[32,6912]{1,0:T(8,128)(2,1)}, bf16[32,6912]{1,0:T(8,128)(2,1)S(1)}, u32[]{:S(2)}, u32[]{:S(2)}) collective-permute-start(bf16[32,6912]{1,0:T(8,128)(2,1)} %shard_map.238.refs_8_.refs_3_), channel_id=1, source_target_pairs={{0,1},{1,0},{2,3},{3,2},{4,5},{5,4},{6,7},{7,6},{8,9},{9,8},{10,11... | collective-permute-start | bytes 1327112 | tf_op jit(solution)/shard_map/ppermute | solution.py:136
  31.8 3.5 %collective-permute-start.7 = (bf16[32,6912]{1,0:T(8,128)(2,1)}, bf16[32,6912]{1,0:T(8,128)(2,1)S(1)}, u32[]{:S(2)}, u32[]{:S(2)}) collective-permute-start(bf16[32,6912]{1,0:T(8,128)(2,1)} %get-tuple-element.86.refs_5_.refs_3_), channel_id=1, source_target_pairs={{0,1},{1,0},{2,3},{3,2},{4,5},{5,4},{6,7},{7,6},{8,9},{9,8},{10,11... | collective-permute-start | bytes 1327112 | tf_op jit(solution)/shard_map/ppermute | solution.py:136
  31.8 5.1 %collective-permute-start.8 = (bf16[32,6912]{1,0:T(8,128)(2,1)}, bf16[32,6912]{1,0:T(8,128)(2,1)S(1)}, u32[]{:S(2)}, u32[]{:S(2)}) collective-permute-start(bf16[32,6912]{1,0:T(8,128)(2,1)} %get-tuple-element.87.refs_7_.refs_2_), channel_id=1, source_target_pairs={{0,1},{1,0},{2,3},{3,2},{4,5},{5,4},{6,7},{7,6},{8,9},{9,8},{10,11... | collective-permute-start | bytes 1327112 | tf_op jit(solution)/shard_map/ppermute | solution.py:136
  32.3 4.6 %collective-permute-start.9 = (bf16[32,6912]{1,0:T(8,128)(2,1)}, bf16[32,6912]{1,0:T(8,128)(2,1)S(1)}, u32[]{:S(2)}, u32[]{:S(2)}) collective-permute-start(bf16[32,6912]{1,0:T(8,128)(2,1)} %get-tuple-element.88.refs_9_.refs_1_), channel_id=1, source_target_pairs={{0,1},{1,0},{2,3},{3,2},{4,5},{5,4},{6,7},{7,6},{8,9},{9,8},{10,11... | collective-permute-start | bytes 1327112 | tf_op jit(solution)/shard_map/ppermute | solution.py:136
  32.3 16.4 %collective-permute-start.13 = (bf16[32,6912]{1,0:T(8,128)(2,1)}, bf16[32,6912]{1,0:T(8,128)(2,1)S(1)}, u32[]{:S(2)}, u32[]{:S(2)}) collective-permute-start(bf16[32,6912]{1,0:T(8,128)(2,1)} %shard_map.243.refs_4_), channel_id=1, source_target_pairs={{0,2},{1,3},{2,0},{3,1},{4,6},{5,7},{6,4},{7,5},{8,10},{9,11},{10,... | collective-permute-start | bytes 1327112 | tf_op jit(solution)/shard_map/ppermute | solution.py:136
  33.8 22.0 %collective-permute-start.12 = (bf16[32,6912]{1,0:T(8,128)(2,1)}, bf16[32,6912]{1,0:T(8,128)(2,1)S(1)}, u32[]{:S(2)}, u32[]{:S(2)}) collective-permute-start(bf16[32,6912]{1,0:T(8,128)(2,1)} %shard_map.243.refs_4_), channel_id=1, source_target_pairs={{0,4},{1,5},{2,6},{3,7},{4,0},{5,1},{6,2},{7,3},{8,12},{9,13},{10,... | collective-permute-start | bytes 1327112 | tf_op jit(solution)/shard_map/ppermute | solution.py:136
  35.4 20.5 %collective-permute-start.11 = (bf16[32,6912]{1,0:T(8,128)(2,1)}, bf16[32,6912]{1,0:T(8,128)(2,1)S(1)}, u32[]{:S(2)}, u32[]{:S(2)}) collective-permute-start(bf16[32,6912]{1,0:T(8,128)(2,1)} %shard_map.243.refs_4_), channel_id=1, source_target_pairs={{0,6},{1,7},{2,4},{3,5},{4,2},{5,3},{6,0},{7,1},{8,14},{9,15},{10,... | collective-permute-start | bytes 1327112 | tf_op jit(solution)/shard_map/ppermute | solution.py:136
  36.9 20.4 %collective-permute-start.10 = (bf16[32,6912]{1,0:T(8,128)(2,1)}, bf16[32,6912]{1,0:T(8,128)(2,1)S(1)}, u32[]{:S(2)}, u32[]{:S(2)}) collective-permute-start(bf16[32,6912]{1,0:T(8,128)(2,1)} %shard_map.243.refs_4_), channel_id=1, source_target_pairs={{0,1},{1,0},{2,3},{3,2},{4,5},{5,4},{6,7},{7,6},{8,9},{9,8},{10,11... | collective-permute-start | bytes 1327112 | tf_op jit(solution)/shard_map/ppermute | solution.py:136
  56.8 2.6 %collective-permute-start.15 = (bf16[32,6912]{1,0:T(8,128)(2,1)}, bf16[32,6912]{1,0:T(8,128)(2,1)S(1)}, u32[]{:S(2)}, u32[]{:S(2)}) collective-permute-start(bf16[32,6912]{1,0:T(8,128)(2,1)} %get-tuple-element.91.refs_8_), channel_id=1, source_target_pairs={{0,1},{1,0},{2,3},{3,2},{4,5},{5,4},{6,7},{7,6},{8,9},{9,8},{10,11... | collective-permute-start | bytes 1327112 | tf_op jit(solution)/shard_map/ppermute | solution.py:136
  57.3 2.8 %collective-permute-start.16 = (bf16[32,6912]{1,0:T(8,128)(2,1)}, bf16[32,6912]{1,0:T(8,128)(2,1)S(1)}, u32[]{:S(2)}, u32[]{:S(2)}) collective-permute-start(bf16[32,6912]{1,0:T(8,128)(2,1)} %get-tuple-element.92.refs_10_), channel_id=1, source_target_pairs={{0,1},{1,0},{2,3},{3,2},{4,5},{5,4},{6,7},{7,6},{8,9},{9,8},{10,11... | collective-permute-start | bytes 1327112 | tf_op jit(solution)/shard_map/ppermute | solution.py:136
  74.1 6.8 %collective-permute-start.21 = (bf16[144,512]{1,0:T(8,128)(2,1)S(1)}, bf16[144,512]{1,0:T(8,128)(2,1)S(1)}, u32[]{:S(2)}, u32[]{:S(2)}) collective-permute-start(bf16[144,512]{1,0:T(8,128)(2,1)S(1)} %add_convert_fusion.6.refs_11_.refs_1_), channel_id=1, source_target_pairs={{0,2},{1,3},{2,0},{3,1},{4,6},{5,7},{6,4},{7,5},{8,10},{9,11},{10,... | collective-permute-start | bytes 442376 | tf_op jit(solution)/shard_map/ppermute | solution.py:136
  75.2 7.3 %collective-permute-start.20 = (bf16[144,512]{1,0:T(8,128)(2,1)S(1)}, bf16[144,512]{1,0:T(8,128)(2,1)S(1)}, u32[]{:S(2)}, u32[]{:S(2)}) collective-permute-start(bf16[144,512]{1,0:T(8,128)(2,1)S(1)} %add_convert_fusion.6.refs_11_.refs_1_), channel_id=1, source_target_pairs={{0,4},{1,5},{2,6},{3,7},{4,0},{5,1},{6,2},{7,3},{8,12},{9,13},{10,... | collective-permute-start | bytes 442376 | tf_op jit(solution)/shard_map/ppermute | solution.py:136
  76.2 8.0 %collective-permute-start.19 = (bf16[144,512]{1,0:T(8,128)(2,1)S(1)}, bf16[144,512]{1,0:T(8,128)(2,1)S(1)}, u32[]{:S(2)}, u32[]{:S(2)}) collective-permute-start(bf16[144,512]{1,0:T(8,128)(2,1)S(1)} %add_convert_fusion.6.refs_11_.refs_1_), channel_id=1, source_target_pairs={{0,6},{1,7},{2,4},{3,5},{4,2},{5,3},{6,0},{7,1},{8,14},{9,15},{10,... | collective-permute-start | bytes 442376 | tf_op jit(solution)/shard_map/ppermute | solution.py:136
  77.6 9.5 %collective-permute-start.24 = (bf16[144,512]{1,0:T(8,128)(2,1)S(1)}, bf16[144,512]{1,0:T(8,128)(2,1)S(1)}, u32[]{:S(2)}, u32[]{:S(2)}) collective-permute-start(bf16[144,512]{1,0:T(8,128)(2,1)S(1)} %add_convert_fusion.6.refs_11_.refs_1_), channel_id=1, source_target_pairs={{0,1},{1,0},{2,3},{3,2},{4,5},{5,4},{6,7},{7,6},{8,9},{9,8},{10,11... | collective-permute-start | bytes 442376 | tf_op jit(solution)/shard_map/ppermute | solution.py:136
  80.8 6.3 %collective-permute-start.25 = (bf16[144,512]{1,0:T(8,128)(2,1)S(1)}, bf16[144,512]{1,0:T(8,128)(2,1)S(1)}, u32[]{:S(2)}, u32[]{:S(2)}) collective-permute-start(bf16[144,512]{1,0:T(8,128)(2,1)S(1)} %collective-permute-done.21.refs_3_.refs_13_), channel_id=1, source_target_pairs={{0,1},{1,0},{2,3},{3,2},{4,5},{5,4},{6,7},{7,6},{8,9},{9,8},{10,11... | collective-permute-start | bytes 442376 | tf_op jit(solution)/shard_map/ppermute | solution.py:136
  82.5 4.7 %collective-permute-start.26 = (bf16[144,512]{1,0:T(8,128)(2,1)S(1)}, bf16[144,512]{1,0:T(8,128)(2,1)S(1)}, u32[]{:S(2)}, u32[]{:S(2)}) collective-permute-start(bf16[144,512]{1,0:T(8,128)(2,1)S(1)} %collective-permute-done.20.refs_2_.refs_15_), channel_id=1, source_target_pairs={{0,1},{1,0},{2,3},{3,2},{4,5},{5,4},{6,7},{7,6},{8,9},{9,8},{10,11... | collective-permute-start | bytes 442376 | tf_op jit(solution)/shard_map/ppermute | solution.py:136
  84.2 3.1 %collective-permute-start.27 = (bf16[144,512]{1,0:T(8,128)(2,1)S(1)}, bf16[144,512]{1,0:T(8,128)(2,1)S(1)}, u32[]{:S(2)}, u32[]{:S(2)}) collective-permute-start(bf16[144,512]{1,0:T(8,128)(2,1)S(1)} %collective-permute-done.19.refs_1_.refs_17_), channel_id=1, source_target_pairs={{0,1},{1,0},{2,3},{3,2},{4,5},{5,4},{6,7},{7,6},{8,9},{9,8},{10,11... | collective-permute-start | bytes 442376 | tf_op jit(solution)/shard_map/ppermute | solution.py:136
  84.8 15.0 %collective-permute-start.23 = (bf16[144,512]{1,0:T(8,128)(2,1)}, bf16[144,512]{1,0:T(8,128)(2,1)S(1)}, u32[]{:S(2)}, u32[]{:S(2)}) collective-permute-start(bf16[144,512]{1,0:T(8,128)(2,1)} %shard_map.246.refs_0_), channel_id=1, source_target_pairs={{0,16},{8,24},{16,0},{24,8},{1,17},{9,25},{17,1},{25,9},{2,18},{10... | collective-permute-start | bytes 442376 | tf_op jit(solution)/shard_map/ppermute | solution.py:136
  87.2 13.8 %collective-permute-start.22 = (bf16[144,512]{1,0:T(8,128)(2,1)}, bf16[144,512]{1,0:T(8,128)(2,1)S(1)}, u32[]{:S(2)}, u32[]{:S(2)}) collective-permute-start(bf16[144,512]{1,0:T(8,128)(2,1)} %shard_map.246.refs_0_), channel_id=1, source_target_pairs={{0,8},{8,0},{16,24},{24,16},{1,9},{9,1},{17,25},{25,17},{2,10},{10... | collective-permute-start | bytes 442376 | tf_op jit(solution)/shard_map/ppermute | solution.py:136
  95.4 15.5 %collective-permute-start.42 = (bf16[16,4608]{1,0:T(8,128)(2,1)}, bf16[16,4608]{1,0:T(8,128)(2,1)S(1)}, u32[]{:S(2)}, u32[]{:S(2)}) collective-permute-start(bf16[16,4608]{1,0:T(8,128)(2,1)} %get-tuple-element.132), channel_id=1, source_target_pairs={{0,8},{8,0},{16,24},{24,16},{1,9},{9,1},{17,25},{25,17},{2,10},{10... | collective-permute-start | bytes 442376 | tf_op jit(solution)/shard_map/ppermute | solution.py:136
  97.4 15.9 %collective-permute-start.35 = (bf16[432,512]{1,0:T(8,128)(2,1)}, bf16[432,512]{1,0:T(8,128)(2,1)S(1)}, u32[]{:S(2)}, u32[]{:S(2)}) collective-permute-start(bf16[432,512]{1,0:T(8,128)(2,1)} %shard_map.251.refs_13_), channel_id=1, source_target_pairs={{0,2},{1,3},{2,0},{3,1},{4,6},{5,7},{6,4},{7,5},{8,10},{9,11},{10,... | collective-permute-start | bytes 1327112 | tf_op jit(solution)/shard_map/ppermute | solution.py:136
  98.3 24.8 %collective-permute-start.34 = (bf16[432,512]{1,0:T(8,128)(2,1)}, bf16[432,512]{1,0:T(8,128)(2,1)S(1)}, u32[]{:S(2)}, u32[]{:S(2)}) collective-permute-start(bf16[432,512]{1,0:T(8,128)(2,1)} %shard_map.251.refs_13_), channel_id=1, source_target_pairs={{0,4},{1,5},{2,6},{3,7},{4,0},{5,1},{6,2},{7,3},{8,12},{9,13},{10,... | collective-permute-start | bytes 1327112 | tf_op jit(solution)/shard_map/ppermute | solution.py:136
  99.8 23.3 %collective-permute-start.33 = (bf16[432,512]{1,0:T(8,128)(2,1)}, bf16[432,512]{1,0:T(8,128)(2,1)S(1)}, u32[]{:S(2)}, u32[]{:S(2)}) collective-permute-start(bf16[432,512]{1,0:T(8,128)(2,1)} %shard_map.251.refs_13_), channel_id=1, source_target_pairs={{0,6},{1,7},{2,4},{3,5},{4,2},{5,3},{6,0},{7,1},{8,14},{9,15},{10,... | collective-permute-start | bytes 1327112 | tf_op jit(solution)/shard_map/ppermute | solution.py:136
  100.9 23.0 %collective-permute-start.28 = (bf16[144,512]{1,0:T(8,128)(2,1)}, bf16[144,512]{1,0:T(8,128)(2,1)S(1)}, u32[]{:S(2)}, u32[]{:S(2)}) collective-permute-start(bf16[144,512]{1,0:T(8,128)(2,1)} %shard_map.248), channel_id=1, source_target_pairs={{0,24},{8,16},{16,8},{24,0},{1,25},{9,17},{17,9},{25,1},{2,26},{10... | collective-permute-start | bytes 442376 | tf_op jit(solution)/shard_map/ppermute | solution.py:136
  112.5 12.5 %collective-permute-start.43 = (bf16[16,4608]{1,0:T(8,128)(2,1)S(1)}, bf16[16,4608]{1,0:T(8,128)(2,1)S(1)}, u32[]{:S(2)}, u32[]{:S(2)}) collective-permute-start(bf16[16,4608]{1,0:T(8,128)(2,1)S(1)} %add_convert_fusion.1), channel_id=1, source_target_pairs={{0,16},{8,24},{16,0},{24,8},{1,17},{9,25},{17,1},{25,9},{2,18},{10... | collective-permute-start | bytes 442376 | tf_op jit(solution)/shard_map/ppermute | solution.py:136
  113.4 11.3 %collective-permute-start.44 = (bf16[16,3328]{1,0:T(8,128)(2,1)}, bf16[16,3328]{1,0:T(8,128)(2,1)S(1)}, u32[]{:S(2)}, u32[]{:S(2)}) collective-permute-start(bf16[16,3328]{1,0:T(8,128)(2,1)} %get-tuple-element.133), channel_id=1, source_target_pairs={{0,8},{8,0},{16,24},{24,16},{1,9},{9,1},{17,25},{25,17},{2,10},{10... | collective-permute-start | bytes 319496 | tf_op jit(solution)/shard_map/ppermute | solution.py:136
  123.0 26.3 %collective-permute-start.17 = (bf16[4,144,512]{2,1,0:T(8,128)(2,1)}, bf16[4,144,512]{2,1,0:T(8,128)(2,1)S(1)}, u32[]{:S(2)}, u32[]{:S(2)}) collective-permute-start(bf16[4,144,512]{2,1,0:T(8,128)(2,1)} %get-tuple-element.94), channel_id=1, source_target_pairs={{0,1},{1,0},{2,3},{3,2},{4,5},{5,4},{6,7},{7,6},{8,9},{9,8},{10,11... | collective-permute-start | bytes 1769480 | tf_op jit(solution)/shard_map/ppermute | solution.py:136
  123.2 3.5 %collective-permute-start.32 = (bf16[432,512]{1,0:T(8,128)(2,1)S(1)}, bf16[432,512]{1,0:T(8,128)(2,1)S(1)}, u32[]{:S(2)}, u32[]{:S(2)}) collective-permute-start(bf16[432,512]{1,0:T(8,128)(2,1)S(1)} %copy-done), channel_id=1, source_target_pairs={{0,1},{1,0},{2,3},{3,2},{4,5},{5,4},{6,7},{7,6},{8,9},{9,8},{10,11... | collective-permute-start | bytes 1327112 | tf_op jit(solution)/shard_map/ppermute | solution.py:136
  124.0 6.4 %collective-permute-start.36 = (bf16[432,512]{1,0:T(8,128)(2,1)}, bf16[432,512]{1,0:T(8,128)(2,1)}, u32[]{:S(2)}, u32[]{:S(2)}) collective-permute-start(bf16[432,512]{1,0:T(8,128)(2,1)} %get-tuple-element.122.refs_15_), channel_id=1, source_target_pairs={{0,1},{1,0},{2,3},{3,2},{4,5},{5,4},{6,7},{7,6},{8,9},{9,8},{10,11... | collective-permute-start | bytes 1327112 | tf_op jit(solution)/shard_map/ppermute | solution.py:136
  124.6 2.2 %collective-permute-start.29 = (bf16[144,512]{1,0:T(8,128)(2,1)}, bf16[144,512]{1,0:T(8,128)(2,1)S(1)}, u32[]{:S(2)}, u32[]{:S(2)}) collective-permute-start(bf16[144,512]{1,0:T(8,128)(2,1)} %get-tuple-element.117.refs_4_), channel_id=1, source_target_pairs={{0,1},{1,0},{2,3},{3,2},{4,5},{5,4},{6,7},{7,6},{8,9},{9,8},{10,11... | collective-permute-start | bytes 442376 | tf_op jit(solution)/shard_map/ppermute | solution.py:136
  126.7 4.4 %collective-permute-start.37 = (bf16[432,512]{1,0:T(8,128)(2,1)}, bf16[432,512]{1,0:T(8,128)(2,1)S(1)}, u32[]{:S(2)}, u32[]{:S(2)}) collective-permute-start(bf16[432,512]{1,0:T(8,128)(2,1)} %get-tuple-element.123.refs_17_), channel_id=1, source_target_pairs={{0,1},{1,0},{2,3},{3,2},{4,5},{5,4},{6,7},{7,6},{8,9},{9,8},{10,11... | collective-permute-start | bytes 1327112 | tf_op jit(solution)/shard_map/ppermute | solution.py:136
  126.9 7.2 %collective-permute-start.38 = (bf16[432,512]{1,0:T(8,128)(2,1)}, bf16[432,512]{1,0:T(8,128)(2,1)S(1)}, u32[]{:S(2)}, u32[]{:S(2)}) collective-permute-start(bf16[432,512]{1,0:T(8,128)(2,1)} %get-tuple-element.124.refs_19_), channel_id=1, source_target_pairs={{0,1},{1,0},{2,3},{3,2},{4,5},{5,4},{6,7},{7,6},{8,9},{9,8},{10,11... | collective-permute-start | bytes 1327112 | tf_op jit(solution)/shard_map/ppermute | solution.py:136
  127.3 2.3 %collective-permute-start.31 = (bf16[144,512]{1,0:T(8,128)(2,1)}, bf16[144,512]{1,0:T(8,128)(2,1)S(1)}, u32[]{:S(2)}, u32[]{:S(2)}) collective-permute-start(bf16[144,512]{1,0:T(8,128)(2,1)} %get-tuple-element.119.refs_6_), channel_id=1, source_target_pairs={{0,1},{1,0},{2,3},{3,2},{4,5},{5,4},{6,7},{7,6},{8,9},{9,8},{10,11... | collective-permute-start | bytes 442376 | tf_op jit(solution)/shard_map/ppermute | solution.py:136
  129.6 22.7 %collective-permute-start.50 = (bf16[32,1280]{1,0:T(8,128)(2,1)S(1)}, bf16[32,1280]{1,0:T(8,128)(2,1)S(1)}, u32[]{:S(2)}, u32[]{:S(2)}) collective-permute-start(bf16[32,1280]{1,0:T(8,128)(2,1)S(1)} %copy-done.54), channel_id=1, source_target_pairs={{0,24},{8,16},{16,8},{24,0},{1,25},{9,17},{17,9},{25,1},{2,26},{10... | collective-permute-start | bytes 245768 | tf_op jit(solution)/shard_map/ppermute | solution.py:136
  130.4 23.5 %collective-permute-start.49 = (bf16[32,1280]{1,0:T(8,128)(2,1)S(1)}, bf16[32,1280]{1,0:T(8,128)(2,1)S(1)}, u32[]{:S(2)}, u32[]{:S(2)}) collective-permute-start(bf16[32,1280]{1,0:T(8,128)(2,1)S(1)} %copy-done.54), channel_id=1, source_target_pairs={{0,16},{8,24},{16,0},{24,8},{1,17},{9,25},{17,1},{25,9},{2,18},{10... | collective-permute-start | bytes 245768 | tf_op jit(solution)/shard_map/ppermute | solution.py:136
  131.1 24.8 %collective-permute-start.48 = (bf16[32,1280]{1,0:T(8,128)(2,1)S(1)}, bf16[32,1280]{1,0:T(8,128)(2,1)S(1)}, u32[]{:S(2)}, u32[]{:S(2)}) collective-permute-start(bf16[32,1280]{1,0:T(8,128)(2,1)S(1)} %copy-done.54), channel_id=1, source_target_pairs={{0,8},{8,0},{16,24},{24,16},{1,9},{9,1},{17,25},{25,17},{2,10},{10... | collective-permute-start | bytes 245768 | tf_op jit(solution)/shard_map/ppermute | solution.py:136
  134.0 17.3 %collective-permute-start.46 = (bf16[16,3328]{1,0:T(8,128)(2,1)S(1)}, bf16[16,3328]{1,0:T(8,128)(2,1)S(1)}, u32[]{:S(2)}, u32[]{:S(2)}) collective-permute-start(bf16[16,3328]{1,0:T(8,128)(2,1)S(1)} %add_convert_fusion.8), channel_id=1, source_target_pairs={{0,16},{8,24},{16,0},{24,8},{1,17},{9,25},{17,1},{25,9},{2,18},{10... | collective-permute-start | bytes 319496 | tf_op jit(solution)/shard_map/ppermute | solution.py:136
  149.4 8.0 %collective-permute-start.45 = (bf16[16,4608]{1,0:T(8,128)(2,1)S(1)}, bf16[16,4608]{1,0:T(8,128)(2,1)S(1)}, u32[]{:S(2)}, u32[]{:S(2)}) collective-permute-start(bf16[16,4608]{1,0:T(8,128)(2,1)S(1)} %add_convert_fusion.refs_1_), channel_id=1, source_target_pairs={{0,8},{8,0},{16,24},{24,16},{1,9},{9,1},{17,25},{25,17},{2,10},{10... | collective-permute-start | bytes 442376 | tf_op jit(solution)/shard_map/ppermute | solution.py:136
  151.4 13.1 %collective-permute-start.39 = (bf16[144,512]{1,0:T(8,128)(2,1)S(1)}, bf16[144,512]{1,0:T(8,128)(2,1)S(1)}, u32[]{:S(2)}, u32[]{:S(2)}) collective-permute-start(bf16[144,512]{1,0:T(8,128)(2,1)S(1)} %get-tuple-element.149), channel_id=1, source_target_pairs={{0,2},{1,3},{2,0},{3,1},{4,6},{5,7},{6,4},{7,5},{8,10},{9,11},{10,... | collective-permute-start | bytes 442376 | tf_op jit(solution)/shard_map/ppermute | solution.py:136
  152.3 12.2 %collective-permute-start.41 = (bf16[144,512]{1,0:T(8,128)(2,1)S(1)}, bf16[144,512]{1,0:T(8,128)(2,1)S(1)}, u32[]{:S(2)}, u32[]{:S(2)}) collective-permute-start(bf16[144,512]{1,0:T(8,128)(2,1)S(1)} %get-tuple-element.150), channel_id=1, source_target_pairs={{0,6},{1,7},{2,4},{3,5},{4,2},{5,3},{6,0},{7,1},{8,14},{9,15},{10,... | collective-permute-start | bytes 442376 | tf_op jit(solution)/shard_map/ppermute | solution.py:136
  153.9 10.6 %collective-permute-start.40 = (bf16[144,512]{1,0:T(8,128)(2,1)S(1)}, bf16[144,512]{1,0:T(8,128)(2,1)S(1)}, u32[]{:S(2)}, u32[]{:S(2)}) collective-permute-start(bf16[144,512]{1,0:T(8,128)(2,1)S(1)} %get-tuple-element.151), channel_id=1, source_target_pairs={{0,4},{1,5},{2,6},{3,7},{4,0},{5,1},{6,2},{7,3},{8,12},{9,13},{10,... | collective-permute-start | bytes 442376 | tf_op jit(solution)/shard_map/ppermute | solution.py:136
  156.0 4.8 %collective-permute-start.47 = (bf16[16,3328]{1,0:T(8,128)(2,1)S(1)}, bf16[16,3328]{1,0:T(8,128)(2,1)S(1)}, u32[]{:S(2)}, u32[]{:S(2)}) collective-permute-start(bf16[16,3328]{1,0:T(8,128)(2,1)S(1)} %add_convert_fusion.7.refs_3_), channel_id=1, source_target_pairs={{0,8},{8,0},{16,24},{24,16},{1,9},{9,1},{17,25},{25,17},{2,10},{10... | collective-permute-start | bytes 319496 | tf_op jit(solution)/shard_map/ppermute | solution.py:136
  (58 other events, 234.5 us)

commit v4 on v3

--- a/solution.py
+++ b/solution.py
@@ -101,7 +101,7 @@
         out_specs=[ANY] * len(outs),
         scratch_shapes=shapes + sems + list(scratch),
         compiler_params=pltpu.CompilerParams(vmem_limit_bytes=vmem << 20),
-        cost_estimate=pl.CostEstimate(flops=flops, bytes_accessed=moved, transcendentals=0),
+        cost_estimate=pl.CostEstimate(flops=0, bytes_accessed=0, transcendentals=0),
     )(*scalars, *args, *plain, *after)
 
 
@@ -162,6 +162,15 @@
         total = (total.astype(F32) + got.astype(F32)).astype(BF16)
         got = ppermute_xor(total, "img", mask)
     return total, got
+
+
+def doubled(parts, held):
+    planes = lax.axis_size("img")
+    for mask in (1 << k for k in range(1, planes.bit_length() - 1)):
+        parts.append(ppermute_xor(held, "img", mask))
+        if 2 * mask < planes:
+            held = join(held, parts[-1])
+    return parts
 
 
 def summed(left, right):
@@ -269,20 +278,23 @@
     chan, mid = out_ref.shape[1], w_ref.shape[0]
     reduce_end, conv_end, expand_end, mid_end, end = columns(chan, mid)
     width = stage.shape[2]
-    copies, weights = [], []
+    parts, copies = [], []
     for r, piece in enumerate(pieces):
-        copies.append(
-            pltpu.make_async_copy(piece.at[:, expand_end : expand_end + width], stage.at[r], sems.at[0, r])
+        parts.append(
+            pltpu.make_async_copy(piece.at[:, expand_end : expand_end + width], stage.at[r], sems.at[2, r])
         )
-        copies[-1].start()
-    for r, piece in enumerate(pieces):
-        rows = pl.ds(pl.multiple_of((me ^ r) * held, held), held)
-        weights.append(pltpu.make_async_copy(piece.at[:, 0:expand_end], w_ref.at[rows, :], sems.at[1, r]))
-        weights[-1].start()
+        parts[-1].start()
+    for k, (start, stop) in enumerate(((0, reduce_end), (reduce_end, expand_end))):
+        for r, piece in enumerate(pieces):
+            rows = pl.ds(pl.multiple_of((me ^ r) * held, held), held)
+            copies.append(
+                pltpu.make_async_copy(piece.at[:, start:stop], w_ref.at[rows, start:stop], sems.at[k, r])
+            )
+            copies[-1].start()
     for copy in then:
         copy.start()
     for r in range(len(pieces)):
-        copies[r].wait()
+        parts[r].wait()
         rows = pl.ds(pl.multiple_of((me ^ r) * held, held), held)
         lanes = pl.ds(pl.multiple_of((me ^ r) * LANES, LANES), LANES)
         scr[rows, :] = stage[r, :, 0:LANES].astype(F32)
@@ -295,8 +307,19 @@
     flat = scr[...].T
     for q in range(4):
         mid_ref[q : q + 1, :] = flat[2 * q : 2 * q + 1, :] + flat[2 * q + 1 : 2 * q + 2, :]
-    for copy in weights:
-        copy.wait()
+
+    def wait(some):
+        def waiting():
+            for copy in some:
+                copy.wait()
+
+        return waiting
+
+    return wait(copies[: len(pieces)]), wait(copies[len(pieces) :])
+
+
+def at_once():
+    pass
 
 
 def sigmoid(value):
@@ -346,13 +369,14 @@
     return field[step + 1, at : at + slots, :].astype(BF16)
 
 
-def forward_body(side, aux, x_ref, w_ref, mid_ref, out_ref, keep, field, act, finish):
+def forward_body(side, aux, x_ref, w_ref, mid_ref, out_ref, keep, field, act, finish, ready=(at_once, at_once)):
     u1, u2, u3, fac, pat = [item() for item in keep]
     slots = x_ref.shape[0]
     chan, mid = out_ref.shape[1], w_ref.shape[0]
     reduce_end, conv_end, expand_end, _, _ = columns(chan, mid)
     pad = pad_of(side)
     clear_edges(field, side, slots)
+    ready[0]()
     u1[...] = dot_nt(x_ref[...], w_ref[:, 0:reduce_end])
 
     def first(rows, start, carry):
@@ -369,6 +393,7 @@
     for j, (rise, step) in enumerate(OFFSETS):
         pat[:, j * mid : (j + 1) * mid] = tap(field, side, slots, rise, step)
     keep[4].send()
+    ready[1]()
     u2[...] = dot_nt(pat[...], w_ref[:, reduce_end:conv_end])
 
     def second(rows, start, carry):
@@ -401,15 +426,21 @@
     aux = ins.pop(0)()
     if pooling:
         spread, finish = ins.pop(0), rest.pop(0)
+    ready, made = (at_once, at_once), []
     if assembled:
         sources = [item() for item in ins]
     else:
-        sources, outs = [item() for item in outs[:4]], outs[4:]
-        assemble(scalars[0][0], plain, *sources, *rest)
+        made, outs = outs[:4], outs[4:]
+        sources = [item() for item in made]
+        ready = assemble(scalars[0][0], plain, *sources, *rest)
     result = outs[0]
     if not pooling:
         finish = result()
-    forward_body(side, aux, *sources, outs[1:], field, act, finish)
+    if made:
+        made[0].send()
+    forward_body(side, aux, *sources, outs[1:], field, act, finish, ready)
+    for item in made:
+        item.send()
     if pooling:
         result()[...] = dot_nn(spread()[...], finish[...]).astype(BF16)
 
@@ -441,7 +472,7 @@
     return [
         pltpu.VMEM((len(pieces), held, 2 * LANES + extra), BF16),
         pltpu.VMEM((mid, LANES), F32),
-        pltpu.SemaphoreType.DMA((2, len(pieces))),
+        pltpu.SemaphoreType.DMA((3, len(pieces))),
     ]
 
 
@@ -584,9 +615,10 @@
 
 
 def late_kernel(side, scalars, ins, outs, plain, up, grads, sg, eg, turned, field, dense, accum):
-    aux, x_in, w_in, mid_in, out_in, u1_in, u2_in, u3_in, fac_in, pat_in, *pieces = ins
+    pieces = ins[:-10]
+    aux, x_in, out_in, u3_in, fac_in, mid_in, u2_in, w_in, pat_in, u1_in = ins[-10:]
     x_grad, mine, theirs, out_rows = outs
-    me, plane = scalars[0][0], scalars[0][1] & 1
+    me, plane = scalars[0][0], scalars[1][0] & 1
     half = pieces[0].buffer.shape[1]
     for odd in range(2):
         core = (me & 1) ^ odd
@@ -609,9 +641,10 @@
     x_grad()[...] = (dot_nn(dense[...].astype(BF16), w_in()[:, 0:reduce_end]) + sg[...]).astype(BF16)
 
 
-def late_backward(side, held, me, aux, pieces, saved):
-    slots, chan = saved[0].shape
-    mid = saved[1].shape[0]
+def late_backward(side, held, me, plane, aux, pieces, saved):
+    x, w, mids, outs, u1, u2, u3, fac, pat = saved
+    slots, chan = x.shape
+    mid = w.shape[0]
     end = columns(chan, mid)[-1]
     return call(
         functools.partial(late_kernel, side),
@@ -621,8 +654,8 @@
             sds((held // 2, end), BF16),
             sds((8, chan), F32),
         ],
-        [me],
-        [aux, *saved, *pieces],
+        [me, plane],
+        [*pieces, aux, x, outs, u3, fac, mids, u2, w, pat, u1],
         [pltpu.VMEM((slots, chan), F32), pltpu.VMEM((held, end), F32)] + back_scratch(side, slots, chan, mid),
         flops=3 * slots * mid * (2 * chan + TAPS * mid),
         moved=40 * slots * chan,
@@ -632,7 +665,7 @@
 def upper_kernel(side, own_lanes, scalars, ins, outs, plain, up, grads, sg, eg, turned, field, dense, accum):
     aux, spread, pooled_grad, x_in, out_in, u3_in, fac_in, mid_in, u2_in, w_in, pat_in = ins
     mine, theirs, conv_grad, sg_own, accum_out, out_rows = outs
-    me, plane = scalars[0][0], scalars[0][1] & 1
+    me, plane = scalars[0][0], scalars[1][0] & 1
     slots = eg.shape[0]
     up[...] = dot_tn(spread()[...], pooled_grad()[...])
     aux, x_ref, out_ref, u3, fac = aux(), x_in(), out_in(), u3_in(), fac_in()
@@ -651,7 +684,7 @@
         sg_own()[...] = sg[...]
 
 
-def upper_backward(side, held, me, aux, spread, pooled_grad, saved, own_lanes):
+def upper_backward(side, held, me, plane, aux, spread, pooled_grad, saved, own_lanes):
     x, w, mids, outs, u1, u2, u3, fac, pat = saved
     slots, chan = x.shape
     mid = w.shape[0]
@@ -666,7 +699,7 @@
             sds((8, mid), F32),
             sds((8, chan), F32),
         ],
-        [me],
+        [me, plane],
         [aux, spread, pooled_grad, x, outs, u3, fac, mids, u2, w, pat],
         [pltpu.VMEM((slots, chan), F32), pltpu.VMEM((held, end), F32)] + back_scratch(side, slots, chan, mid),
         flops=2 * slots * mid * (2 * chan + TAPS * mid),
@@ -800,14 +833,12 @@
 
 
 def second_kernel(side, count, scalars, ins, outs, plain, field, act, stage, scr, sems, full, hid, w1_buf, w2_buf, wsems):
-    aux, x, b1 = [item() for item in ins]
     pieces, (w1, w2) = plain[:count], plain[count:]
     w1, w2 = Later(w1, w1_buf, wsems.at[0]), Later(w2, w2_buf, wsems.at[1])
     me = scalars[0][0]
     sources = [item() for item in outs[:3]]
-    assemble(me, pieces, None, *sources, stage, scr, sems, (w1, w2))
-    for item in outs[:3]:
-        item.send()
+    ready = assemble(me, pieces, None, *sources, stage, scr, sems, (w1, w2))
+    aux, x, b1 = [item() for item in ins]
     readin, keep, rest, cot_out = outs[3], outs[4:9], outs[9:15], outs[15]
     cot = cot_out()
     share = cot.shape[1] // count
@@ -819,8 +850,10 @@
             low_lane = 2 * LANES + low_lane
             cot[row : row + 16, lanes] = stage[r, low_row : low_row + 16, low_lane : low_lane + LANES]
     cot_out.send()
-    forward_body(side, aux, x, *sources, keep, field, act, readin())
+    forward_body(side, aux, x, *sources, keep, field, act, readin(), ready)
     readin.send()
+    for item in outs[:3]:
+        item.send()
     readout_body(me, readin(), w1, b1, w2, cot_out, [hid, *rest], full)
 
 
@@ -853,8 +886,8 @@
     return got[3], [x] + got[:3] + got[4:9], got[9:]
 
 
-def tail_kernel(placed, scalars, ins, outs, plain, stacked, low, cot, w2_buf, buffer, sems, out_sems):
-    readin, w1, b1, *parts, grad = ins
+def tail_kernel(placed, count, scalars, ins, outs, plain, stacked, low, cot, w2_buf, buffer, sems, out_sems):
+    parts, (readin, w1, b1, grad) = ins[:count], ins[count:]
     w1_grad, b1_grad, b2_grad, w2_out = outs
     me = scalars[0][0]
     rows = readin.buffer.shape[0]
@@ -910,10 +943,10 @@
     hidden, width = w2.shape
     chunk = min(width, 1024)
     return call(
-        functools.partial(tail_kernel, placed),
+        functools.partial(tail_kernel, placed, len(parts)),
         [sds((chan, hidden), F32), sds((1, hidden), F32), sds((1, width // n), F32), sds((hidden, width), F32)],
         [me],
-        [readin, w1, b1, *parts, grad],
+        [*parts, readin, w1, b1, grad],
         [
             pltpu.VMEM((total, chan), BF16),
             pltpu.VMEM((total, hidden), BF16),
@@ -936,7 +969,7 @@
     chan, mid = red.shape[2], conv.shape[3]
     held = red.shape[1]
     reduce_end, conv_end, expand_end, mid_end, end = columns(chan, mid)
-    plane = scalars[0][1] & 1
+    plane = scalars[1][0] & 1
     few = held // 2
 
     def from_pair(pair, base, k):
@@ -969,7 +1002,7 @@
         out_bias[k : k + 1, :] = scr[k, 1:2, LANES : LANES + out_bias.shape[1]]
 
 
-def finish(me, late, middle, parts, chan, mid, share):
+def finish(me, plane, late, middle, parts, chan, mid, share):
     held = parts[0].shape[0]
     outs = [
         sds((2, held, chan), F32),
@@ -983,7 +1016,7 @@
     return call(
         functools.partial(finish_kernel, len(parts)),
         outs,
-        [me],
+        [me, plane],
         [*late, *middle, *parts],
         [pltpu.VMEM((2, LANES, 2 * LANES), F32)],
         flops=8 * held * chan,
@@ -1059,7 +1092,8 @@
     aligned = share == LANES and held % 16 == 0
     index = lax.axis_index("ch").astype(jnp.int32)
     planes = lax.axis_size("img")
-    me = jnp.stack([index, lax.axis_index("img").astype(jnp.int32)])
+    me = index[None]
+    plane = lax.axis_index("img").astype(jnp.int32)[None]
 
     feat = jnp.transpose(features[:, 0, :])
     cot = jnp.transpose(cotangent[:, 0, :])
@@ -1076,15 +1110,19 @@
         far = neighbours(first_packet)
         second_packet, cot = pack(1, cot, red, conv, expand_w, *norms, after=[first_packet])
 
-    cot_rest = join(*along_images(cot))
+        (second_packet,) = gate([second_packet], far[2])
+
+    cot_rest = [ppermute_xor(cot, "img", 1)]
+    held_cot = join(cot, cot_rest[0])
 
     if aligned:
-        far = dict(zip(far, gate(list(far.values()), second_packet, cot_rest, spread)))
+        second_far = neighbours(second_packet)
+        far = dict(zip(far, gate(list(far.values()), held_cot, spread)))
+        (held_cot,) = gate([held_cot], *far.values())
+        cot_rest = doubled(cot_rest, held_cot)
         first_pieces = with_cores(first_packet, far)
-        (second_packet,) = gate([second_packet], *far.values())
-        far = neighbours(second_packet)
         pooled, saved_first = block_forward(GRID, chan, mid, me, slot_facts, spread, first_pieces, None)
-        far = dict(zip(far, gate(list(far.values()), pooled)))
+        far = dict(zip(second_far, gate(list(second_far.values()), pooled, *cot_rest)))
         second_pieces = with_cores(second_packet, far)
         readin, saved_second, got = second_forward(
             POOLED, chan, mid, me, few_facts, pooled, second_pieces, read_w1, bias_one, read_w2
@@ -1109,24 +1147,28 @@
         cot_own = lax.all_gather(cot, "ch", axis=1, tiled=True)
         mine, theirs, own_grad, half_in, keep, send = readout(me, readin, read_w1, bias_one, read_w2, cot_own, n)
 
+    if not aligned:
+        cot_rest = doubled(cot_rest, held_cot)
     half = summed(mine, ppermute_xor(theirs, "ch", 1))
     far = neighbours(half)
+    cot_rest = join(*cot_rest, after=[half])
+    far = dict(zip(far, gate(list(far.values()), cot_rest)))
     if aligned:
-        (cot_rest,) = gate([cot_rest], half)
-        cot_far = neighbours(cot_rest)
+        (cot_far,) = gate([cot_rest], *far.values())
+        cot_far = neighbours(cot_far)
     grad_pieces = with_cores(half, far)
-    (half_in,) = gate([half_in], *far.values())
+    (half_in,) = gate([half_in], half)
     parts = [ppermute_xor(half_in, "img", m) for m in (1, 2) if m < planes]
 
     pooled_grad, late_mine, late_theirs, late_out = late_backward(
-        POOLED, held, me, few_facts, grad_pieces, saved_second
+        POOLED, held, me, plane, few_facts, grad_pieces, saved_second
     )
     late_got = ppermute_xor(late_theirs, "img", 1)
     (half_in,) = gate([half_in], pooled_grad)
     parts += [ppermute_xor(half_in, "img", m) for m in range(3, planes)]
     own_lanes = share if aligned else 0
     middle_mine, middle_theirs, *upper = upper_backward(
-        GRID, held, me, slot_facts, spread, pooled_grad, saved_first, own_lanes
+        GRID, held, me, plane, slot_facts, spread, pooled_grad, saved_first, own_lanes
     )
     middle_got = ppermute_xor(middle_theirs, "img", 1)
     (late_got,) = gate([late_got], upper[0])
@@ -1162,13 +1204,14 @@
     got = ppermute_xor(send, "ch", 1)
     (got,) = gate([got], b1_grad)
     shares = [summed(keep[q], got[q]) for q in range(n // 2)]
+    shares = gate(shares, middle_half)
     tokens = shares[0].astype(F32)
     for q in range(1, n // 2):
         tokens = tokens + ppermute_xor(shares[q], "ch", 2 * q).astype(F32)
     tokens = (tokens + read_b2[None, :]).astype(BF16)
 
     red_grad, conv_grad, exp_grad, mid_gain_grad, mid_bias_grad, out_gain_grad, out_bias_grad = finish(
-        me, late, middle, last, chan, mid, share
+        me, plane, late, middle, last, chan, mid, share
     )
     if not aligned:
         feat_grad = lax.dynamic_slice_in_dim(feat_grad, index * share, share, 1)

time: 167 us -> 158 us (0.946)
  Pallas kernels: 69.3 us -> 63.5 us
  starting transfers between devices: 47.5 us -> 42.9 us
    pallas_call x11 -> x12, Pallas kernels: 69.3 us -> 63.4 us  [call(): pl.pallas_call(kernel, out_shape=list(outs), in_specs=[SMEM] * len(scalar...]
    ppermute x51 -> x50, starting transfers between devices: 47.5 us -> 42.9 us  [ppermute_xor(): lax.ppermute(x, axis, [(i, i ^ mask) for i in range(lax.axis_size(axis))])]
    unnamed x110 -> x105, local copies, waits for them, and re-layouts: 9.19 us -> 9.98 us
    ppermute x51 -> x50, waiting for transfers between devices: 30.1 us -> 30.2 us  [ppermute_xor(): lax.ppermute(x, axis, [(i, i ^ mask) for i in range(lax.axis_size(axis))])]
  transfers between devices with their start and end apart: 51 -> 50, of which waited for: 12 -> 12; matrix products, arithmetic and copies ran while one was open for 3% -> 5% of each run, Pallas kernels for 34% -> 33%
where the time goes in v4:
time: 158 us; the launch traced here: 157 us
  Pallas kernels  63.5 us (40%)
  starting transfers between devices  42.9 us (27%)
  waiting for transfers between devices  30.2 us (19%)
  local copies, waits for them, and re-layouts  9.98 us (6%)
  other arithmetic  9.05 us (6%)
  between operations  1.83 us (1%)
    pallas_call x12, Pallas kernels, call(): pl.pallas_call(kernel, out_shape=list(outs), in_specs=[SMEM] * len(scalar...  63.4 us
    ppermute x50, starting transfers between devices, ppermute_xor(): lax.ppermute(x, axis, [(i, i ^ mask) for i in range(lax.axis_size(axis))])  42.9 us
    ppermute x50, waiting for transfers between devices, ppermute_xor(): lax.ppermute(x, axis, [(i, i ^ mask) for i in range(lax.axis_size(axis))])  30.2 us
    unnamed x105, local copies, waits for them, and re-layouts  9.98 us
    convert_element_type x6, other arithmetic, summed(): return (left.astype(F32) + right.astype(F32)).astype(BF16)  7.39 us
  transfers between devices with their start and end apart: 50, of which 12 were waited for; matrix products, arithmetic and copies ran while one was open for 5% of the time, Pallas kernels for 33%

profile of v4, /device:TPU:0, one launch (start us, length us, event | category | flops | bytes accessed | tf_op | source)
XLA Modules:
  0.0 157.4 jit_solution(7102565347974175933)
XLA Ops:
  0.6 1.9 %shard_map.238.refs_8_.refs_3_ = bf16[32,6912]{1,0:T(8,128)(2,1)} custom-call(bf16[576,128]{1,0:T(8,128)(2,1)} %bitcast.34, f32[2,2,32]{2,1,0:T(2,128)} %refs_1_.3, f32[2,2,32]{2,1,0:T(2,128)} %refs_2_.3, f32[2,128]{1,0:T(2,128)} %refs_3_.3, f32[2,128]{1,0:T(2,128)} %refs_4_.3, bf16[2,32,1024]{2,1,0:T(8,128)(2,1)} %bitcast.32, ...), custom_call_target="tpu_custom_call" | custom-call | tf_op jit(solution)/shard_map/pallas_call | solution.py:97
  2.6 3.0 %collective-permute-start.3 = (bf16[32,6912]{1,0:T(8,128)(2,1)}, bf16[32,6912]{1,0:T(8,128)(2,1)S(1)}, u32[]{:S(2)}, u32[]{:S(2)}) collective-permute-start(bf16[32,6912]{1,0:T(8,128)(2,1)} %shard_map.238.refs_8_.refs_3_), channel_id=1, source_target_pairs={{0,2},{1,3},{2,0},{3,1},{4,6},{5,7},{6,4},{7,5},{8,10},{9,11},{10,... | collective-permute-start | bytes 1327112 | tf_op jit(solution)/shard_map/ppermute | solution.py:136
  5.6 1.5 collective-permute-start.2
  7.1 2.0 %shard_map.239 = (bf16[32,6912]{1,0:T(8,128)(2,1)}, bf16[144,512]{1,0:T(8,128)(2,1)}) custom-call(bf16[144,512]{1,0:T(8,128)(2,1)} %bitcast.35, f32[2,2,32]{2,1,0:T(2,128)} %refs_1_.3, f32[2,2,32]{2,1,0:T(2,128)} %refs_2_.3, f32[2,128]{1,0:T(2,128)} %refs_3_.3, f32[2,128]{1,0:T(2,128)} %refs_4_.3, bf16[2,32,1024]{2,1,0:T(8,128)(2,1)} %bitcast.33, ...), custom_call_target="tpu_custom_call" | custom-call | tf_op jit(solution)/shard_map/pallas_call | solution.py:97
  9.1 2.1 %collective-permute-start.4 = (bf16[144,512]{1,0:T(8,128)(2,1)}, bf16[144,512]{1,0:T(8,128)(2,1)S(1)}, u32[]{:S(2)}, u32[]{:S(2)}) collective-permute-start(bf16[144,512]{1,0:T(8,128)(2,1)} %get-tuple-element.91.refs_0_), channel_id=1, source_target_pairs={{0,8},{8,0},{16,24},{24,16},{1,9},{9,1},{17,25},{25,17},{2,10},{10... | collective-permute-start | bytes 442376 | tf_op jit(solution)/shard_map/ppermute | solution.py:136
  11.9 1.1 shard_map.237
  13.0 1.6 %collective-permute-done.4.refs_1_.refs_4_.refs_0_ = bf16[144,512]{1,0:T(8,128)(2,1)S(1)} collective-permute-done((bf16[144,512]{1,0:T(8,128)(2,1)}, bf16[144,512]{1,0:T(8,128)(2,1)S(1)}, u32[]{:S(2)}, u32[]{:S(2)}) %collective-permute-start.4) | collective-permute-done | bytes 147488 | tf_op jit(solution)/shard_map/ppermute | solution.py:136
  15.2 1.7 %shard_map.240.refs_3_.refs_0_ = bf16[288,512]{1,0:T(8,128)(2,1)} custom-call(bf16[144,512]{1,0:T(8,128)(2,1)} %get-tuple-element.91.refs_0_, bf16[144,512]{1,0:T(8,128)(2,1)} %copy-done.16), custom_call_target="tpu_custom_call" | custom-call | tf_op jit(solution)/shard_map/pallas_call | solution.py:97
  17.8 9.1 %collective-permute-done.2.refs_1_ = bf16[32,6912]{1,0:T(8,128)(2,1)S(1)} collective-permute-done((bf16[32,6912]{1,0:T(8,128)(2,1)}, bf16[32,6912]{1,0:T(8,128)(2,1)S(1)}, u32[]{:S(2)}, u32[]{:S(2)}) %collective-permute-start.2) | collective-permute-done | bytes 442400 | tf_op jit(solution)/shard_map/ppermute | solution.py:136
  28.4 1.0 collective-permute-start.11
  29.5 1.0 collective-permute-start.10
  30.5 1.4 collective-permute-start.9
  32.0 2.6 %collective-permute-start.12 = (bf16[288,512]{1,0:T(8,128)(2,1)}, bf16[288,512]{1,0:T(8,128)(2,1)S(1)}, u32[]{:S(2)}, u32[]{:S(2)}) collective-permute-start(bf16[288,512]{1,0:T(8,128)(2,1)} %shard_map.244), channel_id=1, source_target_pairs={{0,16},{8,24},{16,0},{24,8},{1,17},{9,25},{17,1},{25,9},{2,18},{10... | collective-permute-start | bytes 884744 | tf_op jit(solution)/shard_map/ppermute | solution.py:136
  34.6 9.6 %shard_map.242 = (bf16[576,1024]{1,0:T(8,128)(2,1)}, bf16[256,4352]{1,0:T(8,128)(2,1)}, f32[8,256]{1,0:T(8,128)}, f32[8,1024]{1,0:T(8,128)}, bf16[144,1024]{1,0:...) custom-call(s32[1]{0:T(128)} %bitcast.refs_0_, ...), custom_call_target="tpu_custom_call" | custom-call | tf_op jit(solution)/shard_map/pallas_call | solution.py:97
  44.2 3.8 %collective-permute-done.12.refs_5_.refs_1_ = bf16[288,512]{1,0:T(8,128)(2,1)S(1)} collective-permute-done((bf16[288,512]{1,0:T(8,128)(2,1)}, bf16[288,512]{1,0:T(8,128)(2,1)S(1)}, u32[]{:S(2)}, u32[]{:S(2)}) %collective-permute-start.12) | collective-permute-done | bytes 294944 | tf_op jit(solution)/shard_map/ppermute | solution.py:136
  48.0 2.2 %collective-permute-done.10.refs_1_ = bf16[32,6912]{1,0:T(8,128)(2,1)S(1)} collective-permute-done((bf16[32,6912]{1,0:T(8,128)(2,1)}, bf16[32,6912]{1,0:T(8,128)(2,1)S(1)}, u32[]{:S(2)}, u32[]{:S(2)}) %collective-permute-start.10) | collective-permute-done | bytes 442400 | tf_op jit(solution)/shard_map/ppermute | solution.py:136
  50.2 1.5 collective-permute-done.9.refs_0_
  53.0 1.5 collective-permute-done.13.refs_7_
  56.5 9.1 %shard_map.246 = (bf16[256,4352]{1,0:T(8,128)(2,1)}, f32[8,256]{1,0:T(8,128)}, f32[8,1024]{1,0:T(8,128)}, bf16[144,1024]{1,0:T(8,128)(2,1)}, f32[144,256]{1,0:T(...) custom-call(s32[1]{0:T(128)} %bitcast.refs_0_, ...), custom_call_target="tpu_custom_call" | custom-call | tf_op jit(solution)/shard_map/pallas_call | solution.py:97
  65.9 1.4 collective-permute-done.17
  67.3 1.0 add_convert_fusion.7.refs_1_.refs_2_
  68.3 1.0 collective-permute-start.23
  69.3 1.5 collective-permute-start.22
  70.8 1.0 collective-permute-start.21
  71.9 1.9 %shard_map.248.refs_3_.refs_13_ = bf16[432,512]{1,0:T(8,128)(2,1)} custom-call(bf16[144,512]{1,0:T(8,128)(2,1)} %copy-done.16, bf16[288,512]{1,0:T(8,128)(2,1)} %copy-done.17, bf16[144,512]{1,0:T(8,128)(2,1)} %copy-done.5), custom_call_target="tpu_custom_call" | custom-call | tf_op jit(solution)/shard_map/pallas_call | solution.py:97
  73.7 1.3 collective-permute-done.23.refs_2_
  75.1 3.0 %collective-permute-done.22.refs_1_ = bf16[144,512]{1,0:T(8,128)(2,1)S(1)} collective-permute-done((bf16[144,512]{1,0:T(8,128)(2,1)S(1)}, bf16[144,512]{1,0:T(8,128)(2,1)S(1)}, u32[]{:S(2)}, u32[]{:S(2)}) %collective-permute-start.22) | collective-permute-done | bytes 147488 | tf_op jit(solution)/shard_map/ppermute | solution.py:136
  79.9 2.6 %collective-permute-start.19 = (bf16[144,512]{1,0:T(8,128)(2,1)}, bf16[144,512]{1,0:T(8,128)(2,1)S(1)}, u32[]{:S(2)}, u32[]{:S(2)}) collective-permute-start(bf16[144,512]{1,0:T(8,128)(2,1)} %shard_map.247.refs_0_), channel_id=1, source_target_pairs={{0,16},{8,24},{16,0},{24,8},{1,17},{9,25},{17,1},{25,9},{2,18},{10... | collective-permute-start | bytes 442376 | tf_op jit(solution)/shard_map/ppermute | solution.py:136
  82.5 1.6 %collective-permute-start.18 = (bf16[144,512]{1,0:T(8,128)(2,1)}, bf16[144,512]{1,0:T(8,128)(2,1)S(1)}, u32[]{:S(2)}, u32[]{:S(2)}) collective-permute-start(bf16[144,512]{1,0:T(8,128)(2,1)} %shard_map.247.refs_0_), channel_id=1, source_target_pairs={{0,8},{8,0},{16,24},{24,16},{1,9},{9,1},{17,25},{25,17},{2,10},{10... | collective-permute-start | bytes 442376 | tf_op jit(solution)/shard_map/ppermute | solution.py:136
  84.9 5.8 %shard_map.250 = (bf16[144,1024]{1,0:T(8,128)(2,1)}, f32[16,4608]{1,0:T(8,128)}, bf16[16,4608]{1,0:T(8,128)(2,1)}, f32[8,1024]{1,0:T(8,128)}) custom-call(s32[1]{0:T(128)} %bitcast.refs_0_, s32[1]{0:T(128)} %bitcast.8.refs_1_, bf16[144,512]{1,0:T(8,128)(2,1)} %copy-done.5, bf16[144,512]{1,0:T(8,128)(2,1)} %copy-done.40, ...), custom_call_target="tpu_custom_call" | custom-call | tf_op jit(solution)/shard_map/pallas_call | solution.py:97
  92.5 1.5 collective-permute-start.33
  94.0 1.4 collective-permute-start.32
  95.5 1.3 collective-permute-start.27
  96.8 8.4 %shard_map.252 = (f32[16,3328]{1,0:T(8,128)}, bf16[16,3328]{1,0:T(8,128)(2,1)}, f32[576,256]{1,0:T(8,128)}, f32[576,128]{1,0:T(8,128)}, f32[8,256]{1,0:T(8,128)}, /*index=5*/f32[8,1024]{1,0:T(8,128)}) custom-call(s32[1]{0:T(128)} %bitcast.refs_0_, s32[1]{0:T(128)} %bitcast.8.refs_1_, f32[576,128]{1,0:T(8,128)} %get-tuple-element.89.refs_1_.refs_2_, ...), custom_call_target="tpu_custom_call" | custom-call | tf_op jit(solution)/shard_map/pallas_call | solution.py:97
  106.8 1.8 %collective-permute-start.39 = (bf16[16,4608]{1,0:T(8,128)(2,1)S(1)}, bf16[16,4608]{1,0:T(8,128)(2,1)S(1)}, u32[]{:S(2)}, u32[]{:S(2)}) collective-permute-start(bf16[16,4608]{1,0:T(8,128)(2,1)S(1)} %add_convert_fusion.2), channel_id=1, source_target_pairs={{0,16},{8,24},{16,0},{24,8},{1,17},{9,25},{17,1},{25,9},{2,18},{10... | collective-permute-start | bytes 442376 | tf_op jit(solution)/shard_map/ppermute | solution.py:136
  108.6 1.4 collective-permute-start.40
  110.0 6.0 %shard_map.259 = (f32[576,128]{1,0:T(8,128)}, f32[32,1280]{1,0:T(8,128)}, bf16[32,1280]{1,0:T(8,128)(2,1)}) custom-call(s32[1]{0:T(128)} %bitcast.refs_0_, f32[576,128]{1,0:T(8,128)} %get-tuple-element.89.refs_1_.refs_2_, f32[576,256]{1,0:T(8,128)} %get-tuple-element.125.refs_3_.refs_1_.refs_2_, bf16[256,4352]{1,0:T(8,128)(2,1)} %get-tuple-element.123.refs_11_.refs_3_, ...), custom_call_target="tpu_custom_call" | custom-call | tf_op jit(solution)/shard_map/pallas_call | solution.py:97
  121.2 2.7 %collective-permute-start.49 = (bf16[32,1280]{1,0:T(8,128)(2,1)}, bf16[32,1280]{1,0:T(8,128)(2,1)S(1)}, u32[]{:S(2)}, u32[]{:S(2)}) collective-permute-start(bf16[32,1280]{1,0:T(8,128)(2,1)} %get-tuple-element.152), channel_id=1, source_target_pairs={{0,24},{8,16},{16,8},{24,0},{1,25},{9,17},{17,9},{25,1},{2,26},{10... | collective-permute-start | bytes 245768 | tf_op jit(solution)/shard_map/ppermute | solution.py:136
  124.3 1.4 collective-permute-start.47
  125.7 13.5 %shard_map.256 = (f32[1024,512]{1,0:T(8,128)}, f32[1,512]{1,0:T(1,128)}, f32[1,512]{1,0:T(1,128)}, f32[512,4096]{1,0:T(8,128)}) custom-call(s32[1]{0:T(128)} %bitcast.refs_0_, bf16[144,512]{1,0:T(8,128)(2,1)} %get-tuple-element.126.refs_1_, bf16[144,512]{1,0:T(8,128)(2,1)} %get-tuple-element.127.refs_2_, bf16[144,512]{1,0:T(8,128)(2,1)} %get-tuple-element.128.refs_3_, ...), custom_call_target="tpu_custom_call" | custom-call | tf_op jit(solution)/shard_map/pallas_call | solution.py:97
  140.0 1.6 add_convert_fusion.8.refs_4_
  142.4 2.0 %fusion.3 = (bf16[144,512]{1,0:T(8,128)(2,1)}, bf16[144,512]{1,0:T(8,128)(2,1)}, bf16[144,512]{1,0:T(8,128)(2,1)}, bf16[144,512]{1,0:T(8,128)(2,1)}) fusion(bf16[4,144,512]{2,1,0:T(8,128)(2,1)} %shard_map.257, bf16[4,144,512]{2,1,0:T(8,128)(2,1)S(1)} %copy-done.19), kind=kLoop, calls=%fused_computation.13 | loop fusion | flops 1179648 | bytes 1769472 | tf_op jit(solution)/shard_map/convert_element_type | solution.py:177
  145.0 1.5 collective-permute-start.43
  146.5 1.4 collective-permute-start.44
  147.9 1.3 collective-permute-start.46
  149.3 3.4 %collective-permute-done.46.refs_5_ = bf16[16,3328]{1,0:T(8,128)(2,1)S(1)} collective-permute-done((bf16[16,3328]{1,0:T(8,128)(2,1)S(1)}, bf16[16,3328]{1,0:T(8,128)(2,1)S(1)}, u32[]{:S(2)}, u32[]{:S(2)}) %collective-permute-start.46) | collective-permute-done | bytes 106528 | tf_op jit(solution)/shard_map/ppermute | solution.py:136
  153.3 2.4 %shard_map.263 = (f32[2,32,1024]{2,1,0:T(8,128)}, f32[2,9,32,256]{3,2,1,0:T(8,128)}, f32[2,32,1024]{2,1,0:T(8,128)}, f32[2,2,32]{2,1,0:T(2,128)}, f32[2,2,32]{2,...) custom-call(s32[1]{0:T(128)} %bitcast.refs_0_, s32[1]{0:T(128)} %bitcast.8.refs_1_, bf16[16,4608]{1,0:T(8,128)(2,1)} %copy-done.21, ...), custom_call_target="tpu_custom_call" | custom-call | tf_op jit(solution)/shard_map/pallas_call | solution.py:97
  155.7 1.7 %fusion.4 = bf16[512,1,144]{0,2,1:T(8,128)(2,1)} fusion(bf16[144,512]{1,0:T(8,128)(2,1)S(1)} %collective-permute-done.44, bf16[144,512]{1,0:T(8,128)(2,1)S(1)} %collective-permute-done.43, bf16[144,512]{1,0:T(8,128)(2,1)S(1)} %collective-permute-done.42, bf16[144,512]{1,0:T(8,128)(2,1)} %get-tuple-element.146, f32[512]{0:T(512)S(1)} %copy-done.51), kind=kLoop, calls=%fused_computation.14 | loop fusion | flops 663552 | bytes 739328 | tf_op jit(solution)/shard_map/broadcast_in_dim | solution.py:1224
  (191 shorter events, 21.0 us)
Async XLA Ops:
  2.6 14.4 %collective-permute-start.3 = (bf16[32,6912]{1,0:T(8,128)(2,1)}, bf16[32,6912]{1,0:T(8,128)(2,1)S(1)}, u32[]{:S(2)}, u32[]{:S(2)}) collective-permute-start(bf16[32,6912]{1,0:T(8,128)(2,1)} %shard_map.238.refs_8_.refs_3_), channel_id=1, source_target_pairs={{0,2},{1,3},{2,0},{3,1},{4,6},{5,7},{6,4},{7,5},{8,10},{9,11},{10,... | collective-permute-start | bytes 1327112 | tf_op jit(solution)/shard_map/ppermute | solution.py:136
  5.6 21.3 %collective-permute-start.2 = (bf16[32,6912]{1,0:T(8,128)(2,1)}, bf16[32,6912]{1,0:T(8,128)(2,1)S(1)}, u32[]{:S(2)}, u32[]{:S(2)}) collective-permute-start(bf16[32,6912]{1,0:T(8,128)(2,1)} %shard_map.238.refs_8_.refs_3_), channel_id=1, source_target_pairs={{0,4},{1,5},{2,6},{3,7},{4,0},{5,1},{6,2},{7,3},{8,12},{9,13},{10,... | collective-permute-start | bytes 1327112 | tf_op jit(solution)/shard_map/ppermute | solution.py:136
  7.1 19.8 %collective-permute-start.1 = (bf16[32,6912]{1,0:T(8,128)(2,1)}, bf16[32,6912]{1,0:T(8,128)(2,1)S(1)}, u32[]{:S(2)}, u32[]{:S(2)}) collective-permute-start(bf16[32,6912]{1,0:T(8,128)(2,1)} %shard_map.238.refs_8_.refs_3_), channel_id=1, source_target_pairs={{0,6},{1,7},{2,4},{3,5},{4,2},{5,3},{6,0},{7,1},{8,14},{9,15},{10,... | collective-permute-start | bytes 1327112 | tf_op jit(solution)/shard_map/ppermute | solution.py:136
  9.1 5.4 %collective-permute-start.4 = (bf16[144,512]{1,0:T(8,128)(2,1)}, bf16[144,512]{1,0:T(8,128)(2,1)S(1)}, u32[]{:S(2)}, u32[]{:S(2)}) collective-permute-start(bf16[144,512]{1,0:T(8,128)(2,1)} %get-tuple-element.91.refs_0_), channel_id=1, source_target_pairs={{0,8},{8,0},{16,24},{24,16},{1,9},{9,1},{17,25},{25,17},{2,10},{10... | collective-permute-start | bytes 442376 | tf_op jit(solution)/shard_map/ppermute | solution.py:136
  11.2 18.2 %collective-permute-start = (bf16[32,6912]{1,0:T(8,128)(2,1)}, bf16[32,6912]{1,0:T(8,128)(2,1)S(1)}, u32[]{:S(2)}, u32[]{:S(2)}) collective-permute-start(bf16[32,6912]{1,0:T(8,128)(2,1)} %shard_map.238.refs_8_.refs_3_), channel_id=1, source_target_pairs={{0,1},{1,0},{2,3},{3,2},{4,5},{5,4},{6,7},{7,6},{8,9},{9,8},{10,11... | collective-permute-start | bytes 1327112 | tf_op jit(solution)/shard_map/ppermute | solution.py:136
  27.9 2.6 %collective-permute-start.5 = (bf16[32,6912]{1,0:T(8,128)(2,1)}, bf16[32,6912]{1,0:T(8,128)(2,1)S(1)}, u32[]{:S(2)}, u32[]{:S(2)}) collective-permute-start(bf16[32,6912]{1,0:T(8,128)(2,1)} %get-tuple-element.92.refs_5_.refs_3_), channel_id=1, source_target_pairs={{0,1},{1,0},{2,3},{3,2},{4,5},{5,4},{6,7},{7,6},{8,9},{9,8},{10,11... | collective-permute-start | bytes 1327112 | tf_op jit(solution)/shard_map/ppermute | solution.py:136
  27.9 4.0 %collective-permute-start.6 = (bf16[32,6912]{1,0:T(8,128)(2,1)}, bf16[32,6912]{1,0:T(8,128)(2,1)S(1)}, u32[]{:S(2)}, u32[]{:S(2)}) collective-permute-start(bf16[32,6912]{1,0:T(8,128)(2,1)} %get-tuple-element.93.refs_7_.refs_2_), channel_id=1, source_target_pairs={{0,1},{1,0},{2,3},{3,2},{4,5},{5,4},{6,7},{7,6},{8,9},{9,8},{10,11... | collective-permute-start | bytes 1327112 | tf_op jit(solution)/shard_map/ppermute | solution.py:136
  28.4 6.1 %collective-permute-start.7 = (bf16[32,6912]{1,0:T(8,128)(2,1)}, bf16[32,6912]{1,0:T(8,128)(2,1)}, u32[]{:S(2)}, u32[]{:S(2)}) collective-permute-start(bf16[32,6912]{1,0:T(8,128)(2,1)} %get-tuple-element.94.refs_9_.refs_1_), channel_id=1, source_target_pairs={{0,1},{1,0},{2,3},{3,2},{4,5},{5,4},{6,7},{7,6},{8,9},{9,8},{10,11... | collective-permute-start | bytes 1327112 | tf_op jit(solution)/shard_map/ppermute | solution.py:136
  28.4 19.5 %collective-permute-start.11 = (bf16[32,6912]{1,0:T(8,128)(2,1)}, bf16[32,6912]{1,0:T(8,128)(2,1)S(1)}, u32[]{:S(2)}, u32[]{:S(2)}) collective-permute-start(bf16[32,6912]{1,0:T(8,128)(2,1)} %shard_map.243.refs_4_), channel_id=1, source_target_pairs={{0,2},{1,3},{2,0},{3,1},{4,6},{5,7},{6,4},{7,5},{8,10},{9,11},{10,... | collective-permute-start | bytes 1327112 | tf_op jit(solution)/shard_map/ppermute | solution.py:136
  29.5 20.7 %collective-permute-start.10 = (bf16[32,6912]{1,0:T(8,128)(2,1)}, bf16[32,6912]{1,0:T(8,128)(2,1)S(1)}, u32[]{:S(2)}, u32[]{:S(2)}) collective-permute-start(bf16[32,6912]{1,0:T(8,128)(2,1)} %shard_map.243.refs_4_), channel_id=1, source_target_pairs={{0,4},{1,5},{2,6},{3,7},{4,0},{5,1},{6,2},{7,3},{8,12},{9,13},{10,... | collective-permute-start | bytes 1327112 | tf_op jit(solution)/shard_map/ppermute | solution.py:136
  30.5 21.2 %collective-permute-start.9 = (bf16[32,6912]{1,0:T(8,128)(2,1)}, bf16[32,6912]{1,0:T(8,128)(2,1)S(1)}, u32[]{:S(2)}, u32[]{:S(2)}) collective-permute-start(bf16[32,6912]{1,0:T(8,128)(2,1)} %shard_map.243.refs_4_), channel_id=1, source_target_pairs={{0,6},{1,7},{2,4},{3,5},{4,2},{5,3},{6,0},{7,1},{8,14},{9,15},{10,... | collective-permute-start | bytes 1327112 | tf_op jit(solution)/shard_map/ppermute | solution.py:136
  32.0 16.0 %collective-permute-start.12 = (bf16[288,512]{1,0:T(8,128)(2,1)}, bf16[288,512]{1,0:T(8,128)(2,1)S(1)}, u32[]{:S(2)}, u32[]{:S(2)}) collective-permute-start(bf16[288,512]{1,0:T(8,128)(2,1)} %shard_map.244), channel_id=1, source_target_pairs={{0,16},{8,24},{16,0},{24,8},{1,17},{9,25},{17,1},{25,9},{2,18},{10... | collective-permute-start | bytes 884744 | tf_op jit(solution)/shard_map/ppermute | solution.py:136
  34.5 18.4 %collective-permute-start.8 = (bf16[32,6912]{1,0:T(8,128)(2,1)S(1)}, bf16[32,6912]{1,0:T(8,128)(2,1)}, u32[]{:S(2)}, u32[]{:S(2)}) collective-permute-start(bf16[32,6912]{1,0:T(8,128)(2,1)S(1)} %copy-done.9), channel_id=1, source_target_pairs={{0,1},{1,0},{2,3},{3,2},{4,5},{5,4},{6,7},{7,6},{8,9},{9,8},{10,11... | collective-permute-start | bytes 1327112 | tf_op jit(solution)/shard_map/ppermute | solution.py:136
  52.5 2.6 %collective-permute-start.14 = (bf16[32,6912]{1,0:T(8,128)(2,1)}, bf16[32,6912]{1,0:T(8,128)(2,1)S(1)}, u32[]{:S(2)}, u32[]{:S(2)}) collective-permute-start(bf16[32,6912]{1,0:T(8,128)(2,1)} %get-tuple-element.98.refs_8_), channel_id=1, source_target_pairs={{0,1},{1,0},{2,3},{3,2},{4,5},{5,4},{6,7},{7,6},{8,9},{9,8},{10,11... | collective-permute-start | bytes 1327112 | tf_op jit(solution)/shard_map/ppermute | solution.py:136
  53.0 2.8 %collective-permute-start.15 = (bf16[32,6912]{1,0:T(8,128)(2,1)}, bf16[32,6912]{1,0:T(8,128)(2,1)S(1)}, u32[]{:S(2)}, u32[]{:S(2)}) collective-permute-start(bf16[32,6912]{1,0:T(8,128)(2,1)} %get-tuple-element.99.refs_10_), channel_id=1, source_target_pairs={{0,1},{1,0},{2,3},{3,2},{4,5},{5,4},{6,7},{7,6},{8,9},{9,8},{10,11... | collective-permute-start | bytes 1327112 | tf_op jit(solution)/shard_map/ppermute | solution.py:136
  68.3 6.8 %collective-permute-start.23 = (bf16[144,512]{1,0:T(8,128)(2,1)S(1)}, bf16[144,512]{1,0:T(8,128)(2,1)S(1)}, u32[]{:S(2)}, u32[]{:S(2)}) collective-permute-start(bf16[144,512]{1,0:T(8,128)(2,1)S(1)} %add_convert_fusion.7.refs_1_.refs_2_), channel_id=1, source_target_pairs={{0,2},{1,3},{2,0},{3,1},{4,6},{5,7},{6,4},{7,5},{8,10},{9,11},{10,... | collective-permute-start | bytes 442376 | tf_op jit(solution)/shard_map/ppermute | solution.py:136
  69.3 8.8 %collective-permute-start.22 = (bf16[144,512]{1,0:T(8,128)(2,1)S(1)}, bf16[144,512]{1,0:T(8,128)(2,1)S(1)}, u32[]{:S(2)}, u32[]{:S(2)}) collective-permute-start(bf16[144,512]{1,0:T(8,128)(2,1)S(1)} %add_convert_fusion.7.refs_1_.refs_2_), channel_id=1, source_target_pairs={{0,4},{1,5},{2,6},{3,7},{4,0},{5,1},{6,2},{7,3},{8,12},{9,13},{10,... | collective-permute-start | bytes 442376 | tf_op jit(solution)/shard_map/ppermute | solution.py:136
  70.8 7.3 %collective-permute-start.21 = (bf16[144,512]{1,0:T(8,128)(2,1)S(1)}, bf16[144,512]{1,0:T(8,128)(2,1)S(1)}, u32[]{:S(2)}, u32[]{:S(2)}) collective-permute-start(bf16[144,512]{1,0:T(8,128)(2,1)S(1)} %add_convert_fusion.7.refs_1_.refs_2_), channel_id=1, source_target_pairs={{0,6},{1,7},{2,4},{3,5},{4,2},{5,3},{6,0},{7,1},{8,14},{9,15},{10,... | collective-permute-start | bytes 442376 | tf_op jit(solution)/shard_map/ppermute | solution.py:136
  71.9 10.7 %collective-permute-start.20 = (bf16[144,512]{1,0:T(8,128)(2,1)S(1)}, bf16[144,512]{1,0:T(8,128)(2,1)S(1)}, u32[]{:S(2)}, u32[]{:S(2)}) collective-permute-start(bf16[144,512]{1,0:T(8,128)(2,1)S(1)} %add_convert_fusion.7.refs_1_.refs_2_), channel_id=1, source_target_pairs={{0,1},{1,0},{2,3},{3,2},{4,5},{5,4},{6,7},{7,6},{8,9},{9,8},{10,11... | collective-permute-start | bytes 442376 | tf_op jit(solution)/shard_map/ppermute | solution.py:136
  79.4 4.7 %collective-permute-start.24 = (bf16[144,512]{1,0:T(8,128)(2,1)}, bf16[144,512]{1,0:T(8,128)(2,1)S(1)}, u32[]{:S(2)}, u32[]{:S(2)}) collective-permute-start(bf16[144,512]{1,0:T(8,128)(2,1)} %get-tuple-element.105.refs_4_.refs_3_), channel_id=1, source_target_pairs={{0,1},{1,0},{2,3},{3,2},{4,5},{5,4},{6,7},{7,6},{8,9},{9,8},{10,11... | collective-permute-start | bytes 442376 | tf_op jit(solution)/shard_map/ppermute | solution.py:136
  79.4 4.7 %collective-permute-start.25 = (bf16[144,512]{1,0:T(8,128)(2,1)}, bf16[144,512]{1,0:T(8,128)(2,1)S(1)}, u32[]{:S(2)}, u32[]{:S(2)}) collective-permute-start(bf16[144,512]{1,0:T(8,128)(2,1)} %get-tuple-element.106.refs_6_.refs_2_), channel_id=1, source_target_pairs={{0,1},{1,0},{2,3},{3,2},{4,5},{5,4},{6,7},{7,6},{8,9},{9,8},{10,11... | collective-permute-start | bytes 442376 | tf_op jit(solution)/shard_map/ppermute | solution.py:136
  79.9 4.2 %collective-permute-start.26 = (bf16[144,512]{1,0:T(8,128)(2,1)}, bf16[144,512]{1,0:T(8,128)(2,1)S(1)}, u32[]{:S(2)}, u32[]{:S(2)}) collective-permute-start(bf16[144,512]{1,0:T(8,128)(2,1)} %get-tuple-element.107.refs_8_.refs_1_), channel_id=1, source_target_pairs={{0,1},{1,0},{2,3},{3,2},{4,5},{5,4},{6,7},{7,6},{8,9},{9,8},{10,11... | collective-permute-start | bytes 442376 | tf_op jit(solution)/shard_map/ppermute | solution.py:136
  79.9 14.1 %collective-permute-start.19 = (bf16[144,512]{1,0:T(8,128)(2,1)}, bf16[144,512]{1,0:T(8,128)(2,1)S(1)}, u32[]{:S(2)}, u32[]{:S(2)}) collective-permute-start(bf16[144,512]{1,0:T(8,128)(2,1)} %shard_map.247.refs_0_), channel_id=1, source_target_pairs={{0,16},{8,24},{16,0},{24,8},{1,17},{9,25},{17,1},{25,9},{2,18},{10... | collective-permute-start | bytes 442376 | tf_op jit(solution)/shard_map/ppermute | solution.py:136
  82.5 12.9 %collective-permute-start.18 = (bf16[144,512]{1,0:T(8,128)(2,1)}, bf16[144,512]{1,0:T(8,128)(2,1)S(1)}, u32[]{:S(2)}, u32[]{:S(2)}) collective-permute-start(bf16[144,512]{1,0:T(8,128)(2,1)} %shard_map.247.refs_0_), channel_id=1, source_target_pairs={{0,8},{8,0},{16,24},{24,16},{1,9},{9,1},{17,25},{25,17},{2,10},{10... | collective-permute-start | bytes 442376 | tf_op jit(solution)/shard_map/ppermute | solution.py:136
  90.7 14.6 %collective-permute-start.38 = (bf16[16,4608]{1,0:T(8,128)(2,1)}, bf16[16,4608]{1,0:T(8,128)(2,1)S(1)}, u32[]{:S(2)}, u32[]{:S(2)}) collective-permute-start(bf16[16,4608]{1,0:T(8,128)(2,1)} %get-tuple-element.138), channel_id=1, source_target_pairs={{0,8},{8,0},{16,24},{24,16},{1,9},{9,1},{17,25},{25,17},{2,10},{10... | collective-permute-start | bytes 442376 | tf_op jit(solution)/shard_map/ppermute | solution.py:136
  92.0 24.0 %collective-permute-start.34 = (bf16[432,512]{1,0:T(8,128)(2,1)}, bf16[432,512]{1,0:T(8,128)(2,1)S(1)}, u32[]{:S(2)}, u32[]{:S(2)}) collective-permute-start(bf16[432,512]{1,0:T(8,128)(2,1)} %shard_map.254), channel_id=1, source_target_pairs={{0,2},{1,3},{2,0},{3,1},{4,6},{5,7},{6,4},{7,5},{8,10},{9,11},{10,... | collective-permute-start | bytes 1327112 | tf_op jit(solution)/shard_map/ppermute | solution.py:136
  92.5 23.5 %collective-permute-start.33 = (bf16[432,512]{1,0:T(8,128)(2,1)}, bf16[432,512]{1,0:T(8,128)(2,1)S(1)}, u32[]{:S(2)}, u32[]{:S(2)}) collective-permute-start(bf16[432,512]{1,0:T(8,128)(2,1)} %shard_map.254), channel_id=1, source_target_pairs={{0,4},{1,5},{2,6},{3,7},{4,0},{5,1},{6,2},{7,3},{8,12},{9,13},{10,... | collective-permute-start | bytes 1327112 | tf_op jit(solution)/shard_map/ppermute | solution.py:136
  94.0 22.6 %collective-permute-start.32 = (bf16[432,512]{1,0:T(8,128)(2,1)}, bf16[432,512]{1,0:T(8,128)(2,1)S(1)}, u32[]{:S(2)}, u32[]{:S(2)}) collective-permute-start(bf16[432,512]{1,0:T(8,128)(2,1)} %shard_map.254), channel_id=1, source_target_pairs={{0,6},{1,7},{2,4},{3,5},{4,2},{5,3},{6,0},{7,1},{8,14},{9,15},{10,... | collective-permute-start | bytes 1327112 | tf_op jit(solution)/shard_map/ppermute | solution.py:136
  95.5 13.1 %collective-permute-start.27 = (bf16[144,512]{1,0:T(8,128)(2,1)}, bf16[144,512]{1,0:T(8,128)(2,1)S(1)}, u32[]{:S(2)}, u32[]{:S(2)}) collective-permute-start(bf16[144,512]{1,0:T(8,128)(2,1)} %shard_map.251), channel_id=1, source_target_pairs={{0,24},{8,16},{16,8},{24,0},{1,25},{9,17},{17,9},{25,1},{2,26},{10... | collective-permute-start | bytes 442376 | tf_op jit(solution)/shard_map/ppermute | solution.py:136
  106.8 10.7 %collective-permute-start.39 = (bf16[16,4608]{1,0:T(8,128)(2,1)S(1)}, bf16[16,4608]{1,0:T(8,128)(2,1)S(1)}, u32[]{:S(2)}, u32[]{:S(2)}) collective-permute-start(bf16[16,4608]{1,0:T(8,128)(2,1)S(1)} %add_convert_fusion.2), channel_id=1, source_target_pairs={{0,16},{8,24},{16,0},{24,8},{1,17},{9,25},{17,1},{25,9},{2,18},{10... | collective-permute-start | bytes 442376 | tf_op jit(solution)/shard_map/ppermute | solution.py:136
  108.6 8.8 %collective-permute-start.40 = (bf16[16,3328]{1,0:T(8,128)(2,1)}, bf16[16,3328]{1,0:T(8,128)(2,1)S(1)}, u32[]{:S(2)}, u32[]{:S(2)}) collective-permute-start(bf16[16,3328]{1,0:T(8,128)(2,1)} %get-tuple-element.139), channel_id=1, source_target_pairs={{0,8},{8,0},{16,24},{24,16},{1,9},{9,1},{17,25},{25,17},{2,10},{10... | collective-permute-start | bytes 319496 | tf_op jit(solution)/shard_map/ppermute | solution.py:136
  116.0 3.1 %collective-permute-start.31 = (bf16[432,512]{1,0:T(8,128)(2,1)S(1)}, bf16[432,512]{1,0:T(8,128)(2,1)S(1)}, u32[]{:S(2)}, u32[]{:S(2)}) collective-permute-start(bf16[432,512]{1,0:T(8,128)(2,1)S(1)} %copy-done.1), channel_id=1, source_target_pairs={{0,1},{1,0},{2,3},{3,2},{4,5},{5,4},{6,7},{7,6},{8,9},{9,8},{10,11... | collective-permute-start | bytes 1327112 | tf_op jit(solution)/shard_map/ppermute | solution.py:136
  116.1 3.5 %collective-permute-start.28 = (bf16[144,512]{1,0:T(8,128)(2,1)}, bf16[144,512]{1,0:T(8,128)(2,1)S(1)}, u32[]{:S(2)}, u32[]{:S(2)}) collective-permute-start(bf16[144,512]{1,0:T(8,128)(2,1)} %get-tuple-element.126.refs_1_), channel_id=1, source_target_pairs={{0,1},{1,0},{2,3},{3,2},{4,5},{5,4},{6,7},{7,6},{8,9},{9,8},{10,11... | collective-permute-start | bytes 442376 | tf_op jit(solution)/shard_map/ppermute | solution.py:136
  116.6 3.1 %collective-permute-start.29 = (bf16[144,512]{1,0:T(8,128)(2,1)}, bf16[144,512]{1,0:T(8,128)(2,1)S(1)}, u32[]{:S(2)}, u32[]{:S(2)}) collective-permute-start(bf16[144,512]{1,0:T(8,128)(2,1)} %get-tuple-element.127.refs_2_), channel_id=1, source_target_pairs={{0,1},{1,0},{2,3},{3,2},{4,5},{5,4},{6,7},{7,6},{8,9},{9,8},{10,11... | collective-permute-start | bytes 442376 | tf_op jit(solution)/shard_map/ppermute | solution.py:136
  117.4 3.5 %collective-permute-start.30 = (bf16[144,512]{1,0:T(8,128)(2,1)}, bf16[144,512]{1,0:T(8,128)(2,1)S(1)}, u32[]{:S(2)}, u32[]{:S(2)}) collective-permute-start(bf16[144,512]{1,0:T(8,128)(2,1)} %get-tuple-element.128.refs_3_), channel_id=1, source_target_pairs={{0,1},{1,0},{2,3},{3,2},{4,5},{5,4},{6,7},{7,6},{8,9},{9,8},{10,11... | collective-permute-start | bytes 442376 | tf_op jit(solution)/shard_map/ppermute | solution.py:136
  117.5 3.7 %collective-permute-start.35 = (bf16[432,512]{1,0:T(8,128)(2,1)}, bf16[432,512]{1,0:T(8,128)(2,1)S(1)}, u32[]{:S(2)}, u32[]{:S(2)}) collective-permute-start(bf16[432,512]{1,0:T(8,128)(2,1)} %get-tuple-element.132.refs_15_), channel_id=1, source_target_pairs={{0,1},{1,0},{2,3},{3,2},{4,5},{5,4},{6,7},{7,6},{8,9},{9,8},{10,11... | collective-permute-start | bytes 1327112 | tf_op jit(solution)/shard_map/ppermute | solution.py:136
  119.1 4.8 %collective-permute-start.36 = (bf16[432,512]{1,0:T(8,128)(2,1)}, bf16[432,512]{1,0:T(8,128)(2,1)S(1)}, u32[]{:S(2)}, u32[]{:S(2)}) collective-permute-start(bf16[432,512]{1,0:T(8,128)(2,1)} %get-tuple-element.133.refs_17_), channel_id=1, source_target_pairs={{0,1},{1,0},{2,3},{3,2},{4,5},{5,4},{6,7},{7,6},{8,9},{9,8},{10,11... | collective-permute-start | bytes 1327112 | tf_op jit(solution)/shard_map/ppermute | solution.py:136
  119.6 4.7 %collective-permute-start.37 = (bf16[432,512]{1,0:T(8,128)(2,1)}, bf16[432,512]{1,0:T(8,128)(2,1)S(1)}, u32[]{:S(2)}, u32[]{:S(2)}) collective-permute-start(bf16[432,512]{1,0:T(8,128)(2,1)} %get-tuple-element.134.refs_19_), channel_id=1, source_target_pairs={{0,1},{1,0},{2,3},{3,2},{4,5},{5,4},{6,7},{7,6},{8,9},{9,8},{10,11... | collective-permute-start | bytes 1327112 | tf_op jit(solution)/shard_map/ppermute | solution.py:136
  119.7 19.5 %collective-permute-start.41 = (bf16[16,3328]{1,0:T(8,128)(2,1)S(1)}, bf16[16,3328]{1,0:T(8,128)(2,1)S(1)}, u32[]{:S(2)}, u32[]{:S(2)}) collective-permute-start(bf16[16,3328]{1,0:T(8,128)(2,1)S(1)} %add_convert_fusion.9), channel_id=1, source_target_pairs={{0,16},{8,24},{16,0},{24,8},{1,17},{9,25},{17,1},{25,9},{2,18},{10... | collective-permute-start | bytes 319496 | tf_op jit(solution)/shard_map/ppermute | solution.py:136
  120.9 20.7 %collective-permute-start.16 = (bf16[4,144,512]{2,1,0:T(8,128)(2,1)}, bf16[4,144,512]{2,1,0:T(8,128)(2,1)S(1)}, u32[]{:S(2)}, u32[]{:S(2)}) collective-permute-start(bf16[4,144,512]{2,1,0:T(8,128)(2,1)} %get-tuple-element.101), channel_id=1, source_target_pairs={{0,1},{1,0},{2,3},{3,2},{4,5},{5,4},{6,7},{7,6},{8,9},{9,8},{10,11... | collective-permute-start | bytes 1769480 | tf_op jit(solution)/shard_map/ppermute | solution.py:136
  121.2 23.8 %collective-permute-start.49 = (bf16[32,1280]{1,0:T(8,128)(2,1)}, bf16[32,1280]{1,0:T(8,128)(2,1)S(1)}, u32[]{:S(2)}, u32[]{:S(2)}) collective-permute-start(bf16[32,1280]{1,0:T(8,128)(2,1)} %get-tuple-element.152), channel_id=1, source_target_pairs={{0,24},{8,16},{16,8},{24,0},{1,25},{9,17},{17,9},{25,1},{2,26},{10... | collective-permute-start | bytes 245768 | tf_op jit(solution)/shard_map/ppermute | solution.py:136
  123.9 22.6 %collective-permute-start.48 = (bf16[32,1280]{1,0:T(8,128)(2,1)}, bf16[32,1280]{1,0:T(8,128)(2,1)S(1)}, u32[]{:S(2)}, u32[]{:S(2)}) collective-permute-start(bf16[32,1280]{1,0:T(8,128)(2,1)} %get-tuple-element.152), channel_id=1, source_target_pairs={{0,16},{8,24},{16,0},{24,8},{1,17},{9,25},{17,1},{25,9},{2,18},{10... | collective-permute-start | bytes 245768 | tf_op jit(solution)/shard_map/ppermute | solution.py:136
  124.3 23.7 %collective-permute-start.47 = (bf16[32,1280]{1,0:T(8,128)(2,1)}, bf16[32,1280]{1,0:T(8,128)(2,1)}, u32[]{:S(2)}, u32[]{:S(2)}) collective-permute-start(bf16[32,1280]{1,0:T(8,128)(2,1)} %get-tuple-element.152), channel_id=1, source_target_pairs={{0,8},{8,0},{16,24},{24,16},{1,9},{9,1},{17,25},{25,17},{2,10},{10... | collective-permute-start | bytes 245768 | tf_op jit(solution)/shard_map/ppermute | solution.py:136
  139.2 10.0 %collective-permute-start.45 = (bf16[16,4608]{1,0:T(8,128)(2,1)S(1)}, bf16[16,4608]{1,0:T(8,128)(2,1)S(1)}, u32[]{:S(2)}, u32[]{:S(2)}) collective-permute-start(bf16[16,4608]{1,0:T(8,128)(2,1)S(1)} %add_convert_fusion.refs_2_), channel_id=1, source_target_pairs={{0,8},{8,0},{16,24},{24,16},{1,9},{9,1},{17,25},{25,17},{2,10},{10... | collective-permute-start | bytes 442376 | tf_op jit(solution)/shard_map/ppermute | solution.py:136
  144.4 11.3 %collective-permute-start.42 = (bf16[144,512]{1,0:T(8,128)(2,1)}, bf16[144,512]{1,0:T(8,128)(2,1)S(1)}, u32[]{:S(2)}, u32[]{:S(2)}) collective-permute-start(bf16[144,512]{1,0:T(8,128)(2,1)} %get-tuple-element.147), channel_id=1, source_target_pairs={{0,2},{1,3},{2,0},{3,1},{4,6},{5,7},{6,4},{7,5},{8,10},{9,11},{10,... | collective-permute-start | bytes 442376 | tf_op jit(solution)/shard_map/ppermute | solution.py:136
  145.0 10.7 %collective-permute-start.43 = (bf16[144,512]{1,0:T(8,128)(2,1)}, bf16[144,512]{1,0:T(8,128)(2,1)S(1)}, u32[]{:S(2)}, u32[]{:S(2)}) collective-permute-start(bf16[144,512]{1,0:T(8,128)(2,1)} %get-tuple-element.148), channel_id=1, source_target_pairs={{0,4},{1,5},{2,6},{3,7},{4,0},{5,1},{6,2},{7,3},{8,12},{9,13},{10,... | collective-permute-start | bytes 442376 | tf_op jit(solution)/shard_map/ppermute | solution.py:136
  146.5 9.2 %collective-permute-start.44 = (bf16[144,512]{1,0:T(8,128)(2,1)}, bf16[144,512]{1,0:T(8,128)(2,1)S(1)}, u32[]{:S(2)}, u32[]{:S(2)}) collective-permute-start(bf16[144,512]{1,0:T(8,128)(2,1)} %get-tuple-element.149), channel_id=1, source_target_pairs={{0,6},{1,7},{2,4},{3,5},{4,2},{5,3},{6,0},{7,1},{8,14},{9,15},{10,... | collective-permute-start | bytes 442376 | tf_op jit(solution)/shard_map/ppermute | solution.py:136
  147.9 4.7 %collective-permute-start.46 = (bf16[16,3328]{1,0:T(8,128)(2,1)S(1)}, bf16[16,3328]{1,0:T(8,128)(2,1)S(1)}, u32[]{:S(2)}, u32[]{:S(2)}) collective-permute-start(bf16[16,3328]{1,0:T(8,128)(2,1)S(1)} %copy-done.18), channel_id=1, source_target_pairs={{0,8},{8,0},{16,24},{24,16},{1,9},{9,1},{17,25},{25,17},{2,10},{10... | collective-permute-start | bytes 319496 | tf_op jit(solution)/shard_map/ppermute | solution.py:136
  (54 other events, 215.7 us)

commit v5 on v4

--- a/solution.py
+++ b/solution.py
@@ -13,6 +13,7 @@
 OFFSETS = [(-1, -1), (-1, 0), (-1, 1), (0, -1), (0, 0), (0, 1), (1, -1), (1, 0), (1, 1)]
 TAPS = len(OFFSETS)
 LANES = 128
+VMEM_MIB = 64
 BF16 = jnp.bfloat16
 F32 = jnp.float32
 SMEM = pl.BlockSpec(memory_space=pltpu.SMEM)
@@ -62,7 +63,7 @@
             self.sent = True
 
 
-def call(body, outs, scalars, args, scratch=(), vmem=60, flops=0, moved=0, plain=(), after=(), direct=()):
+def call(body, outs, scalars, args, scratch=(),  plain=(), after=(), direct=()):
     count = (len(scalars), len(args), len(plain), len(after), len(outs))
 
     def kernel(*refs):
@@ -100,7 +101,7 @@
         in_specs=[SMEM] * len(scalars) + [ANY] * (len(args) + len(plain) + len(after)),
         out_specs=[ANY] * len(outs),
         scratch_shapes=shapes + sems + list(scratch),
-        compiler_params=pltpu.CompilerParams(vmem_limit_bytes=vmem << 20),
+        compiler_params=pltpu.CompilerParams(vmem_limit_bytes=VMEM_MIB << 20),
         cost_estimate=pl.CostEstimate(flops=0, bytes_accessed=0, transcendentals=0),
     )(*scalars, *args, *plain, *after)
 
@@ -115,6 +116,7 @@
         in_specs=[ANY] * (len(values) + len(after)),
         out_specs=[ANY] * len(values),
         input_output_aliases={i: i for i in range(len(values))},
+        compiler_params=pltpu.CompilerParams(vmem_limit_bytes=VMEM_MIB << 20),
     )(*values, *after)
 
 
@@ -267,7 +269,6 @@
             pltpu.VMEM(exp.shape[1:], BF16),
             pltpu.SemaphoreType.DMA((3,)),
         ],
-        moved=2 * held * width * 2,
         plain=[red, conv, exp],
         after=after,
     )
@@ -495,8 +496,6 @@
         [me],
         args,
         scratch,
-        flops=2 * slots * mid * (2 * chan + TAPS * mid),
-        moved=30 * slots * chan,
         plain=list(pieces or []),
     )
     got = list(got)
@@ -657,8 +656,6 @@
         [me, plane],
         [*pieces, aux, x, outs, u3, fac, mids, u2, w, pat, u1],
         [pltpu.VMEM((slots, chan), F32), pltpu.VMEM((held, end), F32)] + back_scratch(side, slots, chan, mid),
-        flops=3 * slots * mid * (2 * chan + TAPS * mid),
-        moved=40 * slots * chan,
     )
 
 
@@ -674,7 +671,8 @@
         side, me, aux, up, x_ref, w_in, mid_in, out_ref, u2_in, u3, fac, pat_in,
         sg, eg, turned, field, dense, accum, out_rows(), grads,
     )
-    split_rows(grads, plane, mine, theirs, columns(eg.shape[1], dense.shape[1])[0])
+    start = columns(eg.shape[1], dense.shape[1])[0]
+    split_rows(grads, plane, mine, theirs, start)
     pad = pad_of(side)
     conv_grad()[...] = field[1, pad : pad + slots, :]
     accum_out()[...] = accum[0:8, :]
@@ -702,8 +700,6 @@
         [me, plane],
         [aux, spread, pooled_grad, x, outs, u3, fac, mids, u2, w, pat],
         [pltpu.VMEM((slots, chan), F32), pltpu.VMEM((held, end), F32)] + back_scratch(side, slots, chan, mid),
-        flops=2 * slots * mid * (2 * chan + TAPS * mid),
-        moved=40 * slots * chan,
     )
 
 
@@ -748,8 +744,6 @@
         [me],
         [aux, conv_grad, w, u1, fac, mids, x, sg_own, accum, out_rows],
         back_scratch(side, slots, chan, mid)[2:],
-        flops=slots * mid * (2 * chan + TAPS * mid),
-        moved=20 * slots * chan,
     )
 
 
@@ -878,8 +872,6 @@
             pltpu.VMEM(w2.shape, BF16),
             pltpu.SemaphoreType.DMA((2,)),
         ],
-        flops=2 * slots * (mid * (2 * chan + TAPS * mid) + hidden * (2 * chan + width)),
-        moved=30 * slots * chan + 2 * hidden * (chan + width),
         plain=[*pieces, w1, w2],
     )
     got = list(got)
@@ -914,10 +906,11 @@
     hidden = dot_nn(stacked[...], w1()[...]) + b1()[...]
     value, slope = gelu_both(hidden)
     turned = value.T.astype(BF16)
+    low[0:rows, :] = (slope[0:rows] * grad()[...]).astype(BF16)
+    width = buffer.shape[2]
+    flights = []
     for copy in copies:
         copy.wait()
-    width = buffer.shape[2]
-    flights = []
     for r in range(cot.shape[1] // width):
         if r >= 2:
             flights[r - 2].wait()
@@ -925,7 +918,6 @@
         buffer[r % 2] = dot_nn(turned, cot[:, lanes])
         flights.append(pltpu.make_async_copy(buffer.at[r % 2], w2_out.target.at[:, lanes], out_sems.at[r % 2]))
         flights[-1].start()
-    low[0:rows, :] = (slope[0:rows] * grad()[...]).astype(BF16)
     low[rows:, :] = (slope[rows:] * dot_nt(cot[rows:, :], w2()[...])).astype(BF16)
     w1_grad()[...] = dot_tn(stacked[...], low[...])
     w1_grad.send()
@@ -956,16 +948,20 @@
             pltpu.SemaphoreType.DMA((2 + len(rest),)),
             pltpu.SemaphoreType.DMA((2,)),
         ],
-        flops=4 * total * hidden * (chan + width),
-        moved=2 * hidden * (3 * chan + 3 * width),
         plain=[own, w2, *rest],
         direct=(3,),
     )
 
 
 def finish_kernel(count, scalars, ins, outs, plain, scr):
-    red, conv, exp, mid_gain, mid_bias, out_gain, out_bias = [item() for item in outs]
-    late, middle, parts = ins[0:2], ins[2:4], ins[4:]
+    red, conv, exp, mid_gain, mid_bias, out_gain, out_bias, tokens = [item() for item in outs]
+    late, middle, parts = ins[0:2], ins[2:4], ins[4 : 4 + count]
+    bias, *shares = ins[4 + count :]
+    value = bias()[...]
+    for item in shares:
+        value = value + item()[...].astype(F32)
+    tokens[...] = value.astype(BF16)
+    outs[7].send()
     chan, mid = red.shape[2], conv.shape[3]
     held = red.shape[1]
     reduce_end, conv_end, expand_end, mid_end, end = columns(chan, mid)
@@ -1002,7 +998,7 @@
         out_bias[k : k + 1, :] = scr[k, 1:2, LANES : LANES + out_bias.shape[1]]
 
 
-def finish(me, plane, late, middle, parts, chan, mid, share):
+def finish(me, plane, late, middle, parts, chan, mid, share, bias, shares):
     held = parts[0].shape[0]
     outs = [
         sds((2, held, chan), F32),
@@ -1012,15 +1008,14 @@
         sds((2, 2, held), F32),
         sds((2, share), F32),
         sds((2, share), F32),
+        sds(shares[0].shape, BF16),
     ]
     return call(
         functools.partial(finish_kernel, len(parts)),
         outs,
         [me, plane],
-        [*late, *middle, *parts],
+        [*late, *middle, *parts, bias, *shares],
         [pltpu.VMEM((2, LANES, 2 * LANES), F32)],
-        flops=8 * held * chan,
-        moved=40 * held * chan,
     )
 
 
@@ -1149,16 +1144,19 @@
 
     if not aligned:
         cot_rest = doubled(cot_rest, held_cot)
+
     half = summed(mine, ppermute_xor(theirs, "ch", 1))
     far = neighbours(half)
     cot_rest = join(*cot_rest, after=[half])
-    far = dict(zip(far, gate(list(far.values()), cot_rest)))
+    got = ppermute_xor(send, "ch", 1)
+    shares = [summed(keep[q], got[q]) for q in range(n // 2)]
+    far = dict(zip(far, gate(list(far.values()), cot_rest, shares[0])))
     if aligned:
-        (cot_far,) = gate([cot_rest], *far.values())
-        cot_far = neighbours(cot_far)
-    grad_pieces = with_cores(half, far)
+        (cot_rest,) = gate([cot_rest], *far.values())
+        cot_far = neighbours(cot_rest)
     (half_in,) = gate([half_in], half)
     parts = [ppermute_xor(half_in, "img", m) for m in (1, 2) if m < planes]
+    grad_pieces = with_cores(half, far)
 
     pooled_grad, late_mine, late_theirs, late_out = late_backward(
         POOLED, held, me, plane, few_facts, grad_pieces, saved_second
@@ -1200,18 +1198,11 @@
     for mask in (1 << k for k in range(2, planes.bit_length() - 1)):
         middle_half = summed(middle_half, ppermute_xor(middle_half, "img", mask))
     middle = (middle_half, ppermute_xor(middle_half, "img", 1))
-
-    got = ppermute_xor(send, "ch", 1)
-    (got,) = gate([got], b1_grad)
-    shares = [summed(keep[q], got[q]) for q in range(n // 2)]
     shares = gate(shares, middle_half)
-    tokens = shares[0].astype(F32)
-    for q in range(1, n // 2):
-        tokens = tokens + ppermute_xor(shares[q], "ch", 2 * q).astype(F32)
-    tokens = (tokens + read_b2[None, :]).astype(BF16)
-
-    red_grad, conv_grad, exp_grad, mid_gain_grad, mid_bias_grad, out_gain_grad, out_bias_grad = finish(
-        me, plane, late, middle, last, chan, mid, share
+    shares = [shares[0]] + [ppermute_xor(shares[q], "ch", 2 * q) for q in range(1, n // 2)]
+
+    red_grad, conv_grad, exp_grad, mid_gain_grad, mid_bias_grad, out_gain_grad, out_bias_grad, tokens = finish(
+        me, plane, late, middle, last, chan, mid, share, read_b2[None, :], shares
     )
     if not aligned:
         feat_grad = lax.dynamic_slice_in_dim(feat_grad, index * share, share, 1)

time: 158 us -> 151 us (0.956)
  local copies, waits for them, and re-layouts: 9.98 us -> 0 us
  waiting for transfers between devices: 30.2 us -> 32 us
    unnamed x105 -> x0, local copies, waits for them, and re-layouts: 9.98 us -> none
    convert_element_type x6, other arithmetic: 7.39 us -> 10.5 us  [summed(): return (left.astype(F32) + right.astype(F32)).astype(BF16)]
    ppermute x50, waiting for transfers between devices: 30.2 us -> 32 us  [ppermute_xor(): lax.ppermute(x, axis, [(i, i ^ mask) for i in range(lax.axis_size(axis))])]
    broadcast_in_dim x1 -> x0, other arithmetic: 1.66 us -> none  [per_device(): jnp.transpose(tokens)[:, None, :]]
  transfers between devices with their start and end apart: 50 -> 50, of which waited for: 12 -> 13; matrix products, arithmetic and copies ran while one was open for 5% -> 7% of each run, Pallas kernels for 33% -> 33%
where the time goes in v5:
time: 151 us
  Pallas kernels  63.8 us (42%)
  starting transfers between devices  42.8 us (28%)
  waiting for transfers between devices  32 us (21%)
  other arithmetic  10.5 us (7%)
  between operations  1.7 us (1%)
    pallas_call x12, Pallas kernels, call(): pl.pallas_call(kernel, out_shape=list(outs), in_specs=[SMEM] * len(scalar...  63.8 us
    ppermute x50, starting transfers between devices, ppermute_xor(): lax.ppermute(x, axis, [(i, i ^ mask) for i in range(lax.axis_size(axis))])  42.8 us
    ppermute x50, waiting for transfers between devices, ppermute_xor(): lax.ppermute(x, axis, [(i, i ^ mask) for i in range(lax.axis_size(axis))])  32 us
    convert_element_type x6, other arithmetic, summed(): return (left.astype(F32) + right.astype(F32)).astype(BF16)  10.5 us
  transfers between devices with their start and end apart: 50, of which 13 were waited for; matrix products, arithmetic and copies ran while one was open for 7% of the time, Pallas kernels for 33%

profile of v5, /device:TPU:0, one launch (start us, length us, event | category | flops | bytes accessed | tf_op | source)
XLA Modules:
  0.0 150.8 jit_solution(12854577706597188523)
XLA Ops:
  0.6 2.0 %shard_map.238.refs_8_.refs_3_ = bf16[32,6912]{1,0:T(8,128)(2,1)} custom-call(bf16[576,128]{1,0:T(8,128)(2,1)} %bitcast.34, f32[2,2,32]{2,1,0:T(2,128)} %refs_1_.3, f32[2,2,32]{2,1,0:T(2,128)} %refs_2_.3, f32[2,128]{1,0:T(2,128)} %refs_3_.3, f32[2,128]{1,0:T(2,128)} %refs_4_.3, bf16[2,32,1024]{2,1,0:T(8,128)(2,1)} %bitcast.32, ...), custom_call_target="tpu_custom_call" | custom-call | tf_op jit(solution)/shard_map/pallas_call | solution.py:98
  2.6 3.0 %collective-permute-start.3 = (bf16[32,6912]{1,0:T(8,128)(2,1)}, bf16[32,6912]{1,0:T(8,128)(2,1)}, u32[]{:S(2)}, u32[]{:S(2)}) collective-permute-start(bf16[32,6912]{1,0:T(8,128)(2,1)} %shard_map.238.refs_8_.refs_3_), channel_id=1, source_target_pairs={{0,2},{1,3},{2,0},{3,1},{4,6},{5,7},{6,4},{7,5},{8,10},{9,11},{10,... | collective-permute-start | bytes 1327112 | tf_op jit(solution)/shard_map/ppermute | solution.py:138
  5.6 1.5 %collective-permute-start.2 = (bf16[32,6912]{1,0:T(8,128)(2,1)}, bf16[32,6912]{1,0:T(8,128)(2,1)}, u32[]{:S(2)}, u32[]{:S(2)}) collective-permute-start(bf16[32,6912]{1,0:T(8,128)(2,1)} %shard_map.238.refs_8_.refs_3_), channel_id=1, source_target_pairs={{0,4},{1,5},{2,6},{3,7},{4,0},{5,1},{6,2},{7,3},{8,12},{9,13},{10,... | collective-permute-start | bytes 1327112 | tf_op jit(solution)/shard_map/ppermute | solution.py:138
  7.2 2.0 %shard_map.239 = (bf16[32,6912]{1,0:T(8,128)(2,1)}, bf16[144,512]{1,0:T(8,128)(2,1)}) custom-call(bf16[144,512]{1,0:T(8,128)(2,1)} %bitcast.35, f32[2,2,32]{2,1,0:T(2,128)} %refs_1_.3, f32[2,2,32]{2,1,0:T(2,128)} %refs_2_.3, f32[2,128]{1,0:T(2,128)} %refs_3_.3, f32[2,128]{1,0:T(2,128)} %refs_4_.3, bf16[2,32,1024]{2,1,0:T(8,128)(2,1)} %bitcast.33, ...), custom_call_target="tpu_custom_call" | custom-call | tf_op jit(solution)/shard_map/pallas_call | solution.py:98
  9.2 2.1 %collective-permute-start.4 = (bf16[144,512]{1,0:T(8,128)(2,1)}, bf16[144,512]{1,0:T(8,128)(2,1)}, u32[]{:S(2)}, u32[]{:S(2)}) collective-permute-start(bf16[144,512]{1,0:T(8,128)(2,1)} %get-tuple-element.92.refs_0_), channel_id=1, source_target_pairs={{0,8},{8,0},{16,24},{24,16},{1,9},{9,1},{17,25},{25,17},{2,10},{10... | collective-permute-start | bytes 442376 | tf_op jit(solution)/shard_map/ppermute | solution.py:138
  11.9 1.1 shard_map.237
  13.0 1.7 %collective-permute-done.4.refs_1_.refs_4_.refs_0_ = bf16[144,512]{1,0:T(8,128)(2,1)} collective-permute-done((bf16[144,512]{1,0:T(8,128)(2,1)}, bf16[144,512]{1,0:T(8,128)(2,1)}, u32[]{:S(2)}, u32[]{:S(2)}) %collective-permute-start.4) | collective-permute-done | bytes 147488 | tf_op jit(solution)/shard_map/ppermute | solution.py:138
  14.7 1.7 %shard_map.240.refs_3_.refs_0_ = bf16[288,512]{1,0:T(8,128)(2,1)} custom-call(bf16[144,512]{1,0:T(8,128)(2,1)} %get-tuple-element.92.refs_0_, bf16[144,512]{1,0:T(8,128)(2,1)} %collective-permute-done.4.refs_1_.refs_4_.refs_0_), custom_call_target="tpu_custom_call" | custom-call | tf_op jit(solution)/shard_map/pallas_call | solution.py:98
  16.9 10.1 %collective-permute-done.2.refs_1_ = bf16[32,6912]{1,0:T(8,128)(2,1)} collective-permute-done((bf16[32,6912]{1,0:T(8,128)(2,1)}, bf16[32,6912]{1,0:T(8,128)(2,1)}, u32[]{:S(2)}, u32[]{:S(2)}) %collective-permute-start.2) | collective-permute-done | bytes 442400 | tf_op jit(solution)/shard_map/ppermute | solution.py:138
  27.6 1.2 collective-permute-start.11
  29.7 1.4 collective-permute-start.9
  31.1 2.6 %collective-permute-start.12 = (bf16[288,512]{1,0:T(8,128)(2,1)}, bf16[288,512]{1,0:T(8,128)(2,1)}, u32[]{:S(2)}, u32[]{:S(2)}) collective-permute-start(bf16[288,512]{1,0:T(8,128)(2,1)} %shard_map.244), channel_id=1, source_target_pairs={{0,16},{8,24},{16,0},{24,8},{1,17},{9,25},{17,1},{25,9},{2,18},{10... | collective-permute-start | bytes 884744 | tf_op jit(solution)/shard_map/ppermute | solution.py:138
  33.7 9.6 %shard_map.242 = (bf16[576,1024]{1,0:T(8,128)(2,1)}, bf16[256,4352]{1,0:T(8,128)(2,1)}, f32[8,256]{1,0:T(8,128)}, f32[8,1024]{1,0:T(8,128)}, bf16[144,1024]{1,0:...) custom-call(s32[1]{0:T(128)} %bitcast.refs_0_, ...), custom_call_target="tpu_custom_call" | custom-call | tf_op jit(solution)/shard_map/pallas_call | solution.py:98
  43.4 3.8 %collective-permute-done.12.refs_5_.refs_1_ = bf16[288,512]{1,0:T(8,128)(2,1)} collective-permute-done((bf16[288,512]{1,0:T(8,128)(2,1)}, bf16[288,512]{1,0:T(8,128)(2,1)}, u32[]{:S(2)}, u32[]{:S(2)}) %collective-permute-start.12) | collective-permute-done | bytes 294944 | tf_op jit(solution)/shard_map/ppermute | solution.py:138
  47.2 2.1 %collective-permute-done.10.refs_1_ = bf16[32,6912]{1,0:T(8,128)(2,1)} collective-permute-done((bf16[32,6912]{1,0:T(8,128)(2,1)}, bf16[32,6912]{1,0:T(8,128)(2,1)}, u32[]{:S(2)}, u32[]{:S(2)}) %collective-permute-start.10) | collective-permute-done | bytes 442400 | tf_op jit(solution)/shard_map/ppermute | solution.py:138
  49.3 1.6 %collective-permute-done.9.refs_0_ = bf16[32,6912]{1,0:T(8,128)(2,1)} collective-permute-done((bf16[32,6912]{1,0:T(8,128)(2,1)}, bf16[32,6912]{1,0:T(8,128)(2,1)}, u32[]{:S(2)}, u32[]{:S(2)}) %collective-permute-start.9) | collective-permute-done | bytes 442400 | tf_op jit(solution)/shard_map/ppermute | solution.py:138
  51.4 1.6 %collective-permute-done.13.refs_7_ = bf16[32,6912]{1,0:T(8,128)(2,1)} collective-permute-done((bf16[32,6912]{1,0:T(8,128)(2,1)}, bf16[32,6912]{1,0:T(8,128)(2,1)}, u32[]{:S(2)}, u32[]{:S(2)}) %collective-permute-start.13) | collective-permute-done | bytes 442400 | tf_op jit(solution)/shard_map/ppermute | solution.py:138
  54.3 9.1 %shard_map.246 = (bf16[256,4352]{1,0:T(8,128)(2,1)}, f32[8,256]{1,0:T(8,128)}, f32[8,1024]{1,0:T(8,128)}, bf16[144,1024]{1,0:T(8,128)(2,1)}, f32[144,256]{1,0:T(...) custom-call(s32[1]{0:T(128)} %bitcast.refs_0_, ...), custom_call_target="tpu_custom_call" | custom-call | tf_op jit(solution)/shard_map/pallas_call | solution.py:98
  64.0 1.9 %collective-permute-done.16 = bf16[144,512]{1,0:T(8,128)(2,1)S(1)} collective-permute-done((bf16[144,512]{1,0:T(8,128)(2,1)}, bf16[144,512]{1,0:T(8,128)(2,1)S(1)}, u32[]{:S(2)}, u32[]{:S(2)}) %collective-permute-start.16) | collective-permute-done | bytes 147488 | tf_op jit(solution)/shard_map/ppermute | solution.py:138
  65.9 1.7 %add_convert_fusion.6.refs_2_.refs_1_ = bf16[144,512]{1,0:T(8,128)(2,1)} fusion(f32[144,512]{1,0:T(8,128)} %get-tuple-element.101, bf16[144,512]{1,0:T(8,128)(2,1)S(1)} %collective-permute-done.16), kind=kLoop, calls=%fused_computation.6 | loop fusion | flops 221184 | bytes 589824 | tf_op jit(solution)/shard_map/convert_element_type | solution.py:179
  68.4 1.5 %collective-permute-start.19 = (bf16[144,512]{1,0:T(8,128)(2,1)}, bf16[144,512]{1,0:T(8,128)(2,1)}, u32[]{:S(2)}, u32[]{:S(2)}) collective-permute-start(bf16[144,512]{1,0:T(8,128)(2,1)} %add_convert_fusion.6.refs_2_.refs_1_), channel_id=1, source_target_pairs={{0,4},{1,5},{2,6},{3,7},{4,0},{5,1},{6,2},{7,3},{8,12},{9,13},{10,... | collective-permute-start | bytes 442376 | tf_op jit(solution)/shard_map/ppermute | solution.py:138
  69.9 1.2 collective-permute-start.18
  71.1 1.9 %shard_map.247.refs_3_.refs_0_ = bf16[432,512]{1,0:T(8,128)(2,1)} custom-call(bf16[144,512]{1,0:T(8,128)(2,1)} %collective-permute-done.4.refs_1_.refs_4_.refs_0_, bf16[288,512]{1,0:T(8,128)(2,1)} %collective-permute-done.12.refs_5_.refs_1_, bf16[144,512]{1,0:T(8,128)(2,1)} %add_convert_fusion.6.refs_2_.refs_1_), custom_call_target="tpu_custom_call" | custom-call | tf_op jit(solution)/shard_map/pallas_call | solution.py:98
  73.0 2.2 %fusion.3 = (bf16[144,512]{1,0:T(8,128)(2,1)}, bf16[144,512]{1,0:T(8,128)(2,1)}, bf16[144,512]{1,0:T(8,128)(2,1)}, bf16[144,512]{1,0:T(8,128)(2,1)}) fusion(bf16[4,144,512]{2,1,0:T(8,128)(2,1)} %collective-permute-done.21, bf16[4,144,512]{2,1,0:T(8,128)(2,1)} %get-tuple-element.103), kind=kLoop, calls=%fused_computation.12 | loop fusion | flops 1179648 | bytes 1769472 | tf_op jit(solution)/shard_map/convert_element_type | solution.py:179
  75.2 2.3 %collective-permute-done.19.refs_1_ = bf16[144,512]{1,0:T(8,128)(2,1)} collective-permute-done((bf16[144,512]{1,0:T(8,128)(2,1)}, bf16[144,512]{1,0:T(8,128)(2,1)}, u32[]{:S(2)}, u32[]{:S(2)}) %collective-permute-start.19) | collective-permute-done | bytes 147488 | tf_op jit(solution)/shard_map/ppermute | solution.py:138
  78.1 2.6 %collective-permute-start.31 = (bf16[144,512]{1,0:T(8,128)(2,1)}, bf16[144,512]{1,0:T(8,128)(2,1)}, u32[]{:S(2)}, u32[]{:S(2)}) collective-permute-start(bf16[144,512]{1,0:T(8,128)(2,1)} %shard_map.254.refs_0_), channel_id=1, source_target_pairs={{0,16},{8,24},{16,0},{24,8},{1,17},{9,25},{17,1},{25,9},{2,18},{10... | collective-permute-start | bytes 442376 | tf_op jit(solution)/shard_map/ppermute | solution.py:138
  80.7 1.6 %collective-permute-start.30 = (bf16[144,512]{1,0:T(8,128)(2,1)}, bf16[144,512]{1,0:T(8,128)(2,1)}, u32[]{:S(2)}, u32[]{:S(2)}) collective-permute-start(bf16[144,512]{1,0:T(8,128)(2,1)} %shard_map.254.refs_0_), channel_id=1, source_target_pairs={{0,8},{8,0},{16,24},{24,16},{1,9},{9,1},{17,25},{25,17},{2,10},{10... | collective-permute-start | bytes 442376 | tf_op jit(solution)/shard_map/ppermute | solution.py:138
  82.3 5.8 %shard_map.249 = (bf16[144,1024]{1,0:T(8,128)(2,1)}, f32[16,4608]{1,0:T(8,128)}, bf16[16,4608]{1,0:T(8,128)(2,1)}, f32[8,1024]{1,0:T(8,128)}) custom-call(s32[1]{0:T(128)} %bitcast.refs_0_, s32[1]{0:T(128)} %bitcast.1.refs_1_, bf16[144,512]{1,0:T(8,128)(2,1)} %add_convert_fusion.6.refs_2_.refs_1_, bf16[144,512]{1,0:T(8,128)(2,1)} %collective-permute-done.17.refs_3_, ...), custom_call_target="tpu_custom_call" | custom-call | tf_op jit(solution)/shard_map/pallas_call | solution.py:98
  88.5 1.2 collective-permute-start.39
  90.6 1.4 collective-permute-start.37
  92.0 1.6 %collective-permute-start.32 = (bf16[144,512]{1,0:T(8,128)(2,1)}, bf16[144,512]{1,0:T(8,128)(2,1)}, u32[]{:S(2)}, u32[]{:S(2)}) collective-permute-start(bf16[144,512]{1,0:T(8,128)(2,1)} %shard_map.255), channel_id=1, source_target_pairs={{0,24},{8,16},{16,8},{24,0},{1,25},{9,17},{17,9},{25,1},{2,26},{10... | collective-permute-start | bytes 442376 | tf_op jit(solution)/shard_map/ppermute | solution.py:138
  93.6 8.4 %shard_map.250 = (f32[16,3328]{1,0:T(8,128)}, bf16[16,3328]{1,0:T(8,128)(2,1)}, f32[576,256]{1,0:T(8,128)}, f32[576,128]{1,0:T(8,128)}, f32[8,256]{1,0:T(8,128)}, /*index=5*/f32[8,1024]{1,0:T(8,128)}) custom-call(s32[1]{0:T(128)} %bitcast.refs_0_, s32[1]{0:T(128)} %bitcast.1.refs_1_, f32[576,128]{1,0:T(8,128)} %get-tuple-element.90.refs_1_.refs_2_, ...), custom_call_target="tpu_custom_call" | custom-call | tf_op jit(solution)/shard_map/pallas_call | solution.py:98
  102.0 1.7 %add_convert_fusion.4 = bf16[16,4608]{1,0:T(8,128)(2,1)} fusion(f32[16,4608]{1,0:T(8,128)} %get-tuple-element.116, bf16[16,4608]{1,0:T(8,128)(2,1)} %shard_map.251), kind=kLoop, calls=%fused_computation.4 | loop fusion | flops 221184 | bytes 589824 | tf_op jit(solution)/shard_map/convert_element_type | solution.py:179
  103.7 1.4 collective-permute-start.26
  105.2 1.3 collective-permute-start.27
  106.5 6.0 %shard_map.252 = (f32[576,128]{1,0:T(8,128)}, f32[32,1280]{1,0:T(8,128)}, bf16[32,1280]{1,0:T(8,128)(2,1)}) custom-call(s32[1]{0:T(128)} %bitcast.refs_0_, f32[576,128]{1,0:T(8,128)} %get-tuple-element.90.refs_1_.refs_2_, f32[576,256]{1,0:T(8,128)} %get-tuple-element.127.refs_1_.refs_2_.refs_3_, bf16[256,4352]{1,0:T(8,128)(2,1)} %get-tuple-element.125.refs_11_.refs_3_, ...), custom_call_target="tpu_custom_call" | custom-call | tf_op jit(solution)/shard_map/pallas_call | solution.py:98
  113.7 1.7 %add_convert_fusion.8 = bf16[16,3328]{1,0:T(8,128)(2,1)} fusion(f32[16,3328]{1,0:T(8,128)} %get-tuple-element.135, bf16[16,3328]{1,0:T(8,128)(2,1)} %get-tuple-element.136), kind=kLoop, calls=%fused_computation.8 | loop fusion | flops 159744 | bytes 425984 | tf_op jit(solution)/shard_map/convert_element_type | solution.py:179
  116.2 1.7 %add_convert_fusion.3.refs_2_ = bf16[16,4608]{1,0:T(8,128)(2,1)} fusion(bf16[16,4608]{1,0:T(8,128)(2,1)} %get-tuple-element.134, bf16[16,4608]{1,0:T(8,128)(2,1)} %add_convert_fusion.4), kind=kLoop, calls=%fused_computation.3 | loop fusion | flops 294912 | bytes 442368 | tf_op jit(solution)/shard_map/convert_element_type | solution.py:179
  117.9 2.8 %collective-permute-start.46 = (bf16[32,1280]{1,0:T(8,128)(2,1)}, bf16[32,1280]{1,0:T(8,128)(2,1)}, u32[]{:S(2)}, u32[]{:S(2)}) collective-permute-start(bf16[32,1280]{1,0:T(8,128)(2,1)} %get-tuple-element.148), channel_id=1, source_target_pairs={{0,24},{8,16},{16,8},{24,0},{1,25},{9,17},{17,9},{25,1},{2,26},{10... | collective-permute-start | bytes 245768 | tf_op jit(solution)/shard_map/ppermute | solution.py:138
  121.2 1.0 collective-permute-start.44
  122.3 1.0 collective-permute-start.28
  123.3 13.5 %shard_map.259 = (f32[1024,512]{1,0:T(8,128)}, f32[1,512]{1,0:T(1,128)}, f32[1,512]{1,0:T(1,128)}, f32[512,4096]{1,0:T(8,128)}) custom-call(s32[1]{0:T(128)} %bitcast.refs_0_, bf16[144,512]{1,0:T(8,128)(2,1)} %get-tuple-element.138.refs_1_, bf16[144,512]{1,0:T(8,128)(2,1)} %get-tuple-element.139.refs_2_, bf16[144,512]{1,0:T(8,128)(2,1)} %get-tuple-element.140.refs_3_, ...), custom_call_target="tpu_custom_call" | custom-call | tf_op jit(solution)/shard_map/pallas_call | solution.py:98
  136.7 1.6 %add_convert_fusion.7.refs_4_ = bf16[16,3328]{1,0:T(8,128)(2,1)} fusion(bf16[16,3328]{1,0:T(8,128)(2,1)} %shard_map.260, bf16[16,3328]{1,0:T(8,128)(2,1)} %add_convert_fusion.8), kind=kLoop, calls=%fused_computation.7 | loop fusion | flops 212992 | bytes 319488 | tf_op jit(solution)/shard_map/convert_element_type | solution.py:179
  138.4 1.5 collective-permute-start.47
  140.4 1.5 collective-permute-start.49
  141.9 1.0 collective-permute-start.43
  142.9 4.0 %collective-permute-done.43.refs_5_ = bf16[16,3328]{1,0:T(8,128)(2,1)} collective-permute-done((bf16[16,3328]{1,0:T(8,128)(2,1)}, bf16[16,3328]{1,0:T(8,128)(2,1)}, u32[]{:S(2)}, u32[]{:S(2)}) %collective-permute-start.43) | collective-permute-done | bytes 106528 | tf_op jit(solution)/shard_map/ppermute | solution.py:138
  147.8 2.8 %shard_map.262 = (f32[2,32,1024]{2,1,0:T(8,128)}, f32[2,9,32,256]{3,2,1,0:T(8,128)}, f32[2,32,1024]{2,1,0:T(8,128)}, f32[2,2,32]{2,1,0:T(2,128)}, f32[2,2,32]{2,...) custom-call(s32[1]{0:T(128)} %bitcast.refs_0_, s32[1]{0:T(128)} %bitcast.1.refs_1_, ...), custom_call_target="tpu_custom_call" | custom-call | tf_op jit(solution)/shard_map/pallas_call | solution.py:98
  (84 shorter events, 11.2 us)
Async XLA Ops:
  2.6 14.3 %collective-permute-start.3 = (bf16[32,6912]{1,0:T(8,128)(2,1)}, bf16[32,6912]{1,0:T(8,128)(2,1)}, u32[]{:S(2)}, u32[]{:S(2)}) collective-permute-start(bf16[32,6912]{1,0:T(8,128)(2,1)} %shard_map.238.refs_8_.refs_3_), channel_id=1, source_target_pairs={{0,2},{1,3},{2,0},{3,1},{4,6},{5,7},{6,4},{7,5},{8,10},{9,11},{10,... | collective-permute-start | bytes 1327112 | tf_op jit(solution)/shard_map/ppermute | solution.py:138
  5.6 21.4 %collective-permute-start.2 = (bf16[32,6912]{1,0:T(8,128)(2,1)}, bf16[32,6912]{1,0:T(8,128)(2,1)}, u32[]{:S(2)}, u32[]{:S(2)}) collective-permute-start(bf16[32,6912]{1,0:T(8,128)(2,1)} %shard_map.238.refs_8_.refs_3_), channel_id=1, source_target_pairs={{0,4},{1,5},{2,6},{3,7},{4,0},{5,1},{6,2},{7,3},{8,12},{9,13},{10,... | collective-permute-start | bytes 1327112 | tf_op jit(solution)/shard_map/ppermute | solution.py:138
  7.1 19.9 %collective-permute-start.1 = (bf16[32,6912]{1,0:T(8,128)(2,1)}, bf16[32,6912]{1,0:T(8,128)(2,1)}, u32[]{:S(2)}, u32[]{:S(2)}) collective-permute-start(bf16[32,6912]{1,0:T(8,128)(2,1)} %shard_map.238.refs_8_.refs_3_), channel_id=1, source_target_pairs={{0,6},{1,7},{2,4},{3,5},{4,2},{5,3},{6,0},{7,1},{8,14},{9,15},{10,... | collective-permute-start | bytes 1327112 | tf_op jit(solution)/shard_map/ppermute | solution.py:138
  9.2 5.5 %collective-permute-start.4 = (bf16[144,512]{1,0:T(8,128)(2,1)}, bf16[144,512]{1,0:T(8,128)(2,1)}, u32[]{:S(2)}, u32[]{:S(2)}) collective-permute-start(bf16[144,512]{1,0:T(8,128)(2,1)} %get-tuple-element.92.refs_0_), channel_id=1, source_target_pairs={{0,8},{8,0},{16,24},{24,16},{1,9},{9,1},{17,25},{25,17},{2,10},{10... | collective-permute-start | bytes 442376 | tf_op jit(solution)/shard_map/ppermute | solution.py:138
  11.3 17.5 %collective-permute-start = (bf16[32,6912]{1,0:T(8,128)(2,1)}, bf16[32,6912]{1,0:T(8,128)(2,1)}, u32[]{:S(2)}, u32[]{:S(2)}) collective-permute-start(bf16[32,6912]{1,0:T(8,128)(2,1)} %shard_map.238.refs_8_.refs_3_), channel_id=1, source_target_pairs={{0,1},{1,0},{2,3},{3,2},{4,5},{5,4},{6,7},{7,6},{8,9},{9,8},{10,11... | collective-permute-start | bytes 1327112 | tf_op jit(solution)/shard_map/ppermute | solution.py:138
  27.1 2.6 %collective-permute-start.5 = (bf16[32,6912]{1,0:T(8,128)(2,1)}, bf16[32,6912]{1,0:T(8,128)(2,1)}, u32[]{:S(2)}, u32[]{:S(2)}) collective-permute-start(bf16[32,6912]{1,0:T(8,128)(2,1)} %get-tuple-element.93.refs_5_.refs_3_), channel_id=1, source_target_pairs={{0,1},{1,0},{2,3},{3,2},{4,5},{5,4},{6,7},{7,6},{8,9},{9,8},{10,11... | collective-permute-start | bytes 1327112 | tf_op jit(solution)/shard_map/ppermute | solution.py:138
  27.1 4.1 %collective-permute-start.6 = (bf16[32,6912]{1,0:T(8,128)(2,1)}, bf16[32,6912]{1,0:T(8,128)(2,1)}, u32[]{:S(2)}, u32[]{:S(2)}) collective-permute-start(bf16[32,6912]{1,0:T(8,128)(2,1)} %get-tuple-element.94.refs_7_.refs_2_), channel_id=1, source_target_pairs={{0,1},{1,0},{2,3},{3,2},{4,5},{5,4},{6,7},{7,6},{8,9},{9,8},{10,11... | collective-permute-start | bytes 1327112 | tf_op jit(solution)/shard_map/ppermute | solution.py:138
  27.6 6.2 %collective-permute-start.7 = (bf16[32,6912]{1,0:T(8,128)(2,1)}, bf16[32,6912]{1,0:T(8,128)(2,1)}, u32[]{:S(2)}, u32[]{:S(2)}) collective-permute-start(bf16[32,6912]{1,0:T(8,128)(2,1)} %get-tuple-element.95.refs_9_.refs_1_), channel_id=1, source_target_pairs={{0,1},{1,0},{2,3},{3,2},{4,5},{5,4},{6,7},{7,6},{8,9},{9,8},{10,11... | collective-permute-start | bytes 1327112 | tf_op jit(solution)/shard_map/ppermute | solution.py:138
  27.6 19.6 %collective-permute-start.11 = (bf16[32,6912]{1,0:T(8,128)(2,1)}, bf16[32,6912]{1,0:T(8,128)(2,1)}, u32[]{:S(2)}, u32[]{:S(2)}) collective-permute-start(bf16[32,6912]{1,0:T(8,128)(2,1)} %shard_map.243.refs_4_), channel_id=1, source_target_pairs={{0,2},{1,3},{2,0},{3,1},{4,6},{5,7},{6,4},{7,5},{8,10},{9,11},{10,... | collective-permute-start | bytes 1327112 | tf_op jit(solution)/shard_map/ppermute | solution.py:138
  28.8 20.5 %collective-permute-start.10 = (bf16[32,6912]{1,0:T(8,128)(2,1)}, bf16[32,6912]{1,0:T(8,128)(2,1)}, u32[]{:S(2)}, u32[]{:S(2)}) collective-permute-start(bf16[32,6912]{1,0:T(8,128)(2,1)} %shard_map.243.refs_4_), channel_id=1, source_target_pairs={{0,4},{1,5},{2,6},{3,7},{4,0},{5,1},{6,2},{7,3},{8,12},{9,13},{10,... | collective-permute-start | bytes 1327112 | tf_op jit(solution)/shard_map/ppermute | solution.py:138
  29.7 21.2 %collective-permute-start.9 = (bf16[32,6912]{1,0:T(8,128)(2,1)}, bf16[32,6912]{1,0:T(8,128)(2,1)}, u32[]{:S(2)}, u32[]{:S(2)}) collective-permute-start(bf16[32,6912]{1,0:T(8,128)(2,1)} %shard_map.243.refs_4_), channel_id=1, source_target_pairs={{0,6},{1,7},{2,4},{3,5},{4,2},{5,3},{6,0},{7,1},{8,14},{9,15},{10,... | collective-permute-start | bytes 1327112 | tf_op jit(solution)/shard_map/ppermute | solution.py:138
  31.1 16.1 %collective-permute-start.12 = (bf16[288,512]{1,0:T(8,128)(2,1)}, bf16[288,512]{1,0:T(8,128)(2,1)}, u32[]{:S(2)}, u32[]{:S(2)}) collective-permute-start(bf16[288,512]{1,0:T(8,128)(2,1)} %shard_map.244), channel_id=1, source_target_pairs={{0,16},{8,24},{16,0},{24,8},{1,17},{9,25},{17,1},{25,9},{2,18},{10... | collective-permute-start | bytes 884744 | tf_op jit(solution)/shard_map/ppermute | solution.py:138
  33.7 17.7 %collective-permute-start.8 = (bf16[32,6912]{1,0:T(8,128)(2,1)}, bf16[32,6912]{1,0:T(8,128)(2,1)}, u32[]{:S(2)}, u32[]{:S(2)}) collective-permute-start(bf16[32,6912]{1,0:T(8,128)(2,1)} %shard_map.243.refs_4_), channel_id=1, source_target_pairs={{0,1},{1,0},{2,3},{3,2},{4,5},{5,4},{6,7},{7,6},{8,9},{9,8},{10,11... | collective-permute-start | bytes 1327112 | tf_op jit(solution)/shard_map/ppermute | solution.py:138
  50.9 2.8 %collective-permute-start.14 = (bf16[32,6912]{1,0:T(8,128)(2,1)}, bf16[32,6912]{1,0:T(8,128)(2,1)}, u32[]{:S(2)}, u32[]{:S(2)}) collective-permute-start(bf16[32,6912]{1,0:T(8,128)(2,1)} %get-tuple-element.99.refs_8_), channel_id=1, source_target_pairs={{0,1},{1,0},{2,3},{3,2},{4,5},{5,4},{6,7},{7,6},{8,9},{9,8},{10,11... | collective-permute-start | bytes 1327112 | tf_op jit(solution)/shard_map/ppermute | solution.py:138
  51.4 2.9 %collective-permute-start.15 = (bf16[32,6912]{1,0:T(8,128)(2,1)}, bf16[32,6912]{1,0:T(8,128)(2,1)}, u32[]{:S(2)}, u32[]{:S(2)}) collective-permute-start(bf16[32,6912]{1,0:T(8,128)(2,1)} %get-tuple-element.100.refs_10_), channel_id=1, source_target_pairs={{0,1},{1,0},{2,3},{3,2},{4,5},{5,4},{6,7},{7,6},{8,9},{9,8},{10,11... | collective-permute-start | bytes 1327112 | tf_op jit(solution)/shard_map/ppermute | solution.py:138
  63.5 9.5 %collective-permute-start.21 = (bf16[4,144,512]{2,1,0:T(8,128)(2,1)}, bf16[4,144,512]{2,1,0:T(8,128)(2,1)}, u32[]{:S(2)}, u32[]{:S(2)}) collective-permute-start(bf16[4,144,512]{2,1,0:T(8,128)(2,1)} %get-tuple-element.104), channel_id=1, source_target_pairs={{0,1},{1,0},{2,3},{3,2},{4,5},{5,4},{6,7},{7,6},{8,9},{9,8},{10,11... | collective-permute-start | bytes 1769480 | tf_op jit(solution)/shard_map/ppermute | solution.py:138
  67.6 7.6 %collective-permute-start.20 = (bf16[144,512]{1,0:T(8,128)(2,1)}, bf16[144,512]{1,0:T(8,128)(2,1)}, u32[]{:S(2)}, u32[]{:S(2)}) collective-permute-start(bf16[144,512]{1,0:T(8,128)(2,1)} %add_convert_fusion.6.refs_2_.refs_1_), channel_id=1, source_target_pairs={{0,2},{1,3},{2,0},{3,1},{4,6},{5,7},{6,4},{7,5},{8,10},{9,11},{10,... | collective-permute-start | bytes 442376 | tf_op jit(solution)/shard_map/ppermute | solution.py:138
  68.4 9.1 %collective-permute-start.19 = (bf16[144,512]{1,0:T(8,128)(2,1)}, bf16[144,512]{1,0:T(8,128)(2,1)}, u32[]{:S(2)}, u32[]{:S(2)}) collective-permute-start(bf16[144,512]{1,0:T(8,128)(2,1)} %add_convert_fusion.6.refs_2_.refs_1_), channel_id=1, source_target_pairs={{0,4},{1,5},{2,6},{3,7},{4,0},{5,1},{6,2},{7,3},{8,12},{9,13},{10,... | collective-permute-start | bytes 442376 | tf_op jit(solution)/shard_map/ppermute | solution.py:138
  69.9 7.6 %collective-permute-start.18 = (bf16[144,512]{1,0:T(8,128)(2,1)}, bf16[144,512]{1,0:T(8,128)(2,1)}, u32[]{:S(2)}, u32[]{:S(2)}) collective-permute-start(bf16[144,512]{1,0:T(8,128)(2,1)} %add_convert_fusion.6.refs_2_.refs_1_), channel_id=1, source_target_pairs={{0,6},{1,7},{2,4},{3,5},{4,2},{5,3},{6,0},{7,1},{8,14},{9,15},{10,... | collective-permute-start | bytes 442376 | tf_op jit(solution)/shard_map/ppermute | solution.py:138
  71.1 9.6 %collective-permute-start.17 = (bf16[144,512]{1,0:T(8,128)(2,1)}, bf16[144,512]{1,0:T(8,128)(2,1)}, u32[]{:S(2)}, u32[]{:S(2)}) collective-permute-start(bf16[144,512]{1,0:T(8,128)(2,1)} %add_convert_fusion.6.refs_2_.refs_1_), channel_id=1, source_target_pairs={{0,1},{1,0},{2,3},{3,2},{4,5},{5,4},{6,7},{7,6},{8,9},{9,8},{10,11... | collective-permute-start | bytes 442376 | tf_op jit(solution)/shard_map/ppermute | solution.py:138
  77.5 4.7 %collective-permute-start.22 = (bf16[144,512]{1,0:T(8,128)(2,1)}, bf16[144,512]{1,0:T(8,128)(2,1)}, u32[]{:S(2)}, u32[]{:S(2)}) collective-permute-start(bf16[144,512]{1,0:T(8,128)(2,1)} %get-tuple-element.105.refs_4_.refs_3_), channel_id=1, source_target_pairs={{0,1},{1,0},{2,3},{3,2},{4,5},{5,4},{6,7},{7,6},{8,9},{9,8},{10,11... | collective-permute-start | bytes 442376 | tf_op jit(solution)/shard_map/ppermute | solution.py:138
  77.5 4.7 %collective-permute-start.23 = (bf16[144,512]{1,0:T(8,128)(2,1)}, bf16[144,512]{1,0:T(8,128)(2,1)}, u32[]{:S(2)}, u32[]{:S(2)}) collective-permute-start(bf16[144,512]{1,0:T(8,128)(2,1)} %get-tuple-element.106.refs_6_.refs_2_), channel_id=1, source_target_pairs={{0,1},{1,0},{2,3},{3,2},{4,5},{5,4},{6,7},{7,6},{8,9},{9,8},{10,11... | collective-permute-start | bytes 442376 | tf_op jit(solution)/shard_map/ppermute | solution.py:138
  78.0 4.2 %collective-permute-start.24 = (bf16[144,512]{1,0:T(8,128)(2,1)}, bf16[144,512]{1,0:T(8,128)(2,1)}, u32[]{:S(2)}, u32[]{:S(2)}) collective-permute-start(bf16[144,512]{1,0:T(8,128)(2,1)} %get-tuple-element.107.refs_8_.refs_1_), channel_id=1, source_target_pairs={{0,1},{1,0},{2,3},{3,2},{4,5},{5,4},{6,7},{7,6},{8,9},{9,8},{10,11... | collective-permute-start | bytes 442376 | tf_op jit(solution)/shard_map/ppermute | solution.py:138
  78.1 12.5 %collective-permute-start.31 = (bf16[144,512]{1,0:T(8,128)(2,1)}, bf16[144,512]{1,0:T(8,128)(2,1)}, u32[]{:S(2)}, u32[]{:S(2)}) collective-permute-start(bf16[144,512]{1,0:T(8,128)(2,1)} %shard_map.254.refs_0_), channel_id=1, source_target_pairs={{0,16},{8,24},{16,0},{24,8},{1,17},{9,25},{17,1},{25,9},{2,18},{10... | collective-permute-start | bytes 442376 | tf_op jit(solution)/shard_map/ppermute | solution.py:138
  80.7 11.4 %collective-permute-start.30 = (bf16[144,512]{1,0:T(8,128)(2,1)}, bf16[144,512]{1,0:T(8,128)(2,1)}, u32[]{:S(2)}, u32[]{:S(2)}) collective-permute-start(bf16[144,512]{1,0:T(8,128)(2,1)} %shard_map.254.refs_0_), channel_id=1, source_target_pairs={{0,8},{8,0},{16,24},{24,16},{1,9},{9,1},{17,25},{25,17},{2,10},{10... | collective-permute-start | bytes 442376 | tf_op jit(solution)/shard_map/ppermute | solution.py:138
  88.0 14.0 %collective-permute-start.25 = (bf16[16,4608]{1,0:T(8,128)(2,1)}, bf16[16,4608]{1,0:T(8,128)(2,1)}, u32[]{:S(2)}, u32[]{:S(2)}) collective-permute-start(bf16[16,4608]{1,0:T(8,128)(2,1)} %get-tuple-element.117), channel_id=1, source_target_pairs={{0,8},{8,0},{16,24},{24,16},{1,9},{9,1},{17,25},{25,17},{2,10},{10... | collective-permute-start | bytes 442376 | tf_op jit(solution)/shard_map/ppermute | solution.py:138
  88.5 24.0 %collective-permute-start.39 = (bf16[432,512]{1,0:T(8,128)(2,1)}, bf16[432,512]{1,0:T(8,128)(2,1)}, u32[]{:S(2)}, u32[]{:S(2)}) collective-permute-start(bf16[432,512]{1,0:T(8,128)(2,1)} %shard_map.257.refs_13_), channel_id=1, source_target_pairs={{0,2},{1,3},{2,0},{3,1},{4,6},{5,7},{6,4},{7,5},{8,10},{9,11},{10,... | collective-permute-start | bytes 1327112 | tf_op jit(solution)/shard_map/ppermute | solution.py:138
  89.7 22.9 %collective-permute-start.38 = (bf16[432,512]{1,0:T(8,128)(2,1)}, bf16[432,512]{1,0:T(8,128)(2,1)}, u32[]{:S(2)}, u32[]{:S(2)}) collective-permute-start(bf16[432,512]{1,0:T(8,128)(2,1)} %shard_map.257.refs_13_), channel_id=1, source_target_pairs={{0,4},{1,5},{2,6},{3,7},{4,0},{5,1},{6,2},{7,3},{8,12},{9,13},{10,... | collective-permute-start | bytes 1327112 | tf_op jit(solution)/shard_map/ppermute | solution.py:138
  90.6 22.5 %collective-permute-start.37 = (bf16[432,512]{1,0:T(8,128)(2,1)}, bf16[432,512]{1,0:T(8,128)(2,1)}, u32[]{:S(2)}, u32[]{:S(2)}) collective-permute-start(bf16[432,512]{1,0:T(8,128)(2,1)} %shard_map.257.refs_13_), channel_id=1, source_target_pairs={{0,6},{1,7},{2,4},{3,5},{4,2},{5,3},{6,0},{7,1},{8,14},{9,15},{10,... | collective-permute-start | bytes 1327112 | tf_op jit(solution)/shard_map/ppermute | solution.py:138
  92.0 13.1 %collective-permute-start.32 = (bf16[144,512]{1,0:T(8,128)(2,1)}, bf16[144,512]{1,0:T(8,128)(2,1)}, u32[]{:S(2)}, u32[]{:S(2)}) collective-permute-start(bf16[144,512]{1,0:T(8,128)(2,1)} %shard_map.255), channel_id=1, source_target_pairs={{0,24},{8,16},{16,8},{24,0},{1,25},{9,17},{17,9},{25,1},{2,26},{10... | collective-permute-start | bytes 442376 | tf_op jit(solution)/shard_map/ppermute | solution.py:138
  103.7 9.9 %collective-permute-start.26 = (bf16[16,4608]{1,0:T(8,128)(2,1)}, bf16[16,4608]{1,0:T(8,128)(2,1)}, u32[]{:S(2)}, u32[]{:S(2)}) collective-permute-start(bf16[16,4608]{1,0:T(8,128)(2,1)} %add_convert_fusion.4), channel_id=1, source_target_pairs={{0,16},{8,24},{16,0},{24,8},{1,17},{9,25},{17,1},{25,9},{2,18},{10... | collective-permute-start | bytes 442376 | tf_op jit(solution)/shard_map/ppermute | solution.py:138
  105.2 8.0 %collective-permute-start.27 = (bf16[16,3328]{1,0:T(8,128)(2,1)}, bf16[16,3328]{1,0:T(8,128)(2,1)}, u32[]{:S(2)}, u32[]{:S(2)}) collective-permute-start(bf16[16,3328]{1,0:T(8,128)(2,1)} %get-tuple-element.128), channel_id=1, source_target_pairs={{0,8},{8,0},{16,24},{24,16},{1,9},{9,1},{17,25},{25,17},{2,10},{10... | collective-permute-start | bytes 319496 | tf_op jit(solution)/shard_map/ppermute | solution.py:138
  112.5 2.9 %collective-permute-start.36 = (bf16[432,512]{1,0:T(8,128)(2,1)}, bf16[432,512]{1,0:T(8,128)(2,1)}, u32[]{:S(2)}, u32[]{:S(2)}) collective-permute-start(bf16[432,512]{1,0:T(8,128)(2,1)} %shard_map.257.refs_13_), channel_id=1, source_target_pairs={{0,1},{1,0},{2,3},{3,2},{4,5},{5,4},{6,7},{7,6},{8,9},{9,8},{10,11... | collective-permute-start | bytes 1327112 | tf_op jit(solution)/shard_map/ppermute | solution.py:138
  112.6 3.2 %collective-permute-start.33 = (bf16[144,512]{1,0:T(8,128)(2,1)}, bf16[144,512]{1,0:T(8,128)(2,1)}, u32[]{:S(2)}, u32[]{:S(2)}) collective-permute-start(bf16[144,512]{1,0:T(8,128)(2,1)} %get-tuple-element.138.refs_1_), channel_id=1, source_target_pairs={{0,1},{1,0},{2,3},{3,2},{4,5},{5,4},{6,7},{7,6},{8,9},{9,8},{10,11... | collective-permute-start | bytes 442376 | tf_op jit(solution)/shard_map/ppermute | solution.py:138
  113.1 2.8 %collective-permute-start.34 = (bf16[144,512]{1,0:T(8,128)(2,1)}, bf16[144,512]{1,0:T(8,128)(2,1)}, u32[]{:S(2)}, u32[]{:S(2)}) collective-permute-start(bf16[144,512]{1,0:T(8,128)(2,1)} %get-tuple-element.139.refs_2_), channel_id=1, source_target_pairs={{0,1},{1,0},{2,3},{3,2},{4,5},{5,4},{6,7},{7,6},{8,9},{9,8},{10,11... | collective-permute-start | bytes 442376 | tf_op jit(solution)/shard_map/ppermute | solution.py:138
  113.2 4.6 %collective-permute-start.35 = (bf16[144,512]{1,0:T(8,128)(2,1)}, bf16[144,512]{1,0:T(8,128)(2,1)}, u32[]{:S(2)}, u32[]{:S(2)}) collective-permute-start(bf16[144,512]{1,0:T(8,128)(2,1)} %get-tuple-element.140.refs_3_), channel_id=1, source_target_pairs={{0,1},{1,0},{2,3},{3,2},{4,5},{5,4},{6,7},{7,6},{8,9},{9,8},{10,11... | collective-permute-start | bytes 442376 | tf_op jit(solution)/shard_map/ppermute | solution.py:138
  113.6 7.0 %collective-permute-start.40 = (bf16[432,512]{1,0:T(8,128)(2,1)}, bf16[432,512]{1,0:T(8,128)(2,1)}, u32[]{:S(2)}, u32[]{:S(2)}) collective-permute-start(bf16[432,512]{1,0:T(8,128)(2,1)} %get-tuple-element.144.refs_15_), channel_id=1, source_target_pairs={{0,1},{1,0},{2,3},{3,2},{4,5},{5,4},{6,7},{7,6},{8,9},{9,8},{10,11... | collective-permute-start | bytes 1327112 | tf_op jit(solution)/shard_map/ppermute | solution.py:138
  115.4 5.8 %collective-permute-start.41 = (bf16[432,512]{1,0:T(8,128)(2,1)}, bf16[432,512]{1,0:T(8,128)(2,1)}, u32[]{:S(2)}, u32[]{:S(2)}) collective-permute-start(bf16[432,512]{1,0:T(8,128)(2,1)} %get-tuple-element.145.refs_17_), channel_id=1, source_target_pairs={{0,1},{1,0},{2,3},{3,2},{4,5},{5,4},{6,7},{7,6},{8,9},{9,8},{10,11... | collective-permute-start | bytes 1327112 | tf_op jit(solution)/shard_map/ppermute | solution.py:138
  115.8 6.4 %collective-permute-start.42 = (bf16[432,512]{1,0:T(8,128)(2,1)}, bf16[432,512]{1,0:T(8,128)(2,1)}, u32[]{:S(2)}, u32[]{:S(2)}) collective-permute-start(bf16[432,512]{1,0:T(8,128)(2,1)} %get-tuple-element.146.refs_19_), channel_id=1, source_target_pairs={{0,1},{1,0},{2,3},{3,2},{4,5},{5,4},{6,7},{7,6},{8,9},{9,8},{10,11... | collective-permute-start | bytes 1327112 | tf_op jit(solution)/shard_map/ppermute | solution.py:138
  115.9 20.8 %collective-permute-start.29 = (bf16[16,3328]{1,0:T(8,128)(2,1)}, bf16[16,3328]{1,0:T(8,128)(2,1)}, u32[]{:S(2)}, u32[]{:S(2)}) collective-permute-start(bf16[16,3328]{1,0:T(8,128)(2,1)} %add_convert_fusion.8), channel_id=1, source_target_pairs={{0,16},{8,24},{16,0},{24,8},{1,17},{9,25},{17,1},{25,9},{2,18},{10... | collective-permute-start | bytes 319496 | tf_op jit(solution)/shard_map/ppermute | solution.py:138
  117.9 22.0 %collective-permute-start.46 = (bf16[32,1280]{1,0:T(8,128)(2,1)}, bf16[32,1280]{1,0:T(8,128)(2,1)}, u32[]{:S(2)}, u32[]{:S(2)}) collective-permute-start(bf16[32,1280]{1,0:T(8,128)(2,1)} %get-tuple-element.148), channel_id=1, source_target_pairs={{0,24},{8,16},{16,8},{24,0},{1,25},{9,17},{17,9},{25,1},{2,26},{10... | collective-permute-start | bytes 245768 | tf_op jit(solution)/shard_map/ppermute | solution.py:138
  120.6 19.7 %collective-permute-start.45 = (bf16[32,1280]{1,0:T(8,128)(2,1)}, bf16[32,1280]{1,0:T(8,128)(2,1)}, u32[]{:S(2)}, u32[]{:S(2)}) collective-permute-start(bf16[32,1280]{1,0:T(8,128)(2,1)} %get-tuple-element.148), channel_id=1, source_target_pairs={{0,16},{8,24},{16,0},{24,8},{1,17},{9,25},{17,1},{25,9},{2,18},{10... | collective-permute-start | bytes 245768 | tf_op jit(solution)/shard_map/ppermute | solution.py:138
  121.2 20.6 %collective-permute-start.44 = (bf16[32,1280]{1,0:T(8,128)(2,1)}, bf16[32,1280]{1,0:T(8,128)(2,1)}, u32[]{:S(2)}, u32[]{:S(2)}) collective-permute-start(bf16[32,1280]{1,0:T(8,128)(2,1)} %get-tuple-element.148), channel_id=1, source_target_pairs={{0,8},{8,0},{16,24},{24,16},{1,9},{9,1},{17,25},{25,17},{2,10},{10... | collective-permute-start | bytes 245768 | tf_op jit(solution)/shard_map/ppermute | solution.py:138
  122.3 20.6 %collective-permute-start.28 = (bf16[16,4608]{1,0:T(8,128)(2,1)}, bf16[16,4608]{1,0:T(8,128)(2,1)}, u32[]{:S(2)}, u32[]{:S(2)}) collective-permute-start(bf16[16,4608]{1,0:T(8,128)(2,1)} %add_convert_fusion.3.refs_2_), channel_id=1, source_target_pairs={{0,8},{8,0},{16,24},{24,16},{1,9},{9,1},{17,25},{25,17},{2,10},{10... | collective-permute-start | bytes 442376 | tf_op jit(solution)/shard_map/ppermute | solution.py:138
  138.4 8.5 %collective-permute-start.47 = (bf16[144,512]{1,0:T(8,128)(2,1)}, bf16[144,512]{1,0:T(8,128)(2,1)}, u32[]{:S(2)}, u32[]{:S(2)}) collective-permute-start(bf16[144,512]{1,0:T(8,128)(2,1)} %get-tuple-element.150), channel_id=1, source_target_pairs={{0,2},{1,3},{2,0},{3,1},{4,6},{5,7},{6,4},{7,5},{8,10},{9,11},{10,... | collective-permute-start | bytes 442376 | tf_op jit(solution)/shard_map/ppermute | solution.py:138
  139.8 8.0 %collective-permute-start.48 = (bf16[144,512]{1,0:T(8,128)(2,1)}, bf16[144,512]{1,0:T(8,128)(2,1)}, u32[]{:S(2)}, u32[]{:S(2)}) collective-permute-start(bf16[144,512]{1,0:T(8,128)(2,1)} %get-tuple-element.151), channel_id=1, source_target_pairs={{0,4},{1,5},{2,6},{3,7},{4,0},{5,1},{6,2},{7,3},{8,12},{9,13},{10,... | collective-permute-start | bytes 442376 | tf_op jit(solution)/shard_map/ppermute | solution.py:138
  140.4 7.5 %collective-permute-start.49 = (bf16[144,512]{1,0:T(8,128)(2,1)}, bf16[144,512]{1,0:T(8,128)(2,1)}, u32[]{:S(2)}, u32[]{:S(2)}) collective-permute-start(bf16[144,512]{1,0:T(8,128)(2,1)} %get-tuple-element.152), channel_id=1, source_target_pairs={{0,6},{1,7},{2,4},{3,5},{4,2},{5,3},{6,0},{7,1},{8,14},{9,15},{10,... | collective-permute-start | bytes 442376 | tf_op jit(solution)/shard_map/ppermute | solution.py:138
  141.9 5.0 %collective-permute-start.43 = (bf16[16,3328]{1,0:T(8,128)(2,1)}, bf16[16,3328]{1,0:T(8,128)(2,1)}, u32[]{:S(2)}, u32[]{:S(2)}) collective-permute-start(bf16[16,3328]{1,0:T(8,128)(2,1)} %add_convert_fusion.7.refs_4_), channel_id=1, source_target_pairs={{0,8},{8,0},{16,24},{24,16},{1,9},{9,1},{17,25},{25,17},{2,10},{10... | collective-permute-start | bytes 319496 | tf_op jit(solution)/shard_map/ppermute | solution.py:138
  (2 other events, 4.4 us)

commit v6 on v5

--- a/solution.py
+++ b/solution.py
@@ -370,7 +370,7 @@
     return field[step + 1, at : at + slots, :].astype(BF16)
 
 
-def forward_body(side, aux, x_ref, w_ref, mid_ref, out_ref, keep, field, act, finish, ready=(at_once, at_once)):
+def forward_body(side, aux, x_ref, w_ref, mid_ref, out_ref, keep, field, act, finish, ready=(at_once, at_once), between=at_once):
     u1, u2, u3, fac, pat = [item() for item in keep]
     slots = x_ref.shape[0]
     chan, mid = out_ref.shape[1], w_ref.shape[0]
@@ -406,6 +406,7 @@
 
     chunked(slots, second)
     keep[1].send()
+    between()
     u3[...] = dot_nn(act[...], w_ref[:, conv_end:expand_end])
 
     def third(rows, start, carry):
@@ -760,7 +761,7 @@
     return 0.5 * value * (1.0 + curve), slope
 
 
-def readout_body(me, readin, w1, b1, w2, cot, outs, full):
+def readout_body(me, readin, w1, b1, w2, outs, full):
     act, mine, theirs, grad, half_in, keep, send = outs
     half = full.shape[1] // 2
     core = me & 1
@@ -770,19 +771,17 @@
     hidden = dot_nn(readin[...], w1()[...]) + b1[...]
     value, slope = gelu_both(hidden)
     act[...] = value.astype(BF16)
-    grad()[...] = dot_nt(cot()[...], w2()[...])
-    grad.send()
+    width = keep.buffer.shape[2]
+    for odd, out in ((1, send), (0, keep)):
+        for q in range(out.buffer.shape[0]):
+            at = pl.ds(pl.multiple_of((me ^ (2 * q + odd)) * width, width), width)
+            out()[q] = dot_nn(act[...], w2()[:, at]).astype(BF16)
+        out.send()
     full[...] = dot_nt((slope * grad()[...]).astype(BF16), w1()[...])
     theirs()[...] = full[:, pl.ds(pl.multiple_of((1 - core) * half, half), half)].astype(BF16)
     theirs.send()
     mine()[...] = full[:, lanes]
     mine.send()
-    width = keep.buffer.shape[2]
-    for odd, out in ((1, send), (0, keep)):
-        for q in range(out.buffer.shape[0]):
-            lanes = pl.ds(pl.multiple_of((me ^ (2 * q + odd)) * width, width), width)
-            out()[q] = dot_nn(act[...], w2()[:, lanes]).astype(BF16)
-        out.send()
 
 
 def readout_shapes(rows, chan, hidden, width, n):
@@ -798,7 +797,9 @@
 
 def readout_kernel(scalars, ins, outs, plain, full, act):
     readin, w1, b1, w2, cot = ins
-    readout_body(scalars[0][0], readin(), w1, b1(), w2, cot, [act, *outs], full)
+    outs[2]()[...] = dot_nt(cot()[...], w2()[...])
+    outs[2].send()
+    readout_body(scalars[0][0], readin(), w1, b1(), w2, [act, *outs], full)
 
 
 def readout(me, readin, w1, b1, w2, cot, n):
@@ -844,11 +845,16 @@
             low_lane = 2 * LANES + low_lane
             cot[row : row + 16, lanes] = stage[r, low_row : low_row + 16, low_lane : low_lane + LANES]
     cot_out.send()
-    forward_body(side, aux, x, *sources, keep, field, act, readin(), ready)
+
+    def between():
+        rest[2]()[...] = dot_nt(cot[...], w2()[...])
+        rest[2].send()
+
+    forward_body(side, aux, x, *sources, keep, field, act, readin(), ready, between)
     readin.send()
     for item in outs[:3]:
         item.send()
-    readout_body(me, readin(), w1, b1, w2, cot_out, [hid, *rest], full)
+    readout_body(me, readin(), w1, b1, w2, [hid, *rest], full)
 
 
 def second_forward(side, chan, mid, me, aux, x, pieces, w1, b1, w2):
@@ -933,7 +939,7 @@
     rows, chan = readin.shape
     total = rows + sum(x.shape[0] for x in parts) // 2
     hidden, width = w2.shape
-    chunk = min(width, 1024)
+    chunk = min(width, 2048)
     return call(
         functools.partial(tail_kernel, placed, len(parts)),
         [sds((chan, hidden), F32), sds((1, hidden), F32), sds((1, width // n), F32), sds((hidden, width), F32)],

time: 151 us -> 151 us (level)
  no operation moved by 1% of the time
where the time goes in v6:
time: 151 us; the launch traced here: 150 us
  Pallas kernels  63.2 us (42%)
  starting transfers between devices  42.9 us (28%)
  waiting for transfers between devices  31.9 us (21%)
  other arithmetic  10.5 us (7%)
  between operations  1.7 us (1%)
    pallas_call x12, Pallas kernels, call(): pl.pallas_call(kernel, out_shape=list(outs), in_specs=[SMEM] * len(scalar...  63.1 us
    ppermute x50, starting transfers between devices, ppermute_xor(): lax.ppermute(x, axis, [(i, i ^ mask) for i in range(lax.axis_size(axis))])  42.9 us
    ppermute x50, waiting for transfers between devices, ppermute_xor(): lax.ppermute(x, axis, [(i, i ^ mask) for i in range(lax.axis_size(axis))])  31.9 us
    convert_element_type x6, other arithmetic, summed(): return (left.astype(F32) + right.astype(F32)).astype(BF16)  10.5 us
  transfers between devices with their start and end apart: 50, of which 13 were waited for; matrix products, arithmetic and copies ran while one was open for 7% of the time, Pallas kernels for 33%

profile of v6, /device:TPU:0, one launch (start us, length us, event | category | flops | bytes accessed | tf_op | source)
XLA Modules:
  0.0 150.2 jit_solution(9695108459924498948)
XLA Ops:
  0.6 2.0 %shard_map.238.refs_8_.refs_3_ = bf16[32,6912]{1,0:T(8,128)(2,1)} custom-call(bf16[576,128]{1,0:T(8,128)(2,1)} %bitcast.34, f32[2,2,32]{2,1,0:T(2,128)} %refs_1_.3, f32[2,2,32]{2,1,0:T(2,128)} %refs_2_.3, f32[2,128]{1,0:T(2,128)} %refs_3_.3, f32[2,128]{1,0:T(2,128)} %refs_4_.3, bf16[2,32,1024]{2,1,0:T(8,128)(2,1)} %bitcast.32, ...), custom_call_target="tpu_custom_call" | custom-call | tf_op jit(solution)/shard_map/pallas_call | solution.py:98
  2.6 3.0 %collective-permute-start.3 = (bf16[32,6912]{1,0:T(8,128)(2,1)}, bf16[32,6912]{1,0:T(8,128)(2,1)}, u32[]{:S(2)}, u32[]{:S(2)}) collective-permute-start(bf16[32,6912]{1,0:T(8,128)(2,1)} %shard_map.238.refs_8_.refs_3_), channel_id=1, source_target_pairs={{0,2},{1,3},{2,0},{3,1},{4,6},{5,7},{6,4},{7,5},{8,10},{9,11},{10,... | collective-permute-start | bytes 1327112 | tf_op jit(solution)/shard_map/ppermute | solution.py:138
  5.6 1.5 %collective-permute-start.2 = (bf16[32,6912]{1,0:T(8,128)(2,1)}, bf16[32,6912]{1,0:T(8,128)(2,1)}, u32[]{:S(2)}, u32[]{:S(2)}) collective-permute-start(bf16[32,6912]{1,0:T(8,128)(2,1)} %shard_map.238.refs_8_.refs_3_), channel_id=1, source_target_pairs={{0,4},{1,5},{2,6},{3,7},{4,0},{5,1},{6,2},{7,3},{8,12},{9,13},{10,... | collective-permute-start | bytes 1327112 | tf_op jit(solution)/shard_map/ppermute | solution.py:138
  7.2 2.0 %shard_map.239 = (bf16[32,6912]{1,0:T(8,128)(2,1)}, bf16[144,512]{1,0:T(8,128)(2,1)}) custom-call(bf16[144,512]{1,0:T(8,128)(2,1)} %bitcast.35, f32[2,2,32]{2,1,0:T(2,128)} %refs_1_.3, f32[2,2,32]{2,1,0:T(2,128)} %refs_2_.3, f32[2,128]{1,0:T(2,128)} %refs_3_.3, f32[2,128]{1,0:T(2,128)} %refs_4_.3, bf16[2,32,1024]{2,1,0:T(8,128)(2,1)} %bitcast.33, ...), custom_call_target="tpu_custom_call" | custom-call | tf_op jit(solution)/shard_map/pallas_call | solution.py:98
  9.2 2.1 %collective-permute-start.4 = (bf16[144,512]{1,0:T(8,128)(2,1)}, bf16[144,512]{1,0:T(8,128)(2,1)}, u32[]{:S(2)}, u32[]{:S(2)}) collective-permute-start(bf16[144,512]{1,0:T(8,128)(2,1)} %get-tuple-element.92.refs_0_), channel_id=1, source_target_pairs={{0,8},{8,0},{16,24},{24,16},{1,9},{9,1},{17,25},{25,17},{2,10},{10... | collective-permute-start | bytes 442376 | tf_op jit(solution)/shard_map/ppermute | solution.py:138
  11.9 1.1 shard_map.237
  13.0 1.7 %collective-permute-done.4.refs_1_.refs_4_.refs_0_ = bf16[144,512]{1,0:T(8,128)(2,1)} collective-permute-done((bf16[144,512]{1,0:T(8,128)(2,1)}, bf16[144,512]{1,0:T(8,128)(2,1)}, u32[]{:S(2)}, u32[]{:S(2)}) %collective-permute-start.4) | collective-permute-done | bytes 147488 | tf_op jit(solution)/shard_map/ppermute | solution.py:138
  14.7 1.7 %shard_map.240.refs_3_.refs_0_ = bf16[288,512]{1,0:T(8,128)(2,1)} custom-call(bf16[144,512]{1,0:T(8,128)(2,1)} %get-tuple-element.92.refs_0_, bf16[144,512]{1,0:T(8,128)(2,1)} %collective-permute-done.4.refs_1_.refs_4_.refs_0_), custom_call_target="tpu_custom_call" | custom-call | tf_op jit(solution)/shard_map/pallas_call | solution.py:98
  16.9 10.1 %collective-permute-done.2.refs_1_ = bf16[32,6912]{1,0:T(8,128)(2,1)} collective-permute-done((bf16[32,6912]{1,0:T(8,128)(2,1)}, bf16[32,6912]{1,0:T(8,128)(2,1)}, u32[]{:S(2)}, u32[]{:S(2)}) %collective-permute-start.2) | collective-permute-done | bytes 442400 | tf_op jit(solution)/shard_map/ppermute | solution.py:138
  27.6 1.2 collective-permute-start.11
  29.7 1.4 collective-permute-start.9
  31.1 2.6 %collective-permute-start.12 = (bf16[288,512]{1,0:T(8,128)(2,1)}, bf16[288,512]{1,0:T(8,128)(2,1)}, u32[]{:S(2)}, u32[]{:S(2)}) collective-permute-start(bf16[288,512]{1,0:T(8,128)(2,1)} %shard_map.244), channel_id=1, source_target_pairs={{0,16},{8,24},{16,0},{24,8},{1,17},{9,25},{17,1},{25,9},{2,18},{10... | collective-permute-start | bytes 884744 | tf_op jit(solution)/shard_map/ppermute | solution.py:138
  33.7 9.6 %shard_map.242 = (bf16[576,1024]{1,0:T(8,128)(2,1)}, bf16[256,4352]{1,0:T(8,128)(2,1)}, f32[8,256]{1,0:T(8,128)}, f32[8,1024]{1,0:T(8,128)}, bf16[144,1024]{1,0:...) custom-call(s32[1]{0:T(128)} %bitcast.refs_0_, ...), custom_call_target="tpu_custom_call" | custom-call | tf_op jit(solution)/shard_map/pallas_call | solution.py:98
  43.4 3.8 %collective-permute-done.12.refs_5_.refs_1_ = bf16[288,512]{1,0:T(8,128)(2,1)} collective-permute-done((bf16[288,512]{1,0:T(8,128)(2,1)}, bf16[288,512]{1,0:T(8,128)(2,1)}, u32[]{:S(2)}, u32[]{:S(2)}) %collective-permute-start.12) | collective-permute-done | bytes 294944 | tf_op jit(solution)/shard_map/ppermute | solution.py:138
  47.2 2.1 %collective-permute-done.10.refs_1_ = bf16[32,6912]{1,0:T(8,128)(2,1)} collective-permute-done((bf16[32,6912]{1,0:T(8,128)(2,1)}, bf16[32,6912]{1,0:T(8,128)(2,1)}, u32[]{:S(2)}, u32[]{:S(2)}) %collective-permute-start.10) | collective-permute-done | bytes 442400 | tf_op jit(solution)/shard_map/ppermute | solution.py:138
  49.3 1.6 %collective-permute-done.9.refs_0_ = bf16[32,6912]{1,0:T(8,128)(2,1)} collective-permute-done((bf16[32,6912]{1,0:T(8,128)(2,1)}, bf16[32,6912]{1,0:T(8,128)(2,1)}, u32[]{:S(2)}, u32[]{:S(2)}) %collective-permute-start.9) | collective-permute-done | bytes 442400 | tf_op jit(solution)/shard_map/ppermute | solution.py:138
  51.4 1.6 %collective-permute-done.13.refs_7_ = bf16[32,6912]{1,0:T(8,128)(2,1)} collective-permute-done((bf16[32,6912]{1,0:T(8,128)(2,1)}, bf16[32,6912]{1,0:T(8,128)(2,1)}, u32[]{:S(2)}, u32[]{:S(2)}) %collective-permute-start.13) | collective-permute-done | bytes 442400 | tf_op jit(solution)/shard_map/ppermute | solution.py:138
  54.3 9.4 %shard_map.246 = (bf16[256,4352]{1,0:T(8,128)(2,1)}, f32[8,256]{1,0:T(8,128)}, f32[8,1024]{1,0:T(8,128)}, bf16[144,1024]{1,0:T(8,128)(2,1)}, f32[144,256]{1,0:T(...) custom-call(s32[1]{0:T(128)} %bitcast.refs_0_, ...), custom_call_target="tpu_custom_call" | custom-call | tf_op jit(solution)/shard_map/pallas_call | solution.py:98
  64.2 1.9 %collective-permute-done.16 = bf16[144,512]{1,0:T(8,128)(2,1)S(1)} collective-permute-done((bf16[144,512]{1,0:T(8,128)(2,1)}, bf16[144,512]{1,0:T(8,128)(2,1)S(1)}, u32[]{:S(2)}, u32[]{:S(2)}) %collective-permute-start.16) | collective-permute-done | bytes 147488 | tf_op jit(solution)/shard_map/ppermute | solution.py:138
  66.2 1.7 %add_convert_fusion.6.refs_2_.refs_1_ = bf16[144,512]{1,0:T(8,128)(2,1)} fusion(f32[144,512]{1,0:T(8,128)} %get-tuple-element.101, bf16[144,512]{1,0:T(8,128)(2,1)S(1)} %collective-permute-done.16), kind=kLoop, calls=%fused_computation.6 | loop fusion | flops 221184 | bytes 589824 | tf_op jit(solution)/shard_map/convert_element_type | solution.py:179
  68.6 1.5 %collective-permute-start.19 = (bf16[144,512]{1,0:T(8,128)(2,1)}, bf16[144,512]{1,0:T(8,128)(2,1)}, u32[]{:S(2)}, u32[]{:S(2)}) collective-permute-start(bf16[144,512]{1,0:T(8,128)(2,1)} %add_convert_fusion.6.refs_2_.refs_1_), channel_id=1, source_target_pairs={{0,4},{1,5},{2,6},{3,7},{4,0},{5,1},{6,2},{7,3},{8,12},{9,13},{10,... | collective-permute-start | bytes 442376 | tf_op jit(solution)/shard_map/ppermute | solution.py:138
  70.1 1.2 collective-permute-start.18
  71.3 1.9 %shard_map.247.refs_3_.refs_0_ = bf16[432,512]{1,0:T(8,128)(2,1)} custom-call(bf16[144,512]{1,0:T(8,128)(2,1)} %collective-permute-done.4.refs_1_.refs_4_.refs_0_, bf16[288,512]{1,0:T(8,128)(2,1)} %collective-permute-done.12.refs_5_.refs_1_, bf16[144,512]{1,0:T(8,128)(2,1)} %add_convert_fusion.6.refs_2_.refs_1_), custom_call_target="tpu_custom_call" | custom-call | tf_op jit(solution)/shard_map/pallas_call | solution.py:98
  73.2 2.2 %fusion.3 = (bf16[144,512]{1,0:T(8,128)(2,1)}, bf16[144,512]{1,0:T(8,128)(2,1)}, bf16[144,512]{1,0:T(8,128)(2,1)}, bf16[144,512]{1,0:T(8,128)(2,1)}) fusion(bf16[4,144,512]{2,1,0:T(8,128)(2,1)} %collective-permute-done.21, bf16[4,144,512]{2,1,0:T(8,128)(2,1)} %get-tuple-element.103), kind=kLoop, calls=%fused_computation.12 | loop fusion | flops 1179648 | bytes 1769472 | tf_op jit(solution)/shard_map/convert_element_type | solution.py:179
  75.4 2.3 %collective-permute-done.19.refs_1_ = bf16[144,512]{1,0:T(8,128)(2,1)} collective-permute-done((bf16[144,512]{1,0:T(8,128)(2,1)}, bf16[144,512]{1,0:T(8,128)(2,1)}, u32[]{:S(2)}, u32[]{:S(2)}) %collective-permute-start.19) | collective-permute-done | bytes 147488 | tf_op jit(solution)/shard_map/ppermute | solution.py:138
  78.3 2.6 %collective-permute-start.31 = (bf16[144,512]{1,0:T(8,128)(2,1)}, bf16[144,512]{1,0:T(8,128)(2,1)}, u32[]{:S(2)}, u32[]{:S(2)}) collective-permute-start(bf16[144,512]{1,0:T(8,128)(2,1)} %shard_map.254.refs_0_), channel_id=1, source_target_pairs={{0,16},{8,24},{16,0},{24,8},{1,17},{9,25},{17,1},{25,9},{2,18},{10... | collective-permute-start | bytes 442376 | tf_op jit(solution)/shard_map/ppermute | solution.py:138
  80.9 1.6 %collective-permute-start.30 = (bf16[144,512]{1,0:T(8,128)(2,1)}, bf16[144,512]{1,0:T(8,128)(2,1)}, u32[]{:S(2)}, u32[]{:S(2)}) collective-permute-start(bf16[144,512]{1,0:T(8,128)(2,1)} %shard_map.254.refs_0_), channel_id=1, source_target_pairs={{0,8},{8,0},{16,24},{24,16},{1,9},{9,1},{17,25},{25,17},{2,10},{10... | collective-permute-start | bytes 442376 | tf_op jit(solution)/shard_map/ppermute | solution.py:138
  82.5 5.8 %shard_map.249 = (bf16[144,1024]{1,0:T(8,128)(2,1)}, f32[16,4608]{1,0:T(8,128)}, bf16[16,4608]{1,0:T(8,128)(2,1)}, f32[8,1024]{1,0:T(8,128)}) custom-call(s32[1]{0:T(128)} %bitcast.refs_0_, s32[1]{0:T(128)} %bitcast.1.refs_1_, bf16[144,512]{1,0:T(8,128)(2,1)} %add_convert_fusion.6.refs_2_.refs_1_, bf16[144,512]{1,0:T(8,128)(2,1)} %collective-permute-done.17.refs_3_, ...), custom_call_target="tpu_custom_call" | custom-call | tf_op jit(solution)/shard_map/pallas_call | solution.py:98
  88.7 1.2 collective-permute-start.39
  90.8 1.4 collective-permute-start.37
  92.2 1.6 %collective-permute-start.32 = (bf16[144,512]{1,0:T(8,128)(2,1)}, bf16[144,512]{1,0:T(8,128)(2,1)}, u32[]{:S(2)}, u32[]{:S(2)}) collective-permute-start(bf16[144,512]{1,0:T(8,128)(2,1)} %shard_map.255), channel_id=1, source_target_pairs={{0,24},{8,16},{16,8},{24,0},{1,25},{9,17},{17,9},{25,1},{2,26},{10... | collective-permute-start | bytes 442376 | tf_op jit(solution)/shard_map/ppermute | solution.py:138
  93.8 8.4 %shard_map.250 = (f32[16,3328]{1,0:T(8,128)}, bf16[16,3328]{1,0:T(8,128)(2,1)}, f32[576,256]{1,0:T(8,128)}, f32[576,128]{1,0:T(8,128)}, f32[8,256]{1,0:T(8,128)}, /*index=5*/f32[8,1024]{1,0:T(8,128)}) custom-call(s32[1]{0:T(128)} %bitcast.refs_0_, s32[1]{0:T(128)} %bitcast.1.refs_1_, f32[576,128]{1,0:T(8,128)} %get-tuple-element.90.refs_1_.refs_2_, ...), custom_call_target="tpu_custom_call" | custom-call | tf_op jit(solution)/shard_map/pallas_call | solution.py:98
  102.2 1.7 %add_convert_fusion.4 = bf16[16,4608]{1,0:T(8,128)(2,1)} fusion(f32[16,4608]{1,0:T(8,128)} %get-tuple-element.116, bf16[16,4608]{1,0:T(8,128)(2,1)} %shard_map.251), kind=kLoop, calls=%fused_computation.4 | loop fusion | flops 221184 | bytes 589824 | tf_op jit(solution)/shard_map/convert_element_type | solution.py:179
  103.9 1.4 collective-permute-start.26
  105.4 1.3 collective-permute-start.27
  106.7 6.0 %shard_map.252 = (f32[576,128]{1,0:T(8,128)}, f32[32,1280]{1,0:T(8,128)}, bf16[32,1280]{1,0:T(8,128)(2,1)}) custom-call(s32[1]{0:T(128)} %bitcast.refs_0_, f32[576,128]{1,0:T(8,128)} %get-tuple-element.90.refs_1_.refs_2_, f32[576,256]{1,0:T(8,128)} %get-tuple-element.127.refs_1_.refs_2_.refs_3_, bf16[256,4352]{1,0:T(8,128)(2,1)} %get-tuple-element.125.refs_11_.refs_3_, ...), custom_call_target="tpu_custom_call" | custom-call | tf_op jit(solution)/shard_map/pallas_call | solution.py:98
  113.9 1.7 %add_convert_fusion.8 = bf16[16,3328]{1,0:T(8,128)(2,1)} fusion(f32[16,3328]{1,0:T(8,128)} %get-tuple-element.135, bf16[16,3328]{1,0:T(8,128)(2,1)} %get-tuple-element.136), kind=kLoop, calls=%fused_computation.8 | loop fusion | flops 159744 | bytes 425984 | tf_op jit(solution)/shard_map/convert_element_type | solution.py:179
  116.4 1.7 %add_convert_fusion.3.refs_2_ = bf16[16,4608]{1,0:T(8,128)(2,1)} fusion(bf16[16,4608]{1,0:T(8,128)(2,1)} %get-tuple-element.134, bf16[16,4608]{1,0:T(8,128)(2,1)} %add_convert_fusion.4), kind=kLoop, calls=%fused_computation.3 | loop fusion | flops 294912 | bytes 442368 | tf_op jit(solution)/shard_map/convert_element_type | solution.py:179
  118.1 2.8 %collective-permute-start.46 = (bf16[32,1280]{1,0:T(8,128)(2,1)}, bf16[32,1280]{1,0:T(8,128)(2,1)}, u32[]{:S(2)}, u32[]{:S(2)}) collective-permute-start(bf16[32,1280]{1,0:T(8,128)(2,1)} %get-tuple-element.148), channel_id=1, source_target_pairs={{0,24},{8,16},{16,8},{24,0},{1,25},{9,17},{17,9},{25,1},{2,26},{10... | collective-permute-start | bytes 245768 | tf_op jit(solution)/shard_map/ppermute | solution.py:138
  121.4 1.0 collective-permute-start.44
  122.5 1.0 collective-permute-start.28
  123.5 12.6 %shard_map.259 = (f32[1024,512]{1,0:T(8,128)}, f32[1,512]{1,0:T(1,128)}, f32[1,512]{1,0:T(1,128)}, f32[512,4096]{1,0:T(8,128)}) custom-call(s32[1]{0:T(128)} %bitcast.refs_0_, bf16[144,512]{1,0:T(8,128)(2,1)} %get-tuple-element.138.refs_1_, bf16[144,512]{1,0:T(8,128)(2,1)} %get-tuple-element.139.refs_2_, bf16[144,512]{1,0:T(8,128)(2,1)} %get-tuple-element.140.refs_3_, ...), custom_call_target="tpu_custom_call" | custom-call | tf_op jit(solution)/shard_map/pallas_call | solution.py:98
  136.1 1.6 %add_convert_fusion.7.refs_4_ = bf16[16,3328]{1,0:T(8,128)(2,1)} fusion(bf16[16,3328]{1,0:T(8,128)(2,1)} %shard_map.260, bf16[16,3328]{1,0:T(8,128)(2,1)} %add_convert_fusion.8), kind=kLoop, calls=%fused_computation.7 | loop fusion | flops 212992 | bytes 319488 | tf_op jit(solution)/shard_map/convert_element_type | solution.py:179
  137.7 1.5 collective-permute-start.47
  139.7 1.5 %collective-permute-start.49 = (bf16[144,512]{1,0:T(8,128)(2,1)}, bf16[144,512]{1,0:T(8,128)(2,1)}, u32[]{:S(2)}, u32[]{:S(2)}) collective-permute-start(bf16[144,512]{1,0:T(8,128)(2,1)} %get-tuple-element.152), channel_id=1, source_target_pairs={{0,6},{1,7},{2,4},{3,5},{4,2},{5,3},{6,0},{7,1},{8,14},{9,15},{10,... | collective-permute-start | bytes 442376 | tf_op jit(solution)/shard_map/ppermute | solution.py:138
  141.2 1.0 collective-permute-start.43
  142.3 4.0 %collective-permute-done.43.refs_5_ = bf16[16,3328]{1,0:T(8,128)(2,1)} collective-permute-done((bf16[16,3328]{1,0:T(8,128)(2,1)}, bf16[16,3328]{1,0:T(8,128)(2,1)}, u32[]{:S(2)}, u32[]{:S(2)}) %collective-permute-start.43) | collective-permute-done | bytes 106528 | tf_op jit(solution)/shard_map/ppermute | solution.py:138
  147.2 2.8 %shard_map.262 = (f32[2,32,1024]{2,1,0:T(8,128)}, f32[2,9,32,256]{3,2,1,0:T(8,128)}, f32[2,32,1024]{2,1,0:T(8,128)}, f32[2,2,32]{2,1,0:T(2,128)}, f32[2,2,32]{2,...) custom-call(s32[1]{0:T(128)} %bitcast.refs_0_, s32[1]{0:T(128)} %bitcast.1.refs_1_, ...), custom_call_target="tpu_custom_call" | custom-call | tf_op jit(solution)/shard_map/pallas_call | solution.py:98
  (84 shorter events, 11.2 us)
Async XLA Ops:
  2.6 14.3 %collective-permute-start.3 = (bf16[32,6912]{1,0:T(8,128)(2,1)}, bf16[32,6912]{1,0:T(8,128)(2,1)}, u32[]{:S(2)}, u32[]{:S(2)}) collective-permute-start(bf16[32,6912]{1,0:T(8,128)(2,1)} %shard_map.238.refs_8_.refs_3_), channel_id=1, source_target_pairs={{0,2},{1,3},{2,0},{3,1},{4,6},{5,7},{6,4},{7,5},{8,10},{9,11},{10,... | collective-permute-start | bytes 1327112 | tf_op jit(solution)/shard_map/ppermute | solution.py:138
  5.6 21.4 %collective-permute-start.2 = (bf16[32,6912]{1,0:T(8,128)(2,1)}, bf16[32,6912]{1,0:T(8,128)(2,1)}, u32[]{:S(2)}, u32[]{:S(2)}) collective-permute-start(bf16[32,6912]{1,0:T(8,128)(2,1)} %shard_map.238.refs_8_.refs_3_), channel_id=1, source_target_pairs={{0,4},{1,5},{2,6},{3,7},{4,0},{5,1},{6,2},{7,3},{8,12},{9,13},{10,... | collective-permute-start | bytes 1327112 | tf_op jit(solution)/shard_map/ppermute | solution.py:138
  7.1 19.9 %collective-permute-start.1 = (bf16[32,6912]{1,0:T(8,128)(2,1)}, bf16[32,6912]{1,0:T(8,128)(2,1)}, u32[]{:S(2)}, u32[]{:S(2)}) collective-permute-start(bf16[32,6912]{1,0:T(8,128)(2,1)} %shard_map.238.refs_8_.refs_3_), channel_id=1, source_target_pairs={{0,6},{1,7},{2,4},{3,5},{4,2},{5,3},{6,0},{7,1},{8,14},{9,15},{10,... | collective-permute-start | bytes 1327112 | tf_op jit(solution)/shard_map/ppermute | solution.py:138
  9.2 5.5 %collective-permute-start.4 = (bf16[144,512]{1,0:T(8,128)(2,1)}, bf16[144,512]{1,0:T(8,128)(2,1)}, u32[]{:S(2)}, u32[]{:S(2)}) collective-permute-start(bf16[144,512]{1,0:T(8,128)(2,1)} %get-tuple-element.92.refs_0_), channel_id=1, source_target_pairs={{0,8},{8,0},{16,24},{24,16},{1,9},{9,1},{17,25},{25,17},{2,10},{10... | collective-permute-start | bytes 442376 | tf_op jit(solution)/shard_map/ppermute | solution.py:138
  11.3 17.5 %collective-permute-start = (bf16[32,6912]{1,0:T(8,128)(2,1)}, bf16[32,6912]{1,0:T(8,128)(2,1)}, u32[]{:S(2)}, u32[]{:S(2)}) collective-permute-start(bf16[32,6912]{1,0:T(8,128)(2,1)} %shard_map.238.refs_8_.refs_3_), channel_id=1, source_target_pairs={{0,1},{1,0},{2,3},{3,2},{4,5},{5,4},{6,7},{7,6},{8,9},{9,8},{10,11... | collective-permute-start | bytes 1327112 | tf_op jit(solution)/shard_map/ppermute | solution.py:138
  27.1 2.6 %collective-permute-start.5 = (bf16[32,6912]{1,0:T(8,128)(2,1)}, bf16[32,6912]{1,0:T(8,128)(2,1)}, u32[]{:S(2)}, u32[]{:S(2)}) collective-permute-start(bf16[32,6912]{1,0:T(8,128)(2,1)} %get-tuple-element.93.refs_5_.refs_3_), channel_id=1, source_target_pairs={{0,1},{1,0},{2,3},{3,2},{4,5},{5,4},{6,7},{7,6},{8,9},{9,8},{10,11... | collective-permute-start | bytes 1327112 | tf_op jit(solution)/shard_map/ppermute | solution.py:138
  27.1 4.1 %collective-permute-start.6 = (bf16[32,6912]{1,0:T(8,128)(2,1)}, bf16[32,6912]{1,0:T(8,128)(2,1)}, u32[]{:S(2)}, u32[]{:S(2)}) collective-permute-start(bf16[32,6912]{1,0:T(8,128)(2,1)} %get-tuple-element.94.refs_7_.refs_2_), channel_id=1, source_target_pairs={{0,1},{1,0},{2,3},{3,2},{4,5},{5,4},{6,7},{7,6},{8,9},{9,8},{10,11... | collective-permute-start | bytes 1327112 | tf_op jit(solution)/shard_map/ppermute | solution.py:138
  27.6 6.2 %collective-permute-start.7 = (bf16[32,6912]{1,0:T(8,128)(2,1)}, bf16[32,6912]{1,0:T(8,128)(2,1)}, u32[]{:S(2)}, u32[]{:S(2)}) collective-permute-start(bf16[32,6912]{1,0:T(8,128)(2,1)} %get-tuple-element.95.refs_9_.refs_1_), channel_id=1, source_target_pairs={{0,1},{1,0},{2,3},{3,2},{4,5},{5,4},{6,7},{7,6},{8,9},{9,8},{10,11... | collective-permute-start | bytes 1327112 | tf_op jit(solution)/shard_map/ppermute | solution.py:138
  27.6 19.6 %collective-permute-start.11 = (bf16[32,6912]{1,0:T(8,128)(2,1)}, bf16[32,6912]{1,0:T(8,128)(2,1)}, u32[]{:S(2)}, u32[]{:S(2)}) collective-permute-start(bf16[32,6912]{1,0:T(8,128)(2,1)} %shard_map.243.refs_4_), channel_id=1, source_target_pairs={{0,2},{1,3},{2,0},{3,1},{4,6},{5,7},{6,4},{7,5},{8,10},{9,11},{10,... | collective-permute-start | bytes 1327112 | tf_op jit(solution)/shard_map/ppermute | solution.py:138
  28.8 20.5 %collective-permute-start.10 = (bf16[32,6912]{1,0:T(8,128)(2,1)}, bf16[32,6912]{1,0:T(8,128)(2,1)}, u32[]{:S(2)}, u32[]{:S(2)}) collective-permute-start(bf16[32,6912]{1,0:T(8,128)(2,1)} %shard_map.243.refs_4_), channel_id=1, source_target_pairs={{0,4},{1,5},{2,6},{3,7},{4,0},{5,1},{6,2},{7,3},{8,12},{9,13},{10,... | collective-permute-start | bytes 1327112 | tf_op jit(solution)/shard_map/ppermute | solution.py:138
  29.7 21.2 %collective-permute-start.9 = (bf16[32,6912]{1,0:T(8,128)(2,1)}, bf16[32,6912]{1,0:T(8,128)(2,1)}, u32[]{:S(2)}, u32[]{:S(2)}) collective-permute-start(bf16[32,6912]{1,0:T(8,128)(2,1)} %shard_map.243.refs_4_), channel_id=1, source_target_pairs={{0,6},{1,7},{2,4},{3,5},{4,2},{5,3},{6,0},{7,1},{8,14},{9,15},{10,... | collective-permute-start | bytes 1327112 | tf_op jit(solution)/shard_map/ppermute | solution.py:138
  31.1 16.1 %collective-permute-start.12 = (bf16[288,512]{1,0:T(8,128)(2,1)}, bf16[288,512]{1,0:T(8,128)(2,1)}, u32[]{:S(2)}, u32[]{:S(2)}) collective-permute-start(bf16[288,512]{1,0:T(8,128)(2,1)} %shard_map.244), channel_id=1, source_target_pairs={{0,16},{8,24},{16,0},{24,8},{1,17},{9,25},{17,1},{25,9},{2,18},{10... | collective-permute-start | bytes 884744 | tf_op jit(solution)/shard_map/ppermute | solution.py:138
  33.7 17.7 %collective-permute-start.8 = (bf16[32,6912]{1,0:T(8,128)(2,1)}, bf16[32,6912]{1,0:T(8,128)(2,1)}, u32[]{:S(2)}, u32[]{:S(2)}) collective-permute-start(bf16[32,6912]{1,0:T(8,128)(2,1)} %shard_map.243.refs_4_), channel_id=1, source_target_pairs={{0,1},{1,0},{2,3},{3,2},{4,5},{5,4},{6,7},{7,6},{8,9},{9,8},{10,11... | collective-permute-start | bytes 1327112 | tf_op jit(solution)/shard_map/ppermute | solution.py:138
  50.9 2.8 %collective-permute-start.14 = (bf16[32,6912]{1,0:T(8,128)(2,1)}, bf16[32,6912]{1,0:T(8,128)(2,1)}, u32[]{:S(2)}, u32[]{:S(2)}) collective-permute-start(bf16[32,6912]{1,0:T(8,128)(2,1)} %get-tuple-element.99.refs_8_), channel_id=1, source_target_pairs={{0,1},{1,0},{2,3},{3,2},{4,5},{5,4},{6,7},{7,6},{8,9},{9,8},{10,11... | collective-permute-start | bytes 1327112 | tf_op jit(solution)/shard_map/ppermute | solution.py:138
  51.4 2.9 %collective-permute-start.15 = (bf16[32,6912]{1,0:T(8,128)(2,1)}, bf16[32,6912]{1,0:T(8,128)(2,1)}, u32[]{:S(2)}, u32[]{:S(2)}) collective-permute-start(bf16[32,6912]{1,0:T(8,128)(2,1)} %get-tuple-element.100.refs_10_), channel_id=1, source_target_pairs={{0,1},{1,0},{2,3},{3,2},{4,5},{5,4},{6,7},{7,6},{8,9},{9,8},{10,11... | collective-permute-start | bytes 1327112 | tf_op jit(solution)/shard_map/ppermute | solution.py:138
  63.7 9.5 %collective-permute-start.21 = (bf16[4,144,512]{2,1,0:T(8,128)(2,1)}, bf16[4,144,512]{2,1,0:T(8,128)(2,1)}, u32[]{:S(2)}, u32[]{:S(2)}) collective-permute-start(bf16[4,144,512]{2,1,0:T(8,128)(2,1)} %get-tuple-element.104), channel_id=1, source_target_pairs={{0,1},{1,0},{2,3},{3,2},{4,5},{5,4},{6,7},{7,6},{8,9},{9,8},{10,11... | collective-permute-start | bytes 1769480 | tf_op jit(solution)/shard_map/ppermute | solution.py:138
  67.8 7.6 %collective-permute-start.20 = (bf16[144,512]{1,0:T(8,128)(2,1)}, bf16[144,512]{1,0:T(8,128)(2,1)}, u32[]{:S(2)}, u32[]{:S(2)}) collective-permute-start(bf16[144,512]{1,0:T(8,128)(2,1)} %add_convert_fusion.6.refs_2_.refs_1_), channel_id=1, source_target_pairs={{0,2},{1,3},{2,0},{3,1},{4,6},{5,7},{6,4},{7,5},{8,10},{9,11},{10,... | collective-permute-start | bytes 442376 | tf_op jit(solution)/shard_map/ppermute | solution.py:138
  68.6 9.1 %collective-permute-start.19 = (bf16[144,512]{1,0:T(8,128)(2,1)}, bf16[144,512]{1,0:T(8,128)(2,1)}, u32[]{:S(2)}, u32[]{:S(2)}) collective-permute-start(bf16[144,512]{1,0:T(8,128)(2,1)} %add_convert_fusion.6.refs_2_.refs_1_), channel_id=1, source_target_pairs={{0,4},{1,5},{2,6},{3,7},{4,0},{5,1},{6,2},{7,3},{8,12},{9,13},{10,... | collective-permute-start | bytes 442376 | tf_op jit(solution)/shard_map/ppermute | solution.py:138
  70.1 7.6 %collective-permute-start.18 = (bf16[144,512]{1,0:T(8,128)(2,1)}, bf16[144,512]{1,0:T(8,128)(2,1)}, u32[]{:S(2)}, u32[]{:S(2)}) collective-permute-start(bf16[144,512]{1,0:T(8,128)(2,1)} %add_convert_fusion.6.refs_2_.refs_1_), channel_id=1, source_target_pairs={{0,6},{1,7},{2,4},{3,5},{4,2},{5,3},{6,0},{7,1},{8,14},{9,15},{10,... | collective-permute-start | bytes 442376 | tf_op jit(solution)/shard_map/ppermute | solution.py:138
  71.3 9.6 %collective-permute-start.17 = (bf16[144,512]{1,0:T(8,128)(2,1)}, bf16[144,512]{1,0:T(8,128)(2,1)}, u32[]{:S(2)}, u32[]{:S(2)}) collective-permute-start(bf16[144,512]{1,0:T(8,128)(2,1)} %add_convert_fusion.6.refs_2_.refs_1_), channel_id=1, source_target_pairs={{0,1},{1,0},{2,3},{3,2},{4,5},{5,4},{6,7},{7,6},{8,9},{9,8},{10,11... | collective-permute-start | bytes 442376 | tf_op jit(solution)/shard_map/ppermute | solution.py:138
  77.7 4.7 %collective-permute-start.22 = (bf16[144,512]{1,0:T(8,128)(2,1)}, bf16[144,512]{1,0:T(8,128)(2,1)}, u32[]{:S(2)}, u32[]{:S(2)}) collective-permute-start(bf16[144,512]{1,0:T(8,128)(2,1)} %get-tuple-element.105.refs_4_.refs_3_), channel_id=1, source_target_pairs={{0,1},{1,0},{2,3},{3,2},{4,5},{5,4},{6,7},{7,6},{8,9},{9,8},{10,11... | collective-permute-start | bytes 442376 | tf_op jit(solution)/shard_map/ppermute | solution.py:138
  77.7 4.7 %collective-permute-start.23 = (bf16[144,512]{1,0:T(8,128)(2,1)}, bf16[144,512]{1,0:T(8,128)(2,1)}, u32[]{:S(2)}, u32[]{:S(2)}) collective-permute-start(bf16[144,512]{1,0:T(8,128)(2,1)} %get-tuple-element.106.refs_6_.refs_2_), channel_id=1, source_target_pairs={{0,1},{1,0},{2,3},{3,2},{4,5},{5,4},{6,7},{7,6},{8,9},{9,8},{10,11... | collective-permute-start | bytes 442376 | tf_op jit(solution)/shard_map/ppermute | solution.py:138
  78.2 4.2 %collective-permute-start.24 = (bf16[144,512]{1,0:T(8,128)(2,1)}, bf16[144,512]{1,0:T(8,128)(2,1)}, u32[]{:S(2)}, u32[]{:S(2)}) collective-permute-start(bf16[144,512]{1,0:T(8,128)(2,1)} %get-tuple-element.107.refs_8_.refs_1_), channel_id=1, source_target_pairs={{0,1},{1,0},{2,3},{3,2},{4,5},{5,4},{6,7},{7,6},{8,9},{9,8},{10,11... | collective-permute-start | bytes 442376 | tf_op jit(solution)/shard_map/ppermute | solution.py:138
  78.3 12.5 %collective-permute-start.31 = (bf16[144,512]{1,0:T(8,128)(2,1)}, bf16[144,512]{1,0:T(8,128)(2,1)}, u32[]{:S(2)}, u32[]{:S(2)}) collective-permute-start(bf16[144,512]{1,0:T(8,128)(2,1)} %shard_map.254.refs_0_), channel_id=1, source_target_pairs={{0,16},{8,24},{16,0},{24,8},{1,17},{9,25},{17,1},{25,9},{2,18},{10... | collective-permute-start | bytes 442376 | tf_op jit(solution)/shard_map/ppermute | solution.py:138
  80.9 11.4 %collective-permute-start.30 = (bf16[144,512]{1,0:T(8,128)(2,1)}, bf16[144,512]{1,0:T(8,128)(2,1)}, u32[]{:S(2)}, u32[]{:S(2)}) collective-permute-start(bf16[144,512]{1,0:T(8,128)(2,1)} %shard_map.254.refs_0_), channel_id=1, source_target_pairs={{0,8},{8,0},{16,24},{24,16},{1,9},{9,1},{17,25},{25,17},{2,10},{10... | collective-permute-start | bytes 442376 | tf_op jit(solution)/shard_map/ppermute | solution.py:138
  88.2 14.0 %collective-permute-start.25 = (bf16[16,4608]{1,0:T(8,128)(2,1)}, bf16[16,4608]{1,0:T(8,128)(2,1)}, u32[]{:S(2)}, u32[]{:S(2)}) collective-permute-start(bf16[16,4608]{1,0:T(8,128)(2,1)} %get-tuple-element.117), channel_id=1, source_target_pairs={{0,8},{8,0},{16,24},{24,16},{1,9},{9,1},{17,25},{25,17},{2,10},{10... | collective-permute-start | bytes 442376 | tf_op jit(solution)/shard_map/ppermute | solution.py:138
  88.7 24.0 %collective-permute-start.39 = (bf16[432,512]{1,0:T(8,128)(2,1)}, bf16[432,512]{1,0:T(8,128)(2,1)}, u32[]{:S(2)}, u32[]{:S(2)}) collective-permute-start(bf16[432,512]{1,0:T(8,128)(2,1)} %shard_map.257.refs_13_), channel_id=1, source_target_pairs={{0,2},{1,3},{2,0},{3,1},{4,6},{5,7},{6,4},{7,5},{8,10},{9,11},{10,... | collective-permute-start | bytes 1327112 | tf_op jit(solution)/shard_map/ppermute | solution.py:138
  89.9 22.9 %collective-permute-start.38 = (bf16[432,512]{1,0:T(8,128)(2,1)}, bf16[432,512]{1,0:T(8,128)(2,1)}, u32[]{:S(2)}, u32[]{:S(2)}) collective-permute-start(bf16[432,512]{1,0:T(8,128)(2,1)} %shard_map.257.refs_13_), channel_id=1, source_target_pairs={{0,4},{1,5},{2,6},{3,7},{4,0},{5,1},{6,2},{7,3},{8,12},{9,13},{10,... | collective-permute-start | bytes 1327112 | tf_op jit(solution)/shard_map/ppermute | solution.py:138
  90.8 22.5 %collective-permute-start.37 = (bf16[432,512]{1,0:T(8,128)(2,1)}, bf16[432,512]{1,0:T(8,128)(2,1)}, u32[]{:S(2)}, u32[]{:S(2)}) collective-permute-start(bf16[432,512]{1,0:T(8,128)(2,1)} %shard_map.257.refs_13_), channel_id=1, source_target_pairs={{0,6},{1,7},{2,4},{3,5},{4,2},{5,3},{6,0},{7,1},{8,14},{9,15},{10,... | collective-permute-start | bytes 1327112 | tf_op jit(solution)/shard_map/ppermute | solution.py:138
  92.2 13.1 %collective-permute-start.32 = (bf16[144,512]{1,0:T(8,128)(2,1)}, bf16[144,512]{1,0:T(8,128)(2,1)}, u32[]{:S(2)}, u32[]{:S(2)}) collective-permute-start(bf16[144,512]{1,0:T(8,128)(2,1)} %shard_map.255), channel_id=1, source_target_pairs={{0,24},{8,16},{16,8},{24,0},{1,25},{9,17},{17,9},{25,1},{2,26},{10... | collective-permute-start | bytes 442376 | tf_op jit(solution)/shard_map/ppermute | solution.py:138
  103.9 9.9 %collective-permute-start.26 = (bf16[16,4608]{1,0:T(8,128)(2,1)}, bf16[16,4608]{1,0:T(8,128)(2,1)}, u32[]{:S(2)}, u32[]{:S(2)}) collective-permute-start(bf16[16,4608]{1,0:T(8,128)(2,1)} %add_convert_fusion.4), channel_id=1, source_target_pairs={{0,16},{8,24},{16,0},{24,8},{1,17},{9,25},{17,1},{25,9},{2,18},{10... | collective-permute-start | bytes 442376 | tf_op jit(solution)/shard_map/ppermute | solution.py:138
  105.4 8.0 %collective-permute-start.27 = (bf16[16,3328]{1,0:T(8,128)(2,1)}, bf16[16,3328]{1,0:T(8,128)(2,1)}, u32[]{:S(2)}, u32[]{:S(2)}) collective-permute-start(bf16[16,3328]{1,0:T(8,128)(2,1)} %get-tuple-element.128), channel_id=1, source_target_pairs={{0,8},{8,0},{16,24},{24,16},{1,9},{9,1},{17,25},{25,17},{2,10},{10... | collective-permute-start | bytes 319496 | tf_op jit(solution)/shard_map/ppermute | solution.py:138
  112.7 2.9 %collective-permute-start.36 = (bf16[432,512]{1,0:T(8,128)(2,1)}, bf16[432,512]{1,0:T(8,128)(2,1)}, u32[]{:S(2)}, u32[]{:S(2)}) collective-permute-start(bf16[432,512]{1,0:T(8,128)(2,1)} %shard_map.257.refs_13_), channel_id=1, source_target_pairs={{0,1},{1,0},{2,3},{3,2},{4,5},{5,4},{6,7},{7,6},{8,9},{9,8},{10,11... | collective-permute-start | bytes 1327112 | tf_op jit(solution)/shard_map/ppermute | solution.py:138
  112.8 3.2 %collective-permute-start.33 = (bf16[144,512]{1,0:T(8,128)(2,1)}, bf16[144,512]{1,0:T(8,128)(2,1)}, u32[]{:S(2)}, u32[]{:S(2)}) collective-permute-start(bf16[144,512]{1,0:T(8,128)(2,1)} %get-tuple-element.138.refs_1_), channel_id=1, source_target_pairs={{0,1},{1,0},{2,3},{3,2},{4,5},{5,4},{6,7},{7,6},{8,9},{9,8},{10,11... | collective-permute-start | bytes 442376 | tf_op jit(solution)/shard_map/ppermute | solution.py:138
  113.3 2.8 %collective-permute-start.34 = (bf16[144,512]{1,0:T(8,128)(2,1)}, bf16[144,512]{1,0:T(8,128)(2,1)}, u32[]{:S(2)}, u32[]{:S(2)}) collective-permute-start(bf16[144,512]{1,0:T(8,128)(2,1)} %get-tuple-element.139.refs_2_), channel_id=1, source_target_pairs={{0,1},{1,0},{2,3},{3,2},{4,5},{5,4},{6,7},{7,6},{8,9},{9,8},{10,11... | collective-permute-start | bytes 442376 | tf_op jit(solution)/shard_map/ppermute | solution.py:138
  113.4 4.6 %collective-permute-start.35 = (bf16[144,512]{1,0:T(8,128)(2,1)}, bf16[144,512]{1,0:T(8,128)(2,1)}, u32[]{:S(2)}, u32[]{:S(2)}) collective-permute-start(bf16[144,512]{1,0:T(8,128)(2,1)} %get-tuple-element.140.refs_3_), channel_id=1, source_target_pairs={{0,1},{1,0},{2,3},{3,2},{4,5},{5,4},{6,7},{7,6},{8,9},{9,8},{10,11... | collective-permute-start | bytes 442376 | tf_op jit(solution)/shard_map/ppermute | solution.py:138
  113.8 7.0 %collective-permute-start.40 = (bf16[432,512]{1,0:T(8,128)(2,1)}, bf16[432,512]{1,0:T(8,128)(2,1)}, u32[]{:S(2)}, u32[]{:S(2)}) collective-permute-start(bf16[432,512]{1,0:T(8,128)(2,1)} %get-tuple-element.144.refs_15_), channel_id=1, source_target_pairs={{0,1},{1,0},{2,3},{3,2},{4,5},{5,4},{6,7},{7,6},{8,9},{9,8},{10,11... | collective-permute-start | bytes 1327112 | tf_op jit(solution)/shard_map/ppermute | solution.py:138
  115.6 5.8 %collective-permute-start.41 = (bf16[432,512]{1,0:T(8,128)(2,1)}, bf16[432,512]{1,0:T(8,128)(2,1)}, u32[]{:S(2)}, u32[]{:S(2)}) collective-permute-start(bf16[432,512]{1,0:T(8,128)(2,1)} %get-tuple-element.145.refs_17_), channel_id=1, source_target_pairs={{0,1},{1,0},{2,3},{3,2},{4,5},{5,4},{6,7},{7,6},{8,9},{9,8},{10,11... | collective-permute-start | bytes 1327112 | tf_op jit(solution)/shard_map/ppermute | solution.py:138
  116.0 6.4 %collective-permute-start.42 = (bf16[432,512]{1,0:T(8,128)(2,1)}, bf16[432,512]{1,0:T(8,128)(2,1)}, u32[]{:S(2)}, u32[]{:S(2)}) collective-permute-start(bf16[432,512]{1,0:T(8,128)(2,1)} %get-tuple-element.146.refs_19_), channel_id=1, source_target_pairs={{0,1},{1,0},{2,3},{3,2},{4,5},{5,4},{6,7},{7,6},{8,9},{9,8},{10,11... | collective-permute-start | bytes 1327112 | tf_op jit(solution)/shard_map/ppermute | solution.py:138
  116.1 20.0 %collective-permute-start.29 = (bf16[16,3328]{1,0:T(8,128)(2,1)}, bf16[16,3328]{1,0:T(8,128)(2,1)}, u32[]{:S(2)}, u32[]{:S(2)}) collective-permute-start(bf16[16,3328]{1,0:T(8,128)(2,1)} %add_convert_fusion.8), channel_id=1, source_target_pairs={{0,16},{8,24},{16,0},{24,8},{1,17},{9,25},{17,1},{25,9},{2,18},{10... | collective-permute-start | bytes 319496 | tf_op jit(solution)/shard_map/ppermute | solution.py:138
  118.1 21.1 %collective-permute-start.46 = (bf16[32,1280]{1,0:T(8,128)(2,1)}, bf16[32,1280]{1,0:T(8,128)(2,1)}, u32[]{:S(2)}, u32[]{:S(2)}) collective-permute-start(bf16[32,1280]{1,0:T(8,128)(2,1)} %get-tuple-element.148), channel_id=1, source_target_pairs={{0,24},{8,16},{16,8},{24,0},{1,25},{9,17},{17,9},{25,1},{2,26},{10... | collective-permute-start | bytes 245768 | tf_op jit(solution)/shard_map/ppermute | solution.py:138
  120.8 18.9 %collective-permute-start.45 = (bf16[32,1280]{1,0:T(8,128)(2,1)}, bf16[32,1280]{1,0:T(8,128)(2,1)}, u32[]{:S(2)}, u32[]{:S(2)}) collective-permute-start(bf16[32,1280]{1,0:T(8,128)(2,1)} %get-tuple-element.148), channel_id=1, source_target_pairs={{0,16},{8,24},{16,0},{24,8},{1,17},{9,25},{17,1},{25,9},{2,18},{10... | collective-permute-start | bytes 245768 | tf_op jit(solution)/shard_map/ppermute | solution.py:138
  121.4 19.8 %collective-permute-start.44 = (bf16[32,1280]{1,0:T(8,128)(2,1)}, bf16[32,1280]{1,0:T(8,128)(2,1)}, u32[]{:S(2)}, u32[]{:S(2)}) collective-permute-start(bf16[32,1280]{1,0:T(8,128)(2,1)} %get-tuple-element.148), channel_id=1, source_target_pairs={{0,8},{8,0},{16,24},{24,16},{1,9},{9,1},{17,25},{25,17},{2,10},{10... | collective-permute-start | bytes 245768 | tf_op jit(solution)/shard_map/ppermute | solution.py:138
  122.5 19.8 %collective-permute-start.28 = (bf16[16,4608]{1,0:T(8,128)(2,1)}, bf16[16,4608]{1,0:T(8,128)(2,1)}, u32[]{:S(2)}, u32[]{:S(2)}) collective-permute-start(bf16[16,4608]{1,0:T(8,128)(2,1)} %add_convert_fusion.3.refs_2_), channel_id=1, source_target_pairs={{0,8},{8,0},{16,24},{24,16},{1,9},{9,1},{17,25},{25,17},{2,10},{10... | collective-permute-start | bytes 442376 | tf_op jit(solution)/shard_map/ppermute | solution.py:138
  137.7 8.5 %collective-permute-start.47 = (bf16[144,512]{1,0:T(8,128)(2,1)}, bf16[144,512]{1,0:T(8,128)(2,1)}, u32[]{:S(2)}, u32[]{:S(2)}) collective-permute-start(bf16[144,512]{1,0:T(8,128)(2,1)} %get-tuple-element.150), channel_id=1, source_target_pairs={{0,2},{1,3},{2,0},{3,1},{4,6},{5,7},{6,4},{7,5},{8,10},{9,11},{10,... | collective-permute-start | bytes 442376 | tf_op jit(solution)/shard_map/ppermute | solution.py:138
  139.2 8.0 %collective-permute-start.48 = (bf16[144,512]{1,0:T(8,128)(2,1)}, bf16[144,512]{1,0:T(8,128)(2,1)}, u32[]{:S(2)}, u32[]{:S(2)}) collective-permute-start(bf16[144,512]{1,0:T(8,128)(2,1)} %get-tuple-element.151), channel_id=1, source_target_pairs={{0,4},{1,5},{2,6},{3,7},{4,0},{5,1},{6,2},{7,3},{8,12},{9,13},{10,... | collective-permute-start | bytes 442376 | tf_op jit(solution)/shard_map/ppermute | solution.py:138
  139.7 7.5 %collective-permute-start.49 = (bf16[144,512]{1,0:T(8,128)(2,1)}, bf16[144,512]{1,0:T(8,128)(2,1)}, u32[]{:S(2)}, u32[]{:S(2)}) collective-permute-start(bf16[144,512]{1,0:T(8,128)(2,1)} %get-tuple-element.152), channel_id=1, source_target_pairs={{0,6},{1,7},{2,4},{3,5},{4,2},{5,3},{6,0},{7,1},{8,14},{9,15},{10,... | collective-permute-start | bytes 442376 | tf_op jit(solution)/shard_map/ppermute | solution.py:138
  141.2 5.0 %collective-permute-start.43 = (bf16[16,3328]{1,0:T(8,128)(2,1)}, bf16[16,3328]{1,0:T(8,128)(2,1)}, u32[]{:S(2)}, u32[]{:S(2)}) collective-permute-start(bf16[16,3328]{1,0:T(8,128)(2,1)} %add_convert_fusion.7.refs_4_), channel_id=1, source_target_pairs={{0,8},{8,0},{16,24},{24,16},{1,9},{9,1},{17,25},{25,17},{2,10},{10... | collective-permute-start | bytes 319496 | tf_op jit(solution)/shard_map/ppermute | solution.py:138
  (2 other events, 4.4 us)

commit v7 on v6

--- a/solution.py
+++ b/solution.py
@@ -990,10 +990,13 @@
     scr[...] = jnp.zeros_like(scr)
     from_pair(late, 0, 1)
     from_pair(middle, reduce_end, 0)
+    for item in outs[1:3]:
+        item.send()
     total = parts[0]()[...]
     for part in parts[1:]:
         total = total + part()[...].astype(F32)
     red[0] = total[:, 0:reduce_end]
+    outs[0].send()
     scr[0, 0:held, :] = total[:, reduce_end:]
     for k in range(2):
         flat = scr[k, :, 0:LANES].T

time: 151 us -> 151 us (level)
  no operation moved by 1% of the time
where the time goes in v7:
time: 151 us; the launch traced here: 150 us
  Pallas kernels  63.1 us (42%)
  starting transfers between devices  42.9 us (28%)
  waiting for transfers between devices  31.9 us (21%)
  other arithmetic  10.5 us (7%)
  between operations  1.7 us (1%)
    pallas_call x12, Pallas kernels, call(): pl.pallas_call(kernel, out_shape=list(outs), in_specs=[SMEM] * len(scalar...  63.1 us
    ppermute x50, starting transfers between devices, ppermute_xor(): lax.ppermute(x, axis, [(i, i ^ mask) for i in range(lax.axis_size(axis))])  42.9 us
    ppermute x50, waiting for transfers between devices, ppermute_xor(): lax.ppermute(x, axis, [(i, i ^ mask) for i in range(lax.axis_size(axis))])  31.9 us
    convert_element_type x6, other arithmetic, summed(): return (left.astype(F32) + right.astype(F32)).astype(BF16)  10.5 us
  transfers between devices with their start and end apart: 50, of which 13 were waited for; matrix products, arithmetic and copies ran while one was open for 7% of the time, Pallas kernels for 33%

profile of v7, /device:TPU:0, one launch (start us, length us, event | category | flops | bytes accessed | tf_op | source)
XLA Modules:
  0.0 150.1 jit_solution(16285785699949532460)
XLA Ops:
  0.6 2.0 %shard_map.238.refs_8_.refs_3_ = bf16[32,6912]{1,0:T(8,128)(2,1)} custom-call(bf16[576,128]{1,0:T(8,128)(2,1)} %bitcast.34, f32[2,2,32]{2,1,0:T(2,128)} %refs_1_.3, f32[2,2,32]{2,1,0:T(2,128)} %refs_2_.3, f32[2,128]{1,0:T(2,128)} %refs_3_.3, f32[2,128]{1,0:T(2,128)} %refs_4_.3, bf16[2,32,1024]{2,1,0:T(8,128)(2,1)} %bitcast.32, ...), custom_call_target="tpu_custom_call" | custom-call | tf_op jit(solution)/shard_map/pallas_call | solution.py:98
  2.6 3.0 %collective-permute-start.3 = (bf16[32,6912]{1,0:T(8,128)(2,1)}, bf16[32,6912]{1,0:T(8,128)(2,1)}, u32[]{:S(2)}, u32[]{:S(2)}) collective-permute-start(bf16[32,6912]{1,0:T(8,128)(2,1)} %shard_map.238.refs_8_.refs_3_), channel_id=1, source_target_pairs={{0,2},{1,3},{2,0},{3,1},{4,6},{5,7},{6,4},{7,5},{8,10},{9,11},{10,... | collective-permute-start | bytes 1327112 | tf_op jit(solution)/shard_map/ppermute | solution.py:138
  5.6 1.5 %collective-permute-start.2 = (bf16[32,6912]{1,0:T(8,128)(2,1)}, bf16[32,6912]{1,0:T(8,128)(2,1)}, u32[]{:S(2)}, u32[]{:S(2)}) collective-permute-start(bf16[32,6912]{1,0:T(8,128)(2,1)} %shard_map.238.refs_8_.refs_3_), channel_id=1, source_target_pairs={{0,4},{1,5},{2,6},{3,7},{4,0},{5,1},{6,2},{7,3},{8,12},{9,13},{10,... | collective-permute-start | bytes 1327112 | tf_op jit(solution)/shard_map/ppermute | solution.py:138
  7.2 2.0 %shard_map.239 = (bf16[32,6912]{1,0:T(8,128)(2,1)}, bf16[144,512]{1,0:T(8,128)(2,1)}) custom-call(bf16[144,512]{1,0:T(8,128)(2,1)} %bitcast.35, f32[2,2,32]{2,1,0:T(2,128)} %refs_1_.3, f32[2,2,32]{2,1,0:T(2,128)} %refs_2_.3, f32[2,128]{1,0:T(2,128)} %refs_3_.3, f32[2,128]{1,0:T(2,128)} %refs_4_.3, bf16[2,32,1024]{2,1,0:T(8,128)(2,1)} %bitcast.33, ...), custom_call_target="tpu_custom_call" | custom-call | tf_op jit(solution)/shard_map/pallas_call | solution.py:98
  9.2 2.1 %collective-permute-start.4 = (bf16[144,512]{1,0:T(8,128)(2,1)}, bf16[144,512]{1,0:T(8,128)(2,1)}, u32[]{:S(2)}, u32[]{:S(2)}) collective-permute-start(bf16[144,512]{1,0:T(8,128)(2,1)} %get-tuple-element.92.refs_0_), channel_id=1, source_target_pairs={{0,8},{8,0},{16,24},{24,16},{1,9},{9,1},{17,25},{25,17},{2,10},{10... | collective-permute-start | bytes 442376 | tf_op jit(solution)/shard_map/ppermute | solution.py:138
  11.9 1.1 shard_map.237
  13.0 1.7 %collective-permute-done.4.refs_1_.refs_4_.refs_0_ = bf16[144,512]{1,0:T(8,128)(2,1)} collective-permute-done((bf16[144,512]{1,0:T(8,128)(2,1)}, bf16[144,512]{1,0:T(8,128)(2,1)}, u32[]{:S(2)}, u32[]{:S(2)}) %collective-permute-start.4) | collective-permute-done | bytes 147488 | tf_op jit(solution)/shard_map/ppermute | solution.py:138
  14.7 1.7 %shard_map.240.refs_3_.refs_0_ = bf16[288,512]{1,0:T(8,128)(2,1)} custom-call(bf16[144,512]{1,0:T(8,128)(2,1)} %get-tuple-element.92.refs_0_, bf16[144,512]{1,0:T(8,128)(2,1)} %collective-permute-done.4.refs_1_.refs_4_.refs_0_), custom_call_target="tpu_custom_call" | custom-call | tf_op jit(solution)/shard_map/pallas_call | solution.py:98
  16.9 10.1 %collective-permute-done.2.refs_1_ = bf16[32,6912]{1,0:T(8,128)(2,1)} collective-permute-done((bf16[32,6912]{1,0:T(8,128)(2,1)}, bf16[32,6912]{1,0:T(8,128)(2,1)}, u32[]{:S(2)}, u32[]{:S(2)}) %collective-permute-start.2) | collective-permute-done | bytes 442400 | tf_op jit(solution)/shard_map/ppermute | solution.py:138
  27.6 1.2 collective-permute-start.11
  29.7 1.4 collective-permute-start.9
  31.1 2.6 %collective-permute-start.12 = (bf16[288,512]{1,0:T(8,128)(2,1)}, bf16[288,512]{1,0:T(8,128)(2,1)}, u32[]{:S(2)}, u32[]{:S(2)}) collective-permute-start(bf16[288,512]{1,0:T(8,128)(2,1)} %shard_map.244), channel_id=1, source_target_pairs={{0,16},{8,24},{16,0},{24,8},{1,17},{9,25},{17,1},{25,9},{2,18},{10... | collective-permute-start | bytes 884744 | tf_op jit(solution)/shard_map/ppermute | solution.py:138
  33.7 9.6 %shard_map.242 = (bf16[576,1024]{1,0:T(8,128)(2,1)}, bf16[256,4352]{1,0:T(8,128)(2,1)}, f32[8,256]{1,0:T(8,128)}, f32[8,1024]{1,0:T(8,128)}, bf16[144,1024]{1,0:...) custom-call(s32[1]{0:T(128)} %bitcast.refs_0_, ...), custom_call_target="tpu_custom_call" | custom-call | tf_op jit(solution)/shard_map/pallas_call | solution.py:98
  43.4 3.8 %collective-permute-done.12.refs_5_.refs_1_ = bf16[288,512]{1,0:T(8,128)(2,1)} collective-permute-done((bf16[288,512]{1,0:T(8,128)(2,1)}, bf16[288,512]{1,0:T(8,128)(2,1)}, u32[]{:S(2)}, u32[]{:S(2)}) %collective-permute-start.12) | collective-permute-done | bytes 294944 | tf_op jit(solution)/shard_map/ppermute | solution.py:138
  47.2 2.1 %collective-permute-done.10.refs_1_ = bf16[32,6912]{1,0:T(8,128)(2,1)} collective-permute-done((bf16[32,6912]{1,0:T(8,128)(2,1)}, bf16[32,6912]{1,0:T(8,128)(2,1)}, u32[]{:S(2)}, u32[]{:S(2)}) %collective-permute-start.10) | collective-permute-done | bytes 442400 | tf_op jit(solution)/shard_map/ppermute | solution.py:138
  49.3 1.6 %collective-permute-done.9.refs_0_ = bf16[32,6912]{1,0:T(8,128)(2,1)} collective-permute-done((bf16[32,6912]{1,0:T(8,128)(2,1)}, bf16[32,6912]{1,0:T(8,128)(2,1)}, u32[]{:S(2)}, u32[]{:S(2)}) %collective-permute-start.9) | collective-permute-done | bytes 442400 | tf_op jit(solution)/shard_map/ppermute | solution.py:138
  51.4 1.6 %collective-permute-done.13.refs_7_ = bf16[32,6912]{1,0:T(8,128)(2,1)} collective-permute-done((bf16[32,6912]{1,0:T(8,128)(2,1)}, bf16[32,6912]{1,0:T(8,128)(2,1)}, u32[]{:S(2)}, u32[]{:S(2)}) %collective-permute-start.13) | collective-permute-done | bytes 442400 | tf_op jit(solution)/shard_map/ppermute | solution.py:138
  54.3 9.4 %shard_map.246 = (bf16[256,4352]{1,0:T(8,128)(2,1)}, f32[8,256]{1,0:T(8,128)}, f32[8,1024]{1,0:T(8,128)}, bf16[144,1024]{1,0:T(8,128)(2,1)}, f32[144,256]{1,0:T(...) custom-call(s32[1]{0:T(128)} %bitcast.refs_0_, ...), custom_call_target="tpu_custom_call" | custom-call | tf_op jit(solution)/shard_map/pallas_call | solution.py:98
  64.2 1.9 %collective-permute-done.16 = bf16[144,512]{1,0:T(8,128)(2,1)S(1)} collective-permute-done((bf16[144,512]{1,0:T(8,128)(2,1)}, bf16[144,512]{1,0:T(8,128)(2,1)S(1)}, u32[]{:S(2)}, u32[]{:S(2)}) %collective-permute-start.16) | collective-permute-done | bytes 147488 | tf_op jit(solution)/shard_map/ppermute | solution.py:138
  66.2 1.7 %add_convert_fusion.6.refs_2_.refs_1_ = bf16[144,512]{1,0:T(8,128)(2,1)} fusion(f32[144,512]{1,0:T(8,128)} %get-tuple-element.101, bf16[144,512]{1,0:T(8,128)(2,1)S(1)} %collective-permute-done.16), kind=kLoop, calls=%fused_computation.6 | loop fusion | flops 221184 | bytes 589824 | tf_op jit(solution)/shard_map/convert_element_type | solution.py:179
  68.6 1.5 %collective-permute-start.19 = (bf16[144,512]{1,0:T(8,128)(2,1)}, bf16[144,512]{1,0:T(8,128)(2,1)}, u32[]{:S(2)}, u32[]{:S(2)}) collective-permute-start(bf16[144,512]{1,0:T(8,128)(2,1)} %add_convert_fusion.6.refs_2_.refs_1_), channel_id=1, source_target_pairs={{0,4},{1,5},{2,6},{3,7},{4,0},{5,1},{6,2},{7,3},{8,12},{9,13},{10,... | collective-permute-start | bytes 442376 | tf_op jit(solution)/shard_map/ppermute | solution.py:138
  70.1 1.2 collective-permute-start.18
  71.3 1.9 %shard_map.247.refs_3_.refs_0_ = bf16[432,512]{1,0:T(8,128)(2,1)} custom-call(bf16[144,512]{1,0:T(8,128)(2,1)} %collective-permute-done.4.refs_1_.refs_4_.refs_0_, bf16[288,512]{1,0:T(8,128)(2,1)} %collective-permute-done.12.refs_5_.refs_1_, bf16[144,512]{1,0:T(8,128)(2,1)} %add_convert_fusion.6.refs_2_.refs_1_), custom_call_target="tpu_custom_call" | custom-call | tf_op jit(solution)/shard_map/pallas_call | solution.py:98
  73.2 2.2 %fusion.3 = (bf16[144,512]{1,0:T(8,128)(2,1)}, bf16[144,512]{1,0:T(8,128)(2,1)}, bf16[144,512]{1,0:T(8,128)(2,1)}, bf16[144,512]{1,0:T(8,128)(2,1)}) fusion(bf16[4,144,512]{2,1,0:T(8,128)(2,1)} %collective-permute-done.21, bf16[4,144,512]{2,1,0:T(8,128)(2,1)} %get-tuple-element.103), kind=kLoop, calls=%fused_computation.12 | loop fusion | flops 1179648 | bytes 1769472 | tf_op jit(solution)/shard_map/convert_element_type | solution.py:179
  75.4 2.3 %collective-permute-done.19.refs_1_ = bf16[144,512]{1,0:T(8,128)(2,1)} collective-permute-done((bf16[144,512]{1,0:T(8,128)(2,1)}, bf16[144,512]{1,0:T(8,128)(2,1)}, u32[]{:S(2)}, u32[]{:S(2)}) %collective-permute-start.19) | collective-permute-done | bytes 147488 | tf_op jit(solution)/shard_map/ppermute | solution.py:138
  78.3 2.6 %collective-permute-start.31 = (bf16[144,512]{1,0:T(8,128)(2,1)}, bf16[144,512]{1,0:T(8,128)(2,1)}, u32[]{:S(2)}, u32[]{:S(2)}) collective-permute-start(bf16[144,512]{1,0:T(8,128)(2,1)} %shard_map.254.refs_0_), channel_id=1, source_target_pairs={{0,16},{8,24},{16,0},{24,8},{1,17},{9,25},{17,1},{25,9},{2,18},{10... | collective-permute-start | bytes 442376 | tf_op jit(solution)/shard_map/ppermute | solution.py:138
  80.9 1.6 %collective-permute-start.30 = (bf16[144,512]{1,0:T(8,128)(2,1)}, bf16[144,512]{1,0:T(8,128)(2,1)}, u32[]{:S(2)}, u32[]{:S(2)}) collective-permute-start(bf16[144,512]{1,0:T(8,128)(2,1)} %shard_map.254.refs_0_), channel_id=1, source_target_pairs={{0,8},{8,0},{16,24},{24,16},{1,9},{9,1},{17,25},{25,17},{2,10},{10... | collective-permute-start | bytes 442376 | tf_op jit(solution)/shard_map/ppermute | solution.py:138
  82.5 5.8 %shard_map.249 = (bf16[144,1024]{1,0:T(8,128)(2,1)}, f32[16,4608]{1,0:T(8,128)}, bf16[16,4608]{1,0:T(8,128)(2,1)}, f32[8,1024]{1,0:T(8,128)}) custom-call(s32[1]{0:T(128)} %bitcast.refs_0_, s32[1]{0:T(128)} %bitcast.1.refs_1_, bf16[144,512]{1,0:T(8,128)(2,1)} %add_convert_fusion.6.refs_2_.refs_1_, bf16[144,512]{1,0:T(8,128)(2,1)} %collective-permute-done.17.refs_3_, ...), custom_call_target="tpu_custom_call" | custom-call | tf_op jit(solution)/shard_map/pallas_call | solution.py:98
  88.7 1.2 collective-permute-start.39
  90.8 1.4 collective-permute-start.37
  92.2 1.6 %collective-permute-start.32 = (bf16[144,512]{1,0:T(8,128)(2,1)}, bf16[144,512]{1,0:T(8,128)(2,1)}, u32[]{:S(2)}, u32[]{:S(2)}) collective-permute-start(bf16[144,512]{1,0:T(8,128)(2,1)} %shard_map.255), channel_id=1, source_target_pairs={{0,24},{8,16},{16,8},{24,0},{1,25},{9,17},{17,9},{25,1},{2,26},{10... | collective-permute-start | bytes 442376 | tf_op jit(solution)/shard_map/ppermute | solution.py:138
  93.8 8.4 %shard_map.250 = (f32[16,3328]{1,0:T(8,128)}, bf16[16,3328]{1,0:T(8,128)(2,1)}, f32[576,256]{1,0:T(8,128)}, f32[576,128]{1,0:T(8,128)}, f32[8,256]{1,0:T(8,128)}, /*index=5*/f32[8,1024]{1,0:T(8,128)}) custom-call(s32[1]{0:T(128)} %bitcast.refs_0_, s32[1]{0:T(128)} %bitcast.1.refs_1_, f32[576,128]{1,0:T(8,128)} %get-tuple-element.90.refs_1_.refs_2_, ...), custom_call_target="tpu_custom_call" | custom-call | tf_op jit(solution)/shard_map/pallas_call | solution.py:98
  102.2 1.7 %add_convert_fusion.4 = bf16[16,4608]{1,0:T(8,128)(2,1)} fusion(f32[16,4608]{1,0:T(8,128)} %get-tuple-element.116, bf16[16,4608]{1,0:T(8,128)(2,1)} %shard_map.251), kind=kLoop, calls=%fused_computation.4 | loop fusion | flops 221184 | bytes 589824 | tf_op jit(solution)/shard_map/convert_element_type | solution.py:179
  103.9 1.4 collective-permute-start.26
  105.4 1.3 collective-permute-start.27
  106.7 6.0 %shard_map.252 = (f32[576,128]{1,0:T(8,128)}, f32[32,1280]{1,0:T(8,128)}, bf16[32,1280]{1,0:T(8,128)(2,1)}) custom-call(s32[1]{0:T(128)} %bitcast.refs_0_, f32[576,128]{1,0:T(8,128)} %get-tuple-element.90.refs_1_.refs_2_, f32[576,256]{1,0:T(8,128)} %get-tuple-element.127.refs_1_.refs_2_.refs_3_, bf16[256,4352]{1,0:T(8,128)(2,1)} %get-tuple-element.125.refs_11_.refs_3_, ...), custom_call_target="tpu_custom_call" | custom-call | tf_op jit(solution)/shard_map/pallas_call | solution.py:98
  113.9 1.7 %add_convert_fusion.8 = bf16[16,3328]{1,0:T(8,128)(2,1)} fusion(f32[16,3328]{1,0:T(8,128)} %get-tuple-element.135, bf16[16,3328]{1,0:T(8,128)(2,1)} %get-tuple-element.136), kind=kLoop, calls=%fused_computation.8 | loop fusion | flops 159744 | bytes 425984 | tf_op jit(solution)/shard_map/convert_element_type | solution.py:179
  116.4 1.7 %add_convert_fusion.3.refs_2_ = bf16[16,4608]{1,0:T(8,128)(2,1)} fusion(bf16[16,4608]{1,0:T(8,128)(2,1)} %get-tuple-element.134, bf16[16,4608]{1,0:T(8,128)(2,1)} %add_convert_fusion.4), kind=kLoop, calls=%fused_computation.3 | loop fusion | flops 294912 | bytes 442368 | tf_op jit(solution)/shard_map/convert_element_type | solution.py:179
  118.1 2.8 %collective-permute-start.46 = (bf16[32,1280]{1,0:T(8,128)(2,1)}, bf16[32,1280]{1,0:T(8,128)(2,1)}, u32[]{:S(2)}, u32[]{:S(2)}) collective-permute-start(bf16[32,1280]{1,0:T(8,128)(2,1)} %get-tuple-element.148), channel_id=1, source_target_pairs={{0,24},{8,16},{16,8},{24,0},{1,25},{9,17},{17,9},{25,1},{2,26},{10... | collective-permute-start | bytes 245768 | tf_op jit(solution)/shard_map/ppermute | solution.py:138
  121.4 1.0 collective-permute-start.44
  122.5 1.0 collective-permute-start.28
  123.5 12.6 %shard_map.259 = (f32[1024,512]{1,0:T(8,128)}, f32[1,512]{1,0:T(1,128)}, f32[1,512]{1,0:T(1,128)}, f32[512,4096]{1,0:T(8,128)}) custom-call(s32[1]{0:T(128)} %bitcast.refs_0_, bf16[144,512]{1,0:T(8,128)(2,1)} %get-tuple-element.138.refs_1_, bf16[144,512]{1,0:T(8,128)(2,1)} %get-tuple-element.139.refs_2_, bf16[144,512]{1,0:T(8,128)(2,1)} %get-tuple-element.140.refs_3_, ...), custom_call_target="tpu_custom_call" | custom-call | tf_op jit(solution)/shard_map/pallas_call | solution.py:98
  136.1 1.6 %add_convert_fusion.7.refs_4_ = bf16[16,3328]{1,0:T(8,128)(2,1)} fusion(bf16[16,3328]{1,0:T(8,128)(2,1)} %shard_map.260, bf16[16,3328]{1,0:T(8,128)(2,1)} %add_convert_fusion.8), kind=kLoop, calls=%fused_computation.7 | loop fusion | flops 212992 | bytes 319488 | tf_op jit(solution)/shard_map/convert_element_type | solution.py:179
  137.7 1.5 collective-permute-start.47
  139.7 1.5 %collective-permute-start.49 = (bf16[144,512]{1,0:T(8,128)(2,1)}, bf16[144,512]{1,0:T(8,128)(2,1)}, u32[]{:S(2)}, u32[]{:S(2)}) collective-permute-start(bf16[144,512]{1,0:T(8,128)(2,1)} %get-tuple-element.152), channel_id=1, source_target_pairs={{0,6},{1,7},{2,4},{3,5},{4,2},{5,3},{6,0},{7,1},{8,14},{9,15},{10,... | collective-permute-start | bytes 442376 | tf_op jit(solution)/shard_map/ppermute | solution.py:138
  141.2 1.0 collective-permute-start.43
  142.3 4.0 %collective-permute-done.43.refs_5_ = bf16[16,3328]{1,0:T(8,128)(2,1)} collective-permute-done((bf16[16,3328]{1,0:T(8,128)(2,1)}, bf16[16,3328]{1,0:T(8,128)(2,1)}, u32[]{:S(2)}, u32[]{:S(2)}) %collective-permute-start.43) | collective-permute-done | bytes 106528 | tf_op jit(solution)/shard_map/ppermute | solution.py:138
  147.2 2.7 %shard_map.262 = (f32[2,32,1024]{2,1,0:T(8,128)}, f32[2,9,32,256]{3,2,1,0:T(8,128)}, f32[2,32,1024]{2,1,0:T(8,128)}, f32[2,2,32]{2,1,0:T(2,128)}, f32[2,2,32]{2,...) custom-call(s32[1]{0:T(128)} %bitcast.refs_0_, s32[1]{0:T(128)} %bitcast.1.refs_1_, ...), custom_call_target="tpu_custom_call" | custom-call | tf_op jit(solution)/shard_map/pallas_call | solution.py:98
  (84 shorter events, 11.2 us)
Async XLA Ops:
  2.6 14.3 %collective-permute-start.3 = (bf16[32,6912]{1,0:T(8,128)(2,1)}, bf16[32,6912]{1,0:T(8,128)(2,1)}, u32[]{:S(2)}, u32[]{:S(2)}) collective-permute-start(bf16[32,6912]{1,0:T(8,128)(2,1)} %shard_map.238.refs_8_.refs_3_), channel_id=1, source_target_pairs={{0,2},{1,3},{2,0},{3,1},{4,6},{5,7},{6,4},{7,5},{8,10},{9,11},{10,... | collective-permute-start | bytes 1327112 | tf_op jit(solution)/shard_map/ppermute | solution.py:138
  5.6 21.4 %collective-permute-start.2 = (bf16[32,6912]{1,0:T(8,128)(2,1)}, bf16[32,6912]{1,0:T(8,128)(2,1)}, u32[]{:S(2)}, u32[]{:S(2)}) collective-permute-start(bf16[32,6912]{1,0:T(8,128)(2,1)} %shard_map.238.refs_8_.refs_3_), channel_id=1, source_target_pairs={{0,4},{1,5},{2,6},{3,7},{4,0},{5,1},{6,2},{7,3},{8,12},{9,13},{10,... | collective-permute-start | bytes 1327112 | tf_op jit(solution)/shard_map/ppermute | solution.py:138
  7.1 19.9 %collective-permute-start.1 = (bf16[32,6912]{1,0:T(8,128)(2,1)}, bf16[32,6912]{1,0:T(8,128)(2,1)}, u32[]{:S(2)}, u32[]{:S(2)}) collective-permute-start(bf16[32,6912]{1,0:T(8,128)(2,1)} %shard_map.238.refs_8_.refs_3_), channel_id=1, source_target_pairs={{0,6},{1,7},{2,4},{3,5},{4,2},{5,3},{6,0},{7,1},{8,14},{9,15},{10,... | collective-permute-start | bytes 1327112 | tf_op jit(solution)/shard_map/ppermute | solution.py:138
  9.2 5.5 %collective-permute-start.4 = (bf16[144,512]{1,0:T(8,128)(2,1)}, bf16[144,512]{1,0:T(8,128)(2,1)}, u32[]{:S(2)}, u32[]{:S(2)}) collective-permute-start(bf16[144,512]{1,0:T(8,128)(2,1)} %get-tuple-element.92.refs_0_), channel_id=1, source_target_pairs={{0,8},{8,0},{16,24},{24,16},{1,9},{9,1},{17,25},{25,17},{2,10},{10... | collective-permute-start | bytes 442376 | tf_op jit(solution)/shard_map/ppermute | solution.py:138
  11.3 17.5 %collective-permute-start = (bf16[32,6912]{1,0:T(8,128)(2,1)}, bf16[32,6912]{1,0:T(8,128)(2,1)}, u32[]{:S(2)}, u32[]{:S(2)}) collective-permute-start(bf16[32,6912]{1,0:T(8,128)(2,1)} %shard_map.238.refs_8_.refs_3_), channel_id=1, source_target_pairs={{0,1},{1,0},{2,3},{3,2},{4,5},{5,4},{6,7},{7,6},{8,9},{9,8},{10,11... | collective-permute-start | bytes 1327112 | tf_op jit(solution)/shard_map/ppermute | solution.py:138
  27.1 2.6 %collective-permute-start.5 = (bf16[32,6912]{1,0:T(8,128)(2,1)}, bf16[32,6912]{1,0:T(8,128)(2,1)}, u32[]{:S(2)}, u32[]{:S(2)}) collective-permute-start(bf16[32,6912]{1,0:T(8,128)(2,1)} %get-tuple-element.93.refs_5_.refs_3_), channel_id=1, source_target_pairs={{0,1},{1,0},{2,3},{3,2},{4,5},{5,4},{6,7},{7,6},{8,9},{9,8},{10,11... | collective-permute-start | bytes 1327112 | tf_op jit(solution)/shard_map/ppermute | solution.py:138
  27.1 4.1 %collective-permute-start.6 = (bf16[32,6912]{1,0:T(8,128)(2,1)}, bf16[32,6912]{1,0:T(8,128)(2,1)}, u32[]{:S(2)}, u32[]{:S(2)}) collective-permute-start(bf16[32,6912]{1,0:T(8,128)(2,1)} %get-tuple-element.94.refs_7_.refs_2_), channel_id=1, source_target_pairs={{0,1},{1,0},{2,3},{3,2},{4,5},{5,4},{6,7},{7,6},{8,9},{9,8},{10,11... | collective-permute-start | bytes 1327112 | tf_op jit(solution)/shard_map/ppermute | solution.py:138
  27.6 6.2 %collective-permute-start.7 = (bf16[32,6912]{1,0:T(8,128)(2,1)}, bf16[32,6912]{1,0:T(8,128)(2,1)}, u32[]{:S(2)}, u32[]{:S(2)}) collective-permute-start(bf16[32,6912]{1,0:T(8,128)(2,1)} %get-tuple-element.95.refs_9_.refs_1_), channel_id=1, source_target_pairs={{0,1},{1,0},{2,3},{3,2},{4,5},{5,4},{6,7},{7,6},{8,9},{9,8},{10,11... | collective-permute-start | bytes 1327112 | tf_op jit(solution)/shard_map/ppermute | solution.py:138
  27.6 19.6 %collective-permute-start.11 = (bf16[32,6912]{1,0:T(8,128)(2,1)}, bf16[32,6912]{1,0:T(8,128)(2,1)}, u32[]{:S(2)}, u32[]{:S(2)}) collective-permute-start(bf16[32,6912]{1,0:T(8,128)(2,1)} %shard_map.243.refs_4_), channel_id=1, source_target_pairs={{0,2},{1,3},{2,0},{3,1},{4,6},{5,7},{6,4},{7,5},{8,10},{9,11},{10,... | collective-permute-start | bytes 1327112 | tf_op jit(solution)/shard_map/ppermute | solution.py:138
  28.8 20.5 %collective-permute-start.10 = (bf16[32,6912]{1,0:T(8,128)(2,1)}, bf16[32,6912]{1,0:T(8,128)(2,1)}, u32[]{:S(2)}, u32[]{:S(2)}) collective-permute-start(bf16[32,6912]{1,0:T(8,128)(2,1)} %shard_map.243.refs_4_), channel_id=1, source_target_pairs={{0,4},{1,5},{2,6},{3,7},{4,0},{5,1},{6,2},{7,3},{8,12},{9,13},{10,... | collective-permute-start | bytes 1327112 | tf_op jit(solution)/shard_map/ppermute | solution.py:138
  29.7 21.2 %collective-permute-start.9 = (bf16[32,6912]{1,0:T(8,128)(2,1)}, bf16[32,6912]{1,0:T(8,128)(2,1)}, u32[]{:S(2)}, u32[]{:S(2)}) collective-permute-start(bf16[32,6912]{1,0:T(8,128)(2,1)} %shard_map.243.refs_4_), channel_id=1, source_target_pairs={{0,6},{1,7},{2,4},{3,5},{4,2},{5,3},{6,0},{7,1},{8,14},{9,15},{10,... | collective-permute-start | bytes 1327112 | tf_op jit(solution)/shard_map/ppermute | solution.py:138
  31.1 16.1 %collective-permute-start.12 = (bf16[288,512]{1,0:T(8,128)(2,1)}, bf16[288,512]{1,0:T(8,128)(2,1)}, u32[]{:S(2)}, u32[]{:S(2)}) collective-permute-start(bf16[288,512]{1,0:T(8,128)(2,1)} %shard_map.244), channel_id=1, source_target_pairs={{0,16},{8,24},{16,0},{24,8},{1,17},{9,25},{17,1},{25,9},{2,18},{10... | collective-permute-start | bytes 884744 | tf_op jit(solution)/shard_map/ppermute | solution.py:138
  33.7 17.7 %collective-permute-start.8 = (bf16[32,6912]{1,0:T(8,128)(2,1)}, bf16[32,6912]{1,0:T(8,128)(2,1)}, u32[]{:S(2)}, u32[]{:S(2)}) collective-permute-start(bf16[32,6912]{1,0:T(8,128)(2,1)} %shard_map.243.refs_4_), channel_id=1, source_target_pairs={{0,1},{1,0},{2,3},{3,2},{4,5},{5,4},{6,7},{7,6},{8,9},{9,8},{10,11... | collective-permute-start | bytes 1327112 | tf_op jit(solution)/shard_map/ppermute | solution.py:138
  50.9 2.8 %collective-permute-start.14 = (bf16[32,6912]{1,0:T(8,128)(2,1)}, bf16[32,6912]{1,0:T(8,128)(2,1)}, u32[]{:S(2)}, u32[]{:S(2)}) collective-permute-start(bf16[32,6912]{1,0:T(8,128)(2,1)} %get-tuple-element.99.refs_8_), channel_id=1, source_target_pairs={{0,1},{1,0},{2,3},{3,2},{4,5},{5,4},{6,7},{7,6},{8,9},{9,8},{10,11... | collective-permute-start | bytes 1327112 | tf_op jit(solution)/shard_map/ppermute | solution.py:138
  51.4 2.9 %collective-permute-start.15 = (bf16[32,6912]{1,0:T(8,128)(2,1)}, bf16[32,6912]{1,0:T(8,128)(2,1)}, u32[]{:S(2)}, u32[]{:S(2)}) collective-permute-start(bf16[32,6912]{1,0:T(8,128)(2,1)} %get-tuple-element.100.refs_10_), channel_id=1, source_target_pairs={{0,1},{1,0},{2,3},{3,2},{4,5},{5,4},{6,7},{7,6},{8,9},{9,8},{10,11... | collective-permute-start | bytes 1327112 | tf_op jit(solution)/shard_map/ppermute | solution.py:138
  63.7 9.5 %collective-permute-start.21 = (bf16[4,144,512]{2,1,0:T(8,128)(2,1)}, bf16[4,144,512]{2,1,0:T(8,128)(2,1)}, u32[]{:S(2)}, u32[]{:S(2)}) collective-permute-start(bf16[4,144,512]{2,1,0:T(8,128)(2,1)} %get-tuple-element.104), channel_id=1, source_target_pairs={{0,1},{1,0},{2,3},{3,2},{4,5},{5,4},{6,7},{7,6},{8,9},{9,8},{10,11... | collective-permute-start | bytes 1769480 | tf_op jit(solution)/shard_map/ppermute | solution.py:138
  67.8 7.6 %collective-permute-start.20 = (bf16[144,512]{1,0:T(8,128)(2,1)}, bf16[144,512]{1,0:T(8,128)(2,1)}, u32[]{:S(2)}, u32[]{:S(2)}) collective-permute-start(bf16[144,512]{1,0:T(8,128)(2,1)} %add_convert_fusion.6.refs_2_.refs_1_), channel_id=1, source_target_pairs={{0,2},{1,3},{2,0},{3,1},{4,6},{5,7},{6,4},{7,5},{8,10},{9,11},{10,... | collective-permute-start | bytes 442376 | tf_op jit(solution)/shard_map/ppermute | solution.py:138
  68.6 9.1 %collective-permute-start.19 = (bf16[144,512]{1,0:T(8,128)(2,1)}, bf16[144,512]{1,0:T(8,128)(2,1)}, u32[]{:S(2)}, u32[]{:S(2)}) collective-permute-start(bf16[144,512]{1,0:T(8,128)(2,1)} %add_convert_fusion.6.refs_2_.refs_1_), channel_id=1, source_target_pairs={{0,4},{1,5},{2,6},{3,7},{4,0},{5,1},{6,2},{7,3},{8,12},{9,13},{10,... | collective-permute-start | bytes 442376 | tf_op jit(solution)/shard_map/ppermute | solution.py:138
  70.1 7.6 %collective-permute-start.18 = (bf16[144,512]{1,0:T(8,128)(2,1)}, bf16[144,512]{1,0:T(8,128)(2,1)}, u32[]{:S(2)}, u32[]{:S(2)}) collective-permute-start(bf16[144,512]{1,0:T(8,128)(2,1)} %add_convert_fusion.6.refs_2_.refs_1_), channel_id=1, source_target_pairs={{0,6},{1,7},{2,4},{3,5},{4,2},{5,3},{6,0},{7,1},{8,14},{9,15},{10,... | collective-permute-start | bytes 442376 | tf_op jit(solution)/shard_map/ppermute | solution.py:138
  71.3 9.6 %collective-permute-start.17 = (bf16[144,512]{1,0:T(8,128)(2,1)}, bf16[144,512]{1,0:T(8,128)(2,1)}, u32[]{:S(2)}, u32[]{:S(2)}) collective-permute-start(bf16[144,512]{1,0:T(8,128)(2,1)} %add_convert_fusion.6.refs_2_.refs_1_), channel_id=1, source_target_pairs={{0,1},{1,0},{2,3},{3,2},{4,5},{5,4},{6,7},{7,6},{8,9},{9,8},{10,11... | collective-permute-start | bytes 442376 | tf_op jit(solution)/shard_map/ppermute | solution.py:138
  77.7 4.7 %collective-permute-start.22 = (bf16[144,512]{1,0:T(8,128)(2,1)}, bf16[144,512]{1,0:T(8,128)(2,1)}, u32[]{:S(2)}, u32[]{:S(2)}) collective-permute-start(bf16[144,512]{1,0:T(8,128)(2,1)} %get-tuple-element.105.refs_4_.refs_3_), channel_id=1, source_target_pairs={{0,1},{1,0},{2,3},{3,2},{4,5},{5,4},{6,7},{7,6},{8,9},{9,8},{10,11... | collective-permute-start | bytes 442376 | tf_op jit(solution)/shard_map/ppermute | solution.py:138
  77.7 4.7 %collective-permute-start.23 = (bf16[144,512]{1,0:T(8,128)(2,1)}, bf16[144,512]{1,0:T(8,128)(2,1)}, u32[]{:S(2)}, u32[]{:S(2)}) collective-permute-start(bf16[144,512]{1,0:T(8,128)(2,1)} %get-tuple-element.106.refs_6_.refs_2_), channel_id=1, source_target_pairs={{0,1},{1,0},{2,3},{3,2},{4,5},{5,4},{6,7},{7,6},{8,9},{9,8},{10,11... | collective-permute-start | bytes 442376 | tf_op jit(solution)/shard_map/ppermute | solution.py:138
  78.2 4.2 %collective-permute-start.24 = (bf16[144,512]{1,0:T(8,128)(2,1)}, bf16[144,512]{1,0:T(8,128)(2,1)}, u32[]{:S(2)}, u32[]{:S(2)}) collective-permute-start(bf16[144,512]{1,0:T(8,128)(2,1)} %get-tuple-element.107.refs_8_.refs_1_), channel_id=1, source_target_pairs={{0,1},{1,0},{2,3},{3,2},{4,5},{5,4},{6,7},{7,6},{8,9},{9,8},{10,11... | collective-permute-start | bytes 442376 | tf_op jit(solution)/shard_map/ppermute | solution.py:138
  78.3 12.5 %collective-permute-start.31 = (bf16[144,512]{1,0:T(8,128)(2,1)}, bf16[144,512]{1,0:T(8,128)(2,1)}, u32[]{:S(2)}, u32[]{:S(2)}) collective-permute-start(bf16[144,512]{1,0:T(8,128)(2,1)} %shard_map.254.refs_0_), channel_id=1, source_target_pairs={{0,16},{8,24},{16,0},{24,8},{1,17},{9,25},{17,1},{25,9},{2,18},{10... | collective-permute-start | bytes 442376 | tf_op jit(solution)/shard_map/ppermute | solution.py:138
  80.9 11.4 %collective-permute-start.30 = (bf16[144,512]{1,0:T(8,128)(2,1)}, bf16[144,512]{1,0:T(8,128)(2,1)}, u32[]{:S(2)}, u32[]{:S(2)}) collective-permute-start(bf16[144,512]{1,0:T(8,128)(2,1)} %shard_map.254.refs_0_), channel_id=1, source_target_pairs={{0,8},{8,0},{16,24},{24,16},{1,9},{9,1},{17,25},{25,17},{2,10},{10... | collective-permute-start | bytes 442376 | tf_op jit(solution)/shard_map/ppermute | solution.py:138
  88.2 14.0 %collective-permute-start.25 = (bf16[16,4608]{1,0:T(8,128)(2,1)}, bf16[16,4608]{1,0:T(8,128)(2,1)}, u32[]{:S(2)}, u32[]{:S(2)}) collective-permute-start(bf16[16,4608]{1,0:T(8,128)(2,1)} %get-tuple-element.117), channel_id=1, source_target_pairs={{0,8},{8,0},{16,24},{24,16},{1,9},{9,1},{17,25},{25,17},{2,10},{10... | collective-permute-start | bytes 442376 | tf_op jit(solution)/shard_map/ppermute | solution.py:138
  88.7 24.0 %collective-permute-start.39 = (bf16[432,512]{1,0:T(8,128)(2,1)}, bf16[432,512]{1,0:T(8,128)(2,1)}, u32[]{:S(2)}, u32[]{:S(2)}) collective-permute-start(bf16[432,512]{1,0:T(8,128)(2,1)} %shard_map.257.refs_13_), channel_id=1, source_target_pairs={{0,2},{1,3},{2,0},{3,1},{4,6},{5,7},{6,4},{7,5},{8,10},{9,11},{10,... | collective-permute-start | bytes 1327112 | tf_op jit(solution)/shard_map/ppermute | solution.py:138
  89.9 22.9 %collective-permute-start.38 = (bf16[432,512]{1,0:T(8,128)(2,1)}, bf16[432,512]{1,0:T(8,128)(2,1)}, u32[]{:S(2)}, u32[]{:S(2)}) collective-permute-start(bf16[432,512]{1,0:T(8,128)(2,1)} %shard_map.257.refs_13_), channel_id=1, source_target_pairs={{0,4},{1,5},{2,6},{3,7},{4,0},{5,1},{6,2},{7,3},{8,12},{9,13},{10,... | collective-permute-start | bytes 1327112 | tf_op jit(solution)/shard_map/ppermute | solution.py:138
  90.8 22.5 %collective-permute-start.37 = (bf16[432,512]{1,0:T(8,128)(2,1)}, bf16[432,512]{1,0:T(8,128)(2,1)}, u32[]{:S(2)}, u32[]{:S(2)}) collective-permute-start(bf16[432,512]{1,0:T(8,128)(2,1)} %shard_map.257.refs_13_), channel_id=1, source_target_pairs={{0,6},{1,7},{2,4},{3,5},{4,2},{5,3},{6,0},{7,1},{8,14},{9,15},{10,... | collective-permute-start | bytes 1327112 | tf_op jit(solution)/shard_map/ppermute | solution.py:138
  92.2 13.1 %collective-permute-start.32 = (bf16[144,512]{1,0:T(8,128)(2,1)}, bf16[144,512]{1,0:T(8,128)(2,1)}, u32[]{:S(2)}, u32[]{:S(2)}) collective-permute-start(bf16[144,512]{1,0:T(8,128)(2,1)} %shard_map.255), channel_id=1, source_target_pairs={{0,24},{8,16},{16,8},{24,0},{1,25},{9,17},{17,9},{25,1},{2,26},{10... | collective-permute-start | bytes 442376 | tf_op jit(solution)/shard_map/ppermute | solution.py:138
  103.9 9.9 %collective-permute-start.26 = (bf16[16,4608]{1,0:T(8,128)(2,1)}, bf16[16,4608]{1,0:T(8,128)(2,1)}, u32[]{:S(2)}, u32[]{:S(2)}) collective-permute-start(bf16[16,4608]{1,0:T(8,128)(2,1)} %add_convert_fusion.4), channel_id=1, source_target_pairs={{0,16},{8,24},{16,0},{24,8},{1,17},{9,25},{17,1},{25,9},{2,18},{10... | collective-permute-start | bytes 442376 | tf_op jit(solution)/shard_map/ppermute | solution.py:138
  105.4 8.0 %collective-permute-start.27 = (bf16[16,3328]{1,0:T(8,128)(2,1)}, bf16[16,3328]{1,0:T(8,128)(2,1)}, u32[]{:S(2)}, u32[]{:S(2)}) collective-permute-start(bf16[16,3328]{1,0:T(8,128)(2,1)} %get-tuple-element.128), channel_id=1, source_target_pairs={{0,8},{8,0},{16,24},{24,16},{1,9},{9,1},{17,25},{25,17},{2,10},{10... | collective-permute-start | bytes 319496 | tf_op jit(solution)/shard_map/ppermute | solution.py:138
  112.7 2.9 %collective-permute-start.36 = (bf16[432,512]{1,0:T(8,128)(2,1)}, bf16[432,512]{1,0:T(8,128)(2,1)}, u32[]{:S(2)}, u32[]{:S(2)}) collective-permute-start(bf16[432,512]{1,0:T(8,128)(2,1)} %shard_map.257.refs_13_), channel_id=1, source_target_pairs={{0,1},{1,0},{2,3},{3,2},{4,5},{5,4},{6,7},{7,6},{8,9},{9,8},{10,11... | collective-permute-start | bytes 1327112 | tf_op jit(solution)/shard_map/ppermute | solution.py:138
  112.8 3.2 %collective-permute-start.33 = (bf16[144,512]{1,0:T(8,128)(2,1)}, bf16[144,512]{1,0:T(8,128)(2,1)}, u32[]{:S(2)}, u32[]{:S(2)}) collective-permute-start(bf16[144,512]{1,0:T(8,128)(2,1)} %get-tuple-element.138.refs_1_), channel_id=1, source_target_pairs={{0,1},{1,0},{2,3},{3,2},{4,5},{5,4},{6,7},{7,6},{8,9},{9,8},{10,11... | collective-permute-start | bytes 442376 | tf_op jit(solution)/shard_map/ppermute | solution.py:138
  113.3 2.8 %collective-permute-start.34 = (bf16[144,512]{1,0:T(8,128)(2,1)}, bf16[144,512]{1,0:T(8,128)(2,1)}, u32[]{:S(2)}, u32[]{:S(2)}) collective-permute-start(bf16[144,512]{1,0:T(8,128)(2,1)} %get-tuple-element.139.refs_2_), channel_id=1, source_target_pairs={{0,1},{1,0},{2,3},{3,2},{4,5},{5,4},{6,7},{7,6},{8,9},{9,8},{10,11... | collective-permute-start | bytes 442376 | tf_op jit(solution)/shard_map/ppermute | solution.py:138
  113.4 4.6 %collective-permute-start.35 = (bf16[144,512]{1,0:T(8,128)(2,1)}, bf16[144,512]{1,0:T(8,128)(2,1)}, u32[]{:S(2)}, u32[]{:S(2)}) collective-permute-start(bf16[144,512]{1,0:T(8,128)(2,1)} %get-tuple-element.140.refs_3_), channel_id=1, source_target_pairs={{0,1},{1,0},{2,3},{3,2},{4,5},{5,4},{6,7},{7,6},{8,9},{9,8},{10,11... | collective-permute-start | bytes 442376 | tf_op jit(solution)/shard_map/ppermute | solution.py:138
  113.8 7.0 %collective-permute-start.40 = (bf16[432,512]{1,0:T(8,128)(2,1)}, bf16[432,512]{1,0:T(8,128)(2,1)}, u32[]{:S(2)}, u32[]{:S(2)}) collective-permute-start(bf16[432,512]{1,0:T(8,128)(2,1)} %get-tuple-element.144.refs_15_), channel_id=1, source_target_pairs={{0,1},{1,0},{2,3},{3,2},{4,5},{5,4},{6,7},{7,6},{8,9},{9,8},{10,11... | collective-permute-start | bytes 1327112 | tf_op jit(solution)/shard_map/ppermute | solution.py:138
  115.6 5.8 %collective-permute-start.41 = (bf16[432,512]{1,0:T(8,128)(2,1)}, bf16[432,512]{1,0:T(8,128)(2,1)}, u32[]{:S(2)}, u32[]{:S(2)}) collective-permute-start(bf16[432,512]{1,0:T(8,128)(2,1)} %get-tuple-element.145.refs_17_), channel_id=1, source_target_pairs={{0,1},{1,0},{2,3},{3,2},{4,5},{5,4},{6,7},{7,6},{8,9},{9,8},{10,11... | collective-permute-start | bytes 1327112 | tf_op jit(solution)/shard_map/ppermute | solution.py:138
  116.0 6.4 %collective-permute-start.42 = (bf16[432,512]{1,0:T(8,128)(2,1)}, bf16[432,512]{1,0:T(8,128)(2,1)}, u32[]{:S(2)}, u32[]{:S(2)}) collective-permute-start(bf16[432,512]{1,0:T(8,128)(2,1)} %get-tuple-element.146.refs_19_), channel_id=1, source_target_pairs={{0,1},{1,0},{2,3},{3,2},{4,5},{5,4},{6,7},{7,6},{8,9},{9,8},{10,11... | collective-permute-start | bytes 1327112 | tf_op jit(solution)/shard_map/ppermute | solution.py:138
  116.1 20.0 %collective-permute-start.29 = (bf16[16,3328]{1,0:T(8,128)(2,1)}, bf16[16,3328]{1,0:T(8,128)(2,1)}, u32[]{:S(2)}, u32[]{:S(2)}) collective-permute-start(bf16[16,3328]{1,0:T(8,128)(2,1)} %add_convert_fusion.8), channel_id=1, source_target_pairs={{0,16},{8,24},{16,0},{24,8},{1,17},{9,25},{17,1},{25,9},{2,18},{10... | collective-permute-start | bytes 319496 | tf_op jit(solution)/shard_map/ppermute | solution.py:138
  118.1 21.1 %collective-permute-start.46 = (bf16[32,1280]{1,0:T(8,128)(2,1)}, bf16[32,1280]{1,0:T(8,128)(2,1)}, u32[]{:S(2)}, u32[]{:S(2)}) collective-permute-start(bf16[32,1280]{1,0:T(8,128)(2,1)} %get-tuple-element.148), channel_id=1, source_target_pairs={{0,24},{8,16},{16,8},{24,0},{1,25},{9,17},{17,9},{25,1},{2,26},{10... | collective-permute-start | bytes 245768 | tf_op jit(solution)/shard_map/ppermute | solution.py:138
  120.8 18.9 %collective-permute-start.45 = (bf16[32,1280]{1,0:T(8,128)(2,1)}, bf16[32,1280]{1,0:T(8,128)(2,1)}, u32[]{:S(2)}, u32[]{:S(2)}) collective-permute-start(bf16[32,1280]{1,0:T(8,128)(2,1)} %get-tuple-element.148), channel_id=1, source_target_pairs={{0,16},{8,24},{16,0},{24,8},{1,17},{9,25},{17,1},{25,9},{2,18},{10... | collective-permute-start | bytes 245768 | tf_op jit(solution)/shard_map/ppermute | solution.py:138
  121.4 19.8 %collective-permute-start.44 = (bf16[32,1280]{1,0:T(8,128)(2,1)}, bf16[32,1280]{1,0:T(8,128)(2,1)}, u32[]{:S(2)}, u32[]{:S(2)}) collective-permute-start(bf16[32,1280]{1,0:T(8,128)(2,1)} %get-tuple-element.148), channel_id=1, source_target_pairs={{0,8},{8,0},{16,24},{24,16},{1,9},{9,1},{17,25},{25,17},{2,10},{10... | collective-permute-start | bytes 245768 | tf_op jit(solution)/shard_map/ppermute | solution.py:138
  122.5 19.8 %collective-permute-start.28 = (bf16[16,4608]{1,0:T(8,128)(2,1)}, bf16[16,4608]{1,0:T(8,128)(2,1)}, u32[]{:S(2)}, u32[]{:S(2)}) collective-permute-start(bf16[16,4608]{1,0:T(8,128)(2,1)} %add_convert_fusion.3.refs_2_), channel_id=1, source_target_pairs={{0,8},{8,0},{16,24},{24,16},{1,9},{9,1},{17,25},{25,17},{2,10},{10... | collective-permute-start | bytes 442376 | tf_op jit(solution)/shard_map/ppermute | solution.py:138
  137.7 8.5 %collective-permute-start.47 = (bf16[144,512]{1,0:T(8,128)(2,1)}, bf16[144,512]{1,0:T(8,128)(2,1)}, u32[]{:S(2)}, u32[]{:S(2)}) collective-permute-start(bf16[144,512]{1,0:T(8,128)(2,1)} %get-tuple-element.150), channel_id=1, source_target_pairs={{0,2},{1,3},{2,0},{3,1},{4,6},{5,7},{6,4},{7,5},{8,10},{9,11},{10,... | collective-permute-start | bytes 442376 | tf_op jit(solution)/shard_map/ppermute | solution.py:138
  139.2 8.0 %collective-permute-start.48 = (bf16[144,512]{1,0:T(8,128)(2,1)}, bf16[144,512]{1,0:T(8,128)(2,1)}, u32[]{:S(2)}, u32[]{:S(2)}) collective-permute-start(bf16[144,512]{1,0:T(8,128)(2,1)} %get-tuple-element.151), channel_id=1, source_target_pairs={{0,4},{1,5},{2,6},{3,7},{4,0},{5,1},{6,2},{7,3},{8,12},{9,13},{10,... | collective-permute-start | bytes 442376 | tf_op jit(solution)/shard_map/ppermute | solution.py:138
  139.7 7.5 %collective-permute-start.49 = (bf16[144,512]{1,0:T(8,128)(2,1)}, bf16[144,512]{1,0:T(8,128)(2,1)}, u32[]{:S(2)}, u32[]{:S(2)}) collective-permute-start(bf16[144,512]{1,0:T(8,128)(2,1)} %get-tuple-element.152), channel_id=1, source_target_pairs={{0,6},{1,7},{2,4},{3,5},{4,2},{5,3},{6,0},{7,1},{8,14},{9,15},{10,... | collective-permute-start | bytes 442376 | tf_op jit(solution)/shard_map/ppermute | solution.py:138
  141.2 5.0 %collective-permute-start.43 = (bf16[16,3328]{1,0:T(8,128)(2,1)}, bf16[16,3328]{1,0:T(8,128)(2,1)}, u32[]{:S(2)}, u32[]{:S(2)}) collective-permute-start(bf16[16,3328]{1,0:T(8,128)(2,1)} %add_convert_fusion.7.refs_4_), channel_id=1, source_target_pairs={{0,8},{8,0},{16,24},{24,16},{1,9},{9,1},{17,25},{25,17},{2,10},{10... | collective-permute-start | bytes 319496 | tf_op jit(solution)/shard_map/ppermute | solution.py:138
  (2 other events, 4.4 us)
